TPU v7x, 32 devices: a whole 2x2x4 slice. The times are simulated.
32 devices in a mesh: groups: 2 (over y), dp: 16 (over z, x, core), basis: 1.
Axes of the slice: x: 2, y: 2, z: 4, core: 2. Of those that a mesh axis runs over, the one named last changes fastest.
Arguments:
- factors_in: bfloat16 [128, 8192], P(('groups', 'dp'), 'basis'), parts along dimension 0, may hold values from -6 to 6
- factors_out: bfloat16 [128, 8192], P(('groups', 'dp'), 'basis'), parts along dimension 0, may hold values from -0.59765625 to 0.59765625
- basis_in: bfloat16 [8192, 8192], P('basis', 'dp'), may hold values from -0.0625 to 0.0625
- basis_out: bfloat16 [8192, 8192], P('basis', 'dp'), may hold values from -0.0625 to 0.0625
- eigvals: bfloat16 [8192, 8192], P('dp'), may hold values from 0.5 to 4
- live_counts: int32 [32], P(('groups', 'dp')), parts along dimension 0, may hold values from 1 to 4, 48 in all
Outputs:
- eigen_grads: bfloat16 [8, 8192, 8192], P(('groups', 'basis'), 'dp'), parts along dimension 0
There are 2 independent parts, one for each index of `groups`. A program takes and returns all parts, laid end to end along the dimension named above; an argument that names none is the same for every part. Nothing has to cross between parts.
Inputs may be any that keep to these rules, and one draw needn't show every extreme that they name: `live_counts`: the live tokens of each dp index fill its first slots.
All inputs are finite; a program needn't handle non-finite values. No bound on the sum of `live_counts` on one device may be relied on, other than what follows from the above.
Results may differ from a plain program's by a relative error of at most 0.0057.
Values may be sent and summed in bfloat16 or wider, within the bound.
No kernel may reach another device: no remote copies, remote signals or barrier semaphores. Data moves between devices by JAX's collectives and lax.ppermute only.
A program may use at most 128 MiB of HBM per device.

v0:
```python
import jax
import jax.numpy as jnp
from jax import lax
from jax.sharding import PartitionSpec as P

CAND = 4


def per_device(factors_in, factors_out, basis_in, basis_out, eigvals, live_counts):
    slot_rows = factors_in.shape[0]
    keep = (lax.iota(jnp.int32, slot_rows) < live_counts[0])[:, None]
    masked = jnp.where(keep, factors_in, jnp.zeros_like(factors_in))
    partial_in = jnp.dot(
        lax.all_gather(masked, "dp", axis=0, tiled=True),
        basis_in,
        preferred_element_type=jnp.float32,
    )
    partial_out = jnp.dot(
        lax.all_gather(factors_out, "dp", axis=0, tiled=True),
        basis_out,
        preferred_element_type=jnp.float32,
    )
    halves = lax.axis_size("basis")
    all_rows = partial_in.shape[0]
    share = all_rows // halves
    summed_in, summed_out = lax.psum((partial_in, partial_out), "basis")
    first = lax.axis_index("basis") * share
    summed_in = lax.dynamic_slice_in_dim(summed_in, first, share, 0)
    summed_out = lax.dynamic_slice_in_dim(summed_out, first, share, 0)
    proj_in = summed_in.astype(jnp.bfloat16)
    proj_out = summed_out.astype(jnp.bfloat16)
    cand_local = CAND // halves
    per_cand = share // cand_local
    block_cols = proj_out.shape[1]
    pout_grouped = proj_out.reshape(cand_local, per_cand, block_cols)
    shifted = eigvals.astype(jnp.float32) + 0.01
    piece = lax.all_gather(proj_in, "dp", axis=1, tiled=True)
    width = piece.shape[1]
    pin_grouped = piece.reshape(cand_local, per_cand, width)
    summed = jnp.einsum(
        "ati,atj->aij", pout_grouped, pin_grouped, preferred_element_type=jnp.float32
    )
    return (summed / shifted[None, :, :]).astype(jnp.bfloat16)


def solution(mesh):
    placed = (
        P(("groups", "dp"), "basis"),
        P(("groups", "dp"), "basis"),
        P("basis", "dp"),
        P("basis", "dp"),
        P("dp", None),
        P(("groups", "dp")),
    )
    return jax.shard_map(
        per_device,
        mesh=mesh,
        in_specs=placed,
        out_specs=P(("groups", "basis"), "dp", None),
        check_vma=False,
    )
```

profile of v0, /device:TPU:0, one launch (start us, length us, event | category | flops | bytes accessed | tf_op | source)
XLA Modules:
  0.0 154.0 jit_solution(6167103966326941584)
XLA Ops:
  6.5 0.0 all-gather.10.cloned.1.call-start
  7.2 1.6 %select_bitcast_fusion = bf16[1,4,8192]{2,1,0:T(4,128)(2,1)} fusion(bf16[4,8192]{1,0:T(4,128)(2,1)} %param.6, pred[4]{0:T(512)(128)(4,1)S(1)} %iota_compare_fusion), kind=kLoop, calls=%fused_computation.4 | loop fusion | flops 32768 | bytes 131076
  8.8 0.0 all-gather.10.cloned.1.call-update
  8.8 0.0 all-gather.8.cloned.1.call-start
  8.8 0.7 all-gather.8.cloned.1.call-update
  9.5 0.0 all-gather.6.cloned.1.call-start
  9.6 40.6 %all-gather.10.cloned.1.call-done = bf16[16,4,8192]{2,1,0:T(4,128)(2,1)} async-done(((bf16[1,4,8192]{2,1,0:T(4,128)(2,1)}), bf16[16,4,8192]{2,1,0:T(4,128)(2,1)}) %all-gather.10.cloned.1.call-update) | async-done | bytes 1048592 | tf_op jit(solution)/shard_map/all_gather | solution.py:14
  50.2 1.3 reshape.16
  51.5 5.6 %convolution_convert_fusion = bf16[64,512]{1,0:T(8,128)(2,1)} fusion(bf16[64,8192]{1,0:T(8,128)(2,1)S(1)} %reshape.16, bf16[8192,512]{1,0:T(8,128)(2,1)} %param.8), kind=kOutput, calls=%fused_computation.2 | convolution fusion | flops 536903680 | bytes 9502720 | tf_op jit(solution)/shard_map/dot_general | solution.py:13
  57.1 0.0 all-gather.6.cloned.1.call-update
  57.1 11.5 %convert_add_fusion = f32[512,8192]{1,0:T(8,128)} fusion(bf16[512,8192]{1,0:T(8,128)(2,1)} %param.10), kind=kLoop, calls=%fused_computation.1 | loop fusion | flops 8388608 | bytes 25165824 | tf_op jit(solution)/shard_map/add | solution.py:36
  68.6 20.6 %all-gather.8.cloned.1.call-done = bf16[16,4,8192]{2,1,0:T(4,128)(2,1)} async-done(((bf16[1,4,8192]{2,1,0:T(4,128)(2,1)}), bf16[16,4,8192]{2,1,0:T(4,128)(2,1)}) %all-gather.8.cloned.1.call-update) | async-done | bytes 1048592 | tf_op jit(solution)/shard_map/all_gather | solution.py:19
  89.2 1.3 reshape.14
  90.6 4.9 %convolution_convert_fusion.1 = bf16[64,512]{1,0:T(8,128)(2,1)S(1)} fusion(bf16[64,8192]{1,0:T(8,128)(2,1)S(1)} %reshape.14, bf16[8192,512]{1,0:T(8,128)(2,1)} %param.9), kind=kOutput, calls=%fused_computation.3 | convolution fusion | flops 536903680 | bytes 9502720 | tf_op jit(solution)/shard_map/dot_general | solution.py:18
  95.5 31.6 %all-gather.6.cloned.1.call-done = bf16[64,8192]{1,0:T(8,128)(2,1)} async-done(((bf16[64,512]{1,0:T(8,128)(2,1)}), bf16[64,8192]{1,0:T(8,128)(2,1)}) %all-gather.6.cloned.1.call-update) | async-done | bytes 1048592 | tf_op jit(solution)/shard_map/all_gather | solution.py:37
  127.2 20.3 %divide_convert_fusion = bf16[4,512,8192]{2,1,0:T(8,128)(2,1)} fusion(f32[512,8192]{1,0:T(8,128)} %convert_add_fusion, bf16[4,16,512]{2,1,0:T(8,128)(2,1)S(1)} %bitcast.13, bf16[4,16,8192]{2,1,0:T(8,128)(2,1)} %bitcast.15), kind=kOutput, calls=%fused_computation | convolution fusion | flops 570425344 | bytes 51445760 | tf_op jit(solution)/shard_map/ati,atj->aij/dot_general | solution.py:40
  (1 shorter events, 0.0 us)
Async XLA Ops:
  6.5 43.7 %all-gather.10.cloned.1.call-start = ((), (), s32[]{:S(2)}) async-start(), calls=%async_computation.2 | async-start | bytes 1114112 | tf_op jit(solution)/shard_map/all_gather | solution.py:14
  8.8 80.4 %all-gather.8.cloned.1.call-start = ((), (), s32[]{:S(2)}) async-start(), calls=%async_computation.1 | async-start | bytes 1114112 | tf_op jit(solution)/shard_map/all_gather | solution.py:19
  9.5 117.6 %all-gather.6.cloned.1.call-start = ((), (), s32[]{:S(2)}) async-start(), calls=%async_computation | async-start | bytes 1114112 | tf_op jit(solution)/shard_map/all_gather | solution.py:37
Sparse Core Ops, SparseCore 0:
  9.5 40.6 all-gather.9
  52.3 36.8 all-gather.7
  91.4 35.7 all-gather.5
where the time goes:
time: 154 us
  waiting for transfers between devices  93.6 us (61%)
  matrix products  30.8 us (20%)
  between operations  13.8 us (9%)
  other arithmetic  13.1 us (9%)
  local copies, waits for them, and re-layouts  2.67 us (2%)
    all_gather x1, waiting for transfers between devices, per_device(): lax.all_gather(masked, 'dp', axis=0, tiled=True)  40.6 us
    all_gather x1, waiting for transfers between devices, per_device(): piece = lax.all_gather(proj_in, 'dp', axis=1, tiled=True)  31.6 us
    all_gather x1, waiting for transfers between devices, per_device(): lax.all_gather(factors_out, 'dp', axis=0, tiled=True)  20.6 us
    dot_general x1, matrix products, per_device(): jnp.einsum('ati,atj->aij', pout_grouped, pin_grouped, preferred_element_t...  20.3 us
    add x1, other arithmetic, per_device(): shifted = eigvals.astype(jnp.float32) + 0.01  11.5 us
    dot_general x1, matrix products, per_device(): jnp.dot(lax.all_gather(masked, 'dp', axis=0, tiled=True), basis_in, prefe...  5.57 us
    dot_general x1, matrix products, per_device(): jnp.dot(lax.all_gather(factors_out, 'dp', axis=0, tiled=True), basis_out,...  4.94 us
  transfers between devices with their start and end apart: 3, of which 3 were waited for; matrix products, arithmetic and copies ran while one was open for 16% of the time, Pallas kernels for 0%

commit v1 on v0

v1 whole, which is shorter than its diff:
```python
import functools

import jax
import jax.numpy as jnp
from jax import lax
from jax.experimental import pallas as pl
from jax.experimental.pallas import tpu as pltpu
from jax.sharding import PartitionSpec as P

CAND = 4
KBLK = 1024


def general(factors_in, factors_out, basis_in, basis_out, eigvals, live_counts):
    slot_rows = factors_in.shape[0]
    keep = (lax.iota(jnp.int32, slot_rows) < live_counts[0])[:, None]
    masked = jnp.where(keep, factors_in, jnp.zeros_like(factors_in))
    partial_in = jnp.dot(
        lax.all_gather(masked, "dp", axis=0, tiled=True),
        basis_in,
        preferred_element_type=jnp.float32,
    )
    partial_out = jnp.dot(
        lax.all_gather(factors_out, "dp", axis=0, tiled=True),
        basis_out,
        preferred_element_type=jnp.float32,
    )
    halves = lax.axis_size("basis")
    share = partial_in.shape[0] // halves
    summed_in, summed_out = lax.psum((partial_in, partial_out), "basis")
    first = lax.axis_index("basis") * share
    proj_in = lax.dynamic_slice_in_dim(summed_in, first, share, 0).astype(jnp.bfloat16)
    proj_out = lax.dynamic_slice_in_dim(summed_out, first, share, 0).astype(jnp.bfloat16)
    cand_local = CAND // halves
    per_cand = share // cand_local
    pout_grouped = proj_out.reshape(cand_local, per_cand, proj_out.shape[1])
    shifted = eigvals.astype(jnp.float32) + 0.01
    piece = lax.all_gather(proj_in, "dp", axis=1, tiled=True)
    pin_grouped = piece.reshape(cand_local, per_cand, piece.shape[1])
    summed = jnp.einsum(
        "ati,atj->aij", pout_grouped, pin_grouped, preferred_element_type=jnp.float32
    )
    return (summed / shifted[None, :, :]).astype(jnp.bfloat16)


def gather(x, n):
    def swap(y, m):
        return lax.ppermute(y, "dp", [(d, d ^ m) for d in range(n)])

    column = [x] + [swap(x, 4 * k) for k in range(1, n // 4)]
    pair = [swap(y, 2) for y in column]
    lane = [column, pair]
    other = [[swap(y, 1) for y in side] for side in lane]
    return [
        (other if m & 1 else lane)[(m >> 1) & 1][m >> 2] for m in range(n)
    ]


def project_kernel(n, own_ref, *refs):
    pieces, basis_ref, out_ref, rows, acc = refs[:n], refs[n], refs[n + 1], refs[n + 2], refs[n + 3]
    step = pl.program_id(0)
    width = basis_ref.shape[0]
    at = pl.multiple_of(step * width, width)
    slots = pieces[0].shape[0]
    for m in range(n):
        rows[m * slots:(m + 1) * slots, :] = pieces[m][:, pl.ds(at, width)].astype(jnp.float32)
    part = jnp.dot(
        rows[...].astype(jnp.bfloat16), basis_ref[...], preferred_element_type=jnp.float32
    )

    @pl.when(step == 0)
    def _():
        acc[...] = part

    @pl.when(step > 0)
    def _():
        acc[...] += part

    @pl.when(step == pl.num_programs(0) - 1)
    def _():
        total = n * slots
        to = lax.broadcasted_iota(jnp.int32, (total, total), 0)
        held = lax.broadcasted_iota(jnp.int32, (total, total), 1)
        where = jnp.bitwise_xor(held // slots, own_ref[0]) * slots + held % slots
        pick = jnp.where(to == where, 1.0, 0.0).astype(jnp.bfloat16)
        out_ref[...] = jnp.dot(
            pick, acc[...].astype(jnp.bfloat16), preferred_element_type=jnp.float32
        ).astype(jnp.bfloat16)


def project(own, pieces, basis):
    n = len(pieces)
    slots, depth = pieces[0].shape
    cols = basis.shape[1]
    return pl.pallas_call(
        functools.partial(project_kernel, n),
        out_shape=jax.ShapeDtypeStruct((n * slots, cols), jnp.bfloat16),
        grid_spec=pltpu.PrefetchScalarGridSpec(
            num_scalar_prefetch=1,
            grid=(depth // KBLK,),
            in_specs=[pl.BlockSpec((slots, depth), lambda k, own: (0, 0))] * n
            + [pl.BlockSpec((KBLK, cols), lambda k, own: (k, 0))],
            out_specs=pl.BlockSpec((n * slots, cols), lambda k, own: (0, 0)),
            scratch_shapes=[
                pltpu.VMEM((n * slots, KBLK), jnp.float32),
                pltpu.VMEM((n * slots, cols), jnp.float32),
            ],
        ),
        compiler_params=pltpu.CompilerParams(vmem_limit_bytes=24 << 20),
        cost_estimate=pl.CostEstimate(
            flops=2 * n * slots * depth * cols,
            bytes_accessed=2 * depth * (cols + n * slots),
            transcendentals=0,
        ),
    )(own, *pieces, basis)


def outer_kernel(n, own_ref, *refs):
    pieces, pout_ref, eig_ref, out_ref, left, held = refs[:n], *refs[n:]
    step = pl.program_id(0)
    total = pout_ref.shape[0]
    per_cand = total // CAND

    @pl.when(step == 0)
    def _():
        turned = pout_ref[...].astype(jnp.float32).T
        slot = lax.broadcasted_iota(jnp.int32, turned.shape, 1)
        for c in range(CAND):
            left[c] = jnp.where(slot // per_cand == c, turned, 0.0).astype(jnp.bfloat16)

    for m in range(n):
        @pl.when(step == m)
        def _():
            held[...] = pieces[m][...]

    scale = 1.0 / (eig_ref[...].astype(jnp.float32) + 0.01)
    for c in range(CAND):
        summed = jnp.dot(left[c], held[...], preferred_element_type=jnp.float32)
        out_ref[c] = (summed * scale).astype(jnp.bfloat16)


def outer(own, pieces, pout, eigvals):
    n = len(pieces)
    total, cols = pieces[0].shape
    rows, width = eigvals.shape
    return pl.pallas_call(
        functools.partial(outer_kernel, n),
        out_shape=jax.ShapeDtypeStruct((CAND, rows, width), jnp.bfloat16),
        grid_spec=pltpu.PrefetchScalarGridSpec(
            num_scalar_prefetch=1,
            grid=(n,),
            in_specs=[pl.BlockSpec((total, cols), lambda m, own: (0, 0))] * n
            + [
                pl.BlockSpec((total, rows), lambda m, own: (0, 0)),
                pl.BlockSpec((rows, cols), lambda m, own: (0, jnp.bitwise_xor(m, own[0]))),
            ],
            out_specs=pl.BlockSpec(
                (CAND, rows, cols), lambda m, own: (0, 0, jnp.bitwise_xor(m, own[0]))
            ),
            scratch_shapes=[
                pltpu.VMEM((CAND, rows, total), jnp.bfloat16),
                pltpu.VMEM((total, cols), jnp.bfloat16),
            ],
        ),
        compiler_params=pltpu.CompilerParams(vmem_limit_bytes=32 << 20),
        cost_estimate=pl.CostEstimate(
            flops=2 * total * rows * width,
            bytes_accessed=2 * rows * width * (CAND + 1),
            transcendentals=rows * width,
        ),
    )(own, *pieces, pout, eigvals)


def by_swaps(factors_in, factors_out, basis_in, basis_out, eigvals, live_counts):
    n = lax.axis_size("dp")
    own = lax.axis_index("dp").astype(jnp.int32)[None]
    slots = factors_in.shape[0]
    pin = project(own, gather(factors_in, n), basis_in)
    keep = (lax.iota(jnp.int32, slots) < live_counts[0])[:, None]
    masked = jnp.where(keep, factors_out, jnp.zeros_like(factors_out))
    pout = project(own, gather(masked, n), basis_out)
    return outer(own, gather(pin, n), pout, eigvals)


def solution(mesh):
    placed = (
        P(("groups", "dp"), "basis"),
        P(("groups", "dp"), "basis"),
        P("basis", "dp"),
        P("basis", "dp"),
        P("dp", None),
        P(("groups", "dp")),
    )
    chosen = by_swaps if mesh.shape["basis"] == 1 and mesh.shape["dp"] == 16 else general
    return jax.shard_map(
        chosen,
        mesh=mesh,
        in_specs=placed,
        out_specs=P(("groups", "basis"), "dp", None),
        check_vma=False,
    )
```

time: 154 us -> 75.5 us (0.49)
  waiting for transfers between devices: 93.6 us -> 12.4 us
  starting transfers between devices: 0.08 us -> 33 us
  matrix products: 30.8 us -> 0 us
  Pallas kernels: 0 us -> 23.9 us
  between operations: 13.8 us -> 0.79 us
  other arithmetic: 13.1 us -> 0.94 us
  local copies, waits for them, and re-layouts: 2.67 us -> 4.23 us
    all_gather x3 -> x0, waiting for transfers between devices: 92.9 us -> none  [the longest x1 40.6 us: per_device(): lax.all_gather(masked, 'dp', axis=0, tiled=True)]
    ppermute x0 -> x45, starting transfers between devices: none -> 33 us  [swap(): return lax.ppermute(y, 'dp', [(d, d ^ m) for d in range(n)])]
    dot_general x3 -> x0, matrix products: 30.8 us -> none  [the longest x1 20.3 us: per_device(): jnp.einsum('ati,atj->aij', pout_grouped, pin_grouped, preferred_element_t...]
    pallas_call x0 -> x3, Pallas kernels: none -> 23.9 us  [the longest x1 18.1 us: outer(): pl.pallas_call(functools.partial(outer_kernel, n), out_shape=jax.ShapeDty...]
    ppermute x0 -> x45, waiting for transfers between devices: none -> 12.4 us  [swap(): return lax.ppermute(y, 'dp', [(d, d ^ m) for d in range(n)])]
    add x1 -> x0, other arithmetic: 11.5 us -> none  [per_device(): shifted = eigvals.astype(jnp.float32) + 0.01]
    unnamed x1 -> x0, other arithmetic: 1.57 us -> none
    unnamed x2 -> x8, local copies, waits for them, and re-layouts: 2.67 us -> 4.23 us
  transfers between devices with their start and end apart: 3 -> 45, of which waited for: 3 -> 12; matrix products, arithmetic and copies ran while one was open for 16% -> 0% of each run, Pallas kernels for 0% -> 8%
where the time goes in v1:
time: 75.5 us; the launch traced here: 75.3 us
  starting transfers between devices  33 us (44%)
  Pallas kernels  23.9 us (32%)
  waiting for transfers between devices  12.4 us (16%)
  local copies, waits for them, and re-layouts  4.23 us (6%)
  other arithmetic  0.94 us (1%)
  between operations  0.79 us (1%)
    ppermute x45, starting transfers between devices, swap(): return lax.ppermute(y, 'dp', [(d, d ^ m) for d in range(n)])  33 us
    pallas_call x1, Pallas kernels, outer(): pl.pallas_call(functools.partial(outer_kernel, n), out_shape=jax.ShapeDty...  18.1 us
    ppermute x45, waiting for transfers between devices, swap(): return lax.ppermute(y, 'dp', [(d, d ^ m) for d in range(n)])  12.4 us
    pallas_call x2, Pallas kernels, project(): pl.pallas_call(functools.partial(project_kernel, n), out_shape=jax.ShapeD...  5.78 us
    unnamed x8, local copies, waits for them, and re-layouts  4.23 us
  transfers between devices with their start and end apart: 45, of which 12 were waited for; matrix products, arithmetic and copies ran while one was open for 0% of the time, Pallas kernels for 8%

profile of v1, /device:TPU:0, one launch (start us, length us, event | category | flops | bytes accessed | tf_op | source)
XLA Modules:
  0.0 75.3 jit_solution(14091810714703625323)
XLA Ops:
  0.7 0.9 %broadcast_select_fusion.refs_0_ = bf16[4,8192]{1,0:T(4,128)(2,1)S(1)} fusion(bf16[4,8192]{1,0:T(4,128)(2,1)} %param.7, pred[4]{0:T(512)(128)(4,1)S(1)} %iota_compare_fusion), kind=kLoop, calls=%fused_computation | loop fusion | flops 32768 | bytes 131076 | tf_op jit(solution)/shard_map/jit(_where)/select_n | solution.py:180
  1.6 5.1 %collective-permute-start.41 = (bf16[4,8192]{1,0:T(4,128)(2,1)S(1)}, bf16[4,8192]{1,0:T(4,128)(2,1)S(1)}, u32[]{:S(2)}, u32[]{:S(2)}) collective-permute-start(bf16[4,8192]{1,0:T(4,128)(2,1)S(1)} %broadcast_select_fusion.refs_0_), channel_id=1, source_target_pairs={{0,12},{1,13},{2,14},{3,15},{4,8},{5,9},{6,10},{7,11},{8,4},{9,5},... | collective-permute-start | bytes 196616 | tf_op jit(solution)/shard_map/ppermute | solution.py:48
  6.7 0.6 collective-permute-start.33
  7.4 1.6 %collective-permute-start.31 = (bf16[4,8192]{1,0:T(4,128)(2,1)S(1)}, bf16[4,8192]{1,0:T(4,128)(2,1)S(1)}, u32[]{:S(2)}, u32[]{:S(2)}) collective-permute-start(bf16[4,8192]{1,0:T(4,128)(2,1)S(1)} %broadcast_select_fusion.refs_0_), channel_id=1, source_target_pairs={{0,2},{1,3},{2,0},{3,1},{4,6},{5,7},{6,4},{7,5},{8,10},{9,11},{10,... | collective-permute-start | bytes 196616 | tf_op jit(solution)/shard_map/ppermute | solution.py:48
  9.0 0.3 collective-permute-done.41.refs_12_
  9.3 3.6 %collective-permute-start.7 = (bf16[4,8192]{1,0:T(4,128)(2,1)}, bf16[4,8192]{1,0:T(4,128)(2,1)S(1)}, u32[]{:S(2)}, u32[]{:S(2)}) collective-permute-start(bf16[4,8192]{1,0:T(4,128)(2,1)} %refs_0_.1), channel_id=1, source_target_pairs={{0,8},{1,9},{2,10},{3,11},{4,12},{5,13},{6,14},{7,15},{8,0},{9,1},... | collective-permute-start | bytes 196616 | tf_op jit(solution)/shard_map/ppermute | solution.py:48
  12.9 1.2 %collective-permute-start.3 = (bf16[4,8192]{1,0:T(4,128)(2,1)}, bf16[4,8192]{1,0:T(4,128)(2,1)S(1)}, u32[]{:S(2)}, u32[]{:S(2)}) collective-permute-start(bf16[4,8192]{1,0:T(4,128)(2,1)} %refs_0_.1), channel_id=1, source_target_pairs={{0,4},{1,5},{2,6},{3,7},{4,0},{5,1},{6,2},{7,3},{8,12},{9,13},{10,... | collective-permute-start | bytes 196616 | tf_op jit(solution)/shard_map/ppermute | solution.py:48
  14.1 1.5 %collective-permute-start.1 = (bf16[4,8192]{1,0:T(4,128)(2,1)}, bf16[4,8192]{1,0:T(4,128)(2,1)S(1)}, u32[]{:S(2)}, u32[]{:S(2)}) collective-permute-start(bf16[4,8192]{1,0:T(4,128)(2,1)} %refs_0_.1), channel_id=1, source_target_pairs={{0,2},{1,3},{2,0},{3,1},{4,6},{5,7},{6,4},{7,5},{8,10},{9,11},{10,... | collective-permute-start | bytes 196616 | tf_op jit(solution)/shard_map/ppermute | solution.py:48
  15.6 1.1 %collective-permute-start.11 = (bf16[4,8192]{1,0:T(4,128)(2,1)}, bf16[4,8192]{1,0:T(4,128)(2,1)S(1)}, u32[]{:S(2)}, u32[]{:S(2)}) collective-permute-start(bf16[4,8192]{1,0:T(4,128)(2,1)} %refs_0_.1), channel_id=1, source_target_pairs={{0,12},{1,13},{2,14},{3,15},{4,8},{5,9},{6,10},{7,11},{8,4},{9,5},... | collective-permute-start | bytes 196616 | tf_op jit(solution)/shard_map/ppermute | solution.py:48
  16.6 0.5 collective-permute-start.43
  17.2 0.2 collective-permute-done.3.refs_4_
  17.4 1.2 %collective-permute-done.1.refs_2_ = bf16[4,8192]{1,0:T(4,128)(2,1)S(1)} collective-permute-done((bf16[4,8192]{1,0:T(4,128)(2,1)}, bf16[4,8192]{1,0:T(4,128)(2,1)S(1)}, u32[]{:S(2)}, u32[]{:S(2)}) %collective-permute-start.1) | collective-permute-done | bytes 65568 | tf_op jit(solution)/shard_map/ppermute | solution.py:48
  18.5 1.7 %collective-permute-start.39 = (bf16[4,8192]{1,0:T(4,128)(2,1)S(1)}, bf16[4,8192]{1,0:T(4,128)(2,1)S(1)}, u32[]{:S(2)}, u32[]{:S(2)}) collective-permute-start(bf16[4,8192]{1,0:T(4,128)(2,1)S(1)} %collective-permute-done.37.refs_8_), channel_id=1, source_target_pairs={{0,2},{1,3},{2,0},{3,1},{4,6},{5,7},{6,4},{7,5},{8,10},{9,11},{10,... | collective-permute-start | bytes 196616 | tf_op jit(solution)/shard_map/ppermute | solution.py:48
  20.2 1.9 %collective-permute-done.11.refs_12_ = bf16[4,8192]{1,0:T(4,128)(2,1)S(1)} collective-permute-done((bf16[4,8192]{1,0:T(4,128)(2,1)}, bf16[4,8192]{1,0:T(4,128)(2,1)S(1)}, u32[]{:S(2)}, u32[]{:S(2)}) %collective-permute-start.11) | collective-permute-done | bytes 65568 | tf_op jit(solution)/shard_map/ppermute | solution.py:48
  22.1 0.5 collective-permute-start.35
  22.6 1.5 %collective-permute-start.9 = (bf16[4,8192]{1,0:T(4,128)(2,1)S(1)}, bf16[4,8192]{1,0:T(4,128)(2,1)S(1)}, u32[]{:S(2)}, u32[]{:S(2)}) collective-permute-start(bf16[4,8192]{1,0:T(4,128)(2,1)S(1)} %collective-permute-done.7.refs_8_), channel_id=1, source_target_pairs={{0,2},{1,3},{2,0},{3,1},{4,6},{5,7},{6,4},{7,5},{8,10},{9,11},{10,... | collective-permute-start | bytes 196616 | tf_op jit(solution)/shard_map/ppermute | solution.py:48
  24.1 0.6 collective-permute-start.5
  24.7 0.2 collective-permute-start.4
  24.9 1.5 %collective-permute-done.35.refs_6_ = bf16[4,8192]{1,0:T(4,128)(2,1)S(1)} collective-permute-done((bf16[4,8192]{1,0:T(4,128)(2,1)S(1)}, bf16[4,8192]{1,0:T(4,128)(2,1)S(1)}, u32[]{:S(2)}, u32[]{:S(2)}) %collective-permute-start.35) | collective-permute-done | bytes 65568 | tf_op jit(solution)/shard_map/ppermute | solution.py:48
  26.4 1.0 %collective-permute-start.13 = (bf16[4,8192]{1,0:T(4,128)(2,1)S(1)}, bf16[4,8192]{1,0:T(4,128)(2,1)S(1)}, u32[]{:S(2)}, u32[]{:S(2)}) collective-permute-start(bf16[4,8192]{1,0:T(4,128)(2,1)S(1)} %collective-permute-done.11.refs_12_), channel_id=1, source_target_pairs={{0,2},{1,3},{2,0},{3,1},{4,6},{5,7},{6,4},{7,5},{8,10},{9,11},{10,... | collective-permute-start | bytes 196616 | tf_op jit(solution)/shard_map/ppermute | solution.py:48
  27.5 0.5 collective-permute-start.12
  28.0 1.1 %collective-permute-done.5.refs_6_ = bf16[4,8192]{1,0:T(4,128)(2,1)S(1)} collective-permute-done((bf16[4,8192]{1,0:T(4,128)(2,1)S(1)}, bf16[4,8192]{1,0:T(4,128)(2,1)S(1)}, u32[]{:S(2)}, u32[]{:S(2)}) %collective-permute-start.5) | collective-permute-done | bytes 65568 | tf_op jit(solution)/shard_map/ppermute | solution.py:48
  29.1 0.5 collective-permute-start.6
  29.6 1.1 %collective-permute-done.13.refs_14_ = bf16[4,8192]{1,0:T(4,128)(2,1)S(1)} collective-permute-done((bf16[4,8192]{1,0:T(4,128)(2,1)S(1)}, bf16[4,8192]{1,0:T(4,128)(2,1)S(1)}, u32[]{:S(2)}, u32[]{:S(2)}) %collective-permute-start.13) | collective-permute-done | bytes 65568 | tf_op jit(solution)/shard_map/ppermute | solution.py:48
  30.7 0.5 collective-permute-start.34
  31.2 0.1 collective-permute-start.32
  31.3 0.4 collective-permute-start.44
  31.7 0.1 collective-permute-start.40
  31.8 0.1 collective-permute-done.14.refs_15_
  32.0 0.3 collective-permute-start.36
  32.3 3.4 %copy-done = bf16[8192,512]{1,0:T(8,128)(2,1)S(1)} copy-done((bf16[8192,512]{1,0:T(8,128)(2,1)S(1)}, bf16[8192,512]{1,0:T(8,128)(2,1)}, u32[]{:S(2)}) %copy-start) | copy-done | bytes 8388632
  35.6 0.8 %copy-done.3 = bf16[4,8192]{1,0:T(4,128)(2,1)S(1)} copy-done((bf16[4,8192]{1,0:T(4,128)(2,1)S(1)}, bf16[4,8192]{1,0:T(4,128)(2,1)}, u32[]{:S(2)}) %copy-start.3) | copy-done | bytes 65560
  36.5 2.9 %shard_map.64.refs_0_ = bf16[64,512]{1,0:T(8,128)(2,1)S(1)} custom-call(s32[1]{0:T(128)} %bitcast.own_ref, bf16[4,8192]{1,0:T(4,128)(2,1)S(1)} %copy-done.3, bf16[4,8192]{1,0:T(4,128)(2,1)S(1)} %collective-permute-done.refs_1_, bf16[4,8192]{1,0:T(4,128)(2,1)S(1)} %collective-permute-done.1.refs_2_, bf16[4,8192]{1,0:T(4,128)(2,1)S(1)} %collective-permute-done.2.refs_3_, ...), custom_call_target="tpu_custom_call" | custom-call | flops 536870912 | bytes 9437184 | tf_op jit(solution)/shard_map/pallas_call | solution.py:95
  39.4 1.4 %collective-permute-start.26 = (bf16[64,512]{1,0:T(8,128)(2,1)S(1)}, bf16[64,512]{1,0:T(8,128)(2,1)S(1)}, u32[]{:S(2)}, u32[]{:S(2)}) collective-permute-start(bf16[64,512]{1,0:T(8,128)(2,1)S(1)} %shard_map.64.refs_0_), channel_id=1, source_target_pairs={{0,12},{1,13},{2,14},{3,15},{4,8},{5,9},{6,10},{7,11},{8,4},{9,5},... | collective-permute-start | bytes 196616 | tf_op jit(solution)/shard_map/ppermute | solution.py:48
  40.8 3.0 %collective-permute-start.18 = (bf16[64,512]{1,0:T(8,128)(2,1)S(1)}, bf16[64,512]{1,0:T(8,128)(2,1)S(1)}, u32[]{:S(2)}, u32[]{:S(2)}) collective-permute-start(bf16[64,512]{1,0:T(8,128)(2,1)S(1)} %shard_map.64.refs_0_), channel_id=1, source_target_pairs={{0,4},{1,5},{2,6},{3,7},{4,0},{5,1},{6,2},{7,3},{8,12},{9,13},{10,... | collective-permute-start | bytes 196616 | tf_op jit(solution)/shard_map/ppermute | solution.py:48
  43.9 1.1 %collective-permute-start.16 = (bf16[64,512]{1,0:T(8,128)(2,1)S(1)}, bf16[64,512]{1,0:T(8,128)(2,1)S(1)}, u32[]{:S(2)}, u32[]{:S(2)}) collective-permute-start(bf16[64,512]{1,0:T(8,128)(2,1)S(1)} %shard_map.64.refs_0_), channel_id=1, source_target_pairs={{0,2},{1,3},{2,0},{3,1},{4,6},{5,7},{6,4},{7,5},{8,10},{9,11},{10,... | collective-permute-start | bytes 196616 | tf_op jit(solution)/shard_map/ppermute | solution.py:48
  44.9 1.4 %collective-permute-done.26.refs_12_ = bf16[64,512]{1,0:T(8,128)(2,1)S(1)} collective-permute-done((bf16[64,512]{1,0:T(8,128)(2,1)S(1)}, bf16[64,512]{1,0:T(8,128)(2,1)S(1)}, u32[]{:S(2)}, u32[]{:S(2)}) %collective-permute-start.26) | collective-permute-done | bytes 65568 | tf_op jit(solution)/shard_map/ppermute | solution.py:48
  46.3 1.1 %collective-permute-start.28 = (bf16[64,512]{1,0:T(8,128)(2,1)S(1)}, bf16[64,512]{1,0:T(8,128)(2,1)S(1)}, u32[]{:S(2)}, u32[]{:S(2)}) collective-permute-start(bf16[64,512]{1,0:T(8,128)(2,1)S(1)} %collective-permute-done.26.refs_12_), channel_id=1, source_target_pairs={{0,2},{1,3},{2,0},{3,1},{4,6},{5,7},{6,4},{7,5},{8,10},{9,11},{10,... | collective-permute-start | bytes 196616 | tf_op jit(solution)/shard_map/ppermute | solution.py:48
  47.3 1.0 %collective-permute-done.22.refs_8_ = bf16[64,512]{1,0:T(8,128)(2,1)S(1)} collective-permute-done((bf16[64,512]{1,0:T(8,128)(2,1)S(1)}, bf16[64,512]{1,0:T(8,128)(2,1)S(1)}, u32[]{:S(2)}, u32[]{:S(2)}) %collective-permute-start.22) | collective-permute-done | bytes 65568 | tf_op jit(solution)/shard_map/ppermute | solution.py:48
  48.3 1.1 %collective-permute-start.24 = (bf16[64,512]{1,0:T(8,128)(2,1)S(1)}, bf16[64,512]{1,0:T(8,128)(2,1)S(1)}, u32[]{:S(2)}, u32[]{:S(2)}) collective-permute-start(bf16[64,512]{1,0:T(8,128)(2,1)S(1)} %collective-permute-done.22.refs_8_), channel_id=1, source_target_pairs={{0,2},{1,3},{2,0},{3,1},{4,6},{5,7},{6,4},{7,5},{8,10},{9,11},{10,... | collective-permute-start | bytes 196616 | tf_op jit(solution)/shard_map/ppermute | solution.py:48
  49.3 0.2 collective-permute-start.23
  49.6 1.0 %collective-permute-start.20 = (bf16[64,512]{1,0:T(8,128)(2,1)S(1)}, bf16[64,512]{1,0:T(8,128)(2,1)S(1)}, u32[]{:S(2)}, u32[]{:S(2)}) collective-permute-start(bf16[64,512]{1,0:T(8,128)(2,1)S(1)} %collective-permute-done.18.refs_4_), channel_id=1, source_target_pairs={{0,2},{1,3},{2,0},{3,1},{4,6},{5,7},{6,4},{7,5},{8,10},{9,11},{10,... | collective-permute-start | bytes 196616 | tf_op jit(solution)/shard_map/ppermute | solution.py:48
  50.6 0.5 collective-permute-start.17
  51.1 2.1 %collective-permute-done.24.refs_10_ = bf16[64,512]{1,0:T(8,128)(2,1)S(1)} collective-permute-done((bf16[64,512]{1,0:T(8,128)(2,1)S(1)}, bf16[64,512]{1,0:T(8,128)(2,1)S(1)}, u32[]{:S(2)}, u32[]{:S(2)}) %collective-permute-start.24) | collective-permute-done | bytes 65568 | tf_op jit(solution)/shard_map/ppermute | solution.py:48
  53.2 0.5 collective-permute-start.25
  53.7 0.5 collective-permute-done.20.refs_6_
  54.2 2.9 %shard_map.65.refs_16_ = bf16[64,512]{1,0:T(8,128)(2,1)S(1)} custom-call(s32[1]{0:T(128)} %bitcast.own_ref, bf16[4,8192]{1,0:T(4,128)(2,1)S(1)} %broadcast_select_fusion.refs_0_, bf16[4,8192]{1,0:T(4,128)(2,1)S(1)} %collective-permute-done.30.refs_1_, bf16[4,8192]{1,0:T(4,128)(2,1)S(1)} %collective-permute-done.31.refs_2_, ...), custom_call_target="tpu_custom_call" | custom-call | flops 536870912 | bytes 9437184 | tf_op jit(solution)/shard_map/pallas_call | solution.py:95
  57.2 18.1 %shard_map.66 = bf16[4,512,8192]{2,1,0:T(8,128)(2,1)} custom-call(s32[1]{0:T(128)} %bitcast.own_ref, bf16[64,512]{1,0:T(8,128)(2,1)S(1)} %shard_map.64.refs_0_, bf16[64,512]{1,0:T(8,128)(2,1)S(1)} %collective-permute-done.15.refs_1_, bf16[64,512]{1,0:T(8,128)(2,1)S(1)} %collective-permute-done.16.refs_2_, ...), custom_call_target="tpu_custom_call" | custom-call | flops 536870912 | bytes 41943040 | tf_op jit(solution)/shard_map/pallas_call | solution.py:146
  (55 shorter events, 0.2 us)
Async XLA Ops:
  1.6 7.7 %collective-permute-start.41 = (bf16[4,8192]{1,0:T(4,128)(2,1)S(1)}, bf16[4,8192]{1,0:T(4,128)(2,1)S(1)}, u32[]{:S(2)}, u32[]{:S(2)}) collective-permute-start(bf16[4,8192]{1,0:T(4,128)(2,1)S(1)} %broadcast_select_fusion.refs_0_), channel_id=1, source_target_pairs={{0,12},{1,13},{2,14},{3,15},{4,8},{5,9},{6,10},{7,11},{8,4},{9,5},... | collective-permute-start | bytes 196616 | tf_op jit(solution)/shard_map/ppermute | solution.py:48
  6.7 6.2 %collective-permute-start.37 = (bf16[4,8192]{1,0:T(4,128)(2,1)S(1)}, bf16[4,8192]{1,0:T(4,128)(2,1)S(1)}, u32[]{:S(2)}, u32[]{:S(2)}) collective-permute-start(bf16[4,8192]{1,0:T(4,128)(2,1)S(1)} %broadcast_select_fusion.refs_0_), channel_id=1, source_target_pairs={{0,8},{1,9},{2,10},{3,11},{4,12},{5,13},{6,14},{7,15},{8,0},{9,1},... | collective-permute-start | bytes 196616 | tf_op jit(solution)/shard_map/ppermute | solution.py:48
  6.7 7.3 %collective-permute-start.33 = (bf16[4,8192]{1,0:T(4,128)(2,1)S(1)}, bf16[4,8192]{1,0:T(4,128)(2,1)S(1)}, u32[]{:S(2)}, u32[]{:S(2)}) collective-permute-start(bf16[4,8192]{1,0:T(4,128)(2,1)S(1)} %broadcast_select_fusion.refs_0_), channel_id=1, source_target_pairs={{0,4},{1,5},{2,6},{3,7},{4,0},{5,1},{6,2},{7,3},{8,12},{9,13},{10,... | collective-permute-start | bytes 196616 | tf_op jit(solution)/shard_map/ppermute | solution.py:48
  7.4 8.2 %collective-permute-start.31 = (bf16[4,8192]{1,0:T(4,128)(2,1)S(1)}, bf16[4,8192]{1,0:T(4,128)(2,1)S(1)}, u32[]{:S(2)}, u32[]{:S(2)}) collective-permute-start(bf16[4,8192]{1,0:T(4,128)(2,1)S(1)} %broadcast_select_fusion.refs_0_), channel_id=1, source_target_pairs={{0,2},{1,3},{2,0},{3,1},{4,6},{5,7},{6,4},{7,5},{8,10},{9,11},{10,... | collective-permute-start | bytes 196616 | tf_op jit(solution)/shard_map/ppermute | solution.py:48
  9.0 6.6 %collective-permute-start.30 = (bf16[4,8192]{1,0:T(4,128)(2,1)S(1)}, bf16[4,8192]{1,0:T(4,128)(2,1)S(1)}, u32[]{:S(2)}, u32[]{:S(2)}) collective-permute-start(bf16[4,8192]{1,0:T(4,128)(2,1)S(1)} %broadcast_select_fusion.refs_0_), channel_id=1, source_target_pairs={{0,1},{1,0},{2,3},{3,2},{4,5},{5,4},{6,7},{7,6},{8,9},{9,8},{10,11... | collective-permute-start | bytes 196616 | tf_op jit(solution)/shard_map/ppermute | solution.py:48
  9.3 7.3 %collective-permute-start.7 = (bf16[4,8192]{1,0:T(4,128)(2,1)}, bf16[4,8192]{1,0:T(4,128)(2,1)S(1)}, u32[]{:S(2)}, u32[]{:S(2)}) collective-permute-start(bf16[4,8192]{1,0:T(4,128)(2,1)} %refs_0_.1), channel_id=1, source_target_pairs={{0,8},{1,9},{2,10},{3,11},{4,12},{5,13},{6,14},{7,15},{8,0},{9,1},... | collective-permute-start | bytes 196616 | tf_op jit(solution)/shard_map/ppermute | solution.py:48
  12.9 4.5 %collective-permute-start.3 = (bf16[4,8192]{1,0:T(4,128)(2,1)}, bf16[4,8192]{1,0:T(4,128)(2,1)S(1)}, u32[]{:S(2)}, u32[]{:S(2)}) collective-permute-start(bf16[4,8192]{1,0:T(4,128)(2,1)} %refs_0_.1), channel_id=1, source_target_pairs={{0,4},{1,5},{2,6},{3,7},{4,0},{5,1},{6,2},{7,3},{8,12},{9,13},{10,... | collective-permute-start | bytes 196616 | tf_op jit(solution)/shard_map/ppermute | solution.py:48
  14.1 4.5 %collective-permute-start.1 = (bf16[4,8192]{1,0:T(4,128)(2,1)}, bf16[4,8192]{1,0:T(4,128)(2,1)S(1)}, u32[]{:S(2)}, u32[]{:S(2)}) collective-permute-start(bf16[4,8192]{1,0:T(4,128)(2,1)} %refs_0_.1), channel_id=1, source_target_pairs={{0,2},{1,3},{2,0},{3,1},{4,6},{5,7},{6,4},{7,5},{8,10},{9,11},{10,... | collective-permute-start | bytes 196616 | tf_op jit(solution)/shard_map/ppermute | solution.py:48
  15.6 4.6 %collective-permute-start = (bf16[4,8192]{1,0:T(4,128)(2,1)}, bf16[4,8192]{1,0:T(4,128)(2,1)S(1)}, u32[]{:S(2)}, u32[]{:S(2)}) collective-permute-start(bf16[4,8192]{1,0:T(4,128)(2,1)} %refs_0_.1), channel_id=1, source_target_pairs={{0,1},{1,0},{2,3},{3,2},{4,5},{5,4},{6,7},{7,6},{8,9},{9,8},{10,11... | collective-permute-start | bytes 196616 | tf_op jit(solution)/shard_map/ppermute | solution.py:48
  15.6 6.5 %collective-permute-start.11 = (bf16[4,8192]{1,0:T(4,128)(2,1)}, bf16[4,8192]{1,0:T(4,128)(2,1)S(1)}, u32[]{:S(2)}, u32[]{:S(2)}) collective-permute-start(bf16[4,8192]{1,0:T(4,128)(2,1)} %refs_0_.1), channel_id=1, source_target_pairs={{0,12},{1,13},{2,14},{3,15},{4,8},{5,9},{6,10},{7,11},{8,4},{9,5},... | collective-permute-start | bytes 196616 | tf_op jit(solution)/shard_map/ppermute | solution.py:48
  16.6 6.0 %collective-permute-start.43 = (bf16[4,8192]{1,0:T(4,128)(2,1)S(1)}, bf16[4,8192]{1,0:T(4,128)(2,1)S(1)}, u32[]{:S(2)}, u32[]{:S(2)}) collective-permute-start(bf16[4,8192]{1,0:T(4,128)(2,1)S(1)} %collective-permute-done.41.refs_12_), channel_id=1, source_target_pairs={{0,2},{1,3},{2,0},{3,1},{4,6},{5,7},{6,4},{7,5},{8,10},{9,11},{10,... | collective-permute-start | bytes 196616 | tf_op jit(solution)/shard_map/ppermute | solution.py:48
  17.4 6.8 %collective-permute-start.42 = (bf16[4,8192]{1,0:T(4,128)(2,1)S(1)}, bf16[4,8192]{1,0:T(4,128)(2,1)S(1)}, u32[]{:S(2)}, u32[]{:S(2)}) collective-permute-start(bf16[4,8192]{1,0:T(4,128)(2,1)S(1)} %collective-permute-done.41.refs_12_), channel_id=1, source_target_pairs={{0,1},{1,0},{2,3},{3,2},{4,5},{5,4},{6,7},{7,6},{8,9},{9,8},{10,11... | collective-permute-start | bytes 196616 | tf_op jit(solution)/shard_map/ppermute | solution.py:48
  18.5 5.6 %collective-permute-start.39 = (bf16[4,8192]{1,0:T(4,128)(2,1)S(1)}, bf16[4,8192]{1,0:T(4,128)(2,1)S(1)}, u32[]{:S(2)}, u32[]{:S(2)}) collective-permute-start(bf16[4,8192]{1,0:T(4,128)(2,1)S(1)} %collective-permute-done.37.refs_8_), channel_id=1, source_target_pairs={{0,2},{1,3},{2,0},{3,1},{4,6},{5,7},{6,4},{7,5},{8,10},{9,11},{10,... | collective-permute-start | bytes 196616 | tf_op jit(solution)/shard_map/ppermute | solution.py:48
  20.2 4.5 %collective-permute-start.38 = (bf16[4,8192]{1,0:T(4,128)(2,1)S(1)}, bf16[4,8192]{1,0:T(4,128)(2,1)S(1)}, u32[]{:S(2)}, u32[]{:S(2)}) collective-permute-start(bf16[4,8192]{1,0:T(4,128)(2,1)S(1)} %collective-permute-done.37.refs_8_), channel_id=1, source_target_pairs={{0,1},{1,0},{2,3},{3,2},{4,5},{5,4},{6,7},{7,6},{8,9},{9,8},{10,11... | collective-permute-start | bytes 196616 | tf_op jit(solution)/shard_map/ppermute | solution.py:48
  22.1 4.3 %collective-permute-start.35 = (bf16[4,8192]{1,0:T(4,128)(2,1)S(1)}, bf16[4,8192]{1,0:T(4,128)(2,1)S(1)}, u32[]{:S(2)}, u32[]{:S(2)}) collective-permute-start(bf16[4,8192]{1,0:T(4,128)(2,1)S(1)} %collective-permute-done.33.refs_4_), channel_id=1, source_target_pairs={{0,2},{1,3},{2,0},{3,1},{4,6},{5,7},{6,4},{7,5},{8,10},{9,11},{10,... | collective-permute-start | bytes 196616 | tf_op jit(solution)/shard_map/ppermute | solution.py:48
  22.6 4.9 %collective-permute-start.9 = (bf16[4,8192]{1,0:T(4,128)(2,1)S(1)}, bf16[4,8192]{1,0:T(4,128)(2,1)S(1)}, u32[]{:S(2)}, u32[]{:S(2)}) collective-permute-start(bf16[4,8192]{1,0:T(4,128)(2,1)S(1)} %collective-permute-done.7.refs_8_), channel_id=1, source_target_pairs={{0,2},{1,3},{2,0},{3,1},{4,6},{5,7},{6,4},{7,5},{8,10},{9,11},{10,... | collective-permute-start | bytes 196616 | tf_op jit(solution)/shard_map/ppermute | solution.py:48
  24.1 3.4 %collective-permute-start.8 = (bf16[4,8192]{1,0:T(4,128)(2,1)S(1)}, bf16[4,8192]{1,0:T(4,128)(2,1)S(1)}, u32[]{:S(2)}, u32[]{:S(2)}) collective-permute-start(bf16[4,8192]{1,0:T(4,128)(2,1)S(1)} %collective-permute-done.7.refs_8_), channel_id=1, source_target_pairs={{0,1},{1,0},{2,3},{3,2},{4,5},{5,4},{6,7},{7,6},{8,9},{9,8},{10,11... | collective-permute-start | bytes 196616 | tf_op jit(solution)/shard_map/ppermute | solution.py:48
  24.1 5.0 %collective-permute-start.5 = (bf16[4,8192]{1,0:T(4,128)(2,1)S(1)}, bf16[4,8192]{1,0:T(4,128)(2,1)S(1)}, u32[]{:S(2)}, u32[]{:S(2)}) collective-permute-start(bf16[4,8192]{1,0:T(4,128)(2,1)S(1)} %collective-permute-done.3.refs_4_), channel_id=1, source_target_pairs={{0,2},{1,3},{2,0},{3,1},{4,6},{5,7},{6,4},{7,5},{8,10},{9,11},{10,... | collective-permute-start | bytes 196616 | tf_op jit(solution)/shard_map/ppermute | solution.py:48
  24.7 4.4 %collective-permute-start.4 = (bf16[4,8192]{1,0:T(4,128)(2,1)S(1)}, bf16[4,8192]{1,0:T(4,128)(2,1)S(1)}, u32[]{:S(2)}, u32[]{:S(2)}) collective-permute-start(bf16[4,8192]{1,0:T(4,128)(2,1)S(1)} %collective-permute-done.3.refs_4_), channel_id=1, source_target_pairs={{0,1},{1,0},{2,3},{3,2},{4,5},{5,4},{6,7},{7,6},{8,9},{9,8},{10,11... | collective-permute-start | bytes 196616 | tf_op jit(solution)/shard_map/ppermute | solution.py:48
  26.4 4.3 %collective-permute-start.13 = (bf16[4,8192]{1,0:T(4,128)(2,1)S(1)}, bf16[4,8192]{1,0:T(4,128)(2,1)S(1)}, u32[]{:S(2)}, u32[]{:S(2)}) collective-permute-start(bf16[4,8192]{1,0:T(4,128)(2,1)S(1)} %collective-permute-done.11.refs_12_), channel_id=1, source_target_pairs={{0,2},{1,3},{2,0},{3,1},{4,6},{5,7},{6,4},{7,5},{8,10},{9,11},{10,... | collective-permute-start | bytes 196616 | tf_op jit(solution)/shard_map/ppermute | solution.py:48
  27.5 3.2 %collective-permute-start.2 = (bf16[4,8192]{1,0:T(4,128)(2,1)S(1)}, bf16[4,8192]{1,0:T(4,128)(2,1)S(1)}, u32[]{:S(2)}, u32[]{:S(2)}) collective-permute-start(bf16[4,8192]{1,0:T(4,128)(2,1)S(1)} %collective-permute-done.1.refs_2_), channel_id=1, source_target_pairs={{0,1},{1,0},{2,3},{3,2},{4,5},{5,4},{6,7},{7,6},{8,9},{9,8},{10,11... | collective-permute-start | bytes 196616 | tf_op jit(solution)/shard_map/ppermute | solution.py:48
  27.5 3.7 %collective-permute-start.12 = (bf16[4,8192]{1,0:T(4,128)(2,1)S(1)}, bf16[4,8192]{1,0:T(4,128)(2,1)S(1)}, u32[]{:S(2)}, u32[]{:S(2)}) collective-permute-start(bf16[4,8192]{1,0:T(4,128)(2,1)S(1)} %collective-permute-done.11.refs_12_), channel_id=1, source_target_pairs={{0,1},{1,0},{2,3},{3,2},{4,5},{5,4},{6,7},{7,6},{8,9},{9,8},{10,11... | collective-permute-start | bytes 196616 | tf_op jit(solution)/shard_map/ppermute | solution.py:48
  29.1 2.2 %collective-permute-start.10 = (bf16[4,8192]{1,0:T(4,128)(2,1)S(1)}, bf16[4,8192]{1,0:T(4,128)(2,1)S(1)}, u32[]{:S(2)}, u32[]{:S(2)}) collective-permute-start(bf16[4,8192]{1,0:T(4,128)(2,1)S(1)} %collective-permute-done.9.refs_10_), channel_id=1, source_target_pairs={{0,1},{1,0},{2,3},{3,2},{4,5},{5,4},{6,7},{7,6},{8,9},{9,8},{10,11... | collective-permute-start | bytes 196616 | tf_op jit(solution)/shard_map/ppermute | solution.py:48
  29.1 2.6 %collective-permute-start.6 = (bf16[4,8192]{1,0:T(4,128)(2,1)S(1)}, bf16[4,8192]{1,0:T(4,128)(2,1)S(1)}, u32[]{:S(2)}, u32[]{:S(2)}) collective-permute-start(bf16[4,8192]{1,0:T(4,128)(2,1)S(1)} %collective-permute-done.5.refs_6_), channel_id=1, source_target_pairs={{0,1},{1,0},{2,3},{3,2},{4,5},{5,4},{6,7},{7,6},{8,9},{9,8},{10,11... | collective-permute-start | bytes 196616 | tf_op jit(solution)/shard_map/ppermute | solution.py:48
  30.7 1.3 %collective-permute-start.14 = (bf16[4,8192]{1,0:T(4,128)(2,1)S(1)}, bf16[4,8192]{1,0:T(4,128)(2,1)S(1)}, u32[]{:S(2)}, u32[]{:S(2)}) collective-permute-start(bf16[4,8192]{1,0:T(4,128)(2,1)S(1)} %collective-permute-done.13.refs_14_), channel_id=1, source_target_pairs={{0,1},{1,0},{2,3},{3,2},{4,5},{5,4},{6,7},{7,6},{8,9},{9,8},{10,11... | collective-permute-start | bytes 196616 | tf_op jit(solution)/shard_map/ppermute | solution.py:48
  30.7 8.7 %collective-permute-start.34 = (bf16[4,8192]{1,0:T(4,128)(2,1)S(1)}, bf16[4,8192]{1,0:T(4,128)(2,1)S(1)}, u32[]{:S(2)}, u32[]{:S(2)}) collective-permute-start(bf16[4,8192]{1,0:T(4,128)(2,1)S(1)} %collective-permute-done.33.refs_4_), channel_id=1, source_target_pairs={{0,1},{1,0},{2,3},{3,2},{4,5},{5,4},{6,7},{7,6},{8,9},{9,8},{10,11... | collective-permute-start | bytes 196616 | tf_op jit(solution)/shard_map/ppermute | solution.py:48
  31.2 9.6 %collective-permute-start.32 = (bf16[4,8192]{1,0:T(4,128)(2,1)S(1)}, bf16[4,8192]{1,0:T(4,128)(2,1)S(1)}, u32[]{:S(2)}, u32[]{:S(2)}) collective-permute-start(bf16[4,8192]{1,0:T(4,128)(2,1)S(1)} %collective-permute-done.31.refs_2_), channel_id=1, source_target_pairs={{0,1},{1,0},{2,3},{3,2},{4,5},{5,4},{6,7},{7,6},{8,9},{9,8},{10,11... | collective-permute-start | bytes 196616 | tf_op jit(solution)/shard_map/ppermute | solution.py:48
  31.3 9.5 %collective-permute-start.44 = (bf16[4,8192]{1,0:T(4,128)(2,1)S(1)}, bf16[4,8192]{1,0:T(4,128)(2,1)S(1)}, u32[]{:S(2)}, u32[]{:S(2)}) collective-permute-start(bf16[4,8192]{1,0:T(4,128)(2,1)S(1)} %collective-permute-done.43.refs_14_), channel_id=1, source_target_pairs={{0,1},{1,0},{2,3},{3,2},{4,5},{5,4},{6,7},{7,6},{8,9},{9,8},{10,11... | collective-permute-start | bytes 196616 | tf_op jit(solution)/shard_map/ppermute | solution.py:48
  31.7 12.1 %collective-permute-start.40 = (bf16[4,8192]{1,0:T(4,128)(2,1)S(1)}, bf16[4,8192]{1,0:T(4,128)(2,1)S(1)}, u32[]{:S(2)}, u32[]{:S(2)}) collective-permute-start(bf16[4,8192]{1,0:T(4,128)(2,1)S(1)} %collective-permute-done.39.refs_10_), channel_id=1, source_target_pairs={{0,1},{1,0},{2,3},{3,2},{4,5},{5,4},{6,7},{7,6},{8,9},{9,8},{10,11... | collective-permute-start | bytes 196616 | tf_op jit(solution)/shard_map/ppermute | solution.py:48
  32.0 12.9 %collective-permute-start.36 = (bf16[4,8192]{1,0:T(4,128)(2,1)S(1)}, bf16[4,8192]{1,0:T(4,128)(2,1)S(1)}, u32[]{:S(2)}, u32[]{:S(2)}) collective-permute-start(bf16[4,8192]{1,0:T(4,128)(2,1)S(1)} %collective-permute-done.35.refs_6_), channel_id=1, source_target_pairs={{0,1},{1,0},{2,3},{3,2},{4,5},{5,4},{6,7},{7,6},{8,9},{9,8},{10,11... | collective-permute-start | bytes 196616 | tf_op jit(solution)/shard_map/ppermute | solution.py:48
  32.3 3.4 %copy-start = (bf16[8192,512]{1,0:T(8,128)(2,1)S(1)}, bf16[8192,512]{1,0:T(8,128)(2,1)}, u32[]{:S(2)}) copy-start(bf16[8192,512]{1,0:T(8,128)(2,1)} %refs_16_.2) | copy-start | bytes 25165828
  36.5 17.7 %copy-start.1 = (bf16[8192,512]{1,0:T(8,128)(2,1)S(1)}, bf16[8192,512]{1,0:T(8,128)(2,1)}, u32[]{:S(2)}) copy-start(bf16[8192,512]{1,0:T(8,128)(2,1)} %refs_16_.3) | copy-start | bytes 25165828
  36.5 20.7 %copy-start.2 = (bf16[512,8192]{1,0:T(8,128)(2,1)S(1)}, bf16[512,8192]{1,0:T(8,128)(2,1)}, u32[]{:S(2)}) copy-start(bf16[512,8192]{1,0:T(8,128)(2,1)} %refs_17_.1) | copy-start | bytes 25165828
  39.4 6.9 %collective-permute-start.26 = (bf16[64,512]{1,0:T(8,128)(2,1)S(1)}, bf16[64,512]{1,0:T(8,128)(2,1)S(1)}, u32[]{:S(2)}, u32[]{:S(2)}) collective-permute-start(bf16[64,512]{1,0:T(8,128)(2,1)S(1)} %shard_map.64.refs_0_), channel_id=1, source_target_pairs={{0,12},{1,13},{2,14},{3,15},{4,8},{5,9},{6,10},{7,11},{8,4},{9,5},... | collective-permute-start | bytes 196616 | tf_op jit(solution)/shard_map/ppermute | solution.py:48
  40.8 7.5 %collective-permute-start.22 = (bf16[64,512]{1,0:T(8,128)(2,1)S(1)}, bf16[64,512]{1,0:T(8,128)(2,1)S(1)}, u32[]{:S(2)}, u32[]{:S(2)}) collective-permute-start(bf16[64,512]{1,0:T(8,128)(2,1)S(1)} %shard_map.64.refs_0_), channel_id=1, source_target_pairs={{0,8},{1,9},{2,10},{3,11},{4,12},{5,13},{6,14},{7,15},{8,0},{9,1},... | collective-permute-start | bytes 196616 | tf_op jit(solution)/shard_map/ppermute | solution.py:48
  40.8 7.5 %collective-permute-start.18 = (bf16[64,512]{1,0:T(8,128)(2,1)S(1)}, bf16[64,512]{1,0:T(8,128)(2,1)S(1)}, u32[]{:S(2)}, u32[]{:S(2)}) collective-permute-start(bf16[64,512]{1,0:T(8,128)(2,1)S(1)} %shard_map.64.refs_0_), channel_id=1, source_target_pairs={{0,4},{1,5},{2,6},{3,7},{4,0},{5,1},{6,2},{7,3},{8,12},{9,13},{10,... | collective-permute-start | bytes 196616 | tf_op jit(solution)/shard_map/ppermute | solution.py:48
  43.9 5.5 %collective-permute-start.16 = (bf16[64,512]{1,0:T(8,128)(2,1)S(1)}, bf16[64,512]{1,0:T(8,128)(2,1)S(1)}, u32[]{:S(2)}, u32[]{:S(2)}) collective-permute-start(bf16[64,512]{1,0:T(8,128)(2,1)S(1)} %shard_map.64.refs_0_), channel_id=1, source_target_pairs={{0,2},{1,3},{2,0},{3,1},{4,6},{5,7},{6,4},{7,5},{8,10},{9,11},{10,... | collective-permute-start | bytes 196616 | tf_op jit(solution)/shard_map/ppermute | solution.py:48
  44.9 4.7 %collective-permute-start.15 = (bf16[64,512]{1,0:T(8,128)(2,1)S(1)}, bf16[64,512]{1,0:T(8,128)(2,1)S(1)}, u32[]{:S(2)}, u32[]{:S(2)}) collective-permute-start(bf16[64,512]{1,0:T(8,128)(2,1)S(1)} %shard_map.64.refs_0_), channel_id=1, source_target_pairs={{0,1},{1,0},{2,3},{3,2},{4,5},{5,4},{6,7},{7,6},{8,9},{9,8},{10,11... | collective-permute-start | bytes 196616 | tf_op jit(solution)/shard_map/ppermute | solution.py:48
  46.3 4.3 %collective-permute-start.28 = (bf16[64,512]{1,0:T(8,128)(2,1)S(1)}, bf16[64,512]{1,0:T(8,128)(2,1)S(1)}, u32[]{:S(2)}, u32[]{:S(2)}) collective-permute-start(bf16[64,512]{1,0:T(8,128)(2,1)S(1)} %collective-permute-done.26.refs_12_), channel_id=1, source_target_pairs={{0,2},{1,3},{2,0},{3,1},{4,6},{5,7},{6,4},{7,5},{8,10},{9,11},{10,... | collective-permute-start | bytes 196616 | tf_op jit(solution)/shard_map/ppermute | solution.py:48
  48.3 2.3 %collective-permute-start.27 = (bf16[64,512]{1,0:T(8,128)(2,1)S(1)}, bf16[64,512]{1,0:T(8,128)(2,1)S(1)}, u32[]{:S(2)}, u32[]{:S(2)}) collective-permute-start(bf16[64,512]{1,0:T(8,128)(2,1)S(1)} %collective-permute-done.26.refs_12_), channel_id=1, source_target_pairs={{0,1},{1,0},{2,3},{3,2},{4,5},{5,4},{6,7},{7,6},{8,9},{9,8},{10,11... | collective-permute-start | bytes 196616 | tf_op jit(solution)/shard_map/ppermute | solution.py:48
  48.3 4.9 %collective-permute-start.24 = (bf16[64,512]{1,0:T(8,128)(2,1)S(1)}, bf16[64,512]{1,0:T(8,128)(2,1)S(1)}, u32[]{:S(2)}, u32[]{:S(2)}) collective-permute-start(bf16[64,512]{1,0:T(8,128)(2,1)S(1)} %collective-permute-done.22.refs_8_), channel_id=1, source_target_pairs={{0,2},{1,3},{2,0},{3,1},{4,6},{5,7},{6,4},{7,5},{8,10},{9,11},{10,... | collective-permute-start | bytes 196616 | tf_op jit(solution)/shard_map/ppermute | solution.py:48
  49.3 3.8 %collective-permute-start.23 = (bf16[64,512]{1,0:T(8,128)(2,1)S(1)}, bf16[64,512]{1,0:T(8,128)(2,1)S(1)}, u32[]{:S(2)}, u32[]{:S(2)}) collective-permute-start(bf16[64,512]{1,0:T(8,128)(2,1)S(1)} %collective-permute-done.22.refs_8_), channel_id=1, source_target_pairs={{0,1},{1,0},{2,3},{3,2},{4,5},{5,4},{6,7},{7,6},{8,9},{9,8},{10,11... | collective-permute-start | bytes 196616 | tf_op jit(solution)/shard_map/ppermute | solution.py:48
  49.6 4.6 %collective-permute-start.20 = (bf16[64,512]{1,0:T(8,128)(2,1)S(1)}, bf16[64,512]{1,0:T(8,128)(2,1)S(1)}, u32[]{:S(2)}, u32[]{:S(2)}) collective-permute-start(bf16[64,512]{1,0:T(8,128)(2,1)S(1)} %collective-permute-done.18.refs_4_), channel_id=1, source_target_pairs={{0,2},{1,3},{2,0},{3,1},{4,6},{5,7},{6,4},{7,5},{8,10},{9,11},{10,... | collective-permute-start | bytes 196616 | tf_op jit(solution)/shard_map/ppermute | solution.py:48
  50.5 6.6 %collective-permute-start.19 = (bf16[64,512]{1,0:T(8,128)(2,1)S(1)}, bf16[64,512]{1,0:T(8,128)(2,1)S(1)}, u32[]{:S(2)}, u32[]{:S(2)}) collective-permute-start(bf16[64,512]{1,0:T(8,128)(2,1)S(1)} %collective-permute-done.18.refs_4_), channel_id=1, source_target_pairs={{0,1},{1,0},{2,3},{3,2},{4,5},{5,4},{6,7},{7,6},{8,9},{9,8},{10,11... | collective-permute-start | bytes 196616 | tf_op jit(solution)/shard_map/ppermute | solution.py:48
  50.6 6.5 %collective-permute-start.17 = (bf16[64,512]{1,0:T(8,128)(2,1)S(1)}, bf16[64,512]{1,0:T(8,128)(2,1)S(1)}, u32[]{:S(2)}, u32[]{:S(2)}) collective-permute-start(bf16[64,512]{1,0:T(8,128)(2,1)S(1)} %collective-permute-done.16.refs_2_), channel_id=1, source_target_pairs={{0,1},{1,0},{2,3},{3,2},{4,5},{5,4},{6,7},{7,6},{8,9},{9,8},{10,11... | collective-permute-start | bytes 196616 | tf_op jit(solution)/shard_map/ppermute | solution.py:48
  53.2 4.0 %collective-permute-start.29 = (bf16[64,512]{1,0:T(8,128)(2,1)S(1)}, bf16[64,512]{1,0:T(8,128)(2,1)S(1)}, u32[]{:S(2)}, u32[]{:S(2)}) collective-permute-start(bf16[64,512]{1,0:T(8,128)(2,1)S(1)} %collective-permute-done.28.refs_14_), channel_id=1, source_target_pairs={{0,1},{1,0},{2,3},{3,2},{4,5},{5,4},{6,7},{7,6},{8,9},{9,8},{10,11... | collective-permute-start | bytes 196616 | tf_op jit(solution)/shard_map/ppermute | solution.py:48
  53.2 4.0 %collective-permute-start.25 = (bf16[64,512]{1,0:T(8,128)(2,1)S(1)}, bf16[64,512]{1,0:T(8,128)(2,1)S(1)}, u32[]{:S(2)}, u32[]{:S(2)}) collective-permute-start(bf16[64,512]{1,0:T(8,128)(2,1)S(1)} %collective-permute-done.24.refs_10_), channel_id=1, source_target_pairs={{0,1},{1,0},{2,3},{3,2},{4,5},{5,4},{6,7},{7,6},{8,9},{9,8},{10,11... | collective-permute-start | bytes 196616 | tf_op jit(solution)/shard_map/ppermute | solution.py:48
  54.2 3.0 %collective-permute-start.21 = (bf16[64,512]{1,0:T(8,128)(2,1)S(1)}, bf16[64,512]{1,0:T(8,128)(2,1)S(1)}, u32[]{:S(2)}, u32[]{:S(2)}) collective-permute-start(bf16[64,512]{1,0:T(8,128)(2,1)S(1)} %collective-permute-done.20.refs_6_), channel_id=1, source_target_pairs={{0,1},{1,0},{2,3},{3,2},{4,5},{5,4},{6,7},{7,6},{8,9},{9,8},{10,11... | collective-permute-start | bytes 196616 | tf_op jit(solution)/shard_map/ppermute | solution.py:48
  (1 other events, 0.8 us)

commit v2 on v0

v2 whole, which is shorter than its diff:
```python
import functools

import jax
import jax.numpy as jnp
from jax import lax
from jax.experimental import pallas as pl
from jax.experimental.pallas import tpu as pltpu
from jax.sharding import PartitionSpec as P

CAND = 4
KBLK = 1024
RBLK = 128
VMEM = 50 << 20


def general(factors_in, factors_out, basis_in, basis_out, eigvals, live_counts):
    slot_rows = factors_in.shape[0]
    keep = (lax.iota(jnp.int32, slot_rows) < live_counts[0])[:, None]
    masked = jnp.where(keep, factors_in, jnp.zeros_like(factors_in))
    partial_in = jnp.dot(
        lax.all_gather(masked, "dp", axis=0, tiled=True),
        basis_in,
        preferred_element_type=jnp.float32,
    )
    partial_out = jnp.dot(
        lax.all_gather(factors_out, "dp", axis=0, tiled=True),
        basis_out,
        preferred_element_type=jnp.float32,
    )
    halves = lax.axis_size("basis")
    share = partial_in.shape[0] // halves
    summed_in, summed_out = lax.psum((partial_in, partial_out), "basis")
    first = lax.axis_index("basis") * share
    proj_in = lax.dynamic_slice_in_dim(summed_in, first, share, 0).astype(jnp.bfloat16)
    proj_out = lax.dynamic_slice_in_dim(summed_out, first, share, 0).astype(jnp.bfloat16)
    cand_local = CAND // halves
    per_cand = share // cand_local
    pout_grouped = proj_out.reshape(cand_local, per_cand, proj_out.shape[1])
    shifted = eigvals.astype(jnp.float32) + 0.01
    piece = lax.all_gather(proj_in, "dp", axis=1, tiled=True)
    pin_grouped = piece.reshape(cand_local, per_cand, piece.shape[1])
    summed = jnp.einsum(
        "ati,atj->aij", pout_grouped, pin_grouped, preferred_element_type=jnp.float32
    )
    return (summed / shifted[None, :, :]).astype(jnp.bfloat16)


def swap(x, m):
    n = lax.axis_size("dp")
    return lax.ppermute(x, "dp", [(d, d ^ m) for d in range(n)])


def gather(x, n):
    column = [x] + [swap(x, 4 * k) for k in range(1, n // 4)]
    pair = [swap(y, 2) for y in column]
    lane = [column, pair]
    other = [[swap(y, 1) for y in side] for side in lane]
    return [(other if m & 1 else lane)[(m >> 1) & 1][m >> 2] for m in range(n)]


def project_kernel(n, first, turn, own_ref, *refs):
    pieces, (basis_ref, out_ref, acc) = refs[:n], refs[n:]
    step = pl.program_id(0)
    width = basis_ref.shape[0]
    at = pl.multiple_of(step * width, width)
    held = pieces[0].shape[0]
    slots = held // 2
    rows = jnp.concatenate(
        [piece[:, pl.ds(at, width)].astype(jnp.float32) for piece in pieces], axis=0
    ).astype(jnp.bfloat16)
    part = jnp.dot(rows, basis_ref[...], preferred_element_type=jnp.float32)

    @pl.when(step == 0)
    def _():
        acc[...] = part

    @pl.when(step > 0)
    def _():
        acc[...] += part

    @pl.when(step == pl.num_programs(0) - 1)
    def _():
        total = n * slots
        to = lax.broadcasted_iota(jnp.int32, (total, n * held), 0)
        come = lax.broadcasted_iota(jnp.int32, (total, n * held), 1)
        slot = come % held - first
        where = jnp.bitwise_xor(come // held, own_ref[0]) * slots + slot
        chosen = (to == where) & (slot >= 0) & (slot < slots)
        pick = jnp.where(chosen, 1.0, 0.0).astype(jnp.bfloat16)
        proj = jnp.dot(pick, acc[...].astype(jnp.bfloat16), preferred_element_type=jnp.float32)
        if turn:
            turned = proj.T
            token = lax.broadcasted_iota(jnp.int32, turned.shape, 1)
            for c in range(CAND):
                own_tokens = token // (total // CAND) == c
                out_ref[c] = jnp.where(own_tokens, turned, 0.0).astype(jnp.bfloat16)
        else:
            out_ref[...] = proj.astype(jnp.bfloat16)


def project(own, pieces, basis, first, turn):
    n = len(pieces)
    held, depth = pieces[0].shape
    cols = basis.shape[1]
    total = n * held // 2
    shape = (CAND, cols, total) if turn else (total, cols)
    return pl.pallas_call(
        functools.partial(project_kernel, n, first, turn),
        out_shape=jax.ShapeDtypeStruct(shape, jnp.bfloat16),
        grid_spec=pltpu.PrefetchScalarGridSpec(
            num_scalar_prefetch=1,
            grid=(depth // KBLK,),
            in_specs=[pl.BlockSpec((held, depth), lambda k, own: (0, 0))] * n
            + [pl.BlockSpec((KBLK, cols), lambda k, own: (k, 0))],
            out_specs=pl.BlockSpec(shape, lambda k, own: (0,) * len(shape)),
            scratch_shapes=[pltpu.VMEM((n * held, cols), jnp.float32)],
        ),
        compiler_params=pltpu.CompilerParams(vmem_limit_bytes=VMEM),
        cost_estimate=pl.CostEstimate(
            flops=2 * n * held * depth * cols,
            bytes_accessed=2 * depth * cols,
            transcendentals=0,
        ),
    )(own, *pieces, basis)


def outer_kernel(blocks, own_ref, *refs):
    count = len(blocks)
    pieces, (left_ref, eig_ref, *_, out_ref, held) = refs[:count], refs[count:]
    step = pl.program_id(0)
    at = 0
    for piece, (_, entries) in zip(pieces, blocks):
        for e in range(len(entries)):
            @pl.when(step == at)
            def _(piece=piece, e=e):
                held[...] = piece[...] if len(piece.shape) == 2 else piece[e]

            at += 1
    right = held[...]
    rows = out_ref.shape[1]
    for r in range(0, rows, RBLK):
        scale = 1.0 / (eig_ref[r:r + RBLK, :].astype(jnp.float32) + 0.01)
        for c in range(CAND):
            summed = jnp.dot(left_ref[c, r:r + RBLK, :], right, preferred_element_type=jnp.float32)
            out_ref[c, r:r + RBLK, :] = (summed * scale).astype(jnp.bfloat16)


def outer(own, blocks, left, eigvals, before):
    total, cols = blocks[0][0].shape[-2:]
    rows, width = eigvals.shape
    order = [m for _, entries in blocks for m in entries]

    def place(s, own):
        m = jnp.int32(order[0])
        for k in range(1, len(order)):
            m = jnp.where(s == k, order[k], m)
        return jnp.bitwise_xor(m, own[0])

    def whole(shape):
        return pl.BlockSpec(shape, lambda s, own: (0,) * len(shape))

    operands = [own] + [x for x, _ in blocks] + [left, eigvals]
    in_specs = [whole(x.shape) for x, _ in blocks] + [
        whole(left.shape),
        pl.BlockSpec((rows, cols), lambda s, own: (0, place(s, own))),
    ]
    aliases = {}
    if before is not None:
        aliases = {len(operands): 0}
        operands.append(before)
        in_specs.append(pl.BlockSpec(memory_space=pl.ANY))
    share = len(order) * cols
    return pl.pallas_call(
        functools.partial(outer_kernel, [(None, e) for _, e in blocks]),
        out_shape=jax.ShapeDtypeStruct((CAND, rows, width), jnp.bfloat16),
        grid_spec=pltpu.PrefetchScalarGridSpec(
            num_scalar_prefetch=1,
            grid=(len(order),),
            in_specs=in_specs,
            out_specs=pl.BlockSpec((CAND, rows, cols), lambda s, own: (0, 0, place(s, own))),
            scratch_shapes=[pltpu.VMEM((total, cols), jnp.bfloat16)],
        ),
        input_output_aliases=aliases,
        compiler_params=pltpu.CompilerParams(vmem_limit_bytes=VMEM),
        cost_estimate=pl.CostEstimate(
            flops=2 * total * rows * share,
            bytes_accessed=2 * rows * share * (CAND + 1),
            transcendentals=rows * share,
        ),
    )(*operands)


def by_swaps(factors_in, factors_out, basis_in, basis_out, eigvals, live_counts):
    n = lax.axis_size("dp")
    own = lax.axis_index("dp").astype(jnp.int32)[None]
    slots = factors_in.shape[0]
    keep = (lax.iota(jnp.int32, slots) < live_counts[0])[:, None]
    masked = jnp.where(keep, factors_out, jnp.zeros_like(factors_out))
    pieces = gather(jnp.concatenate([factors_in, masked], axis=0), n)
    pin = project(own, pieces, basis_in, 0, False)
    left = project(own, pieces, basis_out, slots, True)

    up = range(4, n, 4)
    core, pair = swap(pin, 1), swap(pin, 2)
    column = [swap(pin, m) for m in up]
    stacked = jnp.stack(column)
    stacked_pair = swap(stacked, 2)
    stacked_core = swap(stacked, 1)
    pair_core = swap(pair, 1)
    last = swap(stacked_pair, 1)
    out = outer(own, [(pin, [0]), (core, [1])], left, eigvals, None)
    out = outer(
        own, [(pair, [2])] + [(x, [m]) for x, m in zip(column, up)], left, eigvals, out
    )
    out = outer(
        own,
        [
            (pair_core, [3]),
            (stacked_core, [m + 1 for m in up]),
            (stacked_pair, [m + 2 for m in up]),
        ],
        left,
        eigvals,
        out,
    )
    return outer(own, [(last, [m + 3 for m in up])], left, eigvals, out)


def solution(mesh):
    placed = (
        P(("groups", "dp"), "basis"),
        P(("groups", "dp"), "basis"),
        P("basis", "dp"),
        P("basis", "dp"),
        P("dp", None),
        P(("groups", "dp")),
    )
    chosen = by_swaps if mesh.shape["basis"] == 1 and mesh.shape["dp"] == 16 else general
    return jax.shard_map(
        chosen,
        mesh=mesh,
        in_specs=placed,
        out_specs=P(("groups", "basis"), "dp", None),
        check_vma=False,
    )
```

time: 154 us -> 86.8 us (0.56)
  waiting for transfers between devices: 93.6 us -> 24 us
  Pallas kernels: 0 us -> 39.7 us
  matrix products: 30.8 us -> 0 us
  starting transfers between devices: 0.08 us -> 19.7 us
  between operations: 13.8 us -> 0.72 us
  other arithmetic: 13.1 us -> 1.88 us
  local copies, waits for them, and re-layouts: 2.67 us -> 0 us
    all_gather x3 -> x0, waiting for transfers between devices: 92.9 us -> none  [the longest x1 40.6 us: per_device(): lax.all_gather(masked, 'dp', axis=0, tiled=True)]
    pallas_call x0 -> x6, Pallas kernels: none -> 39.7 us  [the longest x4 25.4 us: outer(): pl.pallas_call(functools.partial(outer_kernel, [(None, e) for _, e in blo...]
    dot_general x3 -> x0, matrix products: 30.8 us -> none  [the longest x1 20.3 us: per_device(): jnp.einsum('ati,atj->aij', pout_grouped, pin_grouped, preferred_element_t...]
    ppermute x0 -> x24, waiting for transfers between devices: none -> 24 us  [swap(): return lax.ppermute(x, 'dp', [(d, d ^ m) for d in range(n)])]
    ppermute x0 -> x24, starting transfers between devices: none -> 19.7 us  [swap(): return lax.ppermute(x, 'dp', [(d, d ^ m) for d in range(n)])]
    add x1 -> x0, other arithmetic: 11.5 us -> none  [per_device(): shifted = eigvals.astype(jnp.float32) + 0.01]
    unnamed x2 -> x0, local copies, waits for them, and re-layouts: 2.67 us -> none
    unnamed x1 -> x0, other arithmetic: 1.57 us -> none
  transfers between devices with their start and end apart: 3 -> 24, of which waited for: 3 -> 11; matrix products, arithmetic and copies ran while one was open for 16% -> 0% of each run, Pallas kernels for 0% -> 32%
where the time goes in v2:
time: 86.8 us; the launch traced here: 85.9 us
  Pallas kernels  39.7 us (46%)
  waiting for transfers between devices  24 us (28%)
  starting transfers between devices  19.7 us (23%)
  other arithmetic  1.88 us (2%)
    pallas_call x4, Pallas kernels, outer(): pl.pallas_call(functools.partial(outer_kernel, [(None, e) for _, e in blo...  25.4 us
    ppermute x24, waiting for transfers between devices, swap(): return lax.ppermute(x, 'dp', [(d, d ^ m) for d in range(n)])  24 us
    ppermute x24, starting transfers between devices, swap(): return lax.ppermute(x, 'dp', [(d, d ^ m) for d in range(n)])  19.7 us
    pallas_call x2, Pallas kernels, project(): pl.pallas_call(functools.partial(project_kernel, n, first, turn), out_sha...  14.2 us
  transfers between devices with their start and end apart: 24, of which 11 were waited for; matrix products, arithmetic and copies ran while one was open for 0% of the time, Pallas kernels for 32%

profile of v2, /device:TPU:0, one launch (start us, length us, event | category | flops | bytes accessed | tf_op | source)
XLA Modules:
  0.0 85.9 jit_solution(17482290365104585540)
XLA Ops:
  0.7 0.9 %broadcast_select_fusion = bf16[4,8192]{1,0:T(4,128)(2,1)S(1)} fusion(bf16[4,8192]{1,0:T(4,128)(2,1)} %param.7, pred[4]{0:T(512)(128)(4,1)S(1)} %iota_compare_fusion), kind=kLoop, calls=%fused_computation.2 | loop fusion | flops 32768 | bytes 131076 | tf_op jit(solution)/shard_map/jit(_where)/select_n | solution.py:198
  1.6 0.9 %pad_maximum_fusion.1.refs_0_ = bf16[8,8192]{1,0:T(8,128)(2,1)S(1)} fusion(bf16[4,8192]{1,0:T(4,128)(2,1)S(1)} %broadcast_select_fusion, bf16[4,8192]{1,0:T(4,128)(2,1)} %param.6), kind=kLoop, calls=%fused_computation.1 | loop fusion | flops 262144 | bytes 262144 | tf_op jit(solution)/shard_map/concatenate | solution.py:199
  2.5 4.1 %collective-permute-start.7 = (bf16[8,8192]{1,0:T(8,128)(2,1)S(1)}, bf16[8,8192]{1,0:T(8,128)(2,1)S(1)}, u32[]{:S(2)}, u32[]{:S(2)}) collective-permute-start(bf16[8,8192]{1,0:T(8,128)(2,1)S(1)} %pad_maximum_fusion.1.refs_0_), channel_id=1, source_target_pairs={{0,8},{1,9},{2,10},{3,11},{4,12},{5,13},{6,14},{7,15},{8,0},{9,1},... | collective-permute-start | bytes 393224 | tf_op jit(solution)/shard_map/ppermute | solution.py:50
  6.6 1.3 %collective-permute-start.11 = (bf16[8,8192]{1,0:T(8,128)(2,1)S(1)}, bf16[8,8192]{1,0:T(8,128)(2,1)S(1)}, u32[]{:S(2)}, u32[]{:S(2)}) collective-permute-start(bf16[8,8192]{1,0:T(8,128)(2,1)S(1)} %pad_maximum_fusion.1.refs_0_), channel_id=1, source_target_pairs={{0,12},{1,13},{2,14},{3,15},{4,8},{5,9},{6,10},{7,11},{8,4},{9,5},... | collective-permute-start | bytes 393224 | tf_op jit(solution)/shard_map/ppermute | solution.py:50
  8.0 0.2 collective-permute-start.3
  8.2 1.5 %collective-permute-start.1 = (bf16[8,8192]{1,0:T(8,128)(2,1)S(1)}, bf16[8,8192]{1,0:T(8,128)(2,1)S(1)}, u32[]{:S(2)}, u32[]{:S(2)}) collective-permute-start(bf16[8,8192]{1,0:T(8,128)(2,1)S(1)} %pad_maximum_fusion.1.refs_0_), channel_id=1, source_target_pairs={{0,2},{1,3},{2,0},{3,1},{4,6},{5,7},{6,4},{7,5},{8,10},{9,11},{10,... | collective-permute-start | bytes 393224 | tf_op jit(solution)/shard_map/ppermute | solution.py:50
  9.7 0.0 collective-permute-start
  9.7 6.9 %collective-permute-done.7.refs_8_ = bf16[8,8192]{1,0:T(8,128)(2,1)S(1)} collective-permute-done((bf16[8,8192]{1,0:T(8,128)(2,1)S(1)}, bf16[8,8192]{1,0:T(8,128)(2,1)S(1)}, u32[]{:S(2)}, u32[]{:S(2)}) %collective-permute-start.7) | collective-permute-done | bytes 131104 | tf_op jit(solution)/shard_map/ppermute | solution.py:50
  16.6 1.8 %collective-permute-start.9 = (bf16[8,8192]{1,0:T(8,128)(2,1)S(1)}, bf16[8,8192]{1,0:T(8,128)(2,1)S(1)}, u32[]{:S(2)}, u32[]{:S(2)}) collective-permute-start(bf16[8,8192]{1,0:T(8,128)(2,1)S(1)} %collective-permute-done.7.refs_8_), channel_id=1, source_target_pairs={{0,2},{1,3},{2,0},{3,1},{4,6},{5,7},{6,4},{7,5},{8,10},{9,11},{10,... | collective-permute-start | bytes 393224 | tf_op jit(solution)/shard_map/ppermute | solution.py:50
  18.4 0.2 collective-permute-start.13
  18.6 1.8 %collective-permute-start.5 = (bf16[8,8192]{1,0:T(8,128)(2,1)S(1)}, bf16[8,8192]{1,0:T(8,128)(2,1)S(1)}, u32[]{:S(2)}, u32[]{:S(2)}) collective-permute-start(bf16[8,8192]{1,0:T(8,128)(2,1)S(1)} %collective-permute-done.3.refs_4_), channel_id=1, source_target_pairs={{0,2},{1,3},{2,0},{3,1},{4,6},{5,7},{6,4},{7,5},{8,10},{9,11},{10,... | collective-permute-start | bytes 393224 | tf_op jit(solution)/shard_map/ppermute | solution.py:50
  20.5 0.0 collective-permute-done.1.refs_2_
  20.5 0.0 collective-permute-start.12
  20.5 0.0 collective-permute-done.refs_1_
  20.5 0.5 collective-permute-start.4
  21.0 2.0 %collective-permute-done.9.refs_10_ = bf16[8,8192]{1,0:T(8,128)(2,1)S(1)} collective-permute-done((bf16[8,8192]{1,0:T(8,128)(2,1)S(1)}, bf16[8,8192]{1,0:T(8,128)(2,1)S(1)}, u32[]{:S(2)}, u32[]{:S(2)}) %collective-permute-start.9) | collective-permute-done | bytes 131104 | tf_op jit(solution)/shard_map/ppermute | solution.py:50
  23.0 1.6 %collective-permute-done.13.refs_14_ = bf16[8,8192]{1,0:T(8,128)(2,1)S(1)} collective-permute-done((bf16[8,8192]{1,0:T(8,128)(2,1)S(1)}, bf16[8,8192]{1,0:T(8,128)(2,1)S(1)}, u32[]{:S(2)}, u32[]{:S(2)}) %collective-permute-start.13) | collective-permute-done | bytes 131104 | tf_op jit(solution)/shard_map/ppermute | solution.py:50
  24.7 1.4 %collective-permute-done.5.refs_6_ = bf16[8,8192]{1,0:T(8,128)(2,1)S(1)} collective-permute-done((bf16[8,8192]{1,0:T(8,128)(2,1)S(1)}, bf16[8,8192]{1,0:T(8,128)(2,1)S(1)}, u32[]{:S(2)}, u32[]{:S(2)}) %collective-permute-start.5) | collective-permute-done | bytes 131104 | tf_op jit(solution)/shard_map/ppermute | solution.py:50
  26.1 0.0 collective-permute-start.10
  26.1 0.0 collective-permute-done.12.refs_13_
  26.1 0.5 collective-permute-start.14
  26.6 0.0 collective-permute-done.4.refs_5_
  26.6 0.1 collective-permute-start.6
  26.7 0.0 collective-permute-done.8.refs_9_
  26.7 0.0 collective-permute-done.2.refs_3_
  26.7 0.8 collective-permute-done.10.refs_11_
  27.4 0.2 collective-permute-done.14.refs_15_
  27.6 0.3 collective-permute-done.6.refs_7_
  27.9 7.0 %shard_map.64.refs_0_ = bf16[64,512]{1,0:T(8,128)(2,1)S(1)} custom-call(s32[1]{0:T(128)} %bitcast.own_ref, bf16[8,8192]{1,0:T(8,128)(2,1)S(1)} %pad_maximum_fusion.1.refs_0_, bf16[8,8192]{1,0:T(8,128)(2,1)S(1)} %collective-permute-done.refs_1_, bf16[8,8192]{1,0:T(8,128)(2,1)S(1)} %collective-permute-done.1.refs_2_, ...), custom_call_target="tpu_custom_call" | custom-call | flops 1073741824 | bytes 8388608 | tf_op jit(solution)/shard_map/pallas_call | solution.py:107
  35.0 1.5 %collective-permute-start.15 = (bf16[64,512]{1,0:T(8,128)(2,1)S(1)}, bf16[64,512]{1,0:T(8,128)(2,1)S(1)}, u32[]{:S(2)}, u32[]{:S(2)}) collective-permute-start(bf16[64,512]{1,0:T(8,128)(2,1)S(1)} %shard_map.64.refs_0_), channel_id=1, source_target_pairs={{0,4},{1,5},{2,6},{3,7},{4,0},{5,1},{6,2},{7,3},{8,12},{9,13},{10,... | collective-permute-start | bytes 196616 | tf_op jit(solution)/shard_map/ppermute | solution.py:50
  36.5 3.4 %collective-permute-start.16 = (bf16[64,512]{1,0:T(8,128)(2,1)S(1)}, bf16[64,512]{1,0:T(8,128)(2,1)S(1)}, u32[]{:S(2)}, u32[]{:S(2)}) collective-permute-start(bf16[64,512]{1,0:T(8,128)(2,1)S(1)} %shard_map.64.refs_0_), channel_id=1, source_target_pairs={{0,8},{1,9},{2,10},{3,11},{4,12},{5,13},{6,14},{7,15},{8,0},{9,1},... | collective-permute-start | bytes 196616 | tf_op jit(solution)/shard_map/ppermute | solution.py:50
  39.9 0.0 collective-permute-start.17
  39.9 0.0 collective-permute-done.15.refs_1_
  39.9 3.9 %collective-permute-done.16.refs_2_ = bf16[64,512]{1,0:T(8,128)(2,1)S(1)} collective-permute-done((bf16[64,512]{1,0:T(8,128)(2,1)S(1)}, bf16[64,512]{1,0:T(8,128)(2,1)S(1)}, u32[]{:S(2)}, u32[]{:S(2)}) %collective-permute-start.16) | collective-permute-done | bytes 65568 | tf_op jit(solution)/shard_map/ppermute | solution.py:50
  43.8 2.2 %collective-permute-done.17.refs_3_ = bf16[64,512]{1,0:T(8,128)(2,1)S(1)} collective-permute-done((bf16[64,512]{1,0:T(8,128)(2,1)S(1)}, bf16[64,512]{1,0:T(8,128)(2,1)S(1)}, u32[]{:S(2)}, u32[]{:S(2)}) %collective-permute-start.17) | collective-permute-done | bytes 65568 | tf_op jit(solution)/shard_map/ppermute | solution.py:50
  46.1 1.6 %collective-permute-start.18 = (bf16[3,64,512]{2,1,0:T(8,128)(2,1)S(1)}, bf16[3,64,512]{2,1,0:T(8,128)(2,1)S(1)}, u32[]{:S(2)}, u32[]{:S(2)}) collective-permute-start(bf16[3,64,512]{2,1,0:T(8,128)(2,1)S(1)} %pad_maximum_fusion), channel_id=1, source_target_pairs={{0,2},{1,3},{2,0},{3,1},{4,6},{5,7},{6,4},{7,5},{8,10},{9,11},{10,... | collective-permute-start | bytes 589832 | tf_op jit(solution)/shard_map/ppermute | solution.py:50
  47.7 0.5 collective-permute-start.20
  48.2 4.3 %collective-permute-done.18.refs_2_ = bf16[3,64,512]{2,1,0:T(8,128)(2,1)S(1)} collective-permute-done((bf16[3,64,512]{2,1,0:T(8,128)(2,1)S(1)}, bf16[3,64,512]{2,1,0:T(8,128)(2,1)S(1)}, u32[]{:S(2)}, u32[]{:S(2)}) %collective-permute-start.18) | collective-permute-done | bytes 196640 | tf_op jit(solution)/shard_map/ppermute | solution.py:50
  52.5 0.5 collective-permute-start.23
  53.0 0.2 collective-permute-done.20.refs_0_
  53.2 0.0 collective-permute-start.21
  53.2 7.2 %shard_map.65.refs_2_.refs_4_.refs_3_.refs_1_ = bf16[4,512,64]{2,1,0:T(8,128)(2,1)S(1)} custom-call(s32[1]{0:T(128)} %bitcast.own_ref, bf16[8,8192]{1,0:T(8,128)(2,1)S(1)} %pad_maximum_fusion.1.refs_0_, bf16[8,8192]{1,0:T(8,128)(2,1)S(1)} %collective-permute-done.refs_1_, bf16[8,8192]{1,0:T(8,128)(2,1)S(1)} %collective-permute-done.1.refs_2_, ...), custom_call_target="tpu_custom_call" | custom-call | flops 1073741824 | bytes 8388608 | tf_op jit(solution)/shard_map/pallas_call | solution.py:107
  60.5 0.0 collective-permute-done.23.refs_1_
  60.5 3.8 %shard_map.66.refs_6_ = bf16[4,512,8192]{2,1,0:T(8,128)(2,1)} custom-call(s32[1]{0:T(128)} %bitcast.own_ref, bf16[64,512]{1,0:T(8,128)(2,1)S(1)} %shard_map.64.refs_0_, bf16[64,512]{1,0:T(8,128)(2,1)S(1)} %collective-permute-done.23.refs_1_, bf16[4,512,64]{2,1,0:T(8,128)(2,1)S(1)} %shard_map.65.refs_2_.refs_4_.refs_3_.refs_1_, bf16[512,8192]{1,0:T(8,128)(2,1)} %refs_2_.1), custom_call_target="tpu_custom_call" | custom-call | flops 67108864 | bytes 5242880 | tf_op jit(solution)/shard_map/pallas_call | solution.py:173
  64.3 6.5 %shard_map.67.refs_5_ = bf16[4,512,8192]{2,1,0:T(8,128)(2,1)} custom-call(s32[1]{0:T(128)} %bitcast.own_ref, bf16[64,512]{1,0:T(8,128)(2,1)S(1)} %collective-permute-done.20.refs_0_, bf16[64,512]{1,0:T(8,128)(2,1)S(1)} %collective-permute-done.15.refs_1_, bf16[64,512]{1,0:T(8,128)(2,1)S(1)} %collective-permute-done.16.refs_2_, ...), custom_call_target="tpu_custom_call", output_to_operand_aliasing={{}: (7, {})} | custom-call | flops 134217728 | bytes 10485760 | tf_op jit(solution)/shard_map/pallas_call | solution.py:173
  70.7 0.0 collective-permute-done.22.refs_1_
  70.7 10.0 %shard_map.68.refs_3_ = bf16[4,512,8192]{2,1,0:T(8,128)(2,1)} custom-call(s32[1]{0:T(128)} %bitcast.own_ref, bf16[64,512]{1,0:T(8,128)(2,1)S(1)} %collective-permute-done.21.refs_0_, bf16[3,64,512]{2,1,0:T(8,128)(2,1)S(1)} %collective-permute-done.22.refs_1_, ...), custom_call_target="tpu_custom_call", output_to_operand_aliasing={{}: (6, {})} | custom-call | flops 234881024 | bytes 18350080 | tf_op jit(solution)/shard_map/pallas_call | solution.py:173
  80.7 5.2 %shard_map.69 = bf16[4,512,8192]{2,1,0:T(8,128)(2,1)} custom-call(s32[1]{0:T(128)} %bitcast.own_ref, bf16[3,64,512]{2,1,0:T(8,128)(2,1)S(1)} %collective-permute-done.19.refs_0_, bf16[4,512,64]{2,1,0:T(8,128)(2,1)S(1)} %shard_map.65.refs_2_.refs_4_.refs_3_.refs_1_, bf16[512,8192]{1,0:T(8,128)(2,1)} %refs_2_.1, ...), custom_call_target="tpu_custom_call", output_to_operand_aliasing={{}: (4, {})} | custom-call | flops 100663296 | bytes 7864320 | tf_op jit(solution)/shard_map/pallas_call | solution.py:173
  (10 shorter events, 0.1 us)
Async XLA Ops:
  2.5 14.1 %collective-permute-start.7 = (bf16[8,8192]{1,0:T(8,128)(2,1)S(1)}, bf16[8,8192]{1,0:T(8,128)(2,1)S(1)}, u32[]{:S(2)}, u32[]{:S(2)}) collective-permute-start(bf16[8,8192]{1,0:T(8,128)(2,1)S(1)} %pad_maximum_fusion.1.refs_0_), channel_id=1, source_target_pairs={{0,8},{1,9},{2,10},{3,11},{4,12},{5,13},{6,14},{7,15},{8,0},{9,1},... | collective-permute-start | bytes 393224 | tf_op jit(solution)/shard_map/ppermute | solution.py:50
  6.6 11.8 %collective-permute-start.11 = (bf16[8,8192]{1,0:T(8,128)(2,1)S(1)}, bf16[8,8192]{1,0:T(8,128)(2,1)S(1)}, u32[]{:S(2)}, u32[]{:S(2)}) collective-permute-start(bf16[8,8192]{1,0:T(8,128)(2,1)S(1)} %pad_maximum_fusion.1.refs_0_), channel_id=1, source_target_pairs={{0,12},{1,13},{2,14},{3,15},{4,8},{5,9},{6,10},{7,11},{8,4},{9,5},... | collective-permute-start | bytes 393224 | tf_op jit(solution)/shard_map/ppermute | solution.py:50
  8.0 10.7 %collective-permute-start.3 = (bf16[8,8192]{1,0:T(8,128)(2,1)S(1)}, bf16[8,8192]{1,0:T(8,128)(2,1)S(1)}, u32[]{:S(2)}, u32[]{:S(2)}) collective-permute-start(bf16[8,8192]{1,0:T(8,128)(2,1)S(1)} %pad_maximum_fusion.1.refs_0_), channel_id=1, source_target_pairs={{0,4},{1,5},{2,6},{3,7},{4,0},{5,1},{6,2},{7,3},{8,12},{9,13},{10,... | collective-permute-start | bytes 393224 | tf_op jit(solution)/shard_map/ppermute | solution.py:50
  8.2 12.3 %collective-permute-start.1 = (bf16[8,8192]{1,0:T(8,128)(2,1)S(1)}, bf16[8,8192]{1,0:T(8,128)(2,1)S(1)}, u32[]{:S(2)}, u32[]{:S(2)}) collective-permute-start(bf16[8,8192]{1,0:T(8,128)(2,1)S(1)} %pad_maximum_fusion.1.refs_0_), channel_id=1, source_target_pairs={{0,2},{1,3},{2,0},{3,1},{4,6},{5,7},{6,4},{7,5},{8,10},{9,11},{10,... | collective-permute-start | bytes 393224 | tf_op jit(solution)/shard_map/ppermute | solution.py:50
  9.7 10.8 %collective-permute-start = (bf16[8,8192]{1,0:T(8,128)(2,1)S(1)}, bf16[8,8192]{1,0:T(8,128)(2,1)S(1)}, u32[]{:S(2)}, u32[]{:S(2)}) collective-permute-start(bf16[8,8192]{1,0:T(8,128)(2,1)S(1)} %pad_maximum_fusion.1.refs_0_), channel_id=1, source_target_pairs={{0,1},{1,0},{2,3},{3,2},{4,5},{5,4},{6,7},{7,6},{8,9},{9,8},{10,11... | collective-permute-start | bytes 393224 | tf_op jit(solution)/shard_map/ppermute | solution.py:50
  16.6 6.4 %collective-permute-start.9 = (bf16[8,8192]{1,0:T(8,128)(2,1)S(1)}, bf16[8,8192]{1,0:T(8,128)(2,1)S(1)}, u32[]{:S(2)}, u32[]{:S(2)}) collective-permute-start(bf16[8,8192]{1,0:T(8,128)(2,1)S(1)} %collective-permute-done.7.refs_8_), channel_id=1, source_target_pairs={{0,2},{1,3},{2,0},{3,1},{4,6},{5,7},{6,4},{7,5},{8,10},{9,11},{10,... | collective-permute-start | bytes 393224 | tf_op jit(solution)/shard_map/ppermute | solution.py:50
  18.4 6.2 %collective-permute-start.13 = (bf16[8,8192]{1,0:T(8,128)(2,1)S(1)}, bf16[8,8192]{1,0:T(8,128)(2,1)S(1)}, u32[]{:S(2)}, u32[]{:S(2)}) collective-permute-start(bf16[8,8192]{1,0:T(8,128)(2,1)S(1)} %collective-permute-done.11.refs_12_), channel_id=1, source_target_pairs={{0,2},{1,3},{2,0},{3,1},{4,6},{5,7},{6,4},{7,5},{8,10},{9,11},{10,... | collective-permute-start | bytes 393224 | tf_op jit(solution)/shard_map/ppermute | solution.py:50
  18.6 7.4 %collective-permute-start.5 = (bf16[8,8192]{1,0:T(8,128)(2,1)S(1)}, bf16[8,8192]{1,0:T(8,128)(2,1)S(1)}, u32[]{:S(2)}, u32[]{:S(2)}) collective-permute-start(bf16[8,8192]{1,0:T(8,128)(2,1)S(1)} %collective-permute-done.3.refs_4_), channel_id=1, source_target_pairs={{0,2},{1,3},{2,0},{3,1},{4,6},{5,7},{6,4},{7,5},{8,10},{9,11},{10,... | collective-permute-start | bytes 393224 | tf_op jit(solution)/shard_map/ppermute | solution.py:50
  20.5 5.6 %collective-permute-start.12 = (bf16[8,8192]{1,0:T(8,128)(2,1)S(1)}, bf16[8,8192]{1,0:T(8,128)(2,1)S(1)}, u32[]{:S(2)}, u32[]{:S(2)}) collective-permute-start(bf16[8,8192]{1,0:T(8,128)(2,1)S(1)} %collective-permute-done.11.refs_12_), channel_id=1, source_target_pairs={{0,1},{1,0},{2,3},{3,2},{4,5},{5,4},{6,7},{7,6},{8,9},{9,8},{10,11... | collective-permute-start | bytes 393224 | tf_op jit(solution)/shard_map/ppermute | solution.py:50
  20.5 6.1 %collective-permute-start.4 = (bf16[8,8192]{1,0:T(8,128)(2,1)S(1)}, bf16[8,8192]{1,0:T(8,128)(2,1)S(1)}, u32[]{:S(2)}, u32[]{:S(2)}) collective-permute-start(bf16[8,8192]{1,0:T(8,128)(2,1)S(1)} %collective-permute-done.3.refs_4_), channel_id=1, source_target_pairs={{0,1},{1,0},{2,3},{3,2},{4,5},{5,4},{6,7},{7,6},{8,9},{9,8},{10,11... | collective-permute-start | bytes 393224 | tf_op jit(solution)/shard_map/ppermute | solution.py:50
  23.0 3.6 %collective-permute-start.8 = (bf16[8,8192]{1,0:T(8,128)(2,1)S(1)}, bf16[8,8192]{1,0:T(8,128)(2,1)S(1)}, u32[]{:S(2)}, u32[]{:S(2)}) collective-permute-start(bf16[8,8192]{1,0:T(8,128)(2,1)S(1)} %collective-permute-done.7.refs_8_), channel_id=1, source_target_pairs={{0,1},{1,0},{2,3},{3,2},{4,5},{5,4},{6,7},{7,6},{8,9},{9,8},{10,11... | collective-permute-start | bytes 393224 | tf_op jit(solution)/shard_map/ppermute | solution.py:50
  24.7 2.0 %collective-permute-start.2 = (bf16[8,8192]{1,0:T(8,128)(2,1)S(1)}, bf16[8,8192]{1,0:T(8,128)(2,1)S(1)}, u32[]{:S(2)}, u32[]{:S(2)}) collective-permute-start(bf16[8,8192]{1,0:T(8,128)(2,1)S(1)} %collective-permute-done.1.refs_2_), channel_id=1, source_target_pairs={{0,1},{1,0},{2,3},{3,2},{4,5},{5,4},{6,7},{7,6},{8,9},{9,8},{10,11... | collective-permute-start | bytes 393224 | tf_op jit(solution)/shard_map/ppermute | solution.py:50
  26.1 1.3 %collective-permute-start.10 = (bf16[8,8192]{1,0:T(8,128)(2,1)S(1)}, bf16[8,8192]{1,0:T(8,128)(2,1)S(1)}, u32[]{:S(2)}, u32[]{:S(2)}) collective-permute-start(bf16[8,8192]{1,0:T(8,128)(2,1)S(1)} %collective-permute-done.9.refs_10_), channel_id=1, source_target_pairs={{0,1},{1,0},{2,3},{3,2},{4,5},{5,4},{6,7},{7,6},{8,9},{9,8},{10,11... | collective-permute-start | bytes 393224 | tf_op jit(solution)/shard_map/ppermute | solution.py:50
  26.1 1.5 %collective-permute-start.14 = (bf16[8,8192]{1,0:T(8,128)(2,1)S(1)}, bf16[8,8192]{1,0:T(8,128)(2,1)S(1)}, u32[]{:S(2)}, u32[]{:S(2)}) collective-permute-start(bf16[8,8192]{1,0:T(8,128)(2,1)S(1)} %collective-permute-done.13.refs_14_), channel_id=1, source_target_pairs={{0,1},{1,0},{2,3},{3,2},{4,5},{5,4},{6,7},{7,6},{8,9},{9,8},{10,11... | collective-permute-start | bytes 393224 | tf_op jit(solution)/shard_map/ppermute | solution.py:50
  26.6 1.3 %collective-permute-start.6 = (bf16[8,8192]{1,0:T(8,128)(2,1)S(1)}, bf16[8,8192]{1,0:T(8,128)(2,1)S(1)}, u32[]{:S(2)}, u32[]{:S(2)}) collective-permute-start(bf16[8,8192]{1,0:T(8,128)(2,1)S(1)} %collective-permute-done.5.refs_6_), channel_id=1, source_target_pairs={{0,1},{1,0},{2,3},{3,2},{4,5},{5,4},{6,7},{7,6},{8,9},{9,8},{10,11... | collective-permute-start | bytes 393224 | tf_op jit(solution)/shard_map/ppermute | solution.py:50
  35.0 4.9 %collective-permute-start.15 = (bf16[64,512]{1,0:T(8,128)(2,1)S(1)}, bf16[64,512]{1,0:T(8,128)(2,1)S(1)}, u32[]{:S(2)}, u32[]{:S(2)}) collective-permute-start(bf16[64,512]{1,0:T(8,128)(2,1)S(1)} %shard_map.64.refs_0_), channel_id=1, source_target_pairs={{0,4},{1,5},{2,6},{3,7},{4,0},{5,1},{6,2},{7,3},{8,12},{9,13},{10,... | collective-permute-start | bytes 196616 | tf_op jit(solution)/shard_map/ppermute | solution.py:50
  36.5 7.3 %collective-permute-start.16 = (bf16[64,512]{1,0:T(8,128)(2,1)S(1)}, bf16[64,512]{1,0:T(8,128)(2,1)S(1)}, u32[]{:S(2)}, u32[]{:S(2)}) collective-permute-start(bf16[64,512]{1,0:T(8,128)(2,1)S(1)} %shard_map.64.refs_0_), channel_id=1, source_target_pairs={{0,8},{1,9},{2,10},{3,11},{4,12},{5,13},{6,14},{7,15},{8,0},{9,1},... | collective-permute-start | bytes 196616 | tf_op jit(solution)/shard_map/ppermute | solution.py:50
  39.9 6.2 %collective-permute-start.17 = (bf16[64,512]{1,0:T(8,128)(2,1)S(1)}, bf16[64,512]{1,0:T(8,128)(2,1)S(1)}, u32[]{:S(2)}, u32[]{:S(2)}) collective-permute-start(bf16[64,512]{1,0:T(8,128)(2,1)S(1)} %shard_map.64.refs_0_), channel_id=1, source_target_pairs={{0,12},{1,13},{2,14},{3,15},{4,8},{5,9},{6,10},{7,11},{8,4},{9,5},... | collective-permute-start | bytes 196616 | tf_op jit(solution)/shard_map/ppermute | solution.py:50
  46.1 6.4 %collective-permute-start.18 = (bf16[3,64,512]{2,1,0:T(8,128)(2,1)S(1)}, bf16[3,64,512]{2,1,0:T(8,128)(2,1)S(1)}, u32[]{:S(2)}, u32[]{:S(2)}) collective-permute-start(bf16[3,64,512]{2,1,0:T(8,128)(2,1)S(1)} %pad_maximum_fusion), channel_id=1, source_target_pairs={{0,2},{1,3},{2,0},{3,1},{4,6},{5,7},{6,4},{7,5},{8,10},{9,11},{10,... | collective-permute-start | bytes 589832 | tf_op jit(solution)/shard_map/ppermute | solution.py:50
  47.7 23.1 %collective-permute-start.22 = (bf16[3,64,512]{2,1,0:T(8,128)(2,1)S(1)}, bf16[3,64,512]{2,1,0:T(8,128)(2,1)S(1)}, u32[]{:S(2)}, u32[]{:S(2)}) collective-permute-start(bf16[3,64,512]{2,1,0:T(8,128)(2,1)S(1)} %pad_maximum_fusion), channel_id=1, source_target_pairs={{0,1},{1,0},{2,3},{3,2},{4,5},{5,4},{6,7},{7,6},{8,9},{9,8},{10,11... | collective-permute-start | bytes 589832 | tf_op jit(solution)/shard_map/ppermute | solution.py:50
  47.7 5.6 %collective-permute-start.20 = (bf16[64,512]{1,0:T(8,128)(2,1)S(1)}, bf16[64,512]{1,0:T(8,128)(2,1)S(1)}, u32[]{:S(2)}, u32[]{:S(2)}) collective-permute-start(bf16[64,512]{1,0:T(8,128)(2,1)S(1)} %shard_map.64.refs_0_), channel_id=1, source_target_pairs={{0,2},{1,3},{2,0},{3,1},{4,6},{5,7},{6,4},{7,5},{8,10},{9,11},{10,... | collective-permute-start | bytes 196616 | tf_op jit(solution)/shard_map/ppermute | solution.py:50
  52.5 28.2 %collective-permute-start.19 = (bf16[3,64,512]{2,1,0:T(8,128)(2,1)S(1)}, bf16[3,64,512]{2,1,0:T(8,128)(2,1)S(1)}, u32[]{:S(2)}, u32[]{:S(2)}) collective-permute-start(bf16[3,64,512]{2,1,0:T(8,128)(2,1)S(1)} %collective-permute-done.18.refs_2_), channel_id=1, source_target_pairs={{0,1},{1,0},{2,3},{3,2},{4,5},{5,4},{6,7},{7,6},{8,9},{9,8},{10,11... | collective-permute-start | bytes 589832 | tf_op jit(solution)/shard_map/ppermute | solution.py:50
  52.5 7.9 %collective-permute-start.23 = (bf16[64,512]{1,0:T(8,128)(2,1)S(1)}, bf16[64,512]{1,0:T(8,128)(2,1)S(1)}, u32[]{:S(2)}, u32[]{:S(2)}) collective-permute-start(bf16[64,512]{1,0:T(8,128)(2,1)S(1)} %shard_map.64.refs_0_), channel_id=1, source_target_pairs={{0,1},{1,0},{2,3},{3,2},{4,5},{5,4},{6,7},{7,6},{8,9},{9,8},{10,11... | collective-permute-start | bytes 196616 | tf_op jit(solution)/shard_map/ppermute | solution.py:50
  53.2 17.5 %collective-permute-start.21 = (bf16[64,512]{1,0:T(8,128)(2,1)S(1)}, bf16[64,512]{1,0:T(8,128)(2,1)S(1)}, u32[]{:S(2)}, u32[]{:S(2)}) collective-permute-start(bf16[64,512]{1,0:T(8,128)(2,1)S(1)} %collective-permute-done.20.refs_0_), channel_id=1, source_target_pairs={{0,1},{1,0},{2,3},{3,2},{4,5},{5,4},{6,7},{7,6},{8,9},{9,8},{10,11... | collective-permute-start | bytes 196616 | tf_op jit(solution)/shard_map/ppermute | solution.py:50

commit v3 on v2

v3 whole, which is shorter than its diff:
```python
import functools

import jax
import jax.numpy as jnp
from jax import lax
from jax.experimental import pallas as pl
from jax.experimental.pallas import tpu as pltpu
from jax.sharding import PartitionSpec as P

CAND = 4
KBLK = 1024
RBLK = 128
VMEM = 50 << 20


def general(factors_in, factors_out, basis_in, basis_out, eigvals, live_counts):
    slot_rows = factors_in.shape[0]
    keep = (lax.iota(jnp.int32, slot_rows) < live_counts[0])[:, None]
    masked = jnp.where(keep, factors_in, jnp.zeros_like(factors_in))
    partial_in = jnp.dot(
        lax.all_gather(masked, "dp", axis=0, tiled=True),
        basis_in,
        preferred_element_type=jnp.float32,
    )
    partial_out = jnp.dot(
        lax.all_gather(factors_out, "dp", axis=0, tiled=True),
        basis_out,
        preferred_element_type=jnp.float32,
    )
    halves = lax.axis_size("basis")
    share = partial_in.shape[0] // halves
    summed_in, summed_out = lax.psum((partial_in, partial_out), "basis")
    first = lax.axis_index("basis") * share
    proj_in = lax.dynamic_slice_in_dim(summed_in, first, share, 0).astype(jnp.bfloat16)
    proj_out = lax.dynamic_slice_in_dim(summed_out, first, share, 0).astype(jnp.bfloat16)
    cand_local = CAND // halves
    per_cand = share // cand_local
    pout_grouped = proj_out.reshape(cand_local, per_cand, proj_out.shape[1])
    shifted = eigvals.astype(jnp.float32) + 0.01
    piece = lax.all_gather(proj_in, "dp", axis=1, tiled=True)
    pin_grouped = piece.reshape(cand_local, per_cand, piece.shape[1])
    summed = jnp.einsum(
        "ati,atj->aij", pout_grouped, pin_grouped, preferred_element_type=jnp.float32
    )
    return (summed / shifted[None, :, :]).astype(jnp.bfloat16)


def swap(x, m):
    n = lax.axis_size("dp")
    return lax.ppermute(x, "dp", [(d, d ^ m) for d in range(n)])


def after(x, *others):
    return lax.optimization_barrier((x,) + others)[0]


def flat(pieces, blocks):
    return [
        (piece, e if stacked else None, m)
        for piece, (stacked, entries) in zip(pieces, blocks)
        for e, m in enumerate(entries)
    ]


def shape_of(blocks):
    return tuple((x.ndim == 3, tuple(entries)) for x, entries in blocks)


def project_kernel(n, blocks, turn, own_ref, *refs):
    pieces, (basis_ref, out_ref, held, rows, acc, sems) = refs[:len(blocks)], refs[len(blocks):]
    step = pl.program_id(0)
    width = held.shape[1]
    at = pl.multiple_of(step * width, width)
    slots = pieces[0].shape[-2]

    @pl.when(step == 0)
    def _():
        for k in range(held.shape[0]):
            pltpu.make_async_copy(
                basis_ref.at[pl.ds(k * width, width)], held.at[k], sems.at[k]
            ).start()

    for piece, e, m in flat(pieces, blocks):
        part = piece[:, pl.ds(at, width)] if e is None else piece[e, :, pl.ds(at, width)]
        rows[m * slots:(m + 1) * slots, :] = part.astype(jnp.float32)
    pltpu.make_async_copy(basis_ref.at[pl.ds(at, width)], held.at[step], sems.at[step]).wait()
    part = jnp.dot(
        rows[...].astype(jnp.bfloat16), held[step], preferred_element_type=jnp.float32
    )

    @pl.when(step == 0)
    def _():
        acc[...] = part

    @pl.when(step > 0)
    def _():
        acc[...] += part

    @pl.when(step == pl.num_programs(0) - 1)
    def _():
        total = n * slots
        to = lax.broadcasted_iota(jnp.int32, (total, total), 0)
        come = lax.broadcasted_iota(jnp.int32, (total, total), 1)
        where = jnp.bitwise_xor(come // slots, own_ref[0]) * slots + come % slots
        pick = jnp.where(to == where, 1.0, 0.0).astype(jnp.bfloat16)
        proj = jnp.dot(pick, acc[...].astype(jnp.bfloat16), preferred_element_type=jnp.float32)
        if turn:
            turned = proj.T
            token = lax.broadcasted_iota(jnp.int32, turned.shape, 1)
            for c in range(CAND):
                own_tokens = token // (total // CAND) == c
                out_ref[c] = jnp.where(own_tokens, turned, 0.0).astype(jnp.bfloat16)
        else:
            out_ref[...] = proj.astype(jnp.bfloat16)


def whole(shape):
    return pl.BlockSpec(shape, lambda s, own: (0,) * len(shape))


def project(own, n, blocks, basis, turn):
    slots = blocks[0][0].shape[-2]
    depth, cols = basis.shape
    total = n * slots
    shape = (CAND, cols, total) if turn else (total, cols)
    steps = depth // KBLK
    return pl.pallas_call(
        functools.partial(project_kernel, n, shape_of(blocks), turn),
        out_shape=jax.ShapeDtypeStruct(shape, jnp.bfloat16),
        grid_spec=pltpu.PrefetchScalarGridSpec(
            num_scalar_prefetch=1,
            grid=(steps,),
            in_specs=[whole(x.shape) for x, _ in blocks] + [pl.BlockSpec(memory_space=pl.ANY)],
            out_specs=whole(shape),
            scratch_shapes=[
                pltpu.VMEM((steps, KBLK, cols), jnp.bfloat16),
                pltpu.VMEM((total, KBLK), jnp.float32),
                pltpu.VMEM((total, cols), jnp.float32),
                pltpu.SemaphoreType.DMA((steps,)),
            ],
        ),
        compiler_params=pltpu.CompilerParams(vmem_limit_bytes=VMEM),
        cost_estimate=pl.CostEstimate(
            flops=2 * total * depth * cols,
            bytes_accessed=2 * depth * cols,
            transcendentals=0,
        ),
    )(own, *[x for x, _ in blocks], basis)


def outer_kernel(blocks, own_ref, *refs):
    pieces = refs[:len(blocks)]
    left_ref, eig_ref, out_ref, right, eig, out, eig_sems, out_sems = (
        *refs[len(blocks):len(blocks) + 2], *refs[-6:]
    )
    listed = flat(pieces, blocks)
    count = len(listed)
    step = pl.program_id(0)
    rows, cols = eig.shape[1:]

    def columns(s):
        m = jnp.int32(listed[0][2])
        for k in range(1, count):
            m = jnp.where(s == k, listed[k][2], m)
        return pl.ds(pl.multiple_of(jnp.bitwise_xor(m, own_ref[0]) * cols, cols), cols)

    def read(s):
        return pltpu.make_async_copy(eig_ref.at[:, columns(s)], eig.at[s], eig_sems.at[s])

    def write(s, c):
        slot = lax.rem(s, 2)
        return pltpu.make_async_copy(
            out.at[slot, c], out_ref.at[c, :, columns(s)], out_sems.at[slot, c]
        )

    @pl.when(step == 0)
    def _():
        for s in range(count):
            read(s).start()

    for k, (piece, e, _) in enumerate(listed):
        @pl.when(step == k)
        def _(piece=piece, e=e):
            right[...] = piece[...] if e is None else piece[e]

    read(step).wait()
    slot = lax.rem(step, 2)
    for c in range(CAND):
        @pl.when(step >= 2)
        def _(c=c):
            write(step - 2, c).wait()

    for r in range(0, rows, RBLK):
        scale = 1.0 / (eig[step, r:r + RBLK, :].astype(jnp.float32) + 0.01)
        for c in range(CAND):
            summed = jnp.dot(
                left_ref[c, r:r + RBLK, :], right[...], preferred_element_type=jnp.float32
            )
            out[slot, c, r:r + RBLK, :] = (summed * scale).astype(jnp.bfloat16)
    for c in range(CAND):
        write(step, c).start()

    @pl.when(step == count - 1)
    def _():
        for s in range(max(0, count - 2), count):
            for c in range(CAND):
                write(s, c).wait()


def outer(own, blocks, left, eigvals, before):
    total, cols = blocks[0][0].shape[-2:]
    rows, width = eigvals.shape
    count = sum(len(entries) for _, entries in blocks)
    operands = [own] + [x for x, _ in blocks] + [left, eigvals]
    in_specs = [whole(x.shape) for x, _ in blocks] + [
        whole(left.shape),
        pl.BlockSpec(memory_space=pl.ANY),
    ]
    aliases = {}
    if before is not None:
        aliases = {len(operands): 0}
        operands.append(before)
        in_specs.append(pl.BlockSpec(memory_space=pl.ANY))
    share = count * cols
    return pl.pallas_call(
        functools.partial(outer_kernel, shape_of(blocks)),
        out_shape=jax.ShapeDtypeStruct((CAND, rows, width), jnp.bfloat16),
        grid_spec=pltpu.PrefetchScalarGridSpec(
            num_scalar_prefetch=1,
            grid=(count,),
            in_specs=in_specs,
            out_specs=pl.BlockSpec(memory_space=pl.ANY),
            scratch_shapes=[
                pltpu.VMEM((total, cols), jnp.bfloat16),
                pltpu.VMEM((count, rows, cols), jnp.bfloat16),
                pltpu.VMEM((2, CAND, rows, cols), jnp.bfloat16),
                pltpu.SemaphoreType.DMA((count,)),
                pltpu.SemaphoreType.DMA((2, CAND)),
            ],
        ),
        input_output_aliases=aliases,
        compiler_params=pltpu.CompilerParams(vmem_limit_bytes=VMEM),
        cost_estimate=pl.CostEstimate(
            flops=2 * total * rows * share,
            bytes_accessed=2 * rows * share * (CAND + 1),
            transcendentals=rows * share,
        ),
    )(*operands)


def by_swaps(factors_in, factors_out, basis_in, basis_out, eigvals, live_counts):
    n = lax.axis_size("dp")
    own = lax.axis_index("dp").astype(jnp.int32)[None]
    slots = factors_in.shape[0]
    column = (0, 4, 8, 12)
    pair = (2, 6, 10, 14)
    core = (1, 5, 9, 13)
    other = (3, 7, 11, 15)

    def send(x):
        return swap(x, 4), swap(x, 2), swap(x, 8), swap(x, 12)

    a = factors_in
    a1, ap, a2, a3 = send(a)
    keep = (lax.iota(jnp.int32, slots) < live_counts[0])[:, None]
    b = jnp.where(keep, factors_out, jnp.zeros_like(factors_out))
    a1, ap = lax.optimization_barrier((a1, ap))
    ap1 = swap(a1, 2)
    b, a2, a3 = lax.optimization_barrier((b, a2, a3))
    ap23 = swap(jnp.stack([a2, a3]), 2)
    a_column = jnp.stack([a, a1, a2, a3])
    a_core = swap(a_column, 1)
    b1, bp, b2, b3 = send(b)
    a_pair = jnp.stack([ap, ap1, ap23[0], ap23[1]])
    a_other = swap(a_pair, 1)
    b1, b2, b3, bp = lax.optimization_barrier((b1, b2, b3, bp, a_pair))[:4]
    b_column = jnp.stack([b, b1, b2, b3])
    bp123 = swap(b_column[1:], 2)
    b_core = swap(b_column, 1)
    pin = project(
        own, n, [(a_column, column), (a_pair, pair), (a_core, core), (a_other, other)],
        basis_in, False,
    )

    g1, gp, g2, g3 = send(pin)
    b_pair = jnp.concatenate([after(bp, pin)[None], bp123])
    b_other = swap(b_pair, 1)
    left = project(
        own, n, [(b_column, column), (b_pair, pair), (b_core, core), (b_other, other)],
        basis_out, True,
    )
    g1, g2, g3, gp = lax.optimization_barrier((g1, g2, g3, gp, left))[:4]
    g_column = jnp.stack([pin, g1, g2, g3])
    gp123 = swap(g_column[1:], 2)
    g_core = swap(g_column, 1)
    out = outer(own, [(g_column, column)], left, eigvals, None)
    g_pair = jnp.concatenate([gp[None], after(gp123, out)])
    g_other = swap(g_pair, 1)
    out = outer(own, [(g_core, core), (g_pair, pair)], left, eigvals, out)
    return outer(own, [(g_other, other)], left, eigvals, out)


def solution(mesh):
    placed = (
        P(("groups", "dp"), "basis"),
        P(("groups", "dp"), "basis"),
        P("basis", "dp"),
        P("basis", "dp"),
        P("dp", None),
        P(("groups", "dp")),
    )
    chosen = by_swaps if mesh.shape["basis"] == 1 and mesh.shape["dp"] == 16 else general
    return jax.shard_map(
        chosen,
        mesh=mesh,
        in_specs=placed,
        out_specs=P(("groups", "basis"), "dp", None),
        check_vma=False,
    )
```

time: 86.8 us -> 66.2 us (0.76)
  waiting for transfers between devices: 24 us -> 8.17 us
  Pallas kernels: 39.7 us -> 30.3 us
  starting transfers between devices: 19.7 us -> 23.7 us
  other arithmetic: 1.88 us -> 2.94 us
    ppermute x24 -> x22, waiting for transfers between devices: 24 us -> 8.17 us  [swap(): return lax.ppermute(x, 'dp', [(d, d ^ m) for d in range(n)])]
    pallas_call x6 -> x5, Pallas kernels: 39.7 us -> 30.3 us  [the longest x3 21.5 us: outer(): pl.pallas_call(functools.partial(outer_kernel, shape_of(blocks)), out_sha...]
    ppermute x24 -> x22, starting transfers between devices: 19.7 us -> 23.7 us  [swap(): return lax.ppermute(x, 'dp', [(d, d ^ m) for d in range(n)])]
    another operation x1 -> x7, other arithmetic: 0.02 us -> 1.8 us  [the longest x1 1.07 us: by_swaps(): a_column = jnp.stack([a, a1, a2, a3])]
  transfers between devices with their start and end apart: 24 -> 22, of which waited for: 11 -> 6; matrix products, arithmetic and copies ran while one was open for 0% -> 4% of each run, Pallas kernels for 32% -> 37%
where the time goes in v3:
time: 66.2 us; the launch traced here: 65.9 us
  Pallas kernels  30.3 us (46%)
  starting transfers between devices  23.7 us (36%)
  waiting for transfers between devices  8.17 us (12%)
  other arithmetic  2.94 us (4%)
  between operations  0.82 us (1%)
    ppermute x22, starting transfers between devices, swap(): return lax.ppermute(x, 'dp', [(d, d ^ m) for d in range(n)])  23.7 us
    pallas_call x3, Pallas kernels, outer(): pl.pallas_call(functools.partial(outer_kernel, shape_of(blocks)), out_sha...  21.5 us
    pallas_call x2, Pallas kernels, project(): pl.pallas_call(functools.partial(project_kernel, n, shape_of(blocks), tur...  8.8 us
    ppermute x22, waiting for transfers between devices, swap(): return lax.ppermute(x, 'dp', [(d, d ^ m) for d in range(n)])  8.17 us
  transfers between devices with their start and end apart: 22, of which 6 were waited for; matrix products, arithmetic and copies ran while one was open for 4% of the time, Pallas kernels for 37%

profile of v3, /device:TPU:0, one launch (start us, length us, event | category | flops | bytes accessed | tf_op | source)
XLA Modules:
  0.0 65.9 jit_solution(4955438836113031558)
XLA Ops:
  0.0 2.9 %collective-permute-start.1 = (bf16[4,8192]{1,0:T(4,128)(2,1)}, bf16[4,8192]{1,0:T(4,128)(2,1)S(1)}, u32[]{:S(2)}, u32[]{:S(2)}) collective-permute-start(bf16[4,8192]{1,0:T(4,128)(2,1)} %param.6), channel_id=1, source_target_pairs={{0,2},{1,3},{2,0},{3,1},{4,6},{5,7},{6,4},{7,5},{8,10},{9,11},{10,... | collective-permute-start | bytes 196616 | tf_op jit(solution)/shard_map/ppermute | solution.py:50
  2.9 1.6 %collective-permute-start = (bf16[4,8192]{1,0:T(4,128)(2,1)}, bf16[4,8192]{1,0:T(4,128)(2,1)S(1)}, u32[]{:S(2)}, u32[]{:S(2)}) collective-permute-start(bf16[4,8192]{1,0:T(4,128)(2,1)} %param.6), channel_id=1, source_target_pairs={{0,4},{1,5},{2,6},{3,7},{4,0},{5,1},{6,2},{7,3},{8,12},{9,13},{10,... | collective-permute-start | bytes 196616 | tf_op jit(solution)/shard_map/ppermute | solution.py:50
  4.5 2.5 %collective-permute-start.3 = (bf16[4,8192]{1,0:T(4,128)(2,1)}, bf16[4,8192]{1,0:T(4,128)(2,1)S(1)}, u32[]{:S(2)}, u32[]{:S(2)}) collective-permute-start(bf16[4,8192]{1,0:T(4,128)(2,1)} %param.6), channel_id=1, source_target_pairs={{0,12},{1,13},{2,14},{3,15},{4,8},{5,9},{6,10},{7,11},{8,4},{9,5},... | collective-permute-start | bytes 196616 | tf_op jit(solution)/shard_map/ppermute | solution.py:50
  7.0 0.1 collective-permute-start.2
  7.8 0.9 %broadcast_select_fusion = bf16[4,8192]{1,0:T(4,128)(2,1)S(1)} fusion(bf16[4,8192]{1,0:T(4,128)(2,1)} %param.7, pred[4]{0:T(512)(128)(4,1)S(1)} %iota_compare_fusion), kind=kLoop, calls=%fused_computation.9 | loop fusion | flops 32768 | bytes 131076 | tf_op jit(solution)/shard_map/jit(_where)/select_n | solution.py:266
  8.7 2.6 %collective-permute-done.3 = bf16[4,8192]{1,0:T(4,128)(2,1)S(1)} collective-permute-done((bf16[4,8192]{1,0:T(4,128)(2,1)}, bf16[4,8192]{1,0:T(4,128)(2,1)S(1)}, u32[]{:S(2)}, u32[]{:S(2)}) %collective-permute-start.3) | collective-permute-done | bytes 65568 | tf_op jit(solution)/shard_map/ppermute | solution.py:50
  11.3 2.1 %collective-permute-done.2 = bf16[4,8192]{1,0:T(4,128)(2,1)S(1)} collective-permute-done((bf16[4,8192]{1,0:T(4,128)(2,1)}, bf16[4,8192]{1,0:T(4,128)(2,1)S(1)}, u32[]{:S(2)}, u32[]{:S(2)}) %collective-permute-start.2) | collective-permute-done | bytes 65568 | tf_op jit(solution)/shard_map/ppermute | solution.py:50
  13.4 0.5 collective-permute-start.15
  14.0 2.4 %collective-permute-start.14 = (bf16[4,8192]{1,0:T(4,128)(2,1)S(1)}, bf16[4,8192]{1,0:T(4,128)(2,1)S(1)}, u32[]{:S(2)}, u32[]{:S(2)}) collective-permute-start(bf16[4,8192]{1,0:T(4,128)(2,1)S(1)} %broadcast_select_fusion), channel_id=1, source_target_pairs={{0,12},{1,13},{2,14},{3,15},{4,8},{5,9},{6,10},{7,11},{8,4},{9,5},... | collective-permute-start | bytes 196616 | tf_op jit(solution)/shard_map/ppermute | solution.py:50
  16.3 0.0 collective-permute-start.13
  16.3 0.0 collective-permute-done.1
  16.3 1.6 %collective-permute-start.4 = (bf16[4,8192]{1,0:T(4,128)(2,1)S(1)}, bf16[4,8192]{1,0:T(4,128)(2,1)S(1)}, u32[]{:S(2)}, u32[]{:S(2)}) collective-permute-start(bf16[4,8192]{1,0:T(4,128)(2,1)S(1)} %collective-permute-done), channel_id=1, source_target_pairs={{0,2},{1,3},{2,0},{3,1},{4,6},{5,7},{6,4},{7,5},{8,10},{9,11},{10,... | collective-permute-start | bytes 196616 | tf_op jit(solution)/shard_map/ppermute | solution.py:50
  17.9 0.1 pad_maximum_fusion.8
  18.0 0.6 collective-permute-start.5
  18.6 1.1 %pad_maximum_fusion.refs_0_ = bf16[4,4,8192]{2,1,0:T(4,128)(2,1)S(1)} fusion(bf16[1,4,8192]{2,1,0:T(4,128)(2,1)S(1)} %bitcast.26, bf16[1,4,8192]{2,1,0:T(4,128)(2,1)S(1)} %bitcast.28, bf16[1,4,8192]{2,1,0:T(4,128)(2,1)S(1)} %bitcast.40, bf16[1,4,8192]{2,1,0:T(4,128)(2,1)} %bitcast.37), kind=kLoop, calls=%fused_computation | loop fusion | flops 393216 | bytes 524288 | tf_op jit(solution)/shard_map/stack | solution.py:271
  19.7 1.3 %collective-permute-done.4 = bf16[4,8192]{1,0:T(4,128)(2,1)S(1)} collective-permute-done((bf16[4,8192]{1,0:T(4,128)(2,1)S(1)}, bf16[4,8192]{1,0:T(4,128)(2,1)S(1)}, u32[]{:S(2)}, u32[]{:S(2)}) %collective-permute-start.4) | collective-permute-done | bytes 65568 | tf_op jit(solution)/shard_map/ppermute | solution.py:50
  21.0 2.3 %collective-permute-start.12 = (bf16[4,8192]{1,0:T(4,128)(2,1)S(1)}, bf16[4,8192]{1,0:T(4,128)(2,1)S(1)}, u32[]{:S(2)}, u32[]{:S(2)}) collective-permute-start(bf16[4,8192]{1,0:T(4,128)(2,1)S(1)} %broadcast_select_fusion), channel_id=1, source_target_pairs={{0,4},{1,5},{2,6},{3,7},{4,0},{5,1},{6,2},{7,3},{8,12},{9,13},{10,... | collective-permute-start | bytes 196616 | tf_op jit(solution)/shard_map/ppermute | solution.py:50
  23.3 0.0 collective-permute-done.5
  23.3 0.0 collective-permute-start.6
  23.3 0.2 pad_maximum_fusion.1.refs_1_
  23.5 0.0 collective-permute-done.15
  23.5 0.6 collective-permute-start.7
  24.1 1.5 %collective-permute-done.12 = bf16[4,8192]{1,0:T(4,128)(2,1)S(1)} collective-permute-done((bf16[4,8192]{1,0:T(4,128)(2,1)S(1)}, bf16[4,8192]{1,0:T(4,128)(2,1)S(1)}, u32[]{:S(2)}, u32[]{:S(2)}) %collective-permute-start.12) | collective-permute-done | bytes 65568 | tf_op jit(solution)/shard_map/ppermute | solution.py:50
  25.5 0.2 pad_maximum_fusion.6
  25.7 1.0 %collective-permute-start.16 = (bf16[3,4,8192]{2,1,0:T(4,128)(2,1)S(1)}, bf16[3,4,8192]{2,1,0:T(4,128)(2,1)S(1)}, u32[]{:S(2)}, u32[]{:S(2)}) collective-permute-start(bf16[3,4,8192]{2,1,0:T(4,128)(2,1)S(1)} %pad_maximum_fusion.6), channel_id=1, source_target_pairs={{0,2},{1,3},{2,0},{3,1},{4,6},{5,7},{6,4},{7,5},{8,10},{9,11},{10,... | collective-permute-start | bytes 589832 | tf_op jit(solution)/shard_map/ppermute | solution.py:50
  26.7 0.2 pad_maximum_fusion.2.refs_0_
  26.9 0.1 collective-permute-start.17
  27.0 0.0 collective-permute-done.7.refs_3_
  27.0 4.3 %shard_map.64 = bf16[64,512]{1,0:T(8,128)(2,1)S(1)} custom-call(s32[1]{0:T(128)} %bitcast.own_ref, bf16[4,4,8192]{2,1,0:T(4,128)(2,1)S(1)} %pad_maximum_fusion.refs_0_, bf16[4,4,8192]{2,1,0:T(4,128)(2,1)S(1)} %pad_maximum_fusion.1.refs_1_, bf16[4,4,8192]{2,1,0:T(4,128)(2,1)S(1)} %collective-permute-done.6.refs_2_, ...), custom_call_target="tpu_custom_call" | custom-call | flops 536870912 | bytes 8388608 | tf_op jit(solution)/shard_map/pallas_call | solution.py:127
  31.3 0.1 collective-permute-done.16
  31.4 0.2 pad_maximum_fusion.3.refs_1_
  31.6 0.5 collective-permute-start.18
  32.0 1.1 %collective-permute-start.11 = (bf16[64,512]{1,0:T(8,128)(2,1)S(1)}, bf16[64,512]{1,0:T(8,128)(2,1)S(1)}, u32[]{:S(2)}, u32[]{:S(2)}) collective-permute-start(bf16[64,512]{1,0:T(8,128)(2,1)S(1)} %shard_map.64), channel_id=1, source_target_pairs={{0,2},{1,3},{2,0},{3,1},{4,6},{5,7},{6,4},{7,5},{8,10},{9,11},{10,... | collective-permute-start | bytes 196616 | tf_op jit(solution)/shard_map/ppermute | solution.py:50
  33.2 1.8 %collective-permute-start.10 = (bf16[64,512]{1,0:T(8,128)(2,1)S(1)}, bf16[64,512]{1,0:T(8,128)(2,1)S(1)}, u32[]{:S(2)}, u32[]{:S(2)}) collective-permute-start(bf16[64,512]{1,0:T(8,128)(2,1)S(1)} %shard_map.64), channel_id=1, source_target_pairs={{0,12},{1,13},{2,14},{3,15},{4,8},{5,9},{6,10},{7,11},{8,4},{9,5},... | collective-permute-start | bytes 196616 | tf_op jit(solution)/shard_map/ppermute | solution.py:50
  34.9 1.7 %collective-permute-start.9 = (bf16[64,512]{1,0:T(8,128)(2,1)S(1)}, bf16[64,512]{1,0:T(8,128)(2,1)S(1)}, u32[]{:S(2)}, u32[]{:S(2)}) collective-permute-start(bf16[64,512]{1,0:T(8,128)(2,1)S(1)} %shard_map.64), channel_id=1, source_target_pairs={{0,8},{1,9},{2,10},{3,11},{4,12},{5,13},{6,14},{7,15},{8,0},{9,1},... | collective-permute-start | bytes 196616 | tf_op jit(solution)/shard_map/ppermute | solution.py:50
  36.7 0.9 %collective-permute-start.8 = (bf16[64,512]{1,0:T(8,128)(2,1)S(1)}, bf16[64,512]{1,0:T(8,128)(2,1)S(1)}, u32[]{:S(2)}, u32[]{:S(2)}) collective-permute-start(bf16[64,512]{1,0:T(8,128)(2,1)S(1)} %shard_map.64), channel_id=1, source_target_pairs={{0,4},{1,5},{2,6},{3,7},{4,0},{5,1},{6,2},{7,3},{8,12},{9,13},{10,... | collective-permute-start | bytes 196616 | tf_op jit(solution)/shard_map/ppermute | solution.py:50
  37.6 0.0 collective-permute-done.18.refs_3_
  37.6 4.5 %shard_map.65.refs_1_.refs_2_ = bf16[4,512,64]{2,1,0:T(8,128)(2,1)S(1)} custom-call(s32[1]{0:T(128)} %bitcast.own_ref, bf16[4,4,8192]{2,1,0:T(4,128)(2,1)S(1)} %pad_maximum_fusion.2.refs_0_, bf16[4,4,8192]{2,1,0:T(4,128)(2,1)S(1)} %pad_maximum_fusion.3.refs_1_, bf16[4,4,8192]{2,1,0:T(4,128)(2,1)S(1)} %collective-permute-done.17.refs_2_, ...), custom_call_target="tpu_custom_call" | custom-call | flops 536870912 | bytes 8388608 | tf_op jit(solution)/shard_map/pallas_call | solution.py:127
  42.1 0.0 collective-permute-done.10
  42.1 0.6 collective-permute-done.9
  42.7 1.0 %collective-permute-start.19 = (bf16[3,64,512]{2,1,0:T(8,128)(2,1)S(1)}, bf16[3,64,512]{2,1,0:T(8,128)(2,1)S(1)}, u32[]{:S(2)}, u32[]{:S(2)}) collective-permute-start(bf16[3,64,512]{2,1,0:T(8,128)(2,1)S(1)} %pad_maximum_fusion.7), channel_id=1, source_target_pairs={{0,2},{1,3},{2,0},{3,1},{4,6},{5,7},{6,4},{7,5},{8,10},{9,11},{10,... | collective-permute-start | bytes 589832 | tf_op jit(solution)/shard_map/ppermute | solution.py:50
  43.7 0.1 collective-permute-start.21
  43.8 5.8 %shard_map.66.refs_4_ = bf16[4,512,8192]{2,1,0:T(8,128)(2,1)} custom-call(s32[1]{0:T(128)} %bitcast.own_ref, bf16[4,64,512]{2,1,0:T(8,128)(2,1)S(1)} %pad_maximum_fusion.4.refs_0_, bf16[4,512,64]{2,1,0:T(8,128)(2,1)S(1)} %shard_map.65.refs_1_.refs_2_, bf16[512,8192]{1,0:T(8,128)(2,1)} %refs_2_.3), custom_call_target="tpu_custom_call" | custom-call | flops 134217728 | bytes 10485760 | tf_op jit(solution)/shard_map/pallas_call | solution.py:225
  49.7 0.0 collective-permute-done.19
  49.7 0.5 collective-permute-start.20
  50.2 9.8 %shard_map.67.refs_3_ = bf16[4,512,8192]{2,1,0:T(8,128)(2,1)} custom-call(s32[1]{0:T(128)} %bitcast.own_ref, bf16[4,64,512]{2,1,0:T(8,128)(2,1)S(1)} %collective-permute-done.21.refs_0_, bf16[4,64,512]{2,1,0:T(8,128)(2,1)S(1)} %pad_maximum_fusion.5.refs_1_, bf16[4,512,64]{2,1,0:T(8,128)(2,1)S(1)} %shard_map.65.refs_1_.refs_2_, ...), custom_call_target="tpu_custom_call", output_to_operand_aliasing={{}: (5, {})} | custom-call | flops 268435456 | bytes 20971520 | tf_op jit(solution)/shard_map/pallas_call | solution.py:225
  60.0 0.0 collective-permute-done.20.refs_0_
  60.1 5.8 %shard_map.68 = bf16[4,512,8192]{2,1,0:T(8,128)(2,1)} custom-call(s32[1]{0:T(128)} %bitcast.own_ref, bf16[4,64,512]{2,1,0:T(8,128)(2,1)S(1)} %collective-permute-done.20.refs_0_, bf16[4,512,64]{2,1,0:T(8,128)(2,1)S(1)} %shard_map.65.refs_1_.refs_2_, bf16[512,8192]{1,0:T(8,128)(2,1)} %refs_2_.3, ...), custom_call_target="tpu_custom_call", output_to_operand_aliasing={{}: (4, {})} | custom-call | flops 134217728 | bytes 10485760 | tf_op jit(solution)/shard_map/pallas_call | solution.py:225
  (12 shorter events, 0.1 us)
Async XLA Ops:
  0.0 16.3 %collective-permute-start.1 = (bf16[4,8192]{1,0:T(4,128)(2,1)}, bf16[4,8192]{1,0:T(4,128)(2,1)S(1)}, u32[]{:S(2)}, u32[]{:S(2)}) collective-permute-start(bf16[4,8192]{1,0:T(4,128)(2,1)} %param.6), channel_id=1, source_target_pairs={{0,2},{1,3},{2,0},{3,1},{4,6},{5,7},{6,4},{7,5},{8,10},{9,11},{10,... | collective-permute-start | bytes 196616 | tf_op jit(solution)/shard_map/ppermute | solution.py:50
  2.9 13.4 %collective-permute-start = (bf16[4,8192]{1,0:T(4,128)(2,1)}, bf16[4,8192]{1,0:T(4,128)(2,1)S(1)}, u32[]{:S(2)}, u32[]{:S(2)}) collective-permute-start(bf16[4,8192]{1,0:T(4,128)(2,1)} %param.6), channel_id=1, source_target_pairs={{0,4},{1,5},{2,6},{3,7},{4,0},{5,1},{6,2},{7,3},{8,12},{9,13},{10,... | collective-permute-start | bytes 196616 | tf_op jit(solution)/shard_map/ppermute | solution.py:50
  4.5 6.8 %collective-permute-start.3 = (bf16[4,8192]{1,0:T(4,128)(2,1)}, bf16[4,8192]{1,0:T(4,128)(2,1)S(1)}, u32[]{:S(2)}, u32[]{:S(2)}) collective-permute-start(bf16[4,8192]{1,0:T(4,128)(2,1)} %param.6), channel_id=1, source_target_pairs={{0,12},{1,13},{2,14},{3,15},{4,8},{5,9},{6,10},{7,11},{8,4},{9,5},... | collective-permute-start | bytes 196616 | tf_op jit(solution)/shard_map/ppermute | solution.py:50
  7.0 6.4 %collective-permute-start.2 = (bf16[4,8192]{1,0:T(4,128)(2,1)}, bf16[4,8192]{1,0:T(4,128)(2,1)S(1)}, u32[]{:S(2)}, u32[]{:S(2)}) collective-permute-start(bf16[4,8192]{1,0:T(4,128)(2,1)} %param.6), channel_id=1, source_target_pairs={{0,8},{1,9},{2,10},{3,11},{4,12},{5,13},{6,14},{7,15},{8,0},{9,1},... | collective-permute-start | bytes 196616 | tf_op jit(solution)/shard_map/ppermute | solution.py:50
  13.4 10.0 %collective-permute-start.15 = (bf16[4,8192]{1,0:T(4,128)(2,1)S(1)}, bf16[4,8192]{1,0:T(4,128)(2,1)S(1)}, u32[]{:S(2)}, u32[]{:S(2)}) collective-permute-start(bf16[4,8192]{1,0:T(4,128)(2,1)S(1)} %broadcast_select_fusion), channel_id=1, source_target_pairs={{0,2},{1,3},{2,0},{3,1},{4,6},{5,7},{6,4},{7,5},{8,10},{9,11},{10,... | collective-permute-start | bytes 196616 | tf_op jit(solution)/shard_map/ppermute | solution.py:50
  14.0 10.1 %collective-permute-start.14 = (bf16[4,8192]{1,0:T(4,128)(2,1)S(1)}, bf16[4,8192]{1,0:T(4,128)(2,1)S(1)}, u32[]{:S(2)}, u32[]{:S(2)}) collective-permute-start(bf16[4,8192]{1,0:T(4,128)(2,1)S(1)} %broadcast_select_fusion), channel_id=1, source_target_pairs={{0,12},{1,13},{2,14},{3,15},{4,8},{5,9},{6,10},{7,11},{8,4},{9,5},... | collective-permute-start | bytes 196616 | tf_op jit(solution)/shard_map/ppermute | solution.py:50
  16.3 7.7 %collective-permute-start.13 = (bf16[4,8192]{1,0:T(4,128)(2,1)S(1)}, bf16[4,8192]{1,0:T(4,128)(2,1)S(1)}, u32[]{:S(2)}, u32[]{:S(2)}) collective-permute-start(bf16[4,8192]{1,0:T(4,128)(2,1)S(1)} %broadcast_select_fusion), channel_id=1, source_target_pairs={{0,8},{1,9},{2,10},{3,11},{4,12},{5,13},{6,14},{7,15},{8,0},{9,1},... | collective-permute-start | bytes 196616 | tf_op jit(solution)/shard_map/ppermute | solution.py:50
  16.3 4.6 %collective-permute-start.4 = (bf16[4,8192]{1,0:T(4,128)(2,1)S(1)}, bf16[4,8192]{1,0:T(4,128)(2,1)S(1)}, u32[]{:S(2)}, u32[]{:S(2)}) collective-permute-start(bf16[4,8192]{1,0:T(4,128)(2,1)S(1)} %collective-permute-done), channel_id=1, source_target_pairs={{0,2},{1,3},{2,0},{3,1},{4,6},{5,7},{6,4},{7,5},{8,10},{9,11},{10,... | collective-permute-start | bytes 196616 | tf_op jit(solution)/shard_map/ppermute | solution.py:50
  18.0 5.3 %collective-permute-start.5 = (bf16[2,4,8192]{2,1,0:T(4,128)(2,1)S(1)}, bf16[2,4,8192]{2,1,0:T(4,128)(2,1)S(1)}, u32[]{:S(2)}, u32[]{:S(2)}) collective-permute-start(bf16[2,4,8192]{2,1,0:T(4,128)(2,1)S(1)} %pad_maximum_fusion.8), channel_id=1, source_target_pairs={{0,2},{1,3},{2,0},{3,1},{4,6},{5,7},{6,4},{7,5},{8,10},{9,11},{10,... | collective-permute-start | bytes 393224 | tf_op jit(solution)/shard_map/ppermute | solution.py:50
  21.0 4.6 %collective-permute-start.12 = (bf16[4,8192]{1,0:T(4,128)(2,1)S(1)}, bf16[4,8192]{1,0:T(4,128)(2,1)S(1)}, u32[]{:S(2)}, u32[]{:S(2)}) collective-permute-start(bf16[4,8192]{1,0:T(4,128)(2,1)S(1)} %broadcast_select_fusion), channel_id=1, source_target_pairs={{0,4},{1,5},{2,6},{3,7},{4,0},{5,1},{6,2},{7,3},{8,12},{9,13},{10,... | collective-permute-start | bytes 196616 | tf_op jit(solution)/shard_map/ppermute | solution.py:50
  23.3 3.7 %collective-permute-start.6 = (bf16[4,4,8192]{2,1,0:T(4,128)(2,1)S(1)}, bf16[4,4,8192]{2,1,0:T(4,128)(2,1)S(1)}, u32[]{:S(2)}, u32[]{:S(2)}) collective-permute-start(bf16[4,4,8192]{2,1,0:T(4,128)(2,1)S(1)} %pad_maximum_fusion.refs_0_), channel_id=1, source_target_pairs={{0,1},{1,0},{2,3},{3,2},{4,5},{5,4},{6,7},{7,6},{8,9},{9,8},{10,11... | collective-permute-start | bytes 786440 | tf_op jit(solution)/shard_map/ppermute | solution.py:50
  23.5 3.5 %collective-permute-start.7 = (bf16[4,4,8192]{2,1,0:T(4,128)(2,1)S(1)}, bf16[4,4,8192]{2,1,0:T(4,128)(2,1)S(1)}, u32[]{:S(2)}, u32[]{:S(2)}) collective-permute-start(bf16[4,4,8192]{2,1,0:T(4,128)(2,1)S(1)} %pad_maximum_fusion.1.refs_1_), channel_id=1, source_target_pairs={{0,1},{1,0},{2,3},{3,2},{4,5},{5,4},{6,7},{7,6},{8,9},{9,8},{10,11... | collective-permute-start | bytes 786440 | tf_op jit(solution)/shard_map/ppermute | solution.py:50
  25.7 5.7 %collective-permute-start.16 = (bf16[3,4,8192]{2,1,0:T(4,128)(2,1)S(1)}, bf16[3,4,8192]{2,1,0:T(4,128)(2,1)S(1)}, u32[]{:S(2)}, u32[]{:S(2)}) collective-permute-start(bf16[3,4,8192]{2,1,0:T(4,128)(2,1)S(1)} %pad_maximum_fusion.6), channel_id=1, source_target_pairs={{0,2},{1,3},{2,0},{3,1},{4,6},{5,7},{6,4},{7,5},{8,10},{9,11},{10,... | collective-permute-start | bytes 589832 | tf_op jit(solution)/shard_map/ppermute | solution.py:50
  26.9 9.8 %collective-permute-start.17 = (bf16[4,4,8192]{2,1,0:T(4,128)(2,1)S(1)}, bf16[4,4,8192]{2,1,0:T(4,128)(2,1)S(1)}, u32[]{:S(2)}, u32[]{:S(2)}) collective-permute-start(bf16[4,4,8192]{2,1,0:T(4,128)(2,1)S(1)} %pad_maximum_fusion.2.refs_0_), channel_id=1, source_target_pairs={{0,1},{1,0},{2,3},{3,2},{4,5},{5,4},{6,7},{7,6},{8,9},{9,8},{10,11... | collective-permute-start | bytes 786440 | tf_op jit(solution)/shard_map/ppermute | solution.py:50
  31.6 6.0 %collective-permute-start.18 = (bf16[4,4,8192]{2,1,0:T(4,128)(2,1)S(1)}, bf16[4,4,8192]{2,1,0:T(4,128)(2,1)S(1)}, u32[]{:S(2)}, u32[]{:S(2)}) collective-permute-start(bf16[4,4,8192]{2,1,0:T(4,128)(2,1)S(1)} %pad_maximum_fusion.3.refs_1_), channel_id=1, source_target_pairs={{0,1},{1,0},{2,3},{3,2},{4,5},{5,4},{6,7},{7,6},{8,9},{9,8},{10,11... | collective-permute-start | bytes 786440 | tf_op jit(solution)/shard_map/ppermute | solution.py:50
  32.0 10.0 %collective-permute-start.11 = (bf16[64,512]{1,0:T(8,128)(2,1)S(1)}, bf16[64,512]{1,0:T(8,128)(2,1)S(1)}, u32[]{:S(2)}, u32[]{:S(2)}) collective-permute-start(bf16[64,512]{1,0:T(8,128)(2,1)S(1)} %shard_map.64), channel_id=1, source_target_pairs={{0,2},{1,3},{2,0},{3,1},{4,6},{5,7},{6,4},{7,5},{8,10},{9,11},{10,... | collective-permute-start | bytes 196616 | tf_op jit(solution)/shard_map/ppermute | solution.py:50
  33.2 8.9 %collective-permute-start.10 = (bf16[64,512]{1,0:T(8,128)(2,1)S(1)}, bf16[64,512]{1,0:T(8,128)(2,1)S(1)}, u32[]{:S(2)}, u32[]{:S(2)}) collective-permute-start(bf16[64,512]{1,0:T(8,128)(2,1)S(1)} %shard_map.64), channel_id=1, source_target_pairs={{0,12},{1,13},{2,14},{3,15},{4,8},{5,9},{6,10},{7,11},{8,4},{9,5},... | collective-permute-start | bytes 196616 | tf_op jit(solution)/shard_map/ppermute | solution.py:50
  34.9 7.7 %collective-permute-start.9 = (bf16[64,512]{1,0:T(8,128)(2,1)S(1)}, bf16[64,512]{1,0:T(8,128)(2,1)S(1)}, u32[]{:S(2)}, u32[]{:S(2)}) collective-permute-start(bf16[64,512]{1,0:T(8,128)(2,1)S(1)} %shard_map.64), channel_id=1, source_target_pairs={{0,8},{1,9},{2,10},{3,11},{4,12},{5,13},{6,14},{7,15},{8,0},{9,1},... | collective-permute-start | bytes 196616 | tf_op jit(solution)/shard_map/ppermute | solution.py:50
  36.7 6.0 %collective-permute-start.8 = (bf16[64,512]{1,0:T(8,128)(2,1)S(1)}, bf16[64,512]{1,0:T(8,128)(2,1)S(1)}, u32[]{:S(2)}, u32[]{:S(2)}) collective-permute-start(bf16[64,512]{1,0:T(8,128)(2,1)S(1)} %shard_map.64), channel_id=1, source_target_pairs={{0,4},{1,5},{2,6},{3,7},{4,0},{5,1},{6,2},{7,3},{8,12},{9,13},{10,... | collective-permute-start | bytes 196616 | tf_op jit(solution)/shard_map/ppermute | solution.py:50
  42.7 7.0 %collective-permute-start.19 = (bf16[3,64,512]{2,1,0:T(8,128)(2,1)S(1)}, bf16[3,64,512]{2,1,0:T(8,128)(2,1)S(1)}, u32[]{:S(2)}, u32[]{:S(2)}) collective-permute-start(bf16[3,64,512]{2,1,0:T(8,128)(2,1)S(1)} %pad_maximum_fusion.7), channel_id=1, source_target_pairs={{0,2},{1,3},{2,0},{3,1},{4,6},{5,7},{6,4},{7,5},{8,10},{9,11},{10,... | collective-permute-start | bytes 589832 | tf_op jit(solution)/shard_map/ppermute | solution.py:50
  43.7 6.5 %collective-permute-start.21 = (bf16[4,64,512]{2,1,0:T(8,128)(2,1)S(1)}, bf16[4,64,512]{2,1,0:T(8,128)(2,1)S(1)}, u32[]{:S(2)}, u32[]{:S(2)}) collective-permute-start(bf16[4,64,512]{2,1,0:T(8,128)(2,1)S(1)} %pad_maximum_fusion.4.refs_0_), channel_id=1, source_target_pairs={{0,1},{1,0},{2,3},{3,2},{4,5},{5,4},{6,7},{7,6},{8,9},{9,8},{10,11... | collective-permute-start | bytes 786440 | tf_op jit(solution)/shard_map/ppermute | solution.py:50
  49.7 10.3 %collective-permute-start.20 = (bf16[4,64,512]{2,1,0:T(8,128)(2,1)S(1)}, bf16[4,64,512]{2,1,0:T(8,128)(2,1)S(1)}, u32[]{:S(2)}, u32[]{:S(2)}) collective-permute-start(bf16[4,64,512]{2,1,0:T(8,128)(2,1)S(1)} %pad_maximum_fusion.5.refs_1_), channel_id=1, source_target_pairs={{0,1},{1,0},{2,3},{3,2},{4,5},{5,4},{6,7},{7,6},{8,9},{9,8},{10,11... | collective-permute-start | bytes 786440 | tf_op jit(solution)/shard_map/ppermute | solution.py:50

commit v4 on v3

--- a/solution.py
+++ b/solution.py
@@ -9,7 +9,8 @@
 
 CAND = 4
 KBLK = 1024
-RBLK = 128
+RBLK = 256
+FLIGHT = 3
 VMEM = 50 << 20
 
 
@@ -67,7 +68,9 @@
 
 
 def project_kernel(n, blocks, turn, own_ref, *refs):
-    pieces, (basis_ref, out_ref, held, rows, acc, sems) = refs[:len(blocks)], refs[len(blocks):]
+    count = len(blocks)
+    sources, basis_ref, out_ref = refs[:count], refs[count], refs[count + 1]
+    pieces, (held, rows, acc, sems, piece_sems) = refs[count + 2:-5], refs[-5:]
     step = pl.program_id(0)
     width = held.shape[1]
     at = pl.multiple_of(step * width, width)
@@ -75,10 +78,19 @@
 
     @pl.when(step == 0)
     def _():
+        copies = [
+            pltpu.make_async_copy(source, piece, piece_sems.at[k])
+            for k, (source, piece) in enumerate(zip(sources, pieces))
+        ]
         for k in range(held.shape[0]):
             pltpu.make_async_copy(
                 basis_ref.at[pl.ds(k * width, width)], held.at[k], sems.at[k]
             ).start()
+            if k == 0:
+                for copy in copies:
+                    copy.start()
+        for copy in copies:
+            copy.wait()
 
     for piece, e, m in flat(pieces, blocks):
         part = piece[:, pl.ds(at, width)] if e is None else piece[e, :, pl.ds(at, width)]
@@ -114,8 +126,8 @@
             out_ref[...] = proj.astype(jnp.bfloat16)
 
 
-def whole(shape):
-    return pl.BlockSpec(shape, lambda s, own: (0,) * len(shape))
+def anywhere(count):
+    return [pl.BlockSpec(memory_space=pl.ANY)] * count
 
 
 def project(own, n, blocks, basis, turn):
@@ -130,33 +142,31 @@
         grid_spec=pltpu.PrefetchScalarGridSpec(
             num_scalar_prefetch=1,
             grid=(steps,),
-            in_specs=[whole(x.shape) for x, _ in blocks] + [pl.BlockSpec(memory_space=pl.ANY)],
-            out_specs=whole(shape),
-            scratch_shapes=[
+            in_specs=anywhere(len(blocks) + 1),
+            out_specs=pl.BlockSpec(shape, lambda k, own: (0,) * len(shape)),
+            scratch_shapes=[pltpu.VMEM(x.shape, jnp.bfloat16) for x, _ in blocks] + [
                 pltpu.VMEM((steps, KBLK, cols), jnp.bfloat16),
                 pltpu.VMEM((total, KBLK), jnp.float32),
                 pltpu.VMEM((total, cols), jnp.float32),
                 pltpu.SemaphoreType.DMA((steps,)),
+                pltpu.SemaphoreType.DMA((len(blocks),)),
             ],
         ),
         compiler_params=pltpu.CompilerParams(vmem_limit_bytes=VMEM),
-        cost_estimate=pl.CostEstimate(
-            flops=2 * total * depth * cols,
-            bytes_accessed=2 * depth * cols,
-            transcendentals=0,
-        ),
+        cost_estimate=pl.CostEstimate(flops=total, bytes_accessed=total, transcendentals=0),
     )(own, *[x for x, _ in blocks], basis)
 
 
 def outer_kernel(blocks, own_ref, *refs):
-    pieces = refs[:len(blocks)]
-    left_ref, eig_ref, out_ref, right, eig, out, eig_sems, out_sems = (
-        *refs[len(blocks):len(blocks) + 2], *refs[-6:]
-    )
+    given = len(blocks)
+    sources, left_any, eig_ref = refs[:given], refs[given], refs[given + 1]
+    out_ref, *pieces = refs[-9 - given:-8]
+    left, right, eig, out, eig_sems, out_sems, piece_sems, left_sem = refs[-8:]
     listed = flat(pieces, blocks)
     count = len(listed)
     step = pl.program_id(0)
     rows, cols = eig.shape[1:]
+    depth = out.shape[0]
 
     def columns(s):
         m = jnp.int32(listed[0][2])
@@ -168,15 +178,24 @@
         return pltpu.make_async_copy(eig_ref.at[:, columns(s)], eig.at[s], eig_sems.at[s])
 
     def write(s, c):
-        slot = lax.rem(s, 2)
+        slot = lax.rem(s, depth)
         return pltpu.make_async_copy(
             out.at[slot, c], out_ref.at[c, :, columns(s)], out_sems.at[slot, c]
         )
 
     @pl.when(step == 0)
     def _():
+        copies = [pltpu.make_async_copy(left_any, left, left_sem)] + [
+            pltpu.make_async_copy(source, piece, piece_sems.at[k])
+            for k, (source, piece) in enumerate(zip(sources, pieces))
+        ]
         for s in range(count):
             read(s).start()
+            if s == 0:
+                for copy in copies:
+                    copy.start()
+        for copy in copies:
+            copy.wait()
 
     for k, (piece, e, _) in enumerate(listed):
         @pl.when(step == k)
@@ -184,17 +203,19 @@
             right[...] = piece[...] if e is None else piece[e]
 
     read(step).wait()
-    slot = lax.rem(step, 2)
+    slot = lax.rem(step, depth)
     for c in range(CAND):
-        @pl.when(step >= 2)
+        @pl.when(step >= depth)
         def _(c=c):
-            write(step - 2, c).wait()
+            write(step - depth, c).wait()
 
     for r in range(0, rows, RBLK):
-        scale = 1.0 / (eig[step, r:r + RBLK, :].astype(jnp.float32) + 0.01)
+        shifted = eig[step, r:r + RBLK, :].astype(jnp.float32) + 0.01
+        near = pl.reciprocal(shifted, approx=True)
+        scale = near * (2.0 - shifted * near)
         for c in range(CAND):
             summed = jnp.dot(
-                left_ref[c, r:r + RBLK, :], right[...], preferred_element_type=jnp.float32
+                left[c, r:r + RBLK, :], right[...], preferred_element_type=jnp.float32
             )
             out[slot, c, r:r + RBLK, :] = (summed * scale).astype(jnp.bfloat16)
     for c in range(CAND):
@@ -202,7 +223,7 @@
 
     @pl.when(step == count - 1)
     def _():
-        for s in range(max(0, count - 2), count):
+        for s in range(max(0, count - depth), count):
             for c in range(CAND):
                 write(s, c).wait()
 
@@ -212,15 +233,10 @@
     rows, width = eigvals.shape
     count = sum(len(entries) for _, entries in blocks)
     operands = [own] + [x for x, _ in blocks] + [left, eigvals]
-    in_specs = [whole(x.shape) for x, _ in blocks] + [
-        whole(left.shape),
-        pl.BlockSpec(memory_space=pl.ANY),
-    ]
     aliases = {}
     if before is not None:
         aliases = {len(operands): 0}
         operands.append(before)
-        in_specs.append(pl.BlockSpec(memory_space=pl.ANY))
     share = count * cols
     return pl.pallas_call(
         functools.partial(outer_kernel, shape_of(blocks)),
@@ -228,14 +244,17 @@
         grid_spec=pltpu.PrefetchScalarGridSpec(
             num_scalar_prefetch=1,
             grid=(count,),
-            in_specs=in_specs,
+            in_specs=anywhere(len(operands) - 1),
             out_specs=pl.BlockSpec(memory_space=pl.ANY),
-            scratch_shapes=[
+            scratch_shapes=[pltpu.VMEM(x.shape, jnp.bfloat16) for x, _ in blocks] + [
+                pltpu.VMEM(left.shape, jnp.bfloat16),
                 pltpu.VMEM((total, cols), jnp.bfloat16),
                 pltpu.VMEM((count, rows, cols), jnp.bfloat16),
-                pltpu.VMEM((2, CAND, rows, cols), jnp.bfloat16),
+                pltpu.VMEM((FLIGHT, CAND, rows, cols), jnp.bfloat16),
                 pltpu.SemaphoreType.DMA((count,)),
-                pltpu.SemaphoreType.DMA((2, CAND)),
+                pltpu.SemaphoreType.DMA((FLIGHT, CAND)),
+                pltpu.SemaphoreType.DMA((len(blocks),)),
+                pltpu.SemaphoreType.DMA(()),
             ],
         ),
         input_output_aliases=aliases,
@@ -256,48 +275,47 @@
     pair = (2, 6, 10, 14)
     core = (1, 5, 9, 13)
     other = (3, 7, 11, 15)
-
-    def send(x):
-        return swap(x, 4), swap(x, 2), swap(x, 8), swap(x, 12)
-
-    a = factors_in
-    a1, ap, a2, a3 = send(a)
+    tie = lax.optimization_barrier
+
+    a1, ap, a2, a3 = [swap(factors_in, m) for m in (4, 2, 8, 12)]
     keep = (lax.iota(jnp.int32, slots) < live_counts[0])[:, None]
-    b = jnp.where(keep, factors_out, jnp.zeros_like(factors_out))
-    a1, ap = lax.optimization_barrier((a1, ap))
+    a, b = tie(tuple(
+        jnp.where(keep, x, jnp.zeros_like(x)) for x in (factors_in, factors_out)
+    ))
+    a1, ap = tie((a1, ap))
     ap1 = swap(a1, 2)
-    b, a2, a3 = lax.optimization_barrier((b, a2, a3))
     ap23 = swap(jnp.stack([a2, a3]), 2)
     a_column = jnp.stack([a, a1, a2, a3])
     a_core = swap(a_column, 1)
-    b1, bp, b2, b3 = send(b)
+    b = after(b, a1, a2, a3, ap)
+    b1, bp, b2, b3 = [swap(b, m) for m in (4, 2, 8, 12)]
+    ap23, b1 = tie((ap23, b1))
     a_pair = jnp.stack([ap, ap1, ap23[0], ap23[1]])
     a_other = swap(a_pair, 1)
-    b1, b2, b3, bp = lax.optimization_barrier((b1, b2, b3, bp, a_pair))[:4]
+    pin = project(
+        own, n, [(a_column, column), (a_pair, pair), (a_core, core), (a_other, other)],
+        basis_in, False,
+    )
+
+    b1, b2, b3, bp = tie((b1, b2, b3, bp, pin))[:4]
     b_column = jnp.stack([b, b1, b2, b3])
     bp123 = swap(b_column[1:], 2)
     b_core = swap(b_column, 1)
-    pin = project(
-        own, n, [(a_column, column), (a_pair, pair), (a_core, core), (a_other, other)],
-        basis_in, False,
-    )
-
-    g1, gp, g2, g3 = send(pin)
-    b_pair = jnp.concatenate([after(bp, pin)[None], bp123])
+    g1, gp, g2, g3 = [swap(pin, m) for m in (4, 2, 8, 12)]
+    bp123, g1, g2, g3 = tie((bp123, g1, g2, g3))
+    b_pair = jnp.concatenate([bp[None], bp123])
     b_other = swap(b_pair, 1)
     left = project(
         own, n, [(b_column, column), (b_pair, pair), (b_core, core), (b_other, other)],
         basis_out, True,
     )
-    g1, g2, g3, gp = lax.optimization_barrier((g1, g2, g3, gp, left))[:4]
+    g1, g2, g3, gp = tie((g1, g2, g3, gp, left))[:4]
     g_column = jnp.stack([pin, g1, g2, g3])
     gp123 = swap(g_column[1:], 2)
     g_core = swap(g_column, 1)
-    out = outer(own, [(g_column, column)], left, eigvals, None)
-    g_pair = jnp.concatenate([gp[None], after(gp123, out)])
-    g_other = swap(g_pair, 1)
-    out = outer(own, [(g_core, core), (g_pair, pair)], left, eigvals, out)
-    return outer(own, [(g_other, other)], left, eigvals, out)
+    out = outer(own, [(g_column, column), (gp, [2])], left, eigvals, None)
+    g_other = swap(jnp.concatenate([gp[None], after(gp123, out)]), 1)
+    return outer(own, [(g_core, core), (gp123, pair[1:]), (g_other, other)], left, eigvals, out)
 
 
 def solution(mesh):

time: 66.2 us -> 65.1 us (0.983)
  waiting for transfers between devices: 8.17 us -> 13.4 us
  Pallas kernels: 30.3 us -> 26.4 us
  starting transfers between devices: 23.7 us -> 22.2 us
  other arithmetic: 2.94 us -> 2.17 us
    ppermute x22, waiting for transfers between devices: 8.17 us -> 13.4 us  [swap(): return lax.ppermute(x, 'dp', [(d, d ^ m) for d in range(n)])]
    pallas_call x3 -> x2, Pallas kernels: 21.5 us -> 17.6 us  [outer(): pl.pallas_call(functools.partial(outer_kernel, shape_of(blocks)), out_sha...]
    ppermute x22, starting transfers between devices: 23.7 us -> 22.2 us  [swap(): return lax.ppermute(x, 'dp', [(d, d ^ m) for d in range(n)])]
    another operation x1, other arithmetic: 1.07 us -> 0.24 us  [by_swaps(): a_column = jnp.stack([a, a1, a2, a3])]
  transfers between devices with their start and end apart: 22 -> 22, of which waited for: 6 -> 7; matrix products, arithmetic and copies ran while one was open for 4% -> 3% of each run, Pallas kernels for 37% -> 23%
where the time goes in v4:
time: 65.1 us; the launch traced here: 64.9 us
  Pallas kernels  26.4 us (41%)
  starting transfers between devices  22.2 us (34%)
  waiting for transfers between devices  13.4 us (21%)
  other arithmetic  2.17 us (3%)
  between operations  0.82 us (1%)
    ppermute x22, starting transfers between devices, swap(): return lax.ppermute(x, 'dp', [(d, d ^ m) for d in range(n)])  22.2 us
    pallas_call x2, Pallas kernels, outer(): pl.pallas_call(functools.partial(outer_kernel, shape_of(blocks)), out_sha...  17.6 us
    ppermute x22, waiting for transfers between devices, swap(): return lax.ppermute(x, 'dp', [(d, d ^ m) for d in range(n)])  13.4 us
    pallas_call x2, Pallas kernels, project(): pl.pallas_call(functools.partial(project_kernel, n, shape_of(blocks), tur...  8.75 us
  transfers between devices with their start and end apart: 22, of which 7 were waited for; matrix products, arithmetic and copies ran while one was open for 3% of the time, Pallas kernels for 23%

profile of v4, /device:TPU:0, one launch (start us, length us, event | category | flops | bytes accessed | tf_op | source)
XLA Modules:
  0.0 64.9 jit_solution(15632291859077029053)
XLA Ops:
  0.0 2.9 %collective-permute-start.1 = (bf16[4,8192]{1,0:T(4,128)(2,1)}, bf16[4,8192]{1,0:T(4,128)(2,1)S(1)}, u32[]{:S(2)}, u32[]{:S(2)}) collective-permute-start(bf16[4,8192]{1,0:T(4,128)(2,1)} %param.6), channel_id=1, source_target_pairs={{0,2},{1,3},{2,0},{3,1},{4,6},{5,7},{6,4},{7,5},{8,10},{9,11},{10,... | collective-permute-start | bytes 196616 | tf_op jit(solution)/shard_map/ppermute | solution.py:51
  2.9 1.6 %collective-permute-start = (bf16[4,8192]{1,0:T(4,128)(2,1)}, bf16[4,8192]{1,0:T(4,128)(2,1)S(1)}, u32[]{:S(2)}, u32[]{:S(2)}) collective-permute-start(bf16[4,8192]{1,0:T(4,128)(2,1)} %param.6), channel_id=1, source_target_pairs={{0,4},{1,5},{2,6},{3,7},{4,0},{5,1},{6,2},{7,3},{8,12},{9,13},{10,... | collective-permute-start | bytes 196616 | tf_op jit(solution)/shard_map/ppermute | solution.py:51
  4.5 2.5 %collective-permute-start.3 = (bf16[4,8192]{1,0:T(4,128)(2,1)}, bf16[4,8192]{1,0:T(4,128)(2,1)S(1)}, u32[]{:S(2)}, u32[]{:S(2)}) collective-permute-start(bf16[4,8192]{1,0:T(4,128)(2,1)} %param.6), channel_id=1, source_target_pairs={{0,12},{1,13},{2,14},{3,15},{4,8},{5,9},{6,10},{7,11},{8,4},{9,5},... | collective-permute-start | bytes 196616 | tf_op jit(solution)/shard_map/ppermute | solution.py:51
  7.0 0.1 collective-permute-start.2
  7.8 1.0 %broadcast_select_fusion = (bf16[4,8192]{1,0:T(4,128)(2,1)S(1)}, bf16[4,8192]{1,0:T(4,128)(2,1)S(1)}) fusion(bf16[4,8192]{1,0:T(4,128)(2,1)} %param.7, pred[4]{0:T(512)(128)(4,1)S(1)} %iota_compare_fusion, bf16[4,8192]{1,0:T(4,128)(2,1)} %param.6), kind=kLoop, calls=%fused_computation.9 | loop fusion | flops 65536 | bytes 262148 | tf_op jit(solution)/shard_map/jit(_where)/select_n | solution.py:283
  8.8 0.0 collective-permute-done.1
  8.8 0.6 collective-permute-start.4
  9.4 1.9 %collective-permute-done.3 = bf16[4,8192]{1,0:T(4,128)(2,1)S(1)} collective-permute-done((bf16[4,8192]{1,0:T(4,128)(2,1)}, bf16[4,8192]{1,0:T(4,128)(2,1)S(1)}, u32[]{:S(2)}, u32[]{:S(2)}) %collective-permute-start.3) | collective-permute-done | bytes 65568 | tf_op jit(solution)/shard_map/ppermute | solution.py:51
  11.3 2.1 %collective-permute-done.2 = bf16[4,8192]{1,0:T(4,128)(2,1)S(1)} collective-permute-done((bf16[4,8192]{1,0:T(4,128)(2,1)}, bf16[4,8192]{1,0:T(4,128)(2,1)S(1)}, u32[]{:S(2)}, u32[]{:S(2)}) %collective-permute-start.2) | collective-permute-done | bytes 65568 | tf_op jit(solution)/shard_map/ppermute | solution.py:51
  13.4 0.0 collective-permute-start.6
  13.4 0.1 pad_maximum_fusion.8
  13.5 0.6 collective-permute-start.5
  14.1 0.2 pad_maximum_fusion.refs_0_
  14.4 0.1 collective-permute-start.7
  14.4 3.2 %collective-permute-done.6 = bf16[4,8192]{1,0:T(4,128)(2,1)S(1)} collective-permute-done((bf16[4,8192]{1,0:T(4,128)(2,1)S(1)}, bf16[4,8192]{1,0:T(4,128)(2,1)S(1)}, u32[]{:S(2)}, u32[]{:S(2)}) %collective-permute-start.6) | collective-permute-done | bytes 65568 | tf_op jit(solution)/shard_map/ppermute | solution.py:51
  17.7 1.1 %collective-permute-done.5 = bf16[2,4,8192]{2,1,0:T(4,128)(2,1)S(1)} collective-permute-done((bf16[2,4,8192]{2,1,0:T(4,128)(2,1)S(1)}, bf16[2,4,8192]{2,1,0:T(4,128)(2,1)S(1)}, u32[]{:S(2)}, u32[]{:S(2)}) %collective-permute-start.5) | collective-permute-done | bytes 131104 | tf_op jit(solution)/shard_map/ppermute | solution.py:51
  18.8 0.0 collective-permute-done.4
  18.8 0.2 pad_maximum_fusion.1.refs_1_
  19.0 0.1 collective-permute-start.8
  19.0 0.6 collective-permute-start.11
  19.6 2.1 %collective-permute-start.10 = (bf16[4,8192]{1,0:T(4,128)(2,1)S(1)}, bf16[4,8192]{1,0:T(4,128)(2,1)S(1)}, u32[]{:S(2)}, u32[]{:S(2)}) collective-permute-start(bf16[4,8192]{1,0:T(4,128)(2,1)S(1)} %get-tuple-element.29), channel_id=1, source_target_pairs={{0,12},{1,13},{2,14},{3,15},{4,8},{5,9},{6,10},{7,11},{8,4},{9,5},... | collective-permute-start | bytes 196616 | tf_op jit(solution)/shard_map/ppermute | solution.py:51
  21.8 1.1 %collective-permute-start.9 = (bf16[4,8192]{1,0:T(4,128)(2,1)S(1)}, bf16[4,8192]{1,0:T(4,128)(2,1)S(1)}, u32[]{:S(2)}, u32[]{:S(2)}) collective-permute-start(bf16[4,8192]{1,0:T(4,128)(2,1)S(1)} %get-tuple-element.29), channel_id=1, source_target_pairs={{0,8},{1,9},{2,10},{3,11},{4,12},{5,13},{6,14},{7,15},{8,0},{9,1},... | collective-permute-start | bytes 196616 | tf_op jit(solution)/shard_map/ppermute | solution.py:51
  22.9 0.0 collective-permute-done.7.refs_2_
  22.9 0.0 collective-permute-done.8.refs_3_
  22.9 4.3 %shard_map.64 = bf16[64,512]{1,0:T(8,128)(2,1)S(1)} custom-call(s32[1]{0:T(128)} %bitcast.own_ref, bf16[4,4,8192]{2,1,0:T(4,128)(2,1)S(1)} %pad_maximum_fusion.refs_0_, bf16[4,4,8192]{2,1,0:T(4,128)(2,1)S(1)} %pad_maximum_fusion.1.refs_1_, bf16[4,4,8192]{2,1,0:T(4,128)(2,1)S(1)} %collective-permute-done.7.refs_2_, ...), custom_call_target="tpu_custom_call" | custom-call | flops 64 | bytes 64 | tf_op jit(solution)/shard_map/pallas_call | solution.py:139
  27.2 2.4 %collective-permute-start.15 = (bf16[64,512]{1,0:T(8,128)(2,1)S(1)}, bf16[64,512]{1,0:T(8,128)(2,1)S(1)}, u32[]{:S(2)}, u32[]{:S(2)}) collective-permute-start(bf16[64,512]{1,0:T(8,128)(2,1)S(1)} %shard_map.64), channel_id=1, source_target_pairs={{0,12},{1,13},{2,14},{3,15},{4,8},{5,9},{6,10},{7,11},{8,4},{9,5},... | collective-permute-start | bytes 196616 | tf_op jit(solution)/shard_map/ppermute | solution.py:51
  29.6 0.2 collective-permute-start.14
  29.9 0.0 collective-permute-done.11
  29.9 1.8 %collective-permute-start.13 = (bf16[64,512]{1,0:T(8,128)(2,1)S(1)}, bf16[64,512]{1,0:T(8,128)(2,1)S(1)}, u32[]{:S(2)}, u32[]{:S(2)}) collective-permute-start(bf16[64,512]{1,0:T(8,128)(2,1)S(1)} %shard_map.64), channel_id=1, source_target_pairs={{0,4},{1,5},{2,6},{3,7},{4,0},{5,1},{6,2},{7,3},{8,12},{9,13},{10,... | collective-permute-start | bytes 196616 | tf_op jit(solution)/shard_map/ppermute | solution.py:51
  31.7 0.0 collective-permute-done.10
  31.7 0.0 collective-permute-done.9
  31.7 0.2 pad_maximum_fusion.6
  31.9 1.6 %collective-permute-start.12 = (bf16[3,4,8192]{2,1,0:T(4,128)(2,1)S(1)}, bf16[3,4,8192]{2,1,0:T(4,128)(2,1)S(1)}, u32[]{:S(2)}, u32[]{:S(2)}) collective-permute-start(bf16[3,4,8192]{2,1,0:T(4,128)(2,1)S(1)} %pad_maximum_fusion.6), channel_id=1, source_target_pairs={{0,2},{1,3},{2,0},{3,1},{4,6},{5,7},{6,4},{7,5},{8,10},{9,11},{10,... | collective-permute-start | bytes 589832 | tf_op jit(solution)/shard_map/ppermute | solution.py:51
  33.4 0.2 pad_maximum_fusion.2.refs_0_
  33.6 0.1 collective-permute-start.17
  33.7 0.0 collective-permute-done.15
  33.7 2.5 %collective-permute-done.14 = bf16[64,512]{1,0:T(8,128)(2,1)S(1)} collective-permute-done((bf16[64,512]{1,0:T(8,128)(2,1)S(1)}, bf16[64,512]{1,0:T(8,128)(2,1)S(1)}, u32[]{:S(2)}, u32[]{:S(2)}) %collective-permute-start.14) | collective-permute-done | bytes 65568 | tf_op jit(solution)/shard_map/ppermute | solution.py:51
  36.2 1.4 %collective-permute-done.12 = bf16[3,4,8192]{2,1,0:T(4,128)(2,1)S(1)} collective-permute-done((bf16[3,4,8192]{2,1,0:T(4,128)(2,1)S(1)}, bf16[3,4,8192]{2,1,0:T(4,128)(2,1)S(1)}, u32[]{:S(2)}, u32[]{:S(2)}) %collective-permute-start.12) | collective-permute-done | bytes 196640 | tf_op jit(solution)/shard_map/ppermute | solution.py:51
  37.6 0.2 pad_maximum_fusion.3.refs_1_
  37.8 0.1 collective-permute-start.18
  37.8 1.6 %collective-permute-start.16 = (bf16[64,512]{1,0:T(8,128)(2,1)S(1)}, bf16[64,512]{1,0:T(8,128)(2,1)S(1)}, u32[]{:S(2)}, u32[]{:S(2)}) collective-permute-start(bf16[64,512]{1,0:T(8,128)(2,1)S(1)} %shard_map.64), channel_id=1, source_target_pairs={{0,2},{1,3},{2,0},{3,1},{4,6},{5,7},{6,4},{7,5},{8,10},{9,11},{10,... | collective-permute-start | bytes 196616 | tf_op jit(solution)/shard_map/ppermute | solution.py:51
  39.4 4.5 %shard_map.65.refs_2_.refs_3_ = bf16[4,512,64]{2,1,0:T(8,128)(2,1)S(1)} custom-call(s32[1]{0:T(128)} %bitcast.own_ref, bf16[4,4,8192]{2,1,0:T(4,128)(2,1)S(1)} %pad_maximum_fusion.2.refs_0_, bf16[4,4,8192]{2,1,0:T(4,128)(2,1)S(1)} %pad_maximum_fusion.3.refs_1_, bf16[4,4,8192]{2,1,0:T(4,128)(2,1)S(1)} %collective-permute-done.17.refs_2_, ...), custom_call_target="tpu_custom_call" | custom-call | flops 64 | bytes 64 | tf_op jit(solution)/shard_map/pallas_call | solution.py:139
  43.9 1.5 %collective-permute-start.20 = (bf16[3,64,512]{2,1,0:T(8,128)(2,1)S(1)}, bf16[3,64,512]{2,1,0:T(8,128)(2,1)S(1)}, u32[]{:S(2)}, u32[]{:S(2)}) collective-permute-start(bf16[3,64,512]{2,1,0:T(8,128)(2,1)S(1)} %pad_maximum_fusion.7), channel_id=1, source_target_pairs={{0,2},{1,3},{2,0},{3,1},{4,6},{5,7},{6,4},{7,5},{8,10},{9,11},{10,... | collective-permute-start | bytes 589832 | tf_op jit(solution)/shard_map/ppermute | solution.py:51
  45.5 0.1 collective-permute-start.19
  45.5 6.3 %shard_map.66.refs_5_ = bf16[4,512,8192]{2,1,0:T(8,128)(2,1)} custom-call(s32[1]{0:T(128)} %bitcast.own_ref, bf16[4,64,512]{2,1,0:T(8,128)(2,1)S(1)} %pad_maximum_fusion.4.refs_0_, bf16[64,512]{1,0:T(8,128)(2,1)S(1)} %collective-permute-done.16.refs_1_, bf16[4,512,64]{2,1,0:T(8,128)(2,1)S(1)} %shard_map.65.refs_2_.refs_3_, bf16[512,8192]{1,0:T(8,128)(2,1)} %refs_4_.5), custom_call_target="tpu_custom_call" | custom-call | flops 167772160 | bytes 13107200 | tf_op jit(solution)/shard_map/pallas_call | solution.py:241
  51.9 0.6 collective-permute-start.21
  52.4 1.2 %collective-permute-done.21.refs_2_ = bf16[4,64,512]{2,1,0:T(8,128)(2,1)S(1)} collective-permute-done((bf16[4,64,512]{2,1,0:T(8,128)(2,1)S(1)}, bf16[4,64,512]{2,1,0:T(8,128)(2,1)S(1)}, u32[]{:S(2)}, u32[]{:S(2)}) %collective-permute-start.21) | collective-permute-done | bytes 262176 | tf_op jit(solution)/shard_map/ppermute | solution.py:51
  53.6 11.3 %shard_map.67 = bf16[4,512,8192]{2,1,0:T(8,128)(2,1)} custom-call(s32[1]{0:T(128)} %bitcast.own_ref, bf16[4,64,512]{2,1,0:T(8,128)(2,1)S(1)} %collective-permute-done.19.refs_0_, bf16[3,64,512]{2,1,0:T(8,128)(2,1)S(1)} %collective-permute-done.20.refs_1_, bf16[4,64,512]{2,1,0:T(8,128)(2,1)S(1)} %collective-permute-done.21.refs_2_, ...), custom_call_target="tpu_custom_call", output_to_operand_aliasing={{}: (6, {})} | custom-call | flops 369098752 | bytes 28835840 | tf_op jit(solution)/shard_map/pallas_call | solution.py:241
  (11 shorter events, 0.1 us)
Async XLA Ops:
  0.0 8.8 %collective-permute-start.1 = (bf16[4,8192]{1,0:T(4,128)(2,1)}, bf16[4,8192]{1,0:T(4,128)(2,1)S(1)}, u32[]{:S(2)}, u32[]{:S(2)}) collective-permute-start(bf16[4,8192]{1,0:T(4,128)(2,1)} %param.6), channel_id=1, source_target_pairs={{0,2},{1,3},{2,0},{3,1},{4,6},{5,7},{6,4},{7,5},{8,10},{9,11},{10,... | collective-permute-start | bytes 196616 | tf_op jit(solution)/shard_map/ppermute | solution.py:51
  2.9 5.8 %collective-permute-start = (bf16[4,8192]{1,0:T(4,128)(2,1)}, bf16[4,8192]{1,0:T(4,128)(2,1)S(1)}, u32[]{:S(2)}, u32[]{:S(2)}) collective-permute-start(bf16[4,8192]{1,0:T(4,128)(2,1)} %param.6), channel_id=1, source_target_pairs={{0,4},{1,5},{2,6},{3,7},{4,0},{5,1},{6,2},{7,3},{8,12},{9,13},{10,... | collective-permute-start | bytes 196616 | tf_op jit(solution)/shard_map/ppermute | solution.py:51
  4.5 6.8 %collective-permute-start.3 = (bf16[4,8192]{1,0:T(4,128)(2,1)}, bf16[4,8192]{1,0:T(4,128)(2,1)S(1)}, u32[]{:S(2)}, u32[]{:S(2)}) collective-permute-start(bf16[4,8192]{1,0:T(4,128)(2,1)} %param.6), channel_id=1, source_target_pairs={{0,12},{1,13},{2,14},{3,15},{4,8},{5,9},{6,10},{7,11},{8,4},{9,5},... | collective-permute-start | bytes 196616 | tf_op jit(solution)/shard_map/ppermute | solution.py:51
  7.0 6.4 %collective-permute-start.2 = (bf16[4,8192]{1,0:T(4,128)(2,1)}, bf16[4,8192]{1,0:T(4,128)(2,1)S(1)}, u32[]{:S(2)}, u32[]{:S(2)}) collective-permute-start(bf16[4,8192]{1,0:T(4,128)(2,1)} %param.6), channel_id=1, source_target_pairs={{0,8},{1,9},{2,10},{3,11},{4,12},{5,13},{6,14},{7,15},{8,0},{9,1},... | collective-permute-start | bytes 196616 | tf_op jit(solution)/shard_map/ppermute | solution.py:51
  8.8 10.0 %collective-permute-start.4 = (bf16[4,8192]{1,0:T(4,128)(2,1)S(1)}, bf16[4,8192]{1,0:T(4,128)(2,1)S(1)}, u32[]{:S(2)}, u32[]{:S(2)}) collective-permute-start(bf16[4,8192]{1,0:T(4,128)(2,1)S(1)} %collective-permute-done), channel_id=1, source_target_pairs={{0,2},{1,3},{2,0},{3,1},{4,6},{5,7},{6,4},{7,5},{8,10},{9,11},{10,... | collective-permute-start | bytes 196616 | tf_op jit(solution)/shard_map/ppermute | solution.py:51
  13.4 4.3 %collective-permute-start.6 = (bf16[4,8192]{1,0:T(4,128)(2,1)S(1)}, bf16[4,8192]{1,0:T(4,128)(2,1)S(1)}, u32[]{:S(2)}, u32[]{:S(2)}) collective-permute-start(bf16[4,8192]{1,0:T(4,128)(2,1)S(1)} %get-tuple-element.29), channel_id=1, source_target_pairs={{0,4},{1,5},{2,6},{3,7},{4,0},{5,1},{6,2},{7,3},{8,12},{9,13},{10,... | collective-permute-start | bytes 196616 | tf_op jit(solution)/shard_map/ppermute | solution.py:51
  13.5 5.2 %collective-permute-start.5 = (bf16[2,4,8192]{2,1,0:T(4,128)(2,1)S(1)}, bf16[2,4,8192]{2,1,0:T(4,128)(2,1)S(1)}, u32[]{:S(2)}, u32[]{:S(2)}) collective-permute-start(bf16[2,4,8192]{2,1,0:T(4,128)(2,1)S(1)} %pad_maximum_fusion.8), channel_id=1, source_target_pairs={{0,2},{1,3},{2,0},{3,1},{4,6},{5,7},{6,4},{7,5},{8,10},{9,11},{10,... | collective-permute-start | bytes 393224 | tf_op jit(solution)/shard_map/ppermute | solution.py:51
  14.4 8.6 %collective-permute-start.7 = (bf16[4,4,8192]{2,1,0:T(4,128)(2,1)S(1)}, bf16[4,4,8192]{2,1,0:T(4,128)(2,1)S(1)}, u32[]{:S(2)}, u32[]{:S(2)}) collective-permute-start(bf16[4,4,8192]{2,1,0:T(4,128)(2,1)S(1)} %pad_maximum_fusion.refs_0_), channel_id=1, source_target_pairs={{0,1},{1,0},{2,3},{3,2},{4,5},{5,4},{6,7},{7,6},{8,9},{9,8},{10,11... | collective-permute-start | bytes 786440 | tf_op jit(solution)/shard_map/ppermute | solution.py:51
  19.0 4.0 %collective-permute-start.8 = (bf16[4,4,8192]{2,1,0:T(4,128)(2,1)S(1)}, bf16[4,4,8192]{2,1,0:T(4,128)(2,1)S(1)}, u32[]{:S(2)}, u32[]{:S(2)}) collective-permute-start(bf16[4,4,8192]{2,1,0:T(4,128)(2,1)S(1)} %pad_maximum_fusion.1.refs_1_), channel_id=1, source_target_pairs={{0,1},{1,0},{2,3},{3,2},{4,5},{5,4},{6,7},{7,6},{8,9},{9,8},{10,11... | collective-permute-start | bytes 786440 | tf_op jit(solution)/shard_map/ppermute | solution.py:51
  19.0 10.8 %collective-permute-start.11 = (bf16[4,8192]{1,0:T(4,128)(2,1)S(1)}, bf16[4,8192]{1,0:T(4,128)(2,1)S(1)}, u32[]{:S(2)}, u32[]{:S(2)}) collective-permute-start(bf16[4,8192]{1,0:T(4,128)(2,1)S(1)} %get-tuple-element.29), channel_id=1, source_target_pairs={{0,2},{1,3},{2,0},{3,1},{4,6},{5,7},{6,4},{7,5},{8,10},{9,11},{10,... | collective-permute-start | bytes 196616 | tf_op jit(solution)/shard_map/ppermute | solution.py:51
  19.6 12.0 %collective-permute-start.10 = (bf16[4,8192]{1,0:T(4,128)(2,1)S(1)}, bf16[4,8192]{1,0:T(4,128)(2,1)S(1)}, u32[]{:S(2)}, u32[]{:S(2)}) collective-permute-start(bf16[4,8192]{1,0:T(4,128)(2,1)S(1)} %get-tuple-element.29), channel_id=1, source_target_pairs={{0,12},{1,13},{2,14},{3,15},{4,8},{5,9},{6,10},{7,11},{8,4},{9,5},... | collective-permute-start | bytes 196616 | tf_op jit(solution)/shard_map/ppermute | solution.py:51
  21.8 9.9 %collective-permute-start.9 = (bf16[4,8192]{1,0:T(4,128)(2,1)S(1)}, bf16[4,8192]{1,0:T(4,128)(2,1)S(1)}, u32[]{:S(2)}, u32[]{:S(2)}) collective-permute-start(bf16[4,8192]{1,0:T(4,128)(2,1)S(1)} %get-tuple-element.29), channel_id=1, source_target_pairs={{0,8},{1,9},{2,10},{3,11},{4,12},{5,13},{6,14},{7,15},{8,0},{9,1},... | collective-permute-start | bytes 196616 | tf_op jit(solution)/shard_map/ppermute | solution.py:51
  27.2 6.5 %collective-permute-start.15 = (bf16[64,512]{1,0:T(8,128)(2,1)S(1)}, bf16[64,512]{1,0:T(8,128)(2,1)S(1)}, u32[]{:S(2)}, u32[]{:S(2)}) collective-permute-start(bf16[64,512]{1,0:T(8,128)(2,1)S(1)} %shard_map.64), channel_id=1, source_target_pairs={{0,12},{1,13},{2,14},{3,15},{4,8},{5,9},{6,10},{7,11},{8,4},{9,5},... | collective-permute-start | bytes 196616 | tf_op jit(solution)/shard_map/ppermute | solution.py:51
  29.6 6.6 %collective-permute-start.14 = (bf16[64,512]{1,0:T(8,128)(2,1)S(1)}, bf16[64,512]{1,0:T(8,128)(2,1)S(1)}, u32[]{:S(2)}, u32[]{:S(2)}) collective-permute-start(bf16[64,512]{1,0:T(8,128)(2,1)S(1)} %shard_map.64), channel_id=1, source_target_pairs={{0,8},{1,9},{2,10},{3,11},{4,12},{5,13},{6,14},{7,15},{8,0},{9,1},... | collective-permute-start | bytes 196616 | tf_op jit(solution)/shard_map/ppermute | solution.py:51
  29.9 6.3 %collective-permute-start.13 = (bf16[64,512]{1,0:T(8,128)(2,1)S(1)}, bf16[64,512]{1,0:T(8,128)(2,1)S(1)}, u32[]{:S(2)}, u32[]{:S(2)}) collective-permute-start(bf16[64,512]{1,0:T(8,128)(2,1)S(1)} %shard_map.64), channel_id=1, source_target_pairs={{0,4},{1,5},{2,6},{3,7},{4,0},{5,1},{6,2},{7,3},{8,12},{9,13},{10,... | collective-permute-start | bytes 196616 | tf_op jit(solution)/shard_map/ppermute | solution.py:51
  31.9 5.7 %collective-permute-start.12 = (bf16[3,4,8192]{2,1,0:T(4,128)(2,1)S(1)}, bf16[3,4,8192]{2,1,0:T(4,128)(2,1)S(1)}, u32[]{:S(2)}, u32[]{:S(2)}) collective-permute-start(bf16[3,4,8192]{2,1,0:T(4,128)(2,1)S(1)} %pad_maximum_fusion.6), channel_id=1, source_target_pairs={{0,2},{1,3},{2,0},{3,1},{4,6},{5,7},{6,4},{7,5},{8,10},{9,11},{10,... | collective-permute-start | bytes 589832 | tf_op jit(solution)/shard_map/ppermute | solution.py:51
  33.6 5.8 %collective-permute-start.17 = (bf16[4,4,8192]{2,1,0:T(4,128)(2,1)S(1)}, bf16[4,4,8192]{2,1,0:T(4,128)(2,1)S(1)}, u32[]{:S(2)}, u32[]{:S(2)}) collective-permute-start(bf16[4,4,8192]{2,1,0:T(4,128)(2,1)S(1)} %pad_maximum_fusion.2.refs_0_), channel_id=1, source_target_pairs={{0,1},{1,0},{2,3},{3,2},{4,5},{5,4},{6,7},{7,6},{8,9},{9,8},{10,11... | collective-permute-start | bytes 786440 | tf_op jit(solution)/shard_map/ppermute | solution.py:51
  37.8 1.6 %collective-permute-start.18 = (bf16[4,4,8192]{2,1,0:T(4,128)(2,1)S(1)}, bf16[4,4,8192]{2,1,0:T(4,128)(2,1)S(1)}, u32[]{:S(2)}, u32[]{:S(2)}) collective-permute-start(bf16[4,4,8192]{2,1,0:T(4,128)(2,1)S(1)} %pad_maximum_fusion.3.refs_1_), channel_id=1, source_target_pairs={{0,1},{1,0},{2,3},{3,2},{4,5},{5,4},{6,7},{7,6},{8,9},{9,8},{10,11... | collective-permute-start | bytes 786440 | tf_op jit(solution)/shard_map/ppermute | solution.py:51
  37.8 6.0 %collective-permute-start.16 = (bf16[64,512]{1,0:T(8,128)(2,1)S(1)}, bf16[64,512]{1,0:T(8,128)(2,1)S(1)}, u32[]{:S(2)}, u32[]{:S(2)}) collective-permute-start(bf16[64,512]{1,0:T(8,128)(2,1)S(1)} %shard_map.64), channel_id=1, source_target_pairs={{0,2},{1,3},{2,0},{3,1},{4,6},{5,7},{6,4},{7,5},{8,10},{9,11},{10,... | collective-permute-start | bytes 196616 | tf_op jit(solution)/shard_map/ppermute | solution.py:51
  43.9 7.9 %collective-permute-start.20 = (bf16[3,64,512]{2,1,0:T(8,128)(2,1)S(1)}, bf16[3,64,512]{2,1,0:T(8,128)(2,1)S(1)}, u32[]{:S(2)}, u32[]{:S(2)}) collective-permute-start(bf16[3,64,512]{2,1,0:T(8,128)(2,1)S(1)} %pad_maximum_fusion.7), channel_id=1, source_target_pairs={{0,2},{1,3},{2,0},{3,1},{4,6},{5,7},{6,4},{7,5},{8,10},{9,11},{10,... | collective-permute-start | bytes 589832 | tf_op jit(solution)/shard_map/ppermute | solution.py:51
  45.5 7.0 %collective-permute-start.19 = (bf16[4,64,512]{2,1,0:T(8,128)(2,1)S(1)}, bf16[4,64,512]{2,1,0:T(8,128)(2,1)S(1)}, u32[]{:S(2)}, u32[]{:S(2)}) collective-permute-start(bf16[4,64,512]{2,1,0:T(8,128)(2,1)S(1)} %pad_maximum_fusion.4.refs_0_), channel_id=1, source_target_pairs={{0,1},{1,0},{2,3},{3,2},{4,5},{5,4},{6,7},{7,6},{8,9},{9,8},{10,11... | collective-permute-start | bytes 786440 | tf_op jit(solution)/shard_map/ppermute | solution.py:51
  51.9 1.7 %collective-permute-start.21 = (bf16[4,64,512]{2,1,0:T(8,128)(2,1)S(1)}, bf16[4,64,512]{2,1,0:T(8,128)(2,1)S(1)}, u32[]{:S(2)}, u32[]{:S(2)}) collective-permute-start(bf16[4,64,512]{2,1,0:T(8,128)(2,1)S(1)} %pad_maximum_fusion.5), channel_id=1, source_target_pairs={{0,1},{1,0},{2,3},{3,2},{4,5},{5,4},{6,7},{7,6},{8,9},{9,8},{10,11... | collective-permute-start | bytes 786440 | tf_op jit(solution)/shard_map/ppermute | solution.py:51

commit v5 on v0

v5 whole, which is shorter than its diff:
```python
import functools

import jax
import jax.numpy as jnp
from jax import lax
from jax.experimental import pallas as pl
from jax.experimental.pallas import tpu as pltpu
from jax.sharding import PartitionSpec as P

CAND = 4
KBLK = 1024
RBLK = 256
FLIGHT = 3
VMEM = 50 << 20


def general(factors_in, factors_out, basis_in, basis_out, eigvals, live_counts):
    slot_rows = factors_in.shape[0]
    keep = (lax.iota(jnp.int32, slot_rows) < live_counts[0])[:, None]
    masked = jnp.where(keep, factors_in, jnp.zeros_like(factors_in))
    partial_in = jnp.dot(
        lax.all_gather(masked, "dp", axis=0, tiled=True),
        basis_in,
        preferred_element_type=jnp.float32,
    )
    partial_out = jnp.dot(
        lax.all_gather(factors_out, "dp", axis=0, tiled=True),
        basis_out,
        preferred_element_type=jnp.float32,
    )
    halves = lax.axis_size("basis")
    share = partial_in.shape[0] // halves
    summed_in, summed_out = lax.psum((partial_in, partial_out), "basis")
    first = lax.axis_index("basis") * share
    proj_in = lax.dynamic_slice_in_dim(summed_in, first, share, 0).astype(jnp.bfloat16)
    proj_out = lax.dynamic_slice_in_dim(summed_out, first, share, 0).astype(jnp.bfloat16)
    cand_local = CAND // halves
    per_cand = share // cand_local
    pout_grouped = proj_out.reshape(cand_local, per_cand, proj_out.shape[1])
    shifted = eigvals.astype(jnp.float32) + 0.01
    piece = lax.all_gather(proj_in, "dp", axis=1, tiled=True)
    pin_grouped = piece.reshape(cand_local, per_cand, piece.shape[1])
    summed = jnp.einsum(
        "ati,atj->aij", pout_grouped, pin_grouped, preferred_element_type=jnp.float32
    )
    return (summed / shifted[None, :, :]).astype(jnp.bfloat16)


def swap(x, m):
    n = lax.axis_size("dp")
    return lax.ppermute(x, "dp", [(d, d ^ m) for d in range(n)])


def after(x, *others):
    return lax.optimization_barrier((x,) + others)[0]


def project_kernel(blocks, turn, own_ref, *refs):
    count = len(blocks)
    sources, basis_ref, out_ref = refs[:count], refs[count], refs[count + 1]
    pieces, (held, rows, sems, piece_sems) = refs[count + 2:-4], refs[-4:]
    chunks, width = held.shape[:2]
    slots = pieces[0].shape[-2]
    copies = [
        pltpu.make_async_copy(source, piece, piece_sems.at[k])
        for k, (source, piece) in enumerate(zip(sources, pieces))
    ]
    reads = [
        pltpu.make_async_copy(basis_ref.at[pl.ds(k * width, width)], held.at[k], sems.at[k])
        for k in range(chunks)
    ]
    reads[0].start()
    for copy in copies:
        copy.start()
    for read in reads[1:]:
        read.start()
    for copy, piece, entries in zip(copies, pieces, blocks):
        copy.wait()
        for e, m in enumerate(entries):
            rows[m * slots:(m + 1) * slots, :] = piece[e].astype(jnp.float32)
    acc = None
    for k in range(chunks):
        reads[k].wait()
        part = jnp.dot(
            rows[:, k * width:(k + 1) * width].astype(jnp.bfloat16),
            held[k],
            preferred_element_type=jnp.float32,
        )
        acc = part if acc is None else acc + part
    total = rows.shape[0]
    to = lax.broadcasted_iota(jnp.int32, (total, total), 0)
    come = lax.broadcasted_iota(jnp.int32, (total, total), 1)
    where = jnp.bitwise_xor(come // slots, own_ref[0]) * slots + come % slots
    pick = jnp.where(to == where, 1.0, 0.0).astype(jnp.bfloat16)
    proj = jnp.dot(pick, acc.astype(jnp.bfloat16), preferred_element_type=jnp.float32)
    if turn:
        turned = proj.T
        token = lax.broadcasted_iota(jnp.int32, turned.shape, 1)
        for c in range(CAND):
            own_tokens = token // (total // CAND) == c
            out_ref[c] = jnp.where(own_tokens, turned, 0.0).astype(jnp.bfloat16)
    else:
        out_ref[...] = proj.astype(jnp.bfloat16)


def anywhere(count):
    return [pl.BlockSpec(memory_space=pl.ANY)] * count


def project(own, blocks, basis, turn):
    slots = blocks[0][0].shape[-2]
    depth, cols = basis.shape
    total = slots * sum(len(entries) for _, entries in blocks)
    shape = (CAND, cols, total) if turn else (total, cols)
    chunks = depth // KBLK
    return pl.pallas_call(
        functools.partial(project_kernel, [entries for _, entries in blocks], turn),
        out_shape=jax.ShapeDtypeStruct(shape, jnp.bfloat16),
        in_specs=[pl.BlockSpec(memory_space=pltpu.SMEM)] + anywhere(len(blocks) + 1),
        out_specs=pl.BlockSpec(memory_space=pltpu.VMEM),
        scratch_shapes=[pltpu.VMEM(x.shape, jnp.bfloat16) for x, _ in blocks] + [
            pltpu.VMEM((chunks, KBLK, cols), jnp.bfloat16),
            pltpu.VMEM((total, depth), jnp.float32),
            pltpu.SemaphoreType.DMA((chunks,)),
            pltpu.SemaphoreType.DMA((len(blocks),)),
        ],
        compiler_params=pltpu.CompilerParams(vmem_limit_bytes=VMEM),
        cost_estimate=pl.CostEstimate(flops=total, bytes_accessed=total, transcendentals=0),
    )(own, *[x for x, _ in blocks], basis)


def outer_kernel(blocks, own_ref, *refs):
    given = len(blocks)
    sources, left_any, eig_ref = refs[:given], refs[given], refs[given + 1]
    out_ref, left, right, eig, scale, out, eig_sems, out_sems, piece_sems, left_sem = refs[-10:]
    order = [m for entries in blocks for m in entries]
    count = len(order)
    rows, cols = eig.shape[1:]
    depth = out.shape[0]

    def columns(s):
        m = jnp.int32(order[0])
        for k in range(1, count):
            m = jnp.where(s == k, order[k], m)
        return pl.ds(pl.multiple_of(jnp.bitwise_xor(m, own_ref[0]) * cols, cols), cols)

    def read(s):
        return pltpu.make_async_copy(eig_ref.at[:, columns(s)], eig.at[s], eig_sems.at[s])

    def write(s, c):
        slot = lax.rem(s, depth)
        return pltpu.make_async_copy(
            out.at[slot, c], out_ref.at[c, :, columns(s)], out_sems.at[slot, c]
        )

    copies, at = [pltpu.make_async_copy(left_any, left, left_sem)], 0
    for k, (source, entries) in enumerate(zip(sources, blocks)):
        room = right.at[pl.ds(at, len(entries))]
        copies.append(pltpu.make_async_copy(source, room, piece_sems.at[k]))
        at += len(entries)
    read(0).start()
    for copy in copies:
        copy.start()
    for s in range(1, count):
        read(s).start()
    for copy in copies:
        copy.wait()

    @pl.loop(0, count)
    def _(s):
        slot = lax.rem(s, depth)
        read(s).wait()
        shifted = eig[s].astype(jnp.float32) + 0.01
        near = pl.reciprocal(shifted, approx=True)
        scale[...] = near * (2.0 - shifted * near)
        for c in range(CAND):
            @pl.when(s >= depth)
            def _():
                write(s - depth, c).wait()

            for r in range(0, rows, RBLK):
                summed = jnp.dot(
                    left[c, r:r + RBLK, :], right[s], preferred_element_type=jnp.float32
                )
                out[slot, c, r:r + RBLK, :] = (summed * scale[r:r + RBLK, :]).astype(jnp.bfloat16)
            write(s, c).start()

    for s in range(max(0, count - depth), count):
        for c in range(CAND):
            write(s, c).wait()


def outer(own, blocks, left, eigvals, before):
    total, cols = blocks[0][0].shape[-2:]
    rows, width = eigvals.shape
    count = sum(len(entries) for _, entries in blocks)
    operands = [own] + [x for x, _ in blocks] + [left, eigvals]
    aliases = {}
    if before is not None:
        aliases = {len(operands): 0}
        operands.append(before)
    share = count * cols
    return pl.pallas_call(
        functools.partial(outer_kernel, [entries for _, entries in blocks]),
        out_shape=jax.ShapeDtypeStruct((CAND, rows, width), jnp.bfloat16),
        in_specs=[pl.BlockSpec(memory_space=pltpu.SMEM)] + anywhere(len(operands) - 1),
        out_specs=pl.BlockSpec(memory_space=pl.ANY),
        scratch_shapes=[
            pltpu.VMEM(left.shape, jnp.bfloat16),
            pltpu.VMEM((count, total, cols), jnp.bfloat16),
            pltpu.VMEM((count, rows, cols), jnp.bfloat16),
            pltpu.VMEM((rows, cols), jnp.float32),
            pltpu.VMEM((FLIGHT, CAND, rows, cols), jnp.bfloat16),
            pltpu.SemaphoreType.DMA((count,)),
            pltpu.SemaphoreType.DMA((FLIGHT, CAND)),
            pltpu.SemaphoreType.DMA((len(blocks),)),
            pltpu.SemaphoreType.DMA(()),
        ],
        input_output_aliases=aliases,
        compiler_params=pltpu.CompilerParams(vmem_limit_bytes=VMEM),
        cost_estimate=pl.CostEstimate(
            flops=2 * total * rows * share,
            bytes_accessed=2 * rows * share * (CAND + 1),
            transcendentals=rows * share,
        ),
    )(*operands)


def by_swaps(factors_in, factors_out, basis_in, basis_out, eigvals, live_counts):
    own = lax.axis_index("dp").astype(jnp.int32)[None]
    slots = factors_in.shape[0]
    column = (0, 4, 8, 12)
    pair = (2, 6, 10, 14)
    core = (1, 5, 9, 13)
    other = (3, 7, 11, 15)
    tie = lax.optimization_barrier

    a1, ap, a2, a3 = [swap(factors_in, m) for m in (4, 2, 8, 12)]
    keep = (lax.iota(jnp.int32, slots) < live_counts[0])[:, None]
    a, b = tie(tuple(
        jnp.where(keep, x, jnp.zeros_like(x)) for x in (factors_in, factors_out)
    ))
    a1, ap = tie((a1, ap))
    ap1 = swap(a1, 2)
    ap23 = swap(jnp.stack([a2, a3]), 2)
    a_column = jnp.stack([a, a1, a2, a3])
    a_core = swap(a_column, 1)
    b = after(b, a_column)
    b1, bp, b2, b3 = [swap(b, m) for m in (4, 2, 8, 12)]
    ap23, b1 = tie((ap23, b1))
    a_pair = jnp.stack([ap, ap1, ap23[0], ap23[1]])
    a_other = swap(a_pair, 1)
    pin = project(
        own, [(a_column, column), (a_pair, pair), (a_core, core), (a_other, other)],
        basis_in, False,
    )

    b1, b2, b3, bp = tie((b1, b2, b3, bp, pin))[:4]
    bp123 = swap(jnp.stack([b1, b2, b3]), 2)
    b_column = jnp.stack([b, b1, b2, b3])
    b_core = swap(b_column, 1)
    sent, b_column = tie((pin, b_column))
    g1, gp, g2, g3 = [swap(sent, m) for m in (4, 2, 8, 12)]
    bp123, g1, g2, g3 = tie((bp123, g1, g2, g3))
    b_pair = jnp.concatenate([bp[None], bp123])
    b_other = swap(b_pair, 1)
    g_column = jnp.stack([pin, g1, g2, g3])
    gp123 = swap(jnp.stack([g1, g2, g3]), 2)
    g_core = swap(g_column, 1)
    b_other, g_column = tie((b_other, g_column))
    left = project(
        own, [(b_column, column), (b_pair, pair), (b_core, core), (b_other, other)],
        basis_out, True,
    )
    out = outer(own, [(g_column, column), (gp[None], pair[:1])], left, eigvals, None)
    g_other = swap(jnp.concatenate([gp[None], after(gp123, out)]), 1)
    return outer(own, [(g_core, core), (gp123, pair[1:]), (g_other, other)], left, eigvals, out)


def solution(mesh):
    placed = (
        P(("groups", "dp"), "basis"),
        P(("groups", "dp"), "basis"),
        P("basis", "dp"),
        P("basis", "dp"),
        P("dp", None),
        P(("groups", "dp")),
    )
    chosen = by_swaps if mesh.shape["basis"] == 1 and mesh.shape["dp"] == 16 else general
    return jax.shard_map(
        chosen,
        mesh=mesh,
        in_specs=placed,
        out_specs=P(("groups", "basis"), "dp", None),
        check_vma=False,
    )
```

time: 154 us -> 76.1 us (0.49)
  waiting for transfers between devices: 93.6 us -> 19.1 us
  Pallas kernels: 0 us -> 33.1 us
  matrix products: 30.8 us -> 0 us
  starting transfers between devices: 0.08 us -> 20.6 us
  between operations: 13.8 us -> 0.84 us
  other arithmetic: 13.1 us -> 2.17 us
  local copies, waits for them, and re-layouts: 2.67 us -> 0 us
    all_gather x3 -> x0, waiting for transfers between devices: 92.9 us -> none  [the longest x1 40.6 us: per_device(): lax.all_gather(masked, 'dp', axis=0, tiled=True)]
    pallas_call x0 -> x4, Pallas kernels: none -> 33.1 us  [the longest x2 25 us: outer(): pl.pallas_call(functools.partial(outer_kernel, [entries for _, entries in...]
    dot_general x3 -> x0, matrix products: 30.8 us -> none  [the longest x1 20.3 us: per_device(): jnp.einsum('ati,atj->aij', pout_grouped, pin_grouped, preferred_element_t...]
    ppermute x0 -> x22, starting transfers between devices: none -> 20.6 us  [swap(): return lax.ppermute(x, 'dp', [(d, d ^ m) for d in range(n)])]
    ppermute x0 -> x22, waiting for transfers between devices: none -> 19.1 us  [swap(): return lax.ppermute(x, 'dp', [(d, d ^ m) for d in range(n)])]
    add x1 -> x0, other arithmetic: 11.5 us -> none  [per_device(): shifted = eigvals.astype(jnp.float32) + 0.01]
    unnamed x2 -> x0, local copies, waits for them, and re-layouts: 2.67 us -> none
    unnamed x1 -> x0, other arithmetic: 1.57 us -> none
  transfers between devices with their start and end apart: 3 -> 22, of which waited for: 3 -> 10; matrix products, arithmetic and copies ran while one was open for 16% -> 3% of each run, Pallas kernels for 0% -> 22%
where the time goes in v5:
time: 76.1 us; the launch traced here: 75.9 us
  Pallas kernels  33.1 us (43%)
  starting transfers between devices  20.6 us (27%)
  waiting for transfers between devices  19.1 us (25%)
  other arithmetic  2.17 us (3%)
  between operations  0.84 us (1%)
    pallas_call x2, Pallas kernels, outer(): pl.pallas_call(functools.partial(outer_kernel, [entries for _, entries in...  25 us
    ppermute x22, starting transfers between devices, swap(): return lax.ppermute(x, 'dp', [(d, d ^ m) for d in range(n)])  20.6 us
    ppermute x22, waiting for transfers between devices, swap(): return lax.ppermute(x, 'dp', [(d, d ^ m) for d in range(n)])  19.1 us
    pallas_call x2, Pallas kernels, project(): pl.pallas_call(functools.partial(project_kernel, [entries for _, entries...  8.09 us
  transfers between devices with their start and end apart: 22, of which 10 were waited for; matrix products, arithmetic and copies ran while one was open for 3% of the time, Pallas kernels for 22%

profile of v5, /device:TPU:0, one launch (start us, length us, event | category | flops | bytes accessed | tf_op | source)
XLA Modules:
  0.0 75.9 jit_solution(9877122879970507544)
XLA Ops:
  0.0 2.9 %collective-permute-start.1 = (bf16[4,8192]{1,0:T(4,128)(2,1)}, bf16[4,8192]{1,0:T(4,128)(2,1)S(1)}, u32[]{:S(2)}, u32[]{:S(2)}) collective-permute-start(bf16[4,8192]{1,0:T(4,128)(2,1)} %param.6), channel_id=1, source_target_pairs={{0,2},{1,3},{2,0},{3,1},{4,6},{5,7},{6,4},{7,5},{8,10},{9,11},{10,... | collective-permute-start | bytes 196616 | tf_op jit(solution)/shard_map/ppermute | solution.py:51
  2.9 1.6 %collective-permute-start = (bf16[4,8192]{1,0:T(4,128)(2,1)}, bf16[4,8192]{1,0:T(4,128)(2,1)S(1)}, u32[]{:S(2)}, u32[]{:S(2)}) collective-permute-start(bf16[4,8192]{1,0:T(4,128)(2,1)} %param.6), channel_id=1, source_target_pairs={{0,4},{1,5},{2,6},{3,7},{4,0},{5,1},{6,2},{7,3},{8,12},{9,13},{10,... | collective-permute-start | bytes 196616 | tf_op jit(solution)/shard_map/ppermute | solution.py:51
  4.5 2.5 %collective-permute-start.3 = (bf16[4,8192]{1,0:T(4,128)(2,1)}, bf16[4,8192]{1,0:T(4,128)(2,1)S(1)}, u32[]{:S(2)}, u32[]{:S(2)}) collective-permute-start(bf16[4,8192]{1,0:T(4,128)(2,1)} %param.6), channel_id=1, source_target_pairs={{0,12},{1,13},{2,14},{3,15},{4,8},{5,9},{6,10},{7,11},{8,4},{9,5},... | collective-permute-start | bytes 196616 | tf_op jit(solution)/shard_map/ppermute | solution.py:51
  7.0 0.1 collective-permute-start.2
  7.8 1.0 %broadcast_select_fusion = (bf16[4,8192]{1,0:T(4,128)(2,1)S(1)}, bf16[4,8192]{1,0:T(4,128)(2,1)S(1)}) fusion(bf16[4,8192]{1,0:T(4,128)(2,1)} %param.7, pred[4]{0:T(512)(128)(4,1)S(1)} %iota_compare_fusion, bf16[4,8192]{1,0:T(4,128)(2,1)} %param.6), kind=kLoop, calls=%fused_computation.9 | loop fusion | flops 65536 | bytes 262148 | tf_op jit(solution)/shard_map/jit(_where)/select_n | solution.py:241
  8.8 0.0 collective-permute-done.1
  8.8 0.0 collective-permute-done
  8.8 2.5 %collective-permute-done.3 = bf16[4,8192]{1,0:T(4,128)(2,1)S(1)} collective-permute-done((bf16[4,8192]{1,0:T(4,128)(2,1)}, bf16[4,8192]{1,0:T(4,128)(2,1)S(1)}, u32[]{:S(2)}, u32[]{:S(2)}) %collective-permute-start.3) | collective-permute-done | bytes 65568 | tf_op jit(solution)/shard_map/ppermute | solution.py:51
  11.3 2.1 %collective-permute-done.2 = bf16[4,8192]{1,0:T(4,128)(2,1)S(1)} collective-permute-done((bf16[4,8192]{1,0:T(4,128)(2,1)}, bf16[4,8192]{1,0:T(4,128)(2,1)S(1)}, u32[]{:S(2)}, u32[]{:S(2)}) %collective-permute-start.2) | collective-permute-done | bytes 65568 | tf_op jit(solution)/shard_map/ppermute | solution.py:51
  13.4 0.1 pad_maximum_fusion.8
  13.5 0.6 collective-permute-start.5
  14.1 0.2 pad_maximum_fusion.refs_0_
  14.4 0.1 collective-permute-start.6
  14.4 1.6 %collective-permute-start.4 = (bf16[4,8192]{1,0:T(4,128)(2,1)S(1)}, bf16[4,8192]{1,0:T(4,128)(2,1)S(1)}, u32[]{:S(2)}, u32[]{:S(2)}) collective-permute-start(bf16[4,8192]{1,0:T(4,128)(2,1)S(1)} %collective-permute-done), channel_id=1, source_target_pairs={{0,2},{1,3},{2,0},{3,1},{4,6},{5,7},{6,4},{7,5},{8,10},{9,11},{10,... | collective-permute-start | bytes 196616 | tf_op jit(solution)/shard_map/ppermute | solution.py:51
  16.0 0.0 collective-permute-start.7
  16.0 2.7 %collective-permute-done.6 = bf16[4,8192]{1,0:T(4,128)(2,1)S(1)} collective-permute-done((bf16[4,8192]{1,0:T(4,128)(2,1)S(1)}, bf16[4,8192]{1,0:T(4,128)(2,1)S(1)}, u32[]{:S(2)}, u32[]{:S(2)}) %collective-permute-start.6) | collective-permute-done | bytes 65568 | tf_op jit(solution)/shard_map/ppermute | solution.py:51
  18.7 0.8 %collective-permute-done.5 = bf16[2,4,8192]{2,1,0:T(4,128)(2,1)S(1)} collective-permute-done((bf16[2,4,8192]{2,1,0:T(4,128)(2,1)S(1)}, bf16[2,4,8192]{2,1,0:T(4,128)(2,1)S(1)}, u32[]{:S(2)}, u32[]{:S(2)}) %collective-permute-start.5) | collective-permute-done | bytes 131104 | tf_op jit(solution)/shard_map/ppermute | solution.py:51
  19.5 0.7 collective-permute-done.4
  20.2 0.2 pad_maximum_fusion.1.refs_1_
  20.4 0.1 collective-permute-start.8
  20.4 0.6 collective-permute-start.11
  21.0 1.9 %collective-permute-start.10 = (bf16[4,8192]{1,0:T(4,128)(2,1)S(1)}, bf16[4,8192]{1,0:T(4,128)(2,1)S(1)}, u32[]{:S(2)}, u32[]{:S(2)}) collective-permute-start(bf16[4,8192]{1,0:T(4,128)(2,1)S(1)} %get-tuple-element.29), channel_id=1, source_target_pairs={{0,12},{1,13},{2,14},{3,15},{4,8},{5,9},{6,10},{7,11},{8,4},{9,5},... | collective-permute-start | bytes 196616 | tf_op jit(solution)/shard_map/ppermute | solution.py:51
  23.0 1.1 %collective-permute-start.9 = (bf16[4,8192]{1,0:T(4,128)(2,1)S(1)}, bf16[4,8192]{1,0:T(4,128)(2,1)S(1)}, u32[]{:S(2)}, u32[]{:S(2)}) collective-permute-start(bf16[4,8192]{1,0:T(4,128)(2,1)S(1)} %get-tuple-element.29), channel_id=1, source_target_pairs={{0,8},{1,9},{2,10},{3,11},{4,12},{5,13},{6,14},{7,15},{8,0},{9,1},... | collective-permute-start | bytes 196616 | tf_op jit(solution)/shard_map/ppermute | solution.py:51
  24.0 0.0 collective-permute-done.8.refs_3_
  24.0 4.0 %shard_map.64 = bf16[64,512]{1,0:T(8,128)(2,1)S(1)} custom-call(s32[1]{0:T(128)} %bitcast.own_ref, bf16[4,4,8192]{2,1,0:T(4,128)(2,1)S(1)} %pad_maximum_fusion.refs_0_, bf16[4,4,8192]{2,1,0:T(4,128)(2,1)S(1)} %pad_maximum_fusion.1.refs_1_, bf16[4,4,8192]{2,1,0:T(4,128)(2,1)S(1)} %collective-permute-done.7.refs_2_, ...), custom_call_target="tpu_custom_call" | custom-call | flops 64 | bytes 64 | tf_op jit(solution)/shard_map/pallas_call | solution.py:116
  28.0 0.0 collective-permute-done.10
  28.0 2.5 %collective-permute-done.9 = bf16[4,8192]{1,0:T(4,128)(2,1)S(1)} collective-permute-done((bf16[4,8192]{1,0:T(4,128)(2,1)S(1)}, bf16[4,8192]{1,0:T(4,128)(2,1)S(1)}, u32[]{:S(2)}, u32[]{:S(2)}) %collective-permute-start.9) | collective-permute-done | bytes 65568 | tf_op jit(solution)/shard_map/ppermute | solution.py:51
  30.5 0.2 pad_maximum_fusion.6
  30.6 0.9 %collective-permute-start.12 = (bf16[3,4,8192]{2,1,0:T(4,128)(2,1)S(1)}, bf16[3,4,8192]{2,1,0:T(4,128)(2,1)S(1)}, u32[]{:S(2)}, u32[]{:S(2)}) collective-permute-start(bf16[3,4,8192]{2,1,0:T(4,128)(2,1)S(1)} %pad_maximum_fusion.6), channel_id=1, source_target_pairs={{0,2},{1,3},{2,0},{3,1},{4,6},{5,7},{6,4},{7,5},{8,10},{9,11},{10,... | collective-permute-start | bytes 589832 | tf_op jit(solution)/shard_map/ppermute | solution.py:51
  31.5 0.2 pad_maximum_fusion.2.refs_0_
  31.8 2.1 %collective-permute-start.15 = (bf16[64,512]{1,0:T(8,128)(2,1)S(1)}, bf16[64,512]{1,0:T(8,128)(2,1)S(1)}, u32[]{:S(2)}, u32[]{:S(2)}) collective-permute-start(bf16[64,512]{1,0:T(8,128)(2,1)S(1)} %shard_map.64), channel_id=1, source_target_pairs={{0,12},{1,13},{2,14},{3,15},{4,8},{5,9},{6,10},{7,11},{8,4},{9,5},... | collective-permute-start | bytes 196616 | tf_op jit(solution)/shard_map/ppermute | solution.py:51
  33.9 0.0 collective-permute-start.14
  33.9 2.3 %collective-permute-start.13 = (bf16[64,512]{1,0:T(8,128)(2,1)S(1)}, bf16[64,512]{1,0:T(8,128)(2,1)S(1)}, u32[]{:S(2)}, u32[]{:S(2)}) collective-permute-start(bf16[64,512]{1,0:T(8,128)(2,1)S(1)} %shard_map.64), channel_id=1, source_target_pairs={{0,4},{1,5},{2,6},{3,7},{4,0},{5,1},{6,2},{7,3},{8,12},{9,13},{10,... | collective-permute-start | bytes 196616 | tf_op jit(solution)/shard_map/ppermute | solution.py:51
  36.2 2.2 %collective-permute-done.15 = bf16[64,512]{1,0:T(8,128)(2,1)S(1)} collective-permute-done((bf16[64,512]{1,0:T(8,128)(2,1)S(1)}, bf16[64,512]{1,0:T(8,128)(2,1)S(1)}, u32[]{:S(2)}, u32[]{:S(2)}) %collective-permute-start.15) | collective-permute-done | bytes 65568 | tf_op jit(solution)/shard_map/ppermute | solution.py:51
  38.4 1.8 %collective-permute-done.14 = bf16[64,512]{1,0:T(8,128)(2,1)S(1)} collective-permute-done((bf16[64,512]{1,0:T(8,128)(2,1)S(1)}, bf16[64,512]{1,0:T(8,128)(2,1)S(1)}, u32[]{:S(2)}, u32[]{:S(2)}) %collective-permute-start.14) | collective-permute-done | bytes 65568 | tf_op jit(solution)/shard_map/ppermute | solution.py:51
  40.2 0.0 collective-permute-done.13
  40.2 0.0 collective-permute-done.12
  40.2 0.2 pad_maximum_fusion.4.refs_1_
  40.4 0.1 collective-permute-start.19
  40.5 0.8 %collective-permute-start.17 = (bf16[3,64,512]{2,1,0:T(8,128)(2,1)S(1)}, bf16[3,64,512]{2,1,0:T(8,128)(2,1)S(1)}, u32[]{:S(2)}, u32[]{:S(2)}) collective-permute-start(bf16[3,64,512]{2,1,0:T(8,128)(2,1)S(1)} %pad_maximum_fusion.7), channel_id=1, source_target_pairs={{0,2},{1,3},{2,0},{3,1},{4,6},{5,7},{6,4},{7,5},{8,10},{9,11},{10,... | collective-permute-start | bytes 589832 | tf_op jit(solution)/shard_map/ppermute | solution.py:51
  41.3 1.3 %collective-permute-start.18 = (bf16[64,512]{1,0:T(8,128)(2,1)S(1)}, bf16[64,512]{1,0:T(8,128)(2,1)S(1)}, u32[]{:S(2)}, u32[]{:S(2)}) collective-permute-start(bf16[64,512]{1,0:T(8,128)(2,1)S(1)} %shard_map.64), channel_id=1, source_target_pairs={{0,2},{1,3},{2,0},{3,1},{4,6},{5,7},{6,4},{7,5},{8,10},{9,11},{10,... | collective-permute-start | bytes 196616 | tf_op jit(solution)/shard_map/ppermute | solution.py:51
  42.6 0.1 collective-permute-start.16
  42.7 4.1 %shard_map.65.refs_2_.refs_3_ = bf16[4,512,64]{2,1,0:T(8,128)(2,1)S(1)} custom-call(s32[1]{0:T(128)} %bitcast.own_ref, bf16[4,4,8192]{2,1,0:T(4,128)(2,1)S(1)} %pad_maximum_fusion.2.refs_0_, bf16[4,4,8192]{2,1,0:T(4,128)(2,1)S(1)} %pad_maximum_fusion.4.refs_1_, bf16[4,4,8192]{2,1,0:T(4,128)(2,1)S(1)} %collective-permute-done.20.refs_2_, ...), custom_call_target="tpu_custom_call" | custom-call | flops 64 | bytes 64 | tf_op jit(solution)/shard_map/pallas_call | solution.py:116
  46.8 2.4 %collective-permute-done.18 = bf16[64,512]{1,0:T(8,128)(2,1)S(1)} collective-permute-done((bf16[64,512]{1,0:T(8,128)(2,1)S(1)}, bf16[64,512]{1,0:T(8,128)(2,1)S(1)}, u32[]{:S(2)}, u32[]{:S(2)}) %collective-permute-start.18) | collective-permute-done | bytes 65568 | tf_op jit(solution)/shard_map/ppermute | solution.py:51
  49.2 8.6 %shard_map.66.refs_5_ = bf16[4,512,8192]{2,1,0:T(8,128)(2,1)} custom-call(s32[1]{0:T(128)} %bitcast.own_ref, bf16[4,64,512]{2,1,0:T(8,128)(2,1)S(1)} %pad_maximum_fusion.3.refs_0_, bf16[1,64,512]{2,1,0:T(8,128)(2,1)S(1)} %bitcast.20, bf16[4,512,64]{2,1,0:T(8,128)(2,1)S(1)} %shard_map.65.refs_2_.refs_3_, bf16[512,8192]{1,0:T(8,128)(2,1)} %refs_4_.5), custom_call_target="tpu_custom_call" | custom-call | flops 167772160 | bytes 13107200 | tf_op jit(solution)/shard_map/pallas_call | solution.py:203
  57.9 0.1 collective-permute-start.21
  57.9 1.5 %collective-permute-done.21.refs_2_ = bf16[4,64,512]{2,1,0:T(8,128)(2,1)S(1)} collective-permute-done((bf16[4,64,512]{2,1,0:T(8,128)(2,1)S(1)}, bf16[4,64,512]{2,1,0:T(8,128)(2,1)S(1)}, u32[]{:S(2)}, u32[]{:S(2)}) %collective-permute-start.21) | collective-permute-done | bytes 262176 | tf_op jit(solution)/shard_map/ppermute | solution.py:51
  59.5 16.4 %shard_map.67 = bf16[4,512,8192]{2,1,0:T(8,128)(2,1)} custom-call(s32[1]{0:T(128)} %bitcast.own_ref, bf16[4,64,512]{2,1,0:T(8,128)(2,1)S(1)} %collective-permute-done.16.refs_0_, bf16[3,64,512]{2,1,0:T(8,128)(2,1)S(1)} %collective-permute-done.17.refs_1_, bf16[4,64,512]{2,1,0:T(8,128)(2,1)S(1)} %collective-permute-done.21.refs_2_, ...), custom_call_target="tpu_custom_call", output_to_operand_aliasing={{}: (6, {})} | custom-call | flops 369098752 | bytes 28835840 | tf_op jit(solution)/shard_map/pallas_call | solution.py:203
  (11 shorter events, 0.1 us)
Async XLA Ops:
  0.0 8.8 %collective-permute-start.1 = (bf16[4,8192]{1,0:T(4,128)(2,1)}, bf16[4,8192]{1,0:T(4,128)(2,1)S(1)}, u32[]{:S(2)}, u32[]{:S(2)}) collective-permute-start(bf16[4,8192]{1,0:T(4,128)(2,1)} %param.6), channel_id=1, source_target_pairs={{0,2},{1,3},{2,0},{3,1},{4,6},{5,7},{6,4},{7,5},{8,10},{9,11},{10,... | collective-permute-start | bytes 196616 | tf_op jit(solution)/shard_map/ppermute | solution.py:51
  2.9 5.8 %collective-permute-start = (bf16[4,8192]{1,0:T(4,128)(2,1)}, bf16[4,8192]{1,0:T(4,128)(2,1)S(1)}, u32[]{:S(2)}, u32[]{:S(2)}) collective-permute-start(bf16[4,8192]{1,0:T(4,128)(2,1)} %param.6), channel_id=1, source_target_pairs={{0,4},{1,5},{2,6},{3,7},{4,0},{5,1},{6,2},{7,3},{8,12},{9,13},{10,... | collective-permute-start | bytes 196616 | tf_op jit(solution)/shard_map/ppermute | solution.py:51
  4.5 6.8 %collective-permute-start.3 = (bf16[4,8192]{1,0:T(4,128)(2,1)}, bf16[4,8192]{1,0:T(4,128)(2,1)S(1)}, u32[]{:S(2)}, u32[]{:S(2)}) collective-permute-start(bf16[4,8192]{1,0:T(4,128)(2,1)} %param.6), channel_id=1, source_target_pairs={{0,12},{1,13},{2,14},{3,15},{4,8},{5,9},{6,10},{7,11},{8,4},{9,5},... | collective-permute-start | bytes 196616 | tf_op jit(solution)/shard_map/ppermute | solution.py:51
  7.0 6.4 %collective-permute-start.2 = (bf16[4,8192]{1,0:T(4,128)(2,1)}, bf16[4,8192]{1,0:T(4,128)(2,1)S(1)}, u32[]{:S(2)}, u32[]{:S(2)}) collective-permute-start(bf16[4,8192]{1,0:T(4,128)(2,1)} %param.6), channel_id=1, source_target_pairs={{0,8},{1,9},{2,10},{3,11},{4,12},{5,13},{6,14},{7,15},{8,0},{9,1},... | collective-permute-start | bytes 196616 | tf_op jit(solution)/shard_map/ppermute | solution.py:51
  13.5 5.9 %collective-permute-start.5 = (bf16[2,4,8192]{2,1,0:T(4,128)(2,1)S(1)}, bf16[2,4,8192]{2,1,0:T(4,128)(2,1)S(1)}, u32[]{:S(2)}, u32[]{:S(2)}) collective-permute-start(bf16[2,4,8192]{2,1,0:T(4,128)(2,1)S(1)} %pad_maximum_fusion.8), channel_id=1, source_target_pairs={{0,2},{1,3},{2,0},{3,1},{4,6},{5,7},{6,4},{7,5},{8,10},{9,11},{10,... | collective-permute-start | bytes 393224 | tf_op jit(solution)/shard_map/ppermute | solution.py:51
  14.4 4.3 %collective-permute-start.6 = (bf16[4,8192]{1,0:T(4,128)(2,1)S(1)}, bf16[4,8192]{1,0:T(4,128)(2,1)S(1)}, u32[]{:S(2)}, u32[]{:S(2)}) collective-permute-start(bf16[4,8192]{1,0:T(4,128)(2,1)S(1)} %get-tuple-element.29), channel_id=1, source_target_pairs={{0,4},{1,5},{2,6},{3,7},{4,0},{5,1},{6,2},{7,3},{8,12},{9,13},{10,... | collective-permute-start | bytes 196616 | tf_op jit(solution)/shard_map/ppermute | solution.py:51
  14.4 5.7 %collective-permute-start.4 = (bf16[4,8192]{1,0:T(4,128)(2,1)S(1)}, bf16[4,8192]{1,0:T(4,128)(2,1)S(1)}, u32[]{:S(2)}, u32[]{:S(2)}) collective-permute-start(bf16[4,8192]{1,0:T(4,128)(2,1)S(1)} %collective-permute-done), channel_id=1, source_target_pairs={{0,2},{1,3},{2,0},{3,1},{4,6},{5,7},{6,4},{7,5},{8,10},{9,11},{10,... | collective-permute-start | bytes 196616 | tf_op jit(solution)/shard_map/ppermute | solution.py:51
  16.0 8.0 %collective-permute-start.7 = (bf16[4,4,8192]{2,1,0:T(4,128)(2,1)S(1)}, bf16[4,4,8192]{2,1,0:T(4,128)(2,1)S(1)}, u32[]{:S(2)}, u32[]{:S(2)}) collective-permute-start(bf16[4,4,8192]{2,1,0:T(4,128)(2,1)S(1)} %pad_maximum_fusion.refs_0_), channel_id=1, source_target_pairs={{0,1},{1,0},{2,3},{3,2},{4,5},{5,4},{6,7},{7,6},{8,9},{9,8},{10,11... | collective-permute-start | bytes 786440 | tf_op jit(solution)/shard_map/ppermute | solution.py:51
  20.4 3.7 %collective-permute-start.8 = (bf16[4,4,8192]{2,1,0:T(4,128)(2,1)S(1)}, bf16[4,4,8192]{2,1,0:T(4,128)(2,1)S(1)}, u32[]{:S(2)}, u32[]{:S(2)}) collective-permute-start(bf16[4,4,8192]{2,1,0:T(4,128)(2,1)S(1)} %pad_maximum_fusion.1.refs_1_), channel_id=1, source_target_pairs={{0,1},{1,0},{2,3},{3,2},{4,5},{5,4},{6,7},{7,6},{8,9},{9,8},{10,11... | collective-permute-start | bytes 786440 | tf_op jit(solution)/shard_map/ppermute | solution.py:51
  20.4 7.5 %collective-permute-start.11 = (bf16[4,8192]{1,0:T(4,128)(2,1)S(1)}, bf16[4,8192]{1,0:T(4,128)(2,1)S(1)}, u32[]{:S(2)}, u32[]{:S(2)}) collective-permute-start(bf16[4,8192]{1,0:T(4,128)(2,1)S(1)} %get-tuple-element.29), channel_id=1, source_target_pairs={{0,2},{1,3},{2,0},{3,1},{4,6},{5,7},{6,4},{7,5},{8,10},{9,11},{10,... | collective-permute-start | bytes 196616 | tf_op jit(solution)/shard_map/ppermute | solution.py:51
  21.0 7.0 %collective-permute-start.10 = (bf16[4,8192]{1,0:T(4,128)(2,1)S(1)}, bf16[4,8192]{1,0:T(4,128)(2,1)S(1)}, u32[]{:S(2)}, u32[]{:S(2)}) collective-permute-start(bf16[4,8192]{1,0:T(4,128)(2,1)S(1)} %get-tuple-element.29), channel_id=1, source_target_pairs={{0,12},{1,13},{2,14},{3,15},{4,8},{5,9},{6,10},{7,11},{8,4},{9,5},... | collective-permute-start | bytes 196616 | tf_op jit(solution)/shard_map/ppermute | solution.py:51
  23.0 7.5 %collective-permute-start.9 = (bf16[4,8192]{1,0:T(4,128)(2,1)S(1)}, bf16[4,8192]{1,0:T(4,128)(2,1)S(1)}, u32[]{:S(2)}, u32[]{:S(2)}) collective-permute-start(bf16[4,8192]{1,0:T(4,128)(2,1)S(1)} %get-tuple-element.29), channel_id=1, source_target_pairs={{0,8},{1,9},{2,10},{3,11},{4,12},{5,13},{6,14},{7,15},{8,0},{9,1},... | collective-permute-start | bytes 196616 | tf_op jit(solution)/shard_map/ppermute | solution.py:51
  30.6 9.6 %collective-permute-start.12 = (bf16[3,4,8192]{2,1,0:T(4,128)(2,1)S(1)}, bf16[3,4,8192]{2,1,0:T(4,128)(2,1)S(1)}, u32[]{:S(2)}, u32[]{:S(2)}) collective-permute-start(bf16[3,4,8192]{2,1,0:T(4,128)(2,1)S(1)} %pad_maximum_fusion.6), channel_id=1, source_target_pairs={{0,2},{1,3},{2,0},{3,1},{4,6},{5,7},{6,4},{7,5},{8,10},{9,11},{10,... | collective-permute-start | bytes 589832 | tf_op jit(solution)/shard_map/ppermute | solution.py:51
  31.8 6.6 %collective-permute-start.15 = (bf16[64,512]{1,0:T(8,128)(2,1)S(1)}, bf16[64,512]{1,0:T(8,128)(2,1)S(1)}, u32[]{:S(2)}, u32[]{:S(2)}) collective-permute-start(bf16[64,512]{1,0:T(8,128)(2,1)S(1)} %shard_map.64), channel_id=1, source_target_pairs={{0,12},{1,13},{2,14},{3,15},{4,8},{5,9},{6,10},{7,11},{8,4},{9,5},... | collective-permute-start | bytes 196616 | tf_op jit(solution)/shard_map/ppermute | solution.py:51
  33.9 6.3 %collective-permute-start.14 = (bf16[64,512]{1,0:T(8,128)(2,1)S(1)}, bf16[64,512]{1,0:T(8,128)(2,1)S(1)}, u32[]{:S(2)}, u32[]{:S(2)}) collective-permute-start(bf16[64,512]{1,0:T(8,128)(2,1)S(1)} %shard_map.64), channel_id=1, source_target_pairs={{0,8},{1,9},{2,10},{3,11},{4,12},{5,13},{6,14},{7,15},{8,0},{9,1},... | collective-permute-start | bytes 196616 | tf_op jit(solution)/shard_map/ppermute | solution.py:51
  33.9 6.3 %collective-permute-start.13 = (bf16[64,512]{1,0:T(8,128)(2,1)S(1)}, bf16[64,512]{1,0:T(8,128)(2,1)S(1)}, u32[]{:S(2)}, u32[]{:S(2)}) collective-permute-start(bf16[64,512]{1,0:T(8,128)(2,1)S(1)} %shard_map.64), channel_id=1, source_target_pairs={{0,4},{1,5},{2,6},{3,7},{4,0},{5,1},{6,2},{7,3},{8,12},{9,13},{10,... | collective-permute-start | bytes 196616 | tf_op jit(solution)/shard_map/ppermute | solution.py:51
  36.2 6.5 %collective-permute-start.20 = (bf16[4,4,8192]{2,1,0:T(4,128)(2,1)S(1)}, bf16[4,4,8192]{2,1,0:T(4,128)(2,1)S(1)}, u32[]{:S(2)}, u32[]{:S(2)}) collective-permute-start(bf16[4,4,8192]{2,1,0:T(4,128)(2,1)S(1)} %pad_maximum_fusion.2.refs_0_), channel_id=1, source_target_pairs={{0,1},{1,0},{2,3},{3,2},{4,5},{5,4},{6,7},{7,6},{8,9},{9,8},{10,11... | collective-permute-start | bytes 786440 | tf_op jit(solution)/shard_map/ppermute | solution.py:51
  40.4 2.3 %collective-permute-start.19 = (bf16[4,4,8192]{2,1,0:T(4,128)(2,1)S(1)}, bf16[4,4,8192]{2,1,0:T(4,128)(2,1)S(1)}, u32[]{:S(2)}, u32[]{:S(2)}) collective-permute-start(bf16[4,4,8192]{2,1,0:T(4,128)(2,1)S(1)} %pad_maximum_fusion.4.refs_1_), channel_id=1, source_target_pairs={{0,1},{1,0},{2,3},{3,2},{4,5},{5,4},{6,7},{7,6},{8,9},{9,8},{10,11... | collective-permute-start | bytes 786440 | tf_op jit(solution)/shard_map/ppermute | solution.py:51
  40.5 17.4 %collective-permute-start.17 = (bf16[3,64,512]{2,1,0:T(8,128)(2,1)S(1)}, bf16[3,64,512]{2,1,0:T(8,128)(2,1)S(1)}, u32[]{:S(2)}, u32[]{:S(2)}) collective-permute-start(bf16[3,64,512]{2,1,0:T(8,128)(2,1)S(1)} %pad_maximum_fusion.7), channel_id=1, source_target_pairs={{0,2},{1,3},{2,0},{3,1},{4,6},{5,7},{6,4},{7,5},{8,10},{9,11},{10,... | collective-permute-start | bytes 589832 | tf_op jit(solution)/shard_map/ppermute | solution.py:51
  41.3 8.0 %collective-permute-start.18 = (bf16[64,512]{1,0:T(8,128)(2,1)S(1)}, bf16[64,512]{1,0:T(8,128)(2,1)S(1)}, u32[]{:S(2)}, u32[]{:S(2)}) collective-permute-start(bf16[64,512]{1,0:T(8,128)(2,1)S(1)} %shard_map.64), channel_id=1, source_target_pairs={{0,2},{1,3},{2,0},{3,1},{4,6},{5,7},{6,4},{7,5},{8,10},{9,11},{10,... | collective-permute-start | bytes 196616 | tf_op jit(solution)/shard_map/ppermute | solution.py:51
  42.6 15.3 %collective-permute-start.16 = (bf16[4,64,512]{2,1,0:T(8,128)(2,1)S(1)}, bf16[4,64,512]{2,1,0:T(8,128)(2,1)S(1)}, u32[]{:S(2)}, u32[]{:S(2)}) collective-permute-start(bf16[4,64,512]{2,1,0:T(8,128)(2,1)S(1)} %pad_maximum_fusion.3.refs_0_), channel_id=1, source_target_pairs={{0,1},{1,0},{2,3},{3,2},{4,5},{5,4},{6,7},{7,6},{8,9},{9,8},{10,11... | collective-permute-start | bytes 786440 | tf_op jit(solution)/shard_map/ppermute | solution.py:51
  57.9 1.6 %collective-permute-start.21 = (bf16[4,64,512]{2,1,0:T(8,128)(2,1)S(1)}, bf16[4,64,512]{2,1,0:T(8,128)(2,1)S(1)}, u32[]{:S(2)}, u32[]{:S(2)}) collective-permute-start(bf16[4,64,512]{2,1,0:T(8,128)(2,1)S(1)} %pad_maximum_fusion.5), channel_id=1, source_target_pairs={{0,1},{1,0},{2,3},{3,2},{4,5},{5,4},{6,7},{7,6},{8,9},{9,8},{10,11... | collective-permute-start | bytes 786440 | tf_op jit(solution)/shard_map/ppermute | solution.py:51

commit v6 on v5

--- a/solution.py
+++ b/solution.py
@@ -55,14 +55,14 @@
     return lax.optimization_barrier((x,) + others)[0]
 
 
-def project_kernel(blocks, turn, own_ref, *refs):
+def project_kernel(blocks, which, turn, own_ref, *refs):
     count = len(blocks)
     sources, basis_ref, out_ref = refs[:count], refs[count], refs[count + 1]
     pieces, (held, rows, sems, piece_sems) = refs[count + 2:-4], refs[-4:]
     chunks, width = held.shape[:2]
     slots = pieces[0].shape[-2]
     copies = [
-        pltpu.make_async_copy(source, piece, piece_sems.at[k])
+        pltpu.make_async_copy(source.at[:, which], piece, piece_sems.at[k])
         for k, (source, piece) in enumerate(zip(sources, pieces))
     ]
     reads = [
@@ -107,18 +107,20 @@
     return [pl.BlockSpec(memory_space=pl.ANY)] * count
 
 
-def project(own, blocks, basis, turn):
+def project(own, blocks, basis, which, turn):
     slots = blocks[0][0].shape[-2]
     depth, cols = basis.shape
     total = slots * sum(len(entries) for _, entries in blocks)
     shape = (CAND, cols, total) if turn else (total, cols)
     chunks = depth // KBLK
     return pl.pallas_call(
-        functools.partial(project_kernel, [entries for _, entries in blocks], turn),
+        functools.partial(project_kernel, [entries for _, entries in blocks], which, turn),
         out_shape=jax.ShapeDtypeStruct(shape, jnp.bfloat16),
         in_specs=[pl.BlockSpec(memory_space=pltpu.SMEM)] + anywhere(len(blocks) + 1),
         out_specs=pl.BlockSpec(memory_space=pltpu.VMEM),
-        scratch_shapes=[pltpu.VMEM(x.shape, jnp.bfloat16) for x, _ in blocks] + [
+        scratch_shapes=[
+            pltpu.VMEM((len(entries), slots, depth), jnp.bfloat16) for _, entries in blocks
+        ] + [
             pltpu.VMEM((chunks, KBLK, cols), jnp.bfloat16),
             pltpu.VMEM((total, depth), jnp.float32),
             pltpu.SemaphoreType.DMA((chunks,)),
@@ -132,7 +134,7 @@
 def outer_kernel(blocks, own_ref, *refs):
     given = len(blocks)
     sources, left_any, eig_ref = refs[:given], refs[given], refs[given + 1]
-    out_ref, left, right, eig, scale, out, eig_sems, out_sems, piece_sems, left_sem = refs[-10:]
+    out_ref, left, right, eig, out, eig_sems, out_sems, piece_sems, left_sem = refs[-9:]
     order = [m for entries in blocks for m in entries]
     count = len(order)
     rows, cols = eig.shape[1:]
@@ -166,24 +168,28 @@
     for copy in copies:
         copy.wait()
 
-    @pl.loop(0, count)
-    def _(s):
-        slot = lax.rem(s, depth)
+    def work(s, slot):
         read(s).wait()
-        shifted = eig[s].astype(jnp.float32) + 0.01
-        near = pl.reciprocal(shifted, approx=True)
-        scale[...] = near * (2.0 - shifted * near)
-        for c in range(CAND):
-            @pl.when(s >= depth)
-            def _():
-                write(s - depth, c).wait()
-
-            for r in range(0, rows, RBLK):
+        for r in range(0, rows, RBLK):
+            shifted = eig[s, r:r + RBLK, :].astype(jnp.float32) + 0.01
+            near = pl.reciprocal(shifted, approx=True)
+            scale = near * (2.0 - shifted * near)
+            for c in range(CAND):
                 summed = jnp.dot(
                     left[c, r:r + RBLK, :], right[s], preferred_element_type=jnp.float32
                 )
-                out[slot, c, r:r + RBLK, :] = (summed * scale[r:r + RBLK, :]).astype(jnp.bfloat16)
+                out[slot, c, r:r + RBLK, :] = (summed * scale).astype(jnp.bfloat16)
+        for c in range(CAND):
             write(s, c).start()
+
+    for s in range(depth):
+        work(s, s)
+
+    @pl.loop(depth, count)
+    def _(s):
+        for c in range(CAND):
+            write(s - depth, c).wait()
+        work(s, lax.rem(s, depth))
 
     for s in range(max(0, count - depth), count):
         for c in range(CAND):
@@ -209,7 +215,6 @@
             pltpu.VMEM(left.shape, jnp.bfloat16),
             pltpu.VMEM((count, total, cols), jnp.bfloat16),
             pltpu.VMEM((count, rows, cols), jnp.bfloat16),
-            pltpu.VMEM((rows, cols), jnp.float32),
             pltpu.VMEM((FLIGHT, CAND, rows, cols), jnp.bfloat16),
             pltpu.SemaphoreType.DMA((count,)),
             pltpu.SemaphoreType.DMA((FLIGHT, CAND)),
@@ -228,50 +233,32 @@
 
 def by_swaps(factors_in, factors_out, basis_in, basis_out, eigvals, live_counts):
     own = lax.axis_index("dp").astype(jnp.int32)[None]
-    slots = factors_in.shape[0]
     column = (0, 4, 8, 12)
     pair = (2, 6, 10, 14)
     core = (1, 5, 9, 13)
     other = (3, 7, 11, 15)
     tie = lax.optimization_barrier
 
-    a1, ap, a2, a3 = [swap(factors_in, m) for m in (4, 2, 8, 12)]
-    keep = (lax.iota(jnp.int32, slots) < live_counts[0])[:, None]
-    a, b = tie(tuple(
-        jnp.where(keep, x, jnp.zeros_like(x)) for x in (factors_in, factors_out)
-    ))
-    a1, ap = tie((a1, ap))
-    ap1 = swap(a1, 2)
-    ap23 = swap(jnp.stack([a2, a3]), 2)
-    a_column = jnp.stack([a, a1, a2, a3])
-    a_core = swap(a_column, 1)
-    b = after(b, a_column)
-    b1, bp, b2, b3 = [swap(b, m) for m in (4, 2, 8, 12)]
-    ap23, b1 = tie((ap23, b1))
-    a_pair = jnp.stack([ap, ap1, ap23[0], ap23[1]])
-    a_other = swap(a_pair, 1)
-    pin = project(
-        own, [(a_column, column), (a_pair, pair), (a_core, core), (a_other, other)],
-        basis_in, False,
-    )
-
-    b1, b2, b3, bp = tie((b1, b2, b3, bp, pin))[:4]
-    bp123 = swap(jnp.stack([b1, b2, b3]), 2)
-    b_column = jnp.stack([b, b1, b2, b3])
-    b_core = swap(b_column, 1)
-    sent, b_column = tie((pin, b_column))
-    g1, gp, g2, g3 = [swap(sent, m) for m in (4, 2, 8, 12)]
-    bp123, g1, g2, g3 = tie((bp123, g1, g2, g3))
-    b_pair = jnp.concatenate([bp[None], bp123])
-    b_other = swap(b_pair, 1)
+    keep = (lax.iota(jnp.int32, factors_in.shape[0]) < live_counts[0])[:, None]
+    f = jnp.stack([factors_in, jnp.where(keep, factors_out, jnp.zeros_like(factors_out))])
+    f1, fp, f2, f3 = [swap(f, m) for m in (4, 2, 8, 12)]
+    f1, fp = tie((f1, fp))
+    fp1 = swap(f1, 2)
+    f2, f3 = tie((f2, f3, fp1))[:2]
+    fp23 = swap(jnp.stack([f2, f3]), 2)
+    f_column = jnp.stack([f, f1, f2, f3])
+    f_core = swap(f_column, 1)
+    f_pair = jnp.stack([fp, fp1, fp23[0], fp23[1]])
+    f_other = swap(f_pair, 1)
+    blocks = [(f_column, column), (f_pair, pair), (f_core, core), (f_other, other)]
+    pin = project(own, blocks, basis_in, 0, False)
+
+    g1, gp, g2, g3 = [swap(pin, m) for m in (4, 2, 8, 12)]
+    left = project(own, blocks, basis_out, 1, True)
+    g1, g2, g3, gp = tie((g1, g2, g3, gp, left))[:4]
     g_column = jnp.stack([pin, g1, g2, g3])
-    gp123 = swap(jnp.stack([g1, g2, g3]), 2)
+    gp123 = swap(g_column[1:], 2)
     g_core = swap(g_column, 1)
-    b_other, g_column = tie((b_other, g_column))
-    left = project(
-        own, [(b_column, column), (b_pair, pair), (b_core, core), (b_other, other)],
-        basis_out, True,
-    )
     out = outer(own, [(g_column, column), (gp[None], pair[:1])], left, eigvals, None)
     g_other = swap(jnp.concatenate([gp[None], after(gp123, out)]), 1)
     return outer(own, [(g_core, core), (gp123, pair[1:]), (g_other, other)], left, eigvals, out)

time: 76.1 us -> 63.7 us (0.84)
  Pallas kernels: 33.1 us -> 24.9 us
  starting transfers between devices: 20.6 us -> 15.6 us
  other arithmetic: 2.17 us -> 3.01 us
    pallas_call x2, Pallas kernels: 25 us -> 16.8 us  [outer(): pl.pallas_call(functools.partial(outer_kernel, [entries for _, entries in...]
    ppermute x22 -> x15, starting transfers between devices: 20.6 us -> 15.6 us  [swap(): return lax.ppermute(x, 'dp', [(d, d ^ m) for d in range(n)])]
    another operation x6 -> x5, other arithmetic: 0.93 us -> 2.92 us  [the longest x2 1.42 us: by_swaps(): f_column = jnp.stack([f, f1, f2, f3])]
    select_n x1 -> x0, other arithmetic: 1 us -> none  [by_swaps(): jnp.where(keep, x, jnp.zeros_like(x))]
    ppermute x22 -> x15, waiting for transfers between devices: 19.1 us -> 19.2 us  [swap(): return lax.ppermute(x, 'dp', [(d, d ^ m) for d in range(n)])]
  transfers between devices with their start and end apart: 22 -> 15, of which waited for: 10 -> 6; matrix products, arithmetic and copies ran while one was open for 3% -> 1% of each run, Pallas kernels for 22% -> 16%
where the time goes in v6:
time: 63.7 us; the launch traced here: 63.5 us
  Pallas kernels  24.9 us (39%)
  waiting for transfers between devices  19.2 us (30%)
  starting transfers between devices  15.6 us (24%)
  other arithmetic  3.01 us (5%)
  between operations  0.79 us (1%)
    ppermute x15, waiting for transfers between devices, swap(): return lax.ppermute(x, 'dp', [(d, d ^ m) for d in range(n)])  19.2 us
    pallas_call x2, Pallas kernels, outer(): pl.pallas_call(functools.partial(outer_kernel, [entries for _, entries in...  16.8 us
    ppermute x15, starting transfers between devices, swap(): return lax.ppermute(x, 'dp', [(d, d ^ m) for d in range(n)])  15.6 us
    pallas_call x2, Pallas kernels, project(): pl.pallas_call(functools.partial(project_kernel, [entries for _, entries...  8.08 us
    another operation x2, other arithmetic, by_swaps(): f_column = jnp.stack([f, f1, f2, f3])  1.42 us
  transfers between devices with their start and end apart: 15, of which 6 were waited for; matrix products, arithmetic and copies ran while one was open for 1% of the time, Pallas kernels for 16%

profile of v6, /device:TPU:0, one launch (start us, length us, event | category | flops | bytes accessed | tf_op | source)
XLA Modules:
  0.0 63.5 jit_solution(2834993965584951952)
XLA Ops:
  0.7 0.9 %select_bitcast_fusion = bf16[1,4,8192]{2,1,0:T(4,128)(2,1)S(1)} fusion(bf16[4,8192]{1,0:T(4,128)(2,1)} %param.7, pred[4]{0:T(512)(128)(4,1)S(1)} %iota_compare_fusion), kind=kLoop, calls=%fused_computation.7 | loop fusion | flops 32768 | bytes 131076 | tf_op jit(solution)/shard_map/stack | solution.py:243
  1.6 0.9 %fusion = (bf16[1,2,4,8192]{3,2,1,0:T(4,128)(2,1)S(1)}, bf16[2,4,8192]{2,1,0:T(4,128)(2,1)S(1)}) fusion(bf16[1,4,8192]{2,1,0:T(4,128)(2,1)S(1)} %select_bitcast_fusion, bf16[1,4,8192]{2,1,0:T(4,128)(2,1)} %bitcast.34), kind=kLoop, calls=%fused_computation.9 | loop fusion | flops 65536 | bytes 393216 | tf_op jit(solution)/shard_map/stack | solution.py:249
  2.6 3.0 %collective-permute-start.1 = (bf16[2,4,8192]{2,1,0:T(4,128)(2,1)S(1)}, bf16[2,4,8192]{2,1,0:T(4,128)(2,1)S(1)}, u32[]{:S(2)}, u32[]{:S(2)}) collective-permute-start(bf16[2,4,8192]{2,1,0:T(4,128)(2,1)S(1)} %get-tuple-element.24), channel_id=1, source_target_pairs={{0,2},{1,3},{2,0},{3,1},{4,6},{5,7},{6,4},{7,5},{8,10},{9,11},{10,... | collective-permute-start | bytes 393224 | tf_op jit(solution)/shard_map/ppermute | solution.py:51
  5.6 1.6 %collective-permute-start = (bf16[2,4,8192]{2,1,0:T(4,128)(2,1)S(1)}, bf16[2,4,8192]{2,1,0:T(4,128)(2,1)S(1)}, u32[]{:S(2)}, u32[]{:S(2)}) collective-permute-start(bf16[2,4,8192]{2,1,0:T(4,128)(2,1)S(1)} %get-tuple-element.24), channel_id=1, source_target_pairs={{0,4},{1,5},{2,6},{3,7},{4,0},{5,1},{6,2},{7,3},{8,12},{9,13},{10,... | collective-permute-start | bytes 393224 | tf_op jit(solution)/shard_map/ppermute | solution.py:51
  7.1 2.6 %collective-permute-start.2 = (bf16[2,4,8192]{2,1,0:T(4,128)(2,1)S(1)}, bf16[2,4,8192]{2,1,0:T(4,128)(2,1)S(1)}, u32[]{:S(2)}, u32[]{:S(2)}) collective-permute-start(bf16[2,4,8192]{2,1,0:T(4,128)(2,1)S(1)} %get-tuple-element.24), channel_id=1, source_target_pairs={{0,8},{1,9},{2,10},{3,11},{4,12},{5,13},{6,14},{7,15},{8,0},{9,1},... | collective-permute-start | bytes 393224 | tf_op jit(solution)/shard_map/ppermute | solution.py:51
  9.7 0.2 collective-permute-start.3
  9.9 0.0 collective-permute-done.1
  10.0 2.0 %collective-permute-done = bf16[2,4,8192]{2,1,0:T(4,128)(2,1)S(1)} collective-permute-done((bf16[2,4,8192]{2,1,0:T(4,128)(2,1)S(1)}, bf16[2,4,8192]{2,1,0:T(4,128)(2,1)S(1)}, u32[]{:S(2)}, u32[]{:S(2)}) %collective-permute-start) | collective-permute-done | bytes 131104 | tf_op jit(solution)/shard_map/ppermute | solution.py:51
  12.0 0.3 collective-permute-start.4
  12.3 7.5 %collective-permute-done.2 = bf16[2,4,8192]{2,1,0:T(4,128)(2,1)S(1)} collective-permute-done((bf16[2,4,8192]{2,1,0:T(4,128)(2,1)S(1)}, bf16[2,4,8192]{2,1,0:T(4,128)(2,1)S(1)}, u32[]{:S(2)}, u32[]{:S(2)}) %collective-permute-start.2) | collective-permute-done | bytes 131104 | tf_op jit(solution)/shard_map/ppermute | solution.py:51
  19.8 0.0 collective-permute-done.3
  19.8 0.0 collective-permute-done.4
  19.8 0.2 pad_maximum_fusion.2
  20.0 0.6 collective-permute-start.5
  20.6 0.5 pad_maximum_fusion.refs_0_
  21.0 0.1 collective-permute-start.6
  21.1 5.3 %collective-permute-done.5 = bf16[2,2,4,8192]{3,2,1,0:T(4,128)(2,1)S(1)} collective-permute-done((bf16[2,2,4,8192]{3,2,1,0:T(4,128)(2,1)S(1)}, bf16[2,2,4,8192]{3,2,1,0:T(4,128)(2,1)S(1)}, u32[]{:S(2)}, u32[]{:S(2)}) %collective-permute-start.5) | collective-permute-done | bytes 262176 | tf_op jit(solution)/shard_map/ppermute | solution.py:51
  26.4 0.4 pad_maximum_fusion.1.refs_1_
  26.8 0.1 collective-permute-start.7
  26.9 0.0 collective-permute-done.6.refs_2_
  26.9 1.9 %collective-permute-done.7.refs_3_ = bf16[4,2,4,8192]{3,2,1,0:T(4,128)(2,1)S(1)} collective-permute-done((bf16[4,2,4,8192]{3,2,1,0:T(4,128)(2,1)S(1)}, bf16[4,2,4,8192]{3,2,1,0:T(4,128)(2,1)S(1)}, u32[]{:S(2)}, u32[]{:S(2)}) %collective-permute-start.7) | collective-permute-done | bytes 524320 | tf_op jit(solution)/shard_map/ppermute | solution.py:51
  28.8 4.0 %shard_map.64 = bf16[64,512]{1,0:T(8,128)(2,1)S(1)} custom-call(s32[1]{0:T(128)} %bitcast.own_ref, bf16[4,2,4,8192]{3,2,1,0:T(4,128)(2,1)S(1)} %pad_maximum_fusion.refs_0_, bf16[4,2,4,8192]{3,2,1,0:T(4,128)(2,1)S(1)} %pad_maximum_fusion.1.refs_1_, bf16[4,2,4,8192]{3,2,1,0:T(4,128)(2,1)S(1)} %collective-permute-done.6.refs_2_, ...), custom_call_target="tpu_custom_call" | custom-call | flops 64 | bytes 64 | tf_op jit(solution)/shard_map/pallas_call | solution.py:116
  32.7 0.6 collective-permute-start.11
  33.3 2.4 %collective-permute-start.10 = (bf16[64,512]{1,0:T(8,128)(2,1)S(1)}, bf16[64,512]{1,0:T(8,128)(2,1)S(1)}, u32[]{:S(2)}, u32[]{:S(2)}) collective-permute-start(bf16[64,512]{1,0:T(8,128)(2,1)S(1)} %shard_map.64), channel_id=1, source_target_pairs={{0,12},{1,13},{2,14},{3,15},{4,8},{5,9},{6,10},{7,11},{8,4},{9,5},... | collective-permute-start | bytes 196616 | tf_op jit(solution)/shard_map/ppermute | solution.py:51
  35.8 1.2 %collective-permute-start.9 = (bf16[64,512]{1,0:T(8,128)(2,1)S(1)}, bf16[64,512]{1,0:T(8,128)(2,1)S(1)}, u32[]{:S(2)}, u32[]{:S(2)}) collective-permute-start(bf16[64,512]{1,0:T(8,128)(2,1)S(1)} %shard_map.64), channel_id=1, source_target_pairs={{0,8},{1,9},{2,10},{3,11},{4,12},{5,13},{6,14},{7,15},{8,0},{9,1},... | collective-permute-start | bytes 196616 | tf_op jit(solution)/shard_map/ppermute | solution.py:51
  37.0 0.8 %collective-permute-start.8 = (bf16[64,512]{1,0:T(8,128)(2,1)S(1)}, bf16[64,512]{1,0:T(8,128)(2,1)S(1)}, u32[]{:S(2)}, u32[]{:S(2)}) collective-permute-start(bf16[64,512]{1,0:T(8,128)(2,1)S(1)} %shard_map.64), channel_id=1, source_target_pairs={{0,4},{1,5},{2,6},{3,7},{4,0},{5,1},{6,2},{7,3},{8,12},{9,13},{10,... | collective-permute-start | bytes 196616 | tf_op jit(solution)/shard_map/ppermute | solution.py:51
  37.7 4.1 %shard_map.65.refs_2_.refs_3_ = bf16[4,512,64]{2,1,0:T(8,128)(2,1)S(1)} custom-call(s32[1]{0:T(128)} %bitcast.own_ref, bf16[4,2,4,8192]{3,2,1,0:T(4,128)(2,1)S(1)} %pad_maximum_fusion.refs_0_, bf16[4,2,4,8192]{3,2,1,0:T(4,128)(2,1)S(1)} %pad_maximum_fusion.1.refs_1_, bf16[4,2,4,8192]{3,2,1,0:T(4,128)(2,1)S(1)} %collective-permute-done.6.refs_2_, ...), custom_call_target="tpu_custom_call" | custom-call | flops 64 | bytes 64 | tf_op jit(solution)/shard_map/pallas_call | solution.py:116
  41.9 0.0 collective-permute-done.11
  41.9 0.0 collective-permute-done.10
  41.9 1.3 %collective-permute-done.9 = bf16[64,512]{1,0:T(8,128)(2,1)S(1)} collective-permute-done((bf16[64,512]{1,0:T(8,128)(2,1)S(1)}, bf16[64,512]{1,0:T(8,128)(2,1)S(1)}, u32[]{:S(2)}, u32[]{:S(2)}) %collective-permute-start.9) | collective-permute-done | bytes 65568 | tf_op jit(solution)/shard_map/ppermute | solution.py:51
  43.2 0.0 collective-permute-done.8
  43.2 1.6 %collective-permute-start.13 = (bf16[3,64,512]{2,1,0:T(8,128)(2,1)S(1)}, bf16[3,64,512]{2,1,0:T(8,128)(2,1)S(1)}, u32[]{:S(2)}, u32[]{:S(2)}) collective-permute-start(bf16[3,64,512]{2,1,0:T(8,128)(2,1)S(1)} %pad_maximum_fusion.5), channel_id=1, source_target_pairs={{0,2},{1,3},{2,0},{3,1},{4,6},{5,7},{6,4},{7,5},{8,10},{9,11},{10,... | collective-permute-start | bytes 589832 | tf_op jit(solution)/shard_map/ppermute | solution.py:51
  44.8 0.1 collective-permute-start.12
  44.9 6.1 %shard_map.66.refs_5_ = bf16[4,512,8192]{2,1,0:T(8,128)(2,1)} custom-call(s32[1]{0:T(128)} %bitcast.own_ref, bf16[4,64,512]{2,1,0:T(8,128)(2,1)S(1)} %pad_maximum_fusion.3.refs_0_, bf16[1,64,512]{2,1,0:T(8,128)(2,1)S(1)} %bitcast.18, bf16[4,512,64]{2,1,0:T(8,128)(2,1)S(1)} %shard_map.65.refs_2_.refs_3_, bf16[512,8192]{1,0:T(8,128)(2,1)} %refs_4_.5), custom_call_target="tpu_custom_call" | custom-call | flops 167772160 | bytes 13107200 | tf_op jit(solution)/shard_map/pallas_call | solution.py:209
  51.0 0.0 collective-permute-done.13.refs_1_
  51.1 0.6 collective-permute-start.14
  51.6 0.0 collective-permute-done.12.refs_0_
  51.6 1.2 %collective-permute-done.14.refs_2_ = bf16[4,64,512]{2,1,0:T(8,128)(2,1)S(1)} collective-permute-done((bf16[4,64,512]{2,1,0:T(8,128)(2,1)S(1)}, bf16[4,64,512]{2,1,0:T(8,128)(2,1)S(1)}, u32[]{:S(2)}, u32[]{:S(2)}) %collective-permute-start.14) | collective-permute-done | bytes 262176 | tf_op jit(solution)/shard_map/ppermute | solution.py:51
  52.8 10.7 %shard_map.67 = bf16[4,512,8192]{2,1,0:T(8,128)(2,1)} custom-call(s32[1]{0:T(128)} %bitcast.own_ref, bf16[4,64,512]{2,1,0:T(8,128)(2,1)S(1)} %collective-permute-done.12.refs_0_, bf16[3,64,512]{2,1,0:T(8,128)(2,1)S(1)} %collective-permute-done.13.refs_1_, bf16[4,64,512]{2,1,0:T(8,128)(2,1)S(1)} %collective-permute-done.14.refs_2_, ...), custom_call_target="tpu_custom_call", output_to_operand_aliasing={{}: (6, {})} | custom-call | flops 369098752 | bytes 28835840 | tf_op jit(solution)/shard_map/pallas_call | solution.py:209
  (4 shorter events, 0.1 us)
Async XLA Ops:
  2.6 7.4 %collective-permute-start.1 = (bf16[2,4,8192]{2,1,0:T(4,128)(2,1)S(1)}, bf16[2,4,8192]{2,1,0:T(4,128)(2,1)S(1)}, u32[]{:S(2)}, u32[]{:S(2)}) collective-permute-start(bf16[2,4,8192]{2,1,0:T(4,128)(2,1)S(1)} %get-tuple-element.24), channel_id=1, source_target_pairs={{0,2},{1,3},{2,0},{3,1},{4,6},{5,7},{6,4},{7,5},{8,10},{9,11},{10,... | collective-permute-start | bytes 393224 | tf_op jit(solution)/shard_map/ppermute | solution.py:51
  5.6 6.4 %collective-permute-start = (bf16[2,4,8192]{2,1,0:T(4,128)(2,1)S(1)}, bf16[2,4,8192]{2,1,0:T(4,128)(2,1)S(1)}, u32[]{:S(2)}, u32[]{:S(2)}) collective-permute-start(bf16[2,4,8192]{2,1,0:T(4,128)(2,1)S(1)} %get-tuple-element.24), channel_id=1, source_target_pairs={{0,4},{1,5},{2,6},{3,7},{4,0},{5,1},{6,2},{7,3},{8,12},{9,13},{10,... | collective-permute-start | bytes 393224 | tf_op jit(solution)/shard_map/ppermute | solution.py:51
  7.1 12.6 %collective-permute-start.2 = (bf16[2,4,8192]{2,1,0:T(4,128)(2,1)S(1)}, bf16[2,4,8192]{2,1,0:T(4,128)(2,1)S(1)}, u32[]{:S(2)}, u32[]{:S(2)}) collective-permute-start(bf16[2,4,8192]{2,1,0:T(4,128)(2,1)S(1)} %get-tuple-element.24), channel_id=1, source_target_pairs={{0,8},{1,9},{2,10},{3,11},{4,12},{5,13},{6,14},{7,15},{8,0},{9,1},... | collective-permute-start | bytes 393224 | tf_op jit(solution)/shard_map/ppermute | solution.py:51
  9.7 10.1 %collective-permute-start.3 = (bf16[2,4,8192]{2,1,0:T(4,128)(2,1)S(1)}, bf16[2,4,8192]{2,1,0:T(4,128)(2,1)S(1)}, u32[]{:S(2)}, u32[]{:S(2)}) collective-permute-start(bf16[2,4,8192]{2,1,0:T(4,128)(2,1)S(1)} %get-tuple-element.24), channel_id=1, source_target_pairs={{0,12},{1,13},{2,14},{3,15},{4,8},{5,9},{6,10},{7,11},{8,4},{9,5},... | collective-permute-start | bytes 393224 | tf_op jit(solution)/shard_map/ppermute | solution.py:51
  12.0 7.8 %collective-permute-start.4 = (bf16[2,4,8192]{2,1,0:T(4,128)(2,1)S(1)}, bf16[2,4,8192]{2,1,0:T(4,128)(2,1)S(1)}, u32[]{:S(2)}, u32[]{:S(2)}) collective-permute-start(bf16[2,4,8192]{2,1,0:T(4,128)(2,1)S(1)} %collective-permute-done), channel_id=1, source_target_pairs={{0,2},{1,3},{2,0},{3,1},{4,6},{5,7},{6,4},{7,5},{8,10},{9,11},{10,... | collective-permute-start | bytes 393224 | tf_op jit(solution)/shard_map/ppermute | solution.py:51
  20.0 6.4 %collective-permute-start.5 = (bf16[2,2,4,8192]{3,2,1,0:T(4,128)(2,1)S(1)}, bf16[2,2,4,8192]{3,2,1,0:T(4,128)(2,1)S(1)}, u32[]{:S(2)}, u32[]{:S(2)}) collective-permute-start(bf16[2,2,4,8192]{3,2,1,0:T(4,128)(2,1)S(1)} %pad_maximum_fusion.2), channel_id=1, source_target_pairs={{0,2},{1,3},{2,0},{3,1},{4,6},{5,7},{6,4},{7,5},{8,10},{9,11},{10,... | collective-permute-start | bytes 786440 | tf_op jit(solution)/shard_map/ppermute | solution.py:51
  21.0 5.8 %collective-permute-start.6 = (bf16[4,2,4,8192]{3,2,1,0:T(4,128)(2,1)S(1)}, bf16[4,2,4,8192]{3,2,1,0:T(4,128)(2,1)S(1)}, u32[]{:S(2)}, u32[]{:S(2)}) collective-permute-start(bf16[4,2,4,8192]{3,2,1,0:T(4,128)(2,1)S(1)} %pad_maximum_fusion.refs_0_), channel_id=1, source_target_pairs={{0,1},{1,0},{2,3},{3,2},{4,5},{5,4},{6,7},{7,6},{8,9},{9,8},{10,11... | collective-permute-start | bytes 1572872 | tf_op jit(solution)/shard_map/ppermute | solution.py:51
  26.8 2.0 %collective-permute-start.7 = (bf16[4,2,4,8192]{3,2,1,0:T(4,128)(2,1)S(1)}, bf16[4,2,4,8192]{3,2,1,0:T(4,128)(2,1)S(1)}, u32[]{:S(2)}, u32[]{:S(2)}) collective-permute-start(bf16[4,2,4,8192]{3,2,1,0:T(4,128)(2,1)S(1)} %pad_maximum_fusion.1.refs_1_), channel_id=1, source_target_pairs={{0,1},{1,0},{2,3},{3,2},{4,5},{5,4},{6,7},{7,6},{8,9},{9,8},{10,11... | collective-permute-start | bytes 1572872 | tf_op jit(solution)/shard_map/ppermute | solution.py:51
  32.7 9.1 %collective-permute-start.11 = (bf16[64,512]{1,0:T(8,128)(2,1)S(1)}, bf16[64,512]{1,0:T(8,128)(2,1)S(1)}, u32[]{:S(2)}, u32[]{:S(2)}) collective-permute-start(bf16[64,512]{1,0:T(8,128)(2,1)S(1)} %shard_map.64), channel_id=1, source_target_pairs={{0,2},{1,3},{2,0},{3,1},{4,6},{5,7},{6,4},{7,5},{8,10},{9,11},{10,... | collective-permute-start | bytes 196616 | tf_op jit(solution)/shard_map/ppermute | solution.py:51
  33.3 8.5 %collective-permute-start.10 = (bf16[64,512]{1,0:T(8,128)(2,1)S(1)}, bf16[64,512]{1,0:T(8,128)(2,1)S(1)}, u32[]{:S(2)}, u32[]{:S(2)}) collective-permute-start(bf16[64,512]{1,0:T(8,128)(2,1)S(1)} %shard_map.64), channel_id=1, source_target_pairs={{0,12},{1,13},{2,14},{3,15},{4,8},{5,9},{6,10},{7,11},{8,4},{9,5},... | collective-permute-start | bytes 196616 | tf_op jit(solution)/shard_map/ppermute | solution.py:51
  35.8 7.4 %collective-permute-start.9 = (bf16[64,512]{1,0:T(8,128)(2,1)S(1)}, bf16[64,512]{1,0:T(8,128)(2,1)S(1)}, u32[]{:S(2)}, u32[]{:S(2)}) collective-permute-start(bf16[64,512]{1,0:T(8,128)(2,1)S(1)} %shard_map.64), channel_id=1, source_target_pairs={{0,8},{1,9},{2,10},{3,11},{4,12},{5,13},{6,14},{7,15},{8,0},{9,1},... | collective-permute-start | bytes 196616 | tf_op jit(solution)/shard_map/ppermute | solution.py:51
  37.0 6.2 %collective-permute-start.8 = (bf16[64,512]{1,0:T(8,128)(2,1)S(1)}, bf16[64,512]{1,0:T(8,128)(2,1)S(1)}, u32[]{:S(2)}, u32[]{:S(2)}) collective-permute-start(bf16[64,512]{1,0:T(8,128)(2,1)S(1)} %shard_map.64), channel_id=1, source_target_pairs={{0,4},{1,5},{2,6},{3,7},{4,0},{5,1},{6,2},{7,3},{8,12},{9,13},{10,... | collective-permute-start | bytes 196616 | tf_op jit(solution)/shard_map/ppermute | solution.py:51
  43.2 7.8 %collective-permute-start.13 = (bf16[3,64,512]{2,1,0:T(8,128)(2,1)S(1)}, bf16[3,64,512]{2,1,0:T(8,128)(2,1)S(1)}, u32[]{:S(2)}, u32[]{:S(2)}) collective-permute-start(bf16[3,64,512]{2,1,0:T(8,128)(2,1)S(1)} %pad_maximum_fusion.5), channel_id=1, source_target_pairs={{0,2},{1,3},{2,0},{3,1},{4,6},{5,7},{6,4},{7,5},{8,10},{9,11},{10,... | collective-permute-start | bytes 589832 | tf_op jit(solution)/shard_map/ppermute | solution.py:51
  44.8 6.8 %collective-permute-start.12 = (bf16[4,64,512]{2,1,0:T(8,128)(2,1)S(1)}, bf16[4,64,512]{2,1,0:T(8,128)(2,1)S(1)}, u32[]{:S(2)}, u32[]{:S(2)}) collective-permute-start(bf16[4,64,512]{2,1,0:T(8,128)(2,1)S(1)} %pad_maximum_fusion.3.refs_0_), channel_id=1, source_target_pairs={{0,1},{1,0},{2,3},{3,2},{4,5},{5,4},{6,7},{7,6},{8,9},{9,8},{10,11... | collective-permute-start | bytes 786440 | tf_op jit(solution)/shard_map/ppermute | solution.py:51
  51.1 1.7 %collective-permute-start.14 = (bf16[4,64,512]{2,1,0:T(8,128)(2,1)S(1)}, bf16[4,64,512]{2,1,0:T(8,128)(2,1)S(1)}, u32[]{:S(2)}, u32[]{:S(2)}) collective-permute-start(bf16[4,64,512]{2,1,0:T(8,128)(2,1)S(1)} %pad_maximum_fusion.4), channel_id=1, source_target_pairs={{0,1},{1,0},{2,3},{3,2},{4,5},{5,4},{6,7},{7,6},{8,9},{9,8},{10,11... | collective-permute-start | bytes 786440 | tf_op jit(solution)/shard_map/ppermute | solution.py:51

commit v7 on v6

--- a/solution.py
+++ b/solution.py
@@ -11,7 +11,8 @@
 KBLK = 1024
 RBLK = 256
 FLIGHT = 3
-VMEM = 50 << 20
+VMEM = 20 << 20
+PARTS = 4
 
 
 def general(factors_in, factors_out, basis_in, basis_out, eigvals, live_counts):
@@ -231,6 +232,32 @@
     )(*operands)
 
 
+def stage_kernel(count, *refs):
+    sources, (ready_ref, *kept), sems = refs[:count], refs[count:-1], refs[-1]
+    copies = []
+    for k, (source, keep) in enumerate(zip(sources, kept)):
+        part = source.shape[0] // PARTS
+        for p in range(PARTS):
+            rows = pl.ds(p * part, part)
+            copies.append(pltpu.make_async_copy(source.at[rows], keep.at[rows], sems.at[k, p]))
+    for copy in copies:
+        copy.start()
+    for copy in copies:
+        copy.wait()
+
+
+def stage(arrays, ready):
+    return pl.pallas_call(
+        functools.partial(stage_kernel, len(arrays)),
+        out_shape=[pltpu.VMEM(x.shape, x.dtype) for x in arrays],
+        in_specs=anywhere(len(arrays) + 1),
+        out_specs=anywhere(len(arrays)),
+        scratch_shapes=[pltpu.SemaphoreType.DMA((len(arrays), PARTS))],
+        compiler_params=pltpu.CompilerParams(vmem_limit_bytes=1 << 20),
+        cost_estimate=pl.CostEstimate(flops=1, bytes_accessed=1, transcendentals=0),
+    )(*[pltpu.with_memory_space_constraint(x, pltpu.HBM) for x in arrays], ready)
+
+
 def by_swaps(factors_in, factors_out, basis_in, basis_out, eigvals, live_counts):
     own = lax.axis_index("dp").astype(jnp.int32)[None]
     column = (0, 4, 8, 12)
@@ -244,10 +271,13 @@
     f1, fp, f2, f3 = [swap(f, m) for m in (4, 2, 8, 12)]
     f1, fp = tie((f1, fp))
     fp1 = swap(f1, 2)
-    f2, f3 = tie((f2, f3, fp1))[:2]
+    basis_in, basis_out = stage([basis_in, basis_out], f1)
+    f2, f3 = tie((f2, f3, fp1, basis_in, basis_out))[:2]
     fp23 = swap(jnp.stack([f2, f3]), 2)
     f_column = jnp.stack([f, f1, f2, f3])
     f_core = swap(f_column, 1)
+    eigvals, = stage([eigvals], f_column)
+    fp23, eigvals = tie((fp23, eigvals))
     f_pair = jnp.stack([fp, fp1, fp23[0], fp23[1]])
     f_other = swap(f_pair, 1)
     blocks = [(f_column, column), (f_pair, pair), (f_core, core), (f_other, other)]

time: 63.7 us -> 74.6 us (1.17)
  local copies, waits for them, and re-layouts: 0 us -> 16.6 us
  waiting for transfers between devices: 19.2 us -> 4.77 us
  Pallas kernels: 24.9 us -> 31.7 us
  starting transfers between devices: 15.6 us -> 17.3 us
    unnamed x0 -> x14, local copies, waits for them, and re-layouts: none -> 16.6 us
    ppermute x15, waiting for transfers between devices: 19.2 us -> 4.77 us  [swap(): return lax.ppermute(x, 'dp', [(d, d ^ m) for d in range(n)])]
    pallas_call x0 -> x2, Pallas kernels: none -> 9.43 us  [stage(): pl.pallas_call(functools.partial(stage_kernel, len(arrays)), out_shape=[p...]
    pallas_call x2, Pallas kernels: 8.08 us -> 5.93 us  [project(): pl.pallas_call(functools.partial(project_kernel, [entries for _, entries...]
    ppermute x15, starting transfers between devices: 15.6 us -> 17.3 us  [swap(): return lax.ppermute(x, 'dp', [(d, d ^ m) for d in range(n)])]
  transfers between devices with their start and end apart: 15 -> 15, of which waited for: 6 -> 3; matrix products, arithmetic and copies ran while one was open for 1% -> 1% of each run, Pallas kernels for 16% -> 24%
where the time goes in v7:
time: 74.6 us; the launch traced here: 74.3 us
  Pallas kernels  31.7 us (42%)
  starting transfers between devices  17.3 us (23%)
  local copies, waits for them, and re-layouts  16.6 us (22%)
  waiting for transfers between devices  4.77 us (6%)
  other arithmetic  3.01 us (4%)
  between operations  0.86 us (1%)
    ppermute x15, starting transfers between devices, swap(): return lax.ppermute(x, 'dp', [(d, d ^ m) for d in range(n)])  17.3 us
    unnamed x14, local copies, waits for them, and re-layouts  16.6 us
    pallas_call x2, Pallas kernels, outer(): pl.pallas_call(functools.partial(outer_kernel, [entries for _, entries in...  16.4 us
    pallas_call x2, Pallas kernels, stage(): pl.pallas_call(functools.partial(stage_kernel, len(arrays)), out_shape=[p...  9.43 us
    pallas_call x2, Pallas kernels, project(): pl.pallas_call(functools.partial(project_kernel, [entries for _, entries...  5.93 us
    ppermute x15, waiting for transfers between devices, swap(): return lax.ppermute(x, 'dp', [(d, d ^ m) for d in range(n)])  4.77 us
  transfers between devices with their start and end apart: 15, of which 3 were waited for; matrix products, arithmetic and copies ran while one was open for 1% of the time, Pallas kernels for 24%

profile of v7, /device:TPU:0, one launch (start us, length us, event | category | flops | bytes accessed | tf_op | source)
XLA Modules:
  0.0 74.3 jit_solution(17116687007612787777)
XLA Ops:
  0.7 0.9 %select_bitcast_fusion = bf16[1,4,8192]{2,1,0:T(4,128)(2,1)S(1)} fusion(bf16[4,8192]{1,0:T(4,128)(2,1)} %param.7, pred[4]{0:T(512)(128)(4,1)S(1)} %iota_compare_fusion), kind=kLoop, calls=%fused_computation.7 | loop fusion | flops 32768 | bytes 131076 | tf_op jit(solution)/shard_map/stack | solution.py:270
  1.6 0.9 %fusion = (bf16[1,2,4,8192]{3,2,1,0:T(4,128)(2,1)S(1)}, bf16[2,4,8192]{2,1,0:T(4,128)(2,1)S(1)}) fusion(bf16[1,4,8192]{2,1,0:T(4,128)(2,1)S(1)} %select_bitcast_fusion, bf16[1,4,8192]{2,1,0:T(4,128)(2,1)} %bitcast.36), kind=kLoop, calls=%fused_computation.9 | loop fusion | flops 65536 | bytes 393216 | tf_op jit(solution)/shard_map/stack | solution.py:277
  2.6 3.0 %collective-permute-start.1 = (bf16[2,4,8192]{2,1,0:T(4,128)(2,1)S(1)}, bf16[2,4,8192]{2,1,0:T(4,128)(2,1)S(1)}, u32[]{:S(2)}, u32[]{:S(2)}) collective-permute-start(bf16[2,4,8192]{2,1,0:T(4,128)(2,1)S(1)} %get-tuple-element.32), channel_id=1, source_target_pairs={{0,2},{1,3},{2,0},{3,1},{4,6},{5,7},{6,4},{7,5},{8,10},{9,11},{10,... | collective-permute-start | bytes 393224 | tf_op jit(solution)/shard_map/ppermute | solution.py:52
  5.6 1.6 %collective-permute-start = (bf16[2,4,8192]{2,1,0:T(4,128)(2,1)S(1)}, bf16[2,4,8192]{2,1,0:T(4,128)(2,1)S(1)}, u32[]{:S(2)}, u32[]{:S(2)}) collective-permute-start(bf16[2,4,8192]{2,1,0:T(4,128)(2,1)S(1)} %get-tuple-element.32), channel_id=1, source_target_pairs={{0,4},{1,5},{2,6},{3,7},{4,0},{5,1},{6,2},{7,3},{8,12},{9,13},{10,... | collective-permute-start | bytes 393224 | tf_op jit(solution)/shard_map/ppermute | solution.py:52
  7.1 2.6 %collective-permute-start.2 = (bf16[2,4,8192]{2,1,0:T(4,128)(2,1)S(1)}, bf16[2,4,8192]{2,1,0:T(4,128)(2,1)S(1)}, u32[]{:S(2)}, u32[]{:S(2)}) collective-permute-start(bf16[2,4,8192]{2,1,0:T(4,128)(2,1)S(1)} %get-tuple-element.32), channel_id=1, source_target_pairs={{0,8},{1,9},{2,10},{3,11},{4,12},{5,13},{6,14},{7,15},{8,0},{9,1},... | collective-permute-start | bytes 393224 | tf_op jit(solution)/shard_map/ppermute | solution.py:52
  9.7 0.2 collective-permute-start.3
  9.9 0.0 collective-permute-done.1
  10.0 2.0 %collective-permute-done.refs_2_ = bf16[2,4,8192]{2,1,0:T(4,128)(2,1)S(1)} collective-permute-done((bf16[2,4,8192]{2,1,0:T(4,128)(2,1)S(1)}, bf16[2,4,8192]{2,1,0:T(4,128)(2,1)S(1)}, u32[]{:S(2)}, u32[]{:S(2)}) %collective-permute-start) | collective-permute-done | bytes 131104 | tf_op jit(solution)/shard_map/ppermute | solution.py:52
  12.0 0.3 collective-permute-start.4
  12.3 5.9 %shard_map.64 = (bf16[8192,512]{1,0:T(8,128)(2,1)S(1)}, bf16[8192,512]{1,0:T(8,128)(2,1)S(1)}) custom-call(bf16[8192,512]{1,0:T(8,128)(2,1)} %refs_0_.2, bf16[8192,512]{1,0:T(8,128)(2,1)} %refs_1_.1, bf16[2,4,8192]{2,1,0:T(4,128)(2,1)S(1)} %collective-permute-done.refs_2_), custom_call_target="tpu_custom_call" | custom-call | flops 1 | bytes 1 | tf_op jit(solution)/shard_map/pallas_call | solution.py:250
  18.2 3.3 %copy-done.1 = bf16[8192,512]{1,0:T(8,128)(2,1)} copy-done((bf16[8192,512]{1,0:T(8,128)(2,1)}, bf16[8192,512]{1,0:T(8,128)(2,1)S(1)}, u32[]{:S(2)}) %copy-start.1) | copy-done | bytes 8388632
  21.5 3.4 %copy-done.3 = bf16[8192,512]{1,0:T(8,128)(2,1)} copy-done((bf16[8192,512]{1,0:T(8,128)(2,1)}, bf16[8192,512]{1,0:T(8,128)(2,1)S(1)}, u32[]{:S(2)}) %copy-start.3) | copy-done | bytes 8388632
  24.9 0.0 collective-permute-done.2
  24.9 0.0 collective-permute-done.3
  24.9 0.0 collective-permute-done.4
  24.9 0.2 pad_maximum_fusion.2
  25.1 1.8 %collective-permute-start.5 = (bf16[2,2,4,8192]{3,2,1,0:T(4,128)(2,1)S(1)}, bf16[2,2,4,8192]{3,2,1,0:T(4,128)(2,1)S(1)}, u32[]{:S(2)}, u32[]{:S(2)}) collective-permute-start(bf16[2,2,4,8192]{3,2,1,0:T(4,128)(2,1)S(1)} %pad_maximum_fusion.2), channel_id=1, source_target_pairs={{0,2},{1,3},{2,0},{3,1},{4,6},{5,7},{6,4},{7,5},{8,10},{9,11},{10,... | collective-permute-start | bytes 786440 | tf_op jit(solution)/shard_map/ppermute | solution.py:52
  26.9 0.5 pad_maximum_fusion.refs_1_.refs_0_
  27.4 0.1 collective-permute-start.6
  27.4 3.5 %shard_map.65.refs_3_.refs_4_ = bf16[512,8192]{1,0:T(8,128)(2,1)S(1)} custom-call(bf16[512,8192]{1,0:T(8,128)(2,1)} %refs_0_.3, bf16[4,2,4,8192]{3,2,1,0:T(4,128)(2,1)S(1)} %pad_maximum_fusion.refs_1_.refs_0_), custom_call_target="tpu_custom_call" | custom-call | flops 1 | bytes 1 | tf_op jit(solution)/shard_map/pallas_call | solution.py:250
  31.0 3.2 %copy-done = bf16[512,8192]{1,0:T(8,128)(2,1)} copy-done((bf16[512,8192]{1,0:T(8,128)(2,1)}, bf16[512,8192]{1,0:T(8,128)(2,1)S(1)}, u32[]{:S(2)}) %copy-start) | copy-done | bytes 8388632
  34.2 0.0 collective-permute-done.5
  34.2 0.4 pad_maximum_fusion.1.refs_1_
  34.6 0.6 collective-permute-start.7
  35.1 0.0 collective-permute-done.6.refs_2_
  35.1 1.5 %collective-permute-done.7.refs_3_ = bf16[4,2,4,8192]{3,2,1,0:T(4,128)(2,1)S(1)} collective-permute-done((bf16[4,2,4,8192]{3,2,1,0:T(4,128)(2,1)S(1)}, bf16[4,2,4,8192]{3,2,1,0:T(4,128)(2,1)S(1)}, u32[]{:S(2)}, u32[]{:S(2)}) %collective-permute-start.7) | collective-permute-done | bytes 524320 | tf_op jit(solution)/shard_map/ppermute | solution.py:52
  36.7 3.4 %copy-done.4 = bf16[8192,512]{1,0:T(8,128)(2,1)S(1)} copy-done((bf16[8192,512]{1,0:T(8,128)(2,1)S(1)}, bf16[8192,512]{1,0:T(8,128)(2,1)}, u32[]{:S(2)}) %copy-start.4) | copy-done | bytes 8388632
  40.0 2.9 %shard_map.66 = bf16[64,512]{1,0:T(8,128)(2,1)S(1)} custom-call(s32[1]{0:T(128)} %bitcast.own_ref, bf16[4,2,4,8192]{3,2,1,0:T(4,128)(2,1)S(1)} %pad_maximum_fusion.refs_1_.refs_0_, bf16[4,2,4,8192]{3,2,1,0:T(4,128)(2,1)S(1)} %pad_maximum_fusion.1.refs_1_, bf16[4,2,4,8192]{3,2,1,0:T(4,128)(2,1)S(1)} %collective-permute-done.6.refs_2_, ...), custom_call_target="tpu_custom_call" | custom-call | flops 64 | bytes 64 | tf_op jit(solution)/shard_map/pallas_call | solution.py:117
  42.9 0.0 slice-start.1
  42.9 0.4 collective-permute-start.11
  43.3 3.9 %collective-permute-start.10 = (bf16[64,512]{1,0:T(8,128)(2,1)S(1)}, bf16[64,512]{1,0:T(8,128)(2,1)S(1)}, u32[]{:S(2)}, u32[]{:S(2)}) collective-permute-start(bf16[64,512]{1,0:T(8,128)(2,1)S(1)} %shard_map.66), channel_id=1, source_target_pairs={{0,12},{1,13},{2,14},{3,15},{4,8},{5,9},{6,10},{7,11},{8,4},{9,5},... | collective-permute-start | bytes 196616 | tf_op jit(solution)/shard_map/ppermute | solution.py:52
  47.3 0.0 collective-permute-start.9
  47.3 0.6 collective-permute-start.8
  47.8 3.4 %copy-done.2 = bf16[8192,512]{1,0:T(8,128)(2,1)S(1)} copy-done((bf16[8192,512]{1,0:T(8,128)(2,1)S(1)}, bf16[8192,512]{1,0:T(8,128)(2,1)}, u32[]{:S(2)}) %copy-start.2) | copy-done | bytes 8388632
  51.2 3.0 %shard_map.67.refs_2_.refs_3_ = bf16[4,512,64]{2,1,0:T(8,128)(2,1)S(1)} custom-call(s32[1]{0:T(128)} %bitcast.own_ref, bf16[4,2,4,8192]{3,2,1,0:T(4,128)(2,1)S(1)} %pad_maximum_fusion.refs_1_.refs_0_, bf16[4,2,4,8192]{3,2,1,0:T(4,128)(2,1)S(1)} %pad_maximum_fusion.1.refs_1_, bf16[4,2,4,8192]{3,2,1,0:T(4,128)(2,1)S(1)} %collective-permute-done.6.refs_2_, ...), custom_call_target="tpu_custom_call" | custom-call | flops 64 | bytes 64 | tf_op jit(solution)/shard_map/pallas_call | solution.py:117
  54.3 0.0 collective-permute-done.11
  54.3 0.0 collective-permute-done.10
  54.3 0.0 collective-permute-done.9
  54.3 0.0 collective-permute-done.8
  54.3 1.7 %collective-permute-start.13 = (bf16[3,64,512]{2,1,0:T(8,128)(2,1)S(1)}, bf16[3,64,512]{2,1,0:T(8,128)(2,1)S(1)}, u32[]{:S(2)}, u32[]{:S(2)}) collective-permute-start(bf16[3,64,512]{2,1,0:T(8,128)(2,1)S(1)} %pad_maximum_fusion.5), channel_id=1, source_target_pairs={{0,2},{1,3},{2,0},{3,1},{4,6},{5,7},{6,4},{7,5},{8,10},{9,11},{10,... | collective-permute-start | bytes 589832 | tf_op jit(solution)/shard_map/ppermute | solution.py:52
  56.1 0.1 collective-permute-start.12
  56.1 0.0 slice-done
  56.2 5.6 %shard_map.68.refs_5_ = bf16[4,512,8192]{2,1,0:T(8,128)(2,1)} custom-call(s32[1]{0:T(128)} %bitcast.own_ref, bf16[4,64,512]{2,1,0:T(8,128)(2,1)S(1)} %pad_maximum_fusion.3.refs_0_, bf16[1,64,512]{2,1,0:T(8,128)(2,1)S(1)} %bitcast.21, bf16[4,512,64]{2,1,0:T(8,128)(2,1)S(1)} %shard_map.67.refs_2_.refs_3_, bf16[512,8192]{1,0:T(8,128)(2,1)S(1)} %bitcast.19), custom_call_target="tpu_custom_call" | custom-call | flops 167772160 | bytes 13107200 | tf_op jit(solution)/shard_map/pallas_call | solution.py:210
  61.8 0.0 collective-permute-done.13.refs_1_
  61.8 0.5 collective-permute-start.14
  62.3 0.0 collective-permute-done.12.refs_0_
  62.3 1.2 %collective-permute-done.14.refs_2_ = bf16[4,64,512]{2,1,0:T(8,128)(2,1)S(1)} collective-permute-done((bf16[4,64,512]{2,1,0:T(8,128)(2,1)S(1)}, bf16[4,64,512]{2,1,0:T(8,128)(2,1)S(1)}, u32[]{:S(2)}, u32[]{:S(2)}) %collective-permute-start.14) | collective-permute-done | bytes 262176 | tf_op jit(solution)/shard_map/ppermute | solution.py:52
  63.5 10.8 %shard_map.69 = bf16[4,512,8192]{2,1,0:T(8,128)(2,1)} custom-call(s32[1]{0:T(128)} %bitcast.own_ref, bf16[4,64,512]{2,1,0:T(8,128)(2,1)S(1)} %collective-permute-done.12.refs_0_, bf16[3,64,512]{2,1,0:T(8,128)(2,1)S(1)} %collective-permute-done.13.refs_1_, bf16[4,64,512]{2,1,0:T(8,128)(2,1)S(1)} %collective-permute-done.14.refs_2_, ...), custom_call_target="tpu_custom_call", output_to_operand_aliasing={{}: (6, {})} | custom-call | flops 369098752 | bytes 28835840 | tf_op jit(solution)/shard_map/pallas_call | solution.py:210
  (12 shorter events, 0.1 us)
Async XLA Ops:
  2.6 7.4 %collective-permute-start.1 = (bf16[2,4,8192]{2,1,0:T(4,128)(2,1)S(1)}, bf16[2,4,8192]{2,1,0:T(4,128)(2,1)S(1)}, u32[]{:S(2)}, u32[]{:S(2)}) collective-permute-start(bf16[2,4,8192]{2,1,0:T(4,128)(2,1)S(1)} %get-tuple-element.32), channel_id=1, source_target_pairs={{0,2},{1,3},{2,0},{3,1},{4,6},{5,7},{6,4},{7,5},{8,10},{9,11},{10,... | collective-permute-start | bytes 393224 | tf_op jit(solution)/shard_map/ppermute | solution.py:52
  5.6 6.4 %collective-permute-start = (bf16[2,4,8192]{2,1,0:T(4,128)(2,1)S(1)}, bf16[2,4,8192]{2,1,0:T(4,128)(2,1)S(1)}, u32[]{:S(2)}, u32[]{:S(2)}) collective-permute-start(bf16[2,4,8192]{2,1,0:T(4,128)(2,1)S(1)} %get-tuple-element.32), channel_id=1, source_target_pairs={{0,4},{1,5},{2,6},{3,7},{4,0},{5,1},{6,2},{7,3},{8,12},{9,13},{10,... | collective-permute-start | bytes 393224 | tf_op jit(solution)/shard_map/ppermute | solution.py:52
  7.1 17.8 %collective-permute-start.2 = (bf16[2,4,8192]{2,1,0:T(4,128)(2,1)S(1)}, bf16[2,4,8192]{2,1,0:T(4,128)(2,1)S(1)}, u32[]{:S(2)}, u32[]{:S(2)}) collective-permute-start(bf16[2,4,8192]{2,1,0:T(4,128)(2,1)S(1)} %get-tuple-element.32), channel_id=1, source_target_pairs={{0,8},{1,9},{2,10},{3,11},{4,12},{5,13},{6,14},{7,15},{8,0},{9,1},... | collective-permute-start | bytes 393224 | tf_op jit(solution)/shard_map/ppermute | solution.py:52
  9.7 15.2 %collective-permute-start.3 = (bf16[2,4,8192]{2,1,0:T(4,128)(2,1)S(1)}, bf16[2,4,8192]{2,1,0:T(4,128)(2,1)S(1)}, u32[]{:S(2)}, u32[]{:S(2)}) collective-permute-start(bf16[2,4,8192]{2,1,0:T(4,128)(2,1)S(1)} %get-tuple-element.32), channel_id=1, source_target_pairs={{0,12},{1,13},{2,14},{3,15},{4,8},{5,9},{6,10},{7,11},{8,4},{9,5},... | collective-permute-start | bytes 393224 | tf_op jit(solution)/shard_map/ppermute | solution.py:52
  12.0 12.9 %collective-permute-start.4 = (bf16[2,4,8192]{2,1,0:T(4,128)(2,1)S(1)}, bf16[2,4,8192]{2,1,0:T(4,128)(2,1)S(1)}, u32[]{:S(2)}, u32[]{:S(2)}) collective-permute-start(bf16[2,4,8192]{2,1,0:T(4,128)(2,1)S(1)} %collective-permute-done.refs_2_), channel_id=1, source_target_pairs={{0,2},{1,3},{2,0},{3,1},{4,6},{5,7},{6,4},{7,5},{8,10},{9,11},{10,... | collective-permute-start | bytes 393224 | tf_op jit(solution)/shard_map/ppermute | solution.py:52
  18.2 3.3 %copy-start.1 = (bf16[8192,512]{1,0:T(8,128)(2,1)}, bf16[8192,512]{1,0:T(8,128)(2,1)S(1)}, u32[]{:S(2)}) copy-start(bf16[8192,512]{1,0:T(8,128)(2,1)S(1)} %get-tuple-element.20.refs_4_) | copy-start | bytes 25165828
  21.5 3.4 %copy-start.3 = (bf16[8192,512]{1,0:T(8,128)(2,1)}, bf16[8192,512]{1,0:T(8,128)(2,1)S(1)}, u32[]{:S(2)}) copy-start(bf16[8192,512]{1,0:T(8,128)(2,1)S(1)} %get-tuple-element.19.refs_4_) | copy-start | bytes 25165828
  25.1 9.1 %collective-permute-start.5 = (bf16[2,2,4,8192]{3,2,1,0:T(4,128)(2,1)S(1)}, bf16[2,2,4,8192]{3,2,1,0:T(4,128)(2,1)S(1)}, u32[]{:S(2)}, u32[]{:S(2)}) collective-permute-start(bf16[2,2,4,8192]{3,2,1,0:T(4,128)(2,1)S(1)} %pad_maximum_fusion.2), channel_id=1, source_target_pairs={{0,2},{1,3},{2,0},{3,1},{4,6},{5,7},{6,4},{7,5},{8,10},{9,11},{10,... | collective-permute-start | bytes 786440 | tf_op jit(solution)/shard_map/ppermute | solution.py:52
  27.4 7.8 %collective-permute-start.6 = (bf16[4,2,4,8192]{3,2,1,0:T(4,128)(2,1)S(1)}, bf16[4,2,4,8192]{3,2,1,0:T(4,128)(2,1)S(1)}, u32[]{:S(2)}, u32[]{:S(2)}) collective-permute-start(bf16[4,2,4,8192]{3,2,1,0:T(4,128)(2,1)S(1)} %pad_maximum_fusion.refs_1_.refs_0_), channel_id=1, source_target_pairs={{0,1},{1,0},{2,3},{3,2},{4,5},{5,4},{6,7},{7,6},{8,9},{9,8},{10,11... | collective-permute-start | bytes 1572872 | tf_op jit(solution)/shard_map/ppermute | solution.py:52
  30.9 3.2 %copy-start = (bf16[512,8192]{1,0:T(8,128)(2,1)}, bf16[512,8192]{1,0:T(8,128)(2,1)S(1)}, u32[]{:S(2)}) copy-start(bf16[512,8192]{1,0:T(8,128)(2,1)S(1)} %shard_map.65.refs_3_.refs_4_) | copy-start | bytes 25165828
  34.6 2.1 %collective-permute-start.7 = (bf16[4,2,4,8192]{3,2,1,0:T(4,128)(2,1)S(1)}, bf16[4,2,4,8192]{3,2,1,0:T(4,128)(2,1)S(1)}, u32[]{:S(2)}, u32[]{:S(2)}) collective-permute-start(bf16[4,2,4,8192]{3,2,1,0:T(4,128)(2,1)S(1)} %pad_maximum_fusion.1.refs_1_), channel_id=1, source_target_pairs={{0,1},{1,0},{2,3},{3,2},{4,5},{5,4},{6,7},{7,6},{8,9},{9,8},{10,11... | collective-permute-start | bytes 1572872 | tf_op jit(solution)/shard_map/ppermute | solution.py:52
  36.7 3.4 %copy-start.4 = (bf16[8192,512]{1,0:T(8,128)(2,1)S(1)}, bf16[8192,512]{1,0:T(8,128)(2,1)}, u32[]{:S(2)}) copy-start(bf16[8192,512]{1,0:T(8,128)(2,1)} %copy-done.3) | copy-start | bytes 25165828
  40.0 16.1 %slice-start = ((s8[8388608]{0:T(1024)(128)(4,1)}), s8[4194304]{0:T(1024)(128)(4,1)S(1)}, s32[]{:S(2)}) async-start(s8[8388608]{0:T(1024)(128)(4,1)} %bitcast.18), calls=%async_computation | async-start | bytes 8388608
  42.9 13.2 %slice-start.1 = ((s8[8388608]{0:T(1024)(128)(4,1)}), s8[4194304]{0:T(1024)(128)(4,1)S(1)}, s32[]{:S(2)}) async-start(s8[8388608]{0:T(1024)(128)(4,1)} %bitcast.18), calls=%async_computation.1 | async-start | bytes 8388608
  42.9 11.3 %collective-permute-start.11 = (bf16[64,512]{1,0:T(8,128)(2,1)S(1)}, bf16[64,512]{1,0:T(8,128)(2,1)S(1)}, u32[]{:S(2)}, u32[]{:S(2)}) collective-permute-start(bf16[64,512]{1,0:T(8,128)(2,1)S(1)} %shard_map.66), channel_id=1, source_target_pairs={{0,2},{1,3},{2,0},{3,1},{4,6},{5,7},{6,4},{7,5},{8,10},{9,11},{10,... | collective-permute-start | bytes 196616 | tf_op jit(solution)/shard_map/ppermute | solution.py:52
  43.3 11.0 %collective-permute-start.10 = (bf16[64,512]{1,0:T(8,128)(2,1)S(1)}, bf16[64,512]{1,0:T(8,128)(2,1)S(1)}, u32[]{:S(2)}, u32[]{:S(2)}) collective-permute-start(bf16[64,512]{1,0:T(8,128)(2,1)S(1)} %shard_map.66), channel_id=1, source_target_pairs={{0,12},{1,13},{2,14},{3,15},{4,8},{5,9},{6,10},{7,11},{8,4},{9,5},... | collective-permute-start | bytes 196616 | tf_op jit(solution)/shard_map/ppermute | solution.py:52
  47.3 7.0 %collective-permute-start.9 = (bf16[64,512]{1,0:T(8,128)(2,1)S(1)}, bf16[64,512]{1,0:T(8,128)(2,1)S(1)}, u32[]{:S(2)}, u32[]{:S(2)}) collective-permute-start(bf16[64,512]{1,0:T(8,128)(2,1)S(1)} %shard_map.66), channel_id=1, source_target_pairs={{0,8},{1,9},{2,10},{3,11},{4,12},{5,13},{6,14},{7,15},{8,0},{9,1},... | collective-permute-start | bytes 196616 | tf_op jit(solution)/shard_map/ppermute | solution.py:52
  47.3 7.0 %collective-permute-start.8 = (bf16[64,512]{1,0:T(8,128)(2,1)S(1)}, bf16[64,512]{1,0:T(8,128)(2,1)S(1)}, u32[]{:S(2)}, u32[]{:S(2)}) collective-permute-start(bf16[64,512]{1,0:T(8,128)(2,1)S(1)} %shard_map.66), channel_id=1, source_target_pairs={{0,4},{1,5},{2,6},{3,7},{4,0},{5,1},{6,2},{7,3},{8,12},{9,13},{10,... | collective-permute-start | bytes 196616 | tf_op jit(solution)/shard_map/ppermute | solution.py:52
  47.8 3.4 %copy-start.2 = (bf16[8192,512]{1,0:T(8,128)(2,1)S(1)}, bf16[8192,512]{1,0:T(8,128)(2,1)}, u32[]{:S(2)}) copy-start(bf16[8192,512]{1,0:T(8,128)(2,1)} %copy-done.1) | copy-start | bytes 25165828
  54.3 7.4 %collective-permute-start.13 = (bf16[3,64,512]{2,1,0:T(8,128)(2,1)S(1)}, bf16[3,64,512]{2,1,0:T(8,128)(2,1)S(1)}, u32[]{:S(2)}, u32[]{:S(2)}) collective-permute-start(bf16[3,64,512]{2,1,0:T(8,128)(2,1)S(1)} %pad_maximum_fusion.5), channel_id=1, source_target_pairs={{0,2},{1,3},{2,0},{3,1},{4,6},{5,7},{6,4},{7,5},{8,10},{9,11},{10,... | collective-permute-start | bytes 589832 | tf_op jit(solution)/shard_map/ppermute | solution.py:52
  56.1 6.3 %collective-permute-start.12 = (bf16[4,64,512]{2,1,0:T(8,128)(2,1)S(1)}, bf16[4,64,512]{2,1,0:T(8,128)(2,1)S(1)}, u32[]{:S(2)}, u32[]{:S(2)}) collective-permute-start(bf16[4,64,512]{2,1,0:T(8,128)(2,1)S(1)} %pad_maximum_fusion.3.refs_0_), channel_id=1, source_target_pairs={{0,1},{1,0},{2,3},{3,2},{4,5},{5,4},{6,7},{7,6},{8,9},{9,8},{10,11... | collective-permute-start | bytes 786440 | tf_op jit(solution)/shard_map/ppermute | solution.py:52
  61.8 1.7 %collective-permute-start.14 = (bf16[4,64,512]{2,1,0:T(8,128)(2,1)S(1)}, bf16[4,64,512]{2,1,0:T(8,128)(2,1)S(1)}, u32[]{:S(2)}, u32[]{:S(2)}) collective-permute-start(bf16[4,64,512]{2,1,0:T(8,128)(2,1)S(1)} %pad_maximum_fusion.4), channel_id=1, source_target_pairs={{0,1},{1,0},{2,3},{3,2},{4,5},{5,4},{6,7},{7,6},{8,9},{9,8},{10,11... | collective-permute-start | bytes 786440 | tf_op jit(solution)/shard_map/ppermute | solution.py:52

commit v8 on v7

--- a/solution.py
+++ b/solution.py
@@ -11,7 +11,8 @@
 KBLK = 1024
 RBLK = 256
 FLIGHT = 3
-VMEM = 20 << 20
+PROJECT_VMEM = 14 << 20
+OUTER_VMEM = 50 << 20
 PARTS = 4
 
 
@@ -127,7 +128,7 @@
             pltpu.SemaphoreType.DMA((chunks,)),
             pltpu.SemaphoreType.DMA((len(blocks),)),
         ],
-        compiler_params=pltpu.CompilerParams(vmem_limit_bytes=VMEM),
+        compiler_params=pltpu.CompilerParams(vmem_limit_bytes=PROJECT_VMEM),
         cost_estimate=pl.CostEstimate(flops=total, bytes_accessed=total, transcendentals=0),
     )(own, *[x for x, _ in blocks], basis)
 
@@ -223,7 +224,7 @@
             pltpu.SemaphoreType.DMA(()),
         ],
         input_output_aliases=aliases,
-        compiler_params=pltpu.CompilerParams(vmem_limit_bytes=VMEM),
+        compiler_params=pltpu.CompilerParams(vmem_limit_bytes=OUTER_VMEM),
         cost_estimate=pl.CostEstimate(
             flops=2 * total * rows * share,
             bytes_accessed=2 * rows * share * (CAND + 1),
@@ -266,32 +267,36 @@
     other = (3, 7, 11, 15)
     tie = lax.optimization_barrier
 
-    keep = (lax.iota(jnp.int32, factors_in.shape[0]) < live_counts[0])[:, None]
-    f = jnp.stack([factors_in, jnp.where(keep, factors_out, jnp.zeros_like(factors_out))])
+    shape = (2,) + factors_in.shape
+    plane, slot = [lax.broadcasted_iota(jnp.int32, shape, k) for k in (0, 1)]
+    keep = (plane == 0) | (slot < live_counts[0])
+    f = jnp.where(keep, jnp.stack([factors_in, factors_out]), jnp.zeros((), factors_in.dtype))
     f1, fp, f2, f3 = [swap(f, m) for m in (4, 2, 8, 12)]
     f1, fp = tie((f1, fp))
     fp1 = swap(f1, 2)
     basis_in, basis_out = stage([basis_in, basis_out], f1)
-    f2, f3 = tie((f2, f3, fp1, basis_in, basis_out))[:2]
-    fp23 = swap(jnp.stack([f2, f3]), 2)
+    f2, f3, near = tie((f2, f3, fp1, basis_in, basis_out))[:3]
+    near = jnp.stack([fp, near])
+    far = swap(jnp.stack([f2, f3]), 2)
     f_column = jnp.stack([f, f1, f2, f3])
     f_core = swap(f_column, 1)
-    eigvals, = stage([eigvals], f_column)
-    fp23, eigvals = tie((fp23, eigvals))
-    f_pair = jnp.stack([fp, fp1, fp23[0], fp23[1]])
-    f_other = swap(f_pair, 1)
-    blocks = [(f_column, column), (f_pair, pair), (f_core, core), (f_other, other)]
+    near_core = swap(near, 1)
+    far_core = swap(far, 1)
+    blocks = [
+        (f_column, column), (near, pair[:2]), (f_core, core), (near_core, other[:2]),
+        (far, pair[2:]), (far_core, other[2:]),
+    ]
     pin = project(own, blocks, basis_in, 0, False)
 
-    g1, gp, g2, g3 = [swap(pin, m) for m in (4, 2, 8, 12)]
+    g1, g2, g3 = [swap(pin, m) for m in (4, 8, 12)]
     left = project(own, blocks, basis_out, 1, True)
-    g1, g2, g3, gp = tie((g1, g2, g3, gp, left))[:4]
+    g1, g2, g3 = tie((g1, g2, g3, left))[:3]
     g_column = jnp.stack([pin, g1, g2, g3])
-    gp123 = swap(g_column[1:], 2)
+    g_pair = swap(g_column, 2)
     g_core = swap(g_column, 1)
-    out = outer(own, [(g_column, column), (gp[None], pair[:1])], left, eigvals, None)
-    g_other = swap(jnp.concatenate([gp[None], after(gp123, out)]), 1)
-    return outer(own, [(g_core, core), (gp123, pair[1:]), (g_other, other)], left, eigvals, out)
+    out = outer(own, [(g_column, column)], left, eigvals, None)
+    g_other = swap(after(g_pair, out), 1)
+    return outer(own, [(g_core, core), (g_pair, pair), (g_other, other)], left, eigvals, out)
 
 
 def solution(mesh):

time: 74.6 us -> 70.6 us (0.946)
  local copies, waits for them, and re-layouts: 16.6 us -> 10.6 us
  waiting for transfers between devices: 4.77 us -> 9.13 us
  Pallas kernels: 31.7 us -> 29.3 us
    unnamed x14 -> x8, local copies, waits for them, and re-layouts: 16.6 us -> 10.6 us
    ppermute x15, waiting for transfers between devices: 4.77 us -> 9.13 us  [swap(): return lax.ppermute(x, 'dp', [(d, d ^ m) for d in range(n)])]
    pallas_call x2 -> x1, Pallas kernels: 9.43 us -> 5.93 us  [stage(): pl.pallas_call(functools.partial(stage_kernel, len(arrays)), out_shape=[p...]
    select_n x0 -> x2, other arithmetic: none -> 1.97 us  [by_swaps(): jnp.where(keep, jnp.stack([factors_in, factors_out]), jnp.zeros((), facto...]
    another operation x3 -> x2, other arithmetic: 1.5 us -> 0.37 us  [the longest x1 0.18 us: by_swaps(): far = swap(jnp.stack([f2, f3]), 2)]
    another operation x2 -> x1, other arithmetic: 1.42 us -> 0.47 us  [by_swaps(): f_column = jnp.stack([f, f1, f2, f3])]
  transfers between devices with their start and end apart: 15 -> 15, of which waited for: 3 -> 7; matrix products, arithmetic and copies ran while one was open for 1% -> 2% of each run, Pallas kernels for 24% -> 21%
where the time goes in v8:
time: 70.6 us; the launch traced here: 70.4 us
  Pallas kernels  29.3 us (42%)
  starting transfers between devices  17.8 us (25%)
  local copies, waits for them, and re-layouts  10.6 us (15%)
  waiting for transfers between devices  9.13 us (13%)
  other arithmetic  2.86 us (4%)
  between operations  0.77 us (1%)
    ppermute x15, starting transfers between devices, swap(): return lax.ppermute(x, 'dp', [(d, d ^ m) for d in range(n)])  17.8 us
    pallas_call x2, Pallas kernels, outer(): pl.pallas_call(functools.partial(outer_kernel, [entries for _, entries in...  16.8 us
    unnamed x8, local copies, waits for them, and re-layouts  10.6 us
    ppermute x15, waiting for transfers between devices, swap(): return lax.ppermute(x, 'dp', [(d, d ^ m) for d in range(n)])  9.13 us
    pallas_call x2, Pallas kernels, project(): pl.pallas_call(functools.partial(project_kernel, [entries for _, entries...  6.58 us
    pallas_call x1, Pallas kernels, stage(): pl.pallas_call(functools.partial(stage_kernel, len(arrays)), out_shape=[p...  5.93 us
    select_n x2, other arithmetic, by_swaps(): jnp.where(keep, jnp.stack([factors_in, factors_out]), jnp.zeros((), facto...  1.97 us
  transfers between devices with their start and end apart: 15, of which 7 were waited for; matrix products, arithmetic and copies ran while one was open for 2% of the time, Pallas kernels for 21%

profile of v8, /device:TPU:0, one launch (start us, length us, event | category | flops | bytes accessed | tf_op | source)
XLA Modules:
  0.0 70.4 jit_solution(3899612718479124781)
XLA Ops:
  0.7 1.0 %or_select_fusion = bf16[2,4,8192]{2,1,0:T(4,128)(2,1)S(1)} fusion(bf16[1,4,8192]{2,1,0:T(4,128)(2,1)} %bitcast.22, bf16[1,4,8192]{2,1,0:T(4,128)(2,1)} %bitcast.24, pred[4]{0:T(512)(128)(4,1)S(1)} %iota_compare_fusion, pred[2]{0:T(512)(128)(4,1)S(1)} %iota_compare_fusion.1), kind=kLoop, calls=%fused_computation.4 | loop fusion | flops 393216 | bytes 262150 | tf_op jit(solution)/shard_map/jit(_where)/select_n | solution.py:273
  1.7 3.0 %collective-permute-start.1 = (bf16[2,4,8192]{2,1,0:T(4,128)(2,1)S(1)}, bf16[2,4,8192]{2,1,0:T(4,128)(2,1)S(1)}, u32[]{:S(2)}, u32[]{:S(2)}) collective-permute-start(bf16[2,4,8192]{2,1,0:T(4,128)(2,1)S(1)} %or_select_fusion), channel_id=1, source_target_pairs={{0,2},{1,3},{2,0},{3,1},{4,6},{5,7},{6,4},{7,5},{8,10},{9,11},{10,... | collective-permute-start | bytes 393224 | tf_op jit(solution)/shard_map/ppermute | solution.py:53
  4.7 1.6 %collective-permute-start = (bf16[2,4,8192]{2,1,0:T(4,128)(2,1)S(1)}, bf16[2,4,8192]{2,1,0:T(4,128)(2,1)S(1)}, u32[]{:S(2)}, u32[]{:S(2)}) collective-permute-start(bf16[2,4,8192]{2,1,0:T(4,128)(2,1)S(1)} %or_select_fusion), channel_id=1, source_target_pairs={{0,4},{1,5},{2,6},{3,7},{4,0},{5,1},{6,2},{7,3},{8,12},{9,13},{10,... | collective-permute-start | bytes 393224 | tf_op jit(solution)/shard_map/ppermute | solution.py:53
  6.2 2.5 %collective-permute-start.3 = (bf16[2,4,8192]{2,1,0:T(4,128)(2,1)S(1)}, bf16[2,4,8192]{2,1,0:T(4,128)(2,1)S(1)}, u32[]{:S(2)}, u32[]{:S(2)}) collective-permute-start(bf16[2,4,8192]{2,1,0:T(4,128)(2,1)S(1)} %or_select_fusion), channel_id=1, source_target_pairs={{0,12},{1,13},{2,14},{3,15},{4,8},{5,9},{6,10},{7,11},{8,4},{9,5},... | collective-permute-start | bytes 393224 | tf_op jit(solution)/shard_map/ppermute | solution.py:53
  8.7 0.1 collective-permute-start.2
  8.8 0.0 collective-permute-done.1
  8.8 0.8 %collective-permute-done.refs_2_ = bf16[2,4,8192]{2,1,0:T(4,128)(2,1)S(1)} collective-permute-done((bf16[2,4,8192]{2,1,0:T(4,128)(2,1)S(1)}, bf16[2,4,8192]{2,1,0:T(4,128)(2,1)S(1)}, u32[]{:S(2)}, u32[]{:S(2)}) %collective-permute-start) | collective-permute-done | bytes 131104 | tf_op jit(solution)/shard_map/ppermute | solution.py:53
  9.6 0.4 collective-permute-start.4
  10.0 1.0 %or_select_fusion.1 = bf16[1,2,4,8192]{3,2,1,0:T(4,128)(2,1)S(1)} fusion(bf16[1,1,4,8192]{3,2,1,0:T(4,128)(2,1)} %bitcast.23, bf16[1,1,4,8192]{3,2,1,0:T(4,128)(2,1)} %bitcast.25, pred[4]{0:T(512)(128)(4,1)S(1)} %iota_compare_fusion, pred[2]{0:T(512)(128)(4,1)S(1)} %iota_compare_fusion.1), kind=kLoop, calls=%fused_computation.5 | loop fusion | flops 393216 | bytes 262150 | tf_op jit(solution)/shard_map/jit(_where)/select_n | solution.py:273
  11.0 5.9 %shard_map.64 = (bf16[8192,512]{1,0:T(8,128)(2,1)S(1)}, bf16[8192,512]{1,0:T(8,128)(2,1)S(1)}) custom-call(bf16[8192,512]{1,0:T(8,128)(2,1)} %refs_0_.1, bf16[8192,512]{1,0:T(8,128)(2,1)} %refs_1_.1, bf16[2,4,8192]{2,1,0:T(4,128)(2,1)S(1)} %collective-permute-done.refs_2_), custom_call_target="tpu_custom_call" | custom-call | flops 1 | bytes 1 | tf_op jit(solution)/shard_map/pallas_call | solution.py:251
  16.9 0.0 copy-start
  16.9 3.2 %copy-done = bf16[8192,512]{1,0:T(8,128)(2,1)} copy-done((bf16[8192,512]{1,0:T(8,128)(2,1)}, bf16[8192,512]{1,0:T(8,128)(2,1)S(1)}, u32[]{:S(2)}) %copy-start) | copy-done | bytes 8388632
  20.2 0.0 copy-start.2
  20.2 3.4 %copy-done.2 = bf16[8192,512]{1,0:T(8,128)(2,1)} copy-done((bf16[8192,512]{1,0:T(8,128)(2,1)}, bf16[8192,512]{1,0:T(8,128)(2,1)S(1)}, u32[]{:S(2)}) %copy-start.2) | copy-done | bytes 8388632
  23.6 0.0 collective-permute-done.3
  23.6 0.0 collective-permute-done.2
  23.6 0.0 collective-permute-done.4
  23.6 0.2 pad_maximum_fusion.2
  23.8 1.7 %collective-permute-start.7 = (bf16[2,2,4,8192]{3,2,1,0:T(4,128)(2,1)S(1)}, bf16[2,2,4,8192]{3,2,1,0:T(4,128)(2,1)S(1)}, u32[]{:S(2)}, u32[]{:S(2)}) collective-permute-start(bf16[2,2,4,8192]{3,2,1,0:T(4,128)(2,1)S(1)} %pad_maximum_fusion.2), channel_id=1, source_target_pairs={{0,2},{1,3},{2,0},{3,1},{4,6},{5,7},{6,4},{7,5},{8,10},{9,11},{10,... | collective-permute-start | bytes 786440 | tf_op jit(solution)/shard_map/ppermute | solution.py:53
  25.5 0.5 pad_maximum_fusion.refs_0_
  26.0 0.1 collective-permute-start.5
  26.0 0.2 pad_maximum_fusion.1.refs_1_
  26.2 0.6 collective-permute-start.6
  26.8 3.9 %collective-permute-done.7.refs_4_ = bf16[2,2,4,8192]{3,2,1,0:T(4,128)(2,1)S(1)} collective-permute-done((bf16[2,2,4,8192]{3,2,1,0:T(4,128)(2,1)S(1)}, bf16[2,2,4,8192]{3,2,1,0:T(4,128)(2,1)S(1)}, u32[]{:S(2)}, u32[]{:S(2)}) %collective-permute-start.7) | collective-permute-done | bytes 262176 | tf_op jit(solution)/shard_map/ppermute | solution.py:53
  30.7 0.0 collective-permute-start.8
  30.7 0.0 copy-start.1
  30.7 0.0 collective-permute-done.6.refs_3_
  30.7 1.5 %collective-permute-done.8.refs_5_ = bf16[2,2,4,8192]{3,2,1,0:T(4,128)(2,1)S(1)} collective-permute-done((bf16[2,2,4,8192]{3,2,1,0:T(4,128)(2,1)S(1)}, bf16[2,2,4,8192]{3,2,1,0:T(4,128)(2,1)S(1)}, u32[]{:S(2)}, u32[]{:S(2)}) %collective-permute-start.8) | collective-permute-done | bytes 262176 | tf_op jit(solution)/shard_map/ppermute | solution.py:53
  32.3 0.0 collective-permute-done.5.refs_2_
  32.3 0.0 copy-start.3
  32.3 4.0 %copy-done.3 = bf16[8192,512]{1,0:T(8,128)(2,1)S(1)} copy-done((bf16[8192,512]{1,0:T(8,128)(2,1)S(1)}, bf16[8192,512]{1,0:T(8,128)(2,1)}, u32[]{:S(2)}) %copy-start.3) | copy-done | bytes 8388632
  36.3 3.2 %shard_map.65 = bf16[64,512]{1,0:T(8,128)(2,1)S(1)} custom-call(s32[1]{0:T(128)} %bitcast.own_ref, bf16[4,2,4,8192]{3,2,1,0:T(4,128)(2,1)S(1)} %pad_maximum_fusion.refs_0_, bf16[2,2,4,8192]{3,2,1,0:T(4,128)(2,1)S(1)} %pad_maximum_fusion.1.refs_1_, bf16[4,2,4,8192]{3,2,1,0:T(4,128)(2,1)S(1)} %collective-permute-done.5.refs_2_, ...), custom_call_target="tpu_custom_call" | custom-call | flops 64 | bytes 64 | tf_op jit(solution)/shard_map/pallas_call | solution.py:118
  39.5 5.2 %collective-permute-start.11 = (bf16[64,512]{1,0:T(8,128)(2,1)S(1)}, bf16[64,512]{1,0:T(8,128)(2,1)S(1)}, u32[]{:S(2)}, u32[]{:S(2)}) collective-permute-start(bf16[64,512]{1,0:T(8,128)(2,1)S(1)} %shard_map.65), channel_id=1, source_target_pairs={{0,12},{1,13},{2,14},{3,15},{4,8},{5,9},{6,10},{7,11},{8,4},{9,5},... | collective-permute-start | bytes 196616 | tf_op jit(solution)/shard_map/ppermute | solution.py:53
  44.6 0.0 collective-permute-start.10
  44.6 0.6 collective-permute-start.9
  45.3 0.0 copy-done.1
  45.3 3.4 %shard_map.66.refs_1_.refs_3_ = bf16[4,512,64]{2,1,0:T(8,128)(2,1)S(1)} custom-call(s32[1]{0:T(128)} %bitcast.own_ref, bf16[4,2,4,8192]{3,2,1,0:T(4,128)(2,1)S(1)} %pad_maximum_fusion.refs_0_, bf16[2,2,4,8192]{3,2,1,0:T(4,128)(2,1)S(1)} %pad_maximum_fusion.1.refs_1_, bf16[4,2,4,8192]{3,2,1,0:T(4,128)(2,1)S(1)} %collective-permute-done.5.refs_2_, ...), custom_call_target="tpu_custom_call" | custom-call | flops 64 | bytes 64 | tf_op jit(solution)/shard_map/pallas_call | solution.py:118
  48.7 0.0 collective-permute-done.11
  48.7 1.2 %collective-permute-done.10 = bf16[64,512]{1,0:T(8,128)(2,1)S(1)} collective-permute-done((bf16[64,512]{1,0:T(8,128)(2,1)S(1)}, bf16[64,512]{1,0:T(8,128)(2,1)S(1)}, u32[]{:S(2)}, u32[]{:S(2)}) %collective-permute-start.10) | collective-permute-done | bytes 65568 | tf_op jit(solution)/shard_map/ppermute | solution.py:53
  49.9 0.4 collective-permute-done.9
  50.3 1.6 %collective-permute-start.13 = (bf16[4,64,512]{2,1,0:T(8,128)(2,1)S(1)}, bf16[4,64,512]{2,1,0:T(8,128)(2,1)S(1)}, u32[]{:S(2)}, u32[]{:S(2)}) collective-permute-start(bf16[4,64,512]{2,1,0:T(8,128)(2,1)S(1)} %pad_maximum_fusion.3.refs_0_), channel_id=1, source_target_pairs={{0,2},{1,3},{2,0},{3,1},{4,6},{5,7},{6,4},{7,5},{8,10},{9,11},{10,... | collective-permute-start | bytes 786440 | tf_op jit(solution)/shard_map/ppermute | solution.py:53
  51.9 0.0 collective-permute-start.12
  51.9 5.4 %shard_map.67.refs_5_ = bf16[4,512,8192]{2,1,0:T(8,128)(2,1)} custom-call(s32[1]{0:T(128)} %bitcast.own_ref, bf16[4,64,512]{2,1,0:T(8,128)(2,1)S(1)} %pad_maximum_fusion.3.refs_0_, bf16[4,512,64]{2,1,0:T(8,128)(2,1)S(1)} %shard_map.66.refs_1_.refs_3_, bf16[512,8192]{1,0:T(8,128)(2,1)} %refs_4_.1), custom_call_target="tpu_custom_call" | custom-call | flops 134217728 | bytes 10485760 | tf_op jit(solution)/shard_map/pallas_call | solution.py:211
  57.2 0.1 collective-permute-done.13.refs_1_
  57.3 0.5 collective-permute-start.14
  57.8 0.0 collective-permute-done.12.refs_0_
  57.8 1.2 %collective-permute-done.14.refs_2_ = bf16[4,64,512]{2,1,0:T(8,128)(2,1)S(1)} collective-permute-done((bf16[4,64,512]{2,1,0:T(8,128)(2,1)S(1)}, bf16[4,64,512]{2,1,0:T(8,128)(2,1)S(1)}, u32[]{:S(2)}, u32[]{:S(2)}) %collective-permute-start.14) | collective-permute-done | bytes 262176 | tf_op jit(solution)/shard_map/ppermute | solution.py:53
  59.0 11.4 %shard_map.68 = bf16[4,512,8192]{2,1,0:T(8,128)(2,1)} custom-call(s32[1]{0:T(128)} %bitcast.own_ref, bf16[4,64,512]{2,1,0:T(8,128)(2,1)S(1)} %collective-permute-done.12.refs_0_, bf16[4,64,512]{2,1,0:T(8,128)(2,1)S(1)} %collective-permute-done.13.refs_1_, bf16[4,64,512]{2,1,0:T(8,128)(2,1)S(1)} %collective-permute-done.14.refs_2_, ...), custom_call_target="tpu_custom_call", output_to_operand_aliasing={{}: (6, {})} | custom-call | flops 402653184 | bytes 31457280 | tf_op jit(solution)/shard_map/pallas_call | solution.py:211
  (3 shorter events, 0.0 us)
Async XLA Ops:
  1.7 7.2 %collective-permute-start.1 = (bf16[2,4,8192]{2,1,0:T(4,128)(2,1)S(1)}, bf16[2,4,8192]{2,1,0:T(4,128)(2,1)S(1)}, u32[]{:S(2)}, u32[]{:S(2)}) collective-permute-start(bf16[2,4,8192]{2,1,0:T(4,128)(2,1)S(1)} %or_select_fusion), channel_id=1, source_target_pairs={{0,2},{1,3},{2,0},{3,1},{4,6},{5,7},{6,4},{7,5},{8,10},{9,11},{10,... | collective-permute-start | bytes 393224 | tf_op jit(solution)/shard_map/ppermute | solution.py:53
  4.7 5.0 %collective-permute-start = (bf16[2,4,8192]{2,1,0:T(4,128)(2,1)S(1)}, bf16[2,4,8192]{2,1,0:T(4,128)(2,1)S(1)}, u32[]{:S(2)}, u32[]{:S(2)}) collective-permute-start(bf16[2,4,8192]{2,1,0:T(4,128)(2,1)S(1)} %or_select_fusion), channel_id=1, source_target_pairs={{0,4},{1,5},{2,6},{3,7},{4,0},{5,1},{6,2},{7,3},{8,12},{9,13},{10,... | collective-permute-start | bytes 393224 | tf_op jit(solution)/shard_map/ppermute | solution.py:53
  6.2 17.3 %collective-permute-start.3 = (bf16[2,4,8192]{2,1,0:T(4,128)(2,1)S(1)}, bf16[2,4,8192]{2,1,0:T(4,128)(2,1)S(1)}, u32[]{:S(2)}, u32[]{:S(2)}) collective-permute-start(bf16[2,4,8192]{2,1,0:T(4,128)(2,1)S(1)} %or_select_fusion), channel_id=1, source_target_pairs={{0,12},{1,13},{2,14},{3,15},{4,8},{5,9},{6,10},{7,11},{8,4},{9,5},... | collective-permute-start | bytes 393224 | tf_op jit(solution)/shard_map/ppermute | solution.py:53
  8.7 14.8 %collective-permute-start.2 = (bf16[2,4,8192]{2,1,0:T(4,128)(2,1)S(1)}, bf16[2,4,8192]{2,1,0:T(4,128)(2,1)S(1)}, u32[]{:S(2)}, u32[]{:S(2)}) collective-permute-start(bf16[2,4,8192]{2,1,0:T(4,128)(2,1)S(1)} %or_select_fusion), channel_id=1, source_target_pairs={{0,8},{1,9},{2,10},{3,11},{4,12},{5,13},{6,14},{7,15},{8,0},{9,1},... | collective-permute-start | bytes 393224 | tf_op jit(solution)/shard_map/ppermute | solution.py:53
  9.6 13.9 %collective-permute-start.4 = (bf16[2,4,8192]{2,1,0:T(4,128)(2,1)S(1)}, bf16[2,4,8192]{2,1,0:T(4,128)(2,1)S(1)}, u32[]{:S(2)}, u32[]{:S(2)}) collective-permute-start(bf16[2,4,8192]{2,1,0:T(4,128)(2,1)S(1)} %collective-permute-done.refs_2_), channel_id=1, source_target_pairs={{0,2},{1,3},{2,0},{3,1},{4,6},{5,7},{6,4},{7,5},{8,10},{9,11},{10,... | collective-permute-start | bytes 393224 | tf_op jit(solution)/shard_map/ppermute | solution.py:53
  16.9 3.2 %copy-start = (bf16[8192,512]{1,0:T(8,128)(2,1)}, bf16[8192,512]{1,0:T(8,128)(2,1)S(1)}, u32[]{:S(2)}) copy-start(bf16[8192,512]{1,0:T(8,128)(2,1)S(1)} %get-tuple-element.18.refs_6_) | copy-start | bytes 25165828
  20.2 3.4 %copy-start.2 = (bf16[8192,512]{1,0:T(8,128)(2,1)}, bf16[8192,512]{1,0:T(8,128)(2,1)S(1)}, u32[]{:S(2)}) copy-start(bf16[8192,512]{1,0:T(8,128)(2,1)S(1)} %get-tuple-element.17.refs_6_) | copy-start | bytes 25165828
  23.8 7.0 %collective-permute-start.7 = (bf16[2,2,4,8192]{3,2,1,0:T(4,128)(2,1)S(1)}, bf16[2,2,4,8192]{3,2,1,0:T(4,128)(2,1)S(1)}, u32[]{:S(2)}, u32[]{:S(2)}) collective-permute-start(bf16[2,2,4,8192]{3,2,1,0:T(4,128)(2,1)S(1)} %pad_maximum_fusion.2), channel_id=1, source_target_pairs={{0,2},{1,3},{2,0},{3,1},{4,6},{5,7},{6,4},{7,5},{8,10},{9,11},{10,... | collective-permute-start | bytes 786440 | tf_op jit(solution)/shard_map/ppermute | solution.py:53
  26.0 6.3 %collective-permute-start.5 = (bf16[4,2,4,8192]{3,2,1,0:T(4,128)(2,1)S(1)}, bf16[4,2,4,8192]{3,2,1,0:T(4,128)(2,1)S(1)}, u32[]{:S(2)}, u32[]{:S(2)}) collective-permute-start(bf16[4,2,4,8192]{3,2,1,0:T(4,128)(2,1)S(1)} %pad_maximum_fusion.refs_0_), channel_id=1, source_target_pairs={{0,1},{1,0},{2,3},{3,2},{4,5},{5,4},{6,7},{7,6},{8,9},{9,8},{10,11... | collective-permute-start | bytes 1572872 | tf_op jit(solution)/shard_map/ppermute | solution.py:53
  26.2 4.5 %collective-permute-start.6 = (bf16[2,2,4,8192]{3,2,1,0:T(4,128)(2,1)S(1)}, bf16[2,2,4,8192]{3,2,1,0:T(4,128)(2,1)S(1)}, u32[]{:S(2)}, u32[]{:S(2)}) collective-permute-start(bf16[2,2,4,8192]{3,2,1,0:T(4,128)(2,1)S(1)} %pad_maximum_fusion.1.refs_1_), channel_id=1, source_target_pairs={{0,1},{1,0},{2,3},{3,2},{4,5},{5,4},{6,7},{7,6},{8,9},{9,8},{10,11... | collective-permute-start | bytes 786440 | tf_op jit(solution)/shard_map/ppermute | solution.py:53
  30.7 1.5 %collective-permute-start.8 = (bf16[2,2,4,8192]{3,2,1,0:T(4,128)(2,1)S(1)}, bf16[2,2,4,8192]{3,2,1,0:T(4,128)(2,1)S(1)}, u32[]{:S(2)}, u32[]{:S(2)}) collective-permute-start(bf16[2,2,4,8192]{3,2,1,0:T(4,128)(2,1)S(1)} %collective-permute-done.7.refs_4_), channel_id=1, source_target_pairs={{0,1},{1,0},{2,3},{3,2},{4,5},{5,4},{6,7},{7,6},{8,9},{9,8},{10,11... | collective-permute-start | bytes 786440 | tf_op jit(solution)/shard_map/ppermute | solution.py:53
  30.7 14.6 %copy-start.1 = (bf16[8192,512]{1,0:T(8,128)(2,1)S(1)}, bf16[8192,512]{1,0:T(8,128)(2,1)}, u32[]{:S(2)}) copy-start(bf16[8192,512]{1,0:T(8,128)(2,1)} %copy-done) | copy-start | bytes 25165828
  32.3 4.0 %copy-start.3 = (bf16[8192,512]{1,0:T(8,128)(2,1)S(1)}, bf16[8192,512]{1,0:T(8,128)(2,1)}, u32[]{:S(2)}) copy-start(bf16[8192,512]{1,0:T(8,128)(2,1)} %copy-done.2) | copy-start | bytes 25165828
  39.5 9.2 %collective-permute-start.11 = (bf16[64,512]{1,0:T(8,128)(2,1)S(1)}, bf16[64,512]{1,0:T(8,128)(2,1)S(1)}, u32[]{:S(2)}, u32[]{:S(2)}) collective-permute-start(bf16[64,512]{1,0:T(8,128)(2,1)S(1)} %shard_map.65), channel_id=1, source_target_pairs={{0,12},{1,13},{2,14},{3,15},{4,8},{5,9},{6,10},{7,11},{8,4},{9,5},... | collective-permute-start | bytes 196616 | tf_op jit(solution)/shard_map/ppermute | solution.py:53
  44.6 5.3 %collective-permute-start.10 = (bf16[64,512]{1,0:T(8,128)(2,1)S(1)}, bf16[64,512]{1,0:T(8,128)(2,1)S(1)}, u32[]{:S(2)}, u32[]{:S(2)}) collective-permute-start(bf16[64,512]{1,0:T(8,128)(2,1)S(1)} %shard_map.65), channel_id=1, source_target_pairs={{0,8},{1,9},{2,10},{3,11},{4,12},{5,13},{6,14},{7,15},{8,0},{9,1},... | collective-permute-start | bytes 196616 | tf_op jit(solution)/shard_map/ppermute | solution.py:53
  44.6 5.6 %collective-permute-start.9 = (bf16[64,512]{1,0:T(8,128)(2,1)S(1)}, bf16[64,512]{1,0:T(8,128)(2,1)S(1)}, u32[]{:S(2)}, u32[]{:S(2)}) collective-permute-start(bf16[64,512]{1,0:T(8,128)(2,1)S(1)} %shard_map.65), channel_id=1, source_target_pairs={{0,4},{1,5},{2,6},{3,7},{4,0},{5,1},{6,2},{7,3},{8,12},{9,13},{10,... | collective-permute-start | bytes 196616 | tf_op jit(solution)/shard_map/ppermute | solution.py:53
  50.3 7.0 %collective-permute-start.13 = (bf16[4,64,512]{2,1,0:T(8,128)(2,1)S(1)}, bf16[4,64,512]{2,1,0:T(8,128)(2,1)S(1)}, u32[]{:S(2)}, u32[]{:S(2)}) collective-permute-start(bf16[4,64,512]{2,1,0:T(8,128)(2,1)S(1)} %pad_maximum_fusion.3.refs_0_), channel_id=1, source_target_pairs={{0,2},{1,3},{2,0},{3,1},{4,6},{5,7},{6,4},{7,5},{8,10},{9,11},{10,... | collective-permute-start | bytes 786440 | tf_op jit(solution)/shard_map/ppermute | solution.py:53
  51.9 6.0 %collective-permute-start.12 = (bf16[4,64,512]{2,1,0:T(8,128)(2,1)S(1)}, bf16[4,64,512]{2,1,0:T(8,128)(2,1)S(1)}, u32[]{:S(2)}, u32[]{:S(2)}) collective-permute-start(bf16[4,64,512]{2,1,0:T(8,128)(2,1)S(1)} %pad_maximum_fusion.3.refs_0_), channel_id=1, source_target_pairs={{0,1},{1,0},{2,3},{3,2},{4,5},{5,4},{6,7},{7,6},{8,9},{9,8},{10,11... | collective-permute-start | bytes 786440 | tf_op jit(solution)/shard_map/ppermute | solution.py:53
  57.3 1.7 %collective-permute-start.14 = (bf16[4,64,512]{2,1,0:T(8,128)(2,1)S(1)}, bf16[4,64,512]{2,1,0:T(8,128)(2,1)S(1)}, u32[]{:S(2)}, u32[]{:S(2)}) collective-permute-start(bf16[4,64,512]{2,1,0:T(8,128)(2,1)S(1)} %collective-permute-done.13.refs_1_), channel_id=1, source_target_pairs={{0,1},{1,0},{2,3},{3,2},{4,5},{5,4},{6,7},{7,6},{8,9},{9,8},{10,11... | collective-permute-start | bytes 786440 | tf_op jit(solution)/shard_map/ppermute | solution.py:53

commit v9 on v6

--- a/solution.py
+++ b/solution.py
@@ -239,29 +239,35 @@
     other = (3, 7, 11, 15)
     tie = lax.optimization_barrier
 
-    keep = (lax.iota(jnp.int32, factors_in.shape[0]) < live_counts[0])[:, None]
-    f = jnp.stack([factors_in, jnp.where(keep, factors_out, jnp.zeros_like(factors_out))])
+    shape = (2,) + factors_in.shape
+    plane, slot = [lax.broadcasted_iota(jnp.int32, shape, k) for k in (0, 1)]
+    keep = (plane == 0) | (slot < live_counts[0])
+    f = jnp.where(keep, jnp.stack([factors_in, factors_out]), jnp.zeros((), factors_in.dtype))
     f1, fp, f2, f3 = [swap(f, m) for m in (4, 2, 8, 12)]
     f1, fp = tie((f1, fp))
     fp1 = swap(f1, 2)
-    f2, f3 = tie((f2, f3, fp1))[:2]
-    fp23 = swap(jnp.stack([f2, f3]), 2)
+    f2, f3, near = tie((f2, f3, fp1))
+    near = jnp.stack([fp, near])
+    far = swap(jnp.stack([f2, f3]), 2)
     f_column = jnp.stack([f, f1, f2, f3])
     f_core = swap(f_column, 1)
-    f_pair = jnp.stack([fp, fp1, fp23[0], fp23[1]])
-    f_other = swap(f_pair, 1)
-    blocks = [(f_column, column), (f_pair, pair), (f_core, core), (f_other, other)]
+    near_core = swap(near, 1)
+    far_core = swap(far, 1)
+    blocks = [
+        (f_column, column), (near, pair[:2]), (f_core, core), (near_core, other[:2]),
+        (far, pair[2:]), (far_core, other[2:]),
+    ]
     pin = project(own, blocks, basis_in, 0, False)
 
-    g1, gp, g2, g3 = [swap(pin, m) for m in (4, 2, 8, 12)]
+    g1, g2, g3 = [swap(pin, m) for m in (4, 8, 12)]
     left = project(own, blocks, basis_out, 1, True)
-    g1, g2, g3, gp = tie((g1, g2, g3, gp, left))[:4]
+    g1, g2, g3 = tie((g1, g2, g3, left))[:3]
     g_column = jnp.stack([pin, g1, g2, g3])
-    gp123 = swap(g_column[1:], 2)
+    g_pair = swap(g_column, 2)
     g_core = swap(g_column, 1)
-    out = outer(own, [(g_column, column), (gp[None], pair[:1])], left, eigvals, None)
-    g_other = swap(jnp.concatenate([gp[None], after(gp123, out)]), 1)
-    return outer(own, [(g_core, core), (gp123, pair[1:]), (g_other, other)], left, eigvals, out)
+    out = outer(own, [(g_column, column)], left, eigvals, None)
+    g_other = swap(after(g_pair, out), 1)
+    return outer(own, [(g_core, core), (g_pair, pair), (g_other, other)], left, eigvals, out)
 
 
 def solution(mesh):

time: 63.7 us -> 63.7 us (level)
  starting transfers between devices: 15.6 us -> 13.8 us
  waiting for transfers between devices: 19.2 us -> 20.9 us
    select_n x0 -> x2, other arithmetic: none -> 1.97 us  [by_swaps(): jnp.where(keep, jnp.stack([factors_in, factors_out]), jnp.zeros((), facto...]
    ppermute x15, starting transfers between devices: 15.6 us -> 13.8 us  [swap(): return lax.ppermute(x, 'dp', [(d, d ^ m) for d in range(n)])]
    ppermute x15, waiting for transfers between devices: 19.2 us -> 20.9 us  [swap(): return lax.ppermute(x, 'dp', [(d, d ^ m) for d in range(n)])]
    another operation x3 -> x2, other arithmetic: 1.5 us -> 0.37 us  [the longest x1 0.18 us: by_swaps(): near = jnp.stack([fp, near])]
    another operation x2 -> x1, other arithmetic: 1.42 us -> 0.47 us  [by_swaps(): f_column = jnp.stack([f, f1, f2, f3])]
  transfers between devices with their start and end apart: 15 -> 15, of which waited for: 6 -> 8; matrix products, arithmetic and copies ran while one was open for 1% -> 3% of each run, Pallas kernels for 16% -> 15%
where the time goes in v9:
time: 63.7 us; the launch traced here: 63.4 us
  Pallas kernels  25.1 us (39%)
  waiting for transfers between devices  20.9 us (33%)
  starting transfers between devices  13.8 us (22%)
  other arithmetic  2.85 us (4%)
  between operations  0.74 us (1%)
    ppermute x15, waiting for transfers between devices, swap(): return lax.ppermute(x, 'dp', [(d, d ^ m) for d in range(n)])  20.9 us
    pallas_call x2, Pallas kernels, outer(): pl.pallas_call(functools.partial(outer_kernel, [entries for _, entries in...  16.8 us
    ppermute x15, starting transfers between devices, swap(): return lax.ppermute(x, 'dp', [(d, d ^ m) for d in range(n)])  13.8 us
    pallas_call x2, Pallas kernels, project(): pl.pallas_call(functools.partial(project_kernel, [entries for _, entries...  8.34 us
    select_n x2, other arithmetic, by_swaps(): jnp.where(keep, jnp.stack([factors_in, factors_out]), jnp.zeros((), facto...  1.97 us
  transfers between devices with their start and end apart: 15, of which 8 were waited for; matrix products, arithmetic and copies ran while one was open for 3% of the time, Pallas kernels for 15%

profile of v9, /device:TPU:0, one launch (start us, length us, event | category | flops | bytes accessed | tf_op | source)
XLA Modules:
  0.0 63.4 jit_solution(4461809250372534933)
XLA Ops:
  0.7 1.0 %or_select_fusion = bf16[2,4,8192]{2,1,0:T(4,128)(2,1)S(1)} fusion(bf16[1,4,8192]{2,1,0:T(4,128)(2,1)} %bitcast.21, bf16[1,4,8192]{2,1,0:T(4,128)(2,1)} %bitcast.23, pred[4]{0:T(512)(128)(4,1)S(1)} %iota_compare_fusion, pred[2]{0:T(512)(128)(4,1)S(1)} %iota_compare_fusion.1), kind=kLoop, calls=%fused_computation.4 | loop fusion | flops 393216 | bytes 262150 | tf_op jit(solution)/shard_map/jit(_where)/select_n | solution.py:245
  1.7 3.0 %collective-permute-start.1 = (bf16[2,4,8192]{2,1,0:T(4,128)(2,1)S(1)}, bf16[2,4,8192]{2,1,0:T(4,128)(2,1)S(1)}, u32[]{:S(2)}, u32[]{:S(2)}) collective-permute-start(bf16[2,4,8192]{2,1,0:T(4,128)(2,1)S(1)} %or_select_fusion), channel_id=1, source_target_pairs={{0,2},{1,3},{2,0},{3,1},{4,6},{5,7},{6,4},{7,5},{8,10},{9,11},{10,... | collective-permute-start | bytes 393224 | tf_op jit(solution)/shard_map/ppermute | solution.py:51
  4.7 1.6 %collective-permute-start = (bf16[2,4,8192]{2,1,0:T(4,128)(2,1)S(1)}, bf16[2,4,8192]{2,1,0:T(4,128)(2,1)S(1)}, u32[]{:S(2)}, u32[]{:S(2)}) collective-permute-start(bf16[2,4,8192]{2,1,0:T(4,128)(2,1)S(1)} %or_select_fusion), channel_id=1, source_target_pairs={{0,4},{1,5},{2,6},{3,7},{4,0},{5,1},{6,2},{7,3},{8,12},{9,13},{10,... | collective-permute-start | bytes 393224 | tf_op jit(solution)/shard_map/ppermute | solution.py:51
  6.2 2.5 %collective-permute-start.3 = (bf16[2,4,8192]{2,1,0:T(4,128)(2,1)S(1)}, bf16[2,4,8192]{2,1,0:T(4,128)(2,1)S(1)}, u32[]{:S(2)}, u32[]{:S(2)}) collective-permute-start(bf16[2,4,8192]{2,1,0:T(4,128)(2,1)S(1)} %or_select_fusion), channel_id=1, source_target_pairs={{0,12},{1,13},{2,14},{3,15},{4,8},{5,9},{6,10},{7,11},{8,4},{9,5},... | collective-permute-start | bytes 393224 | tf_op jit(solution)/shard_map/ppermute | solution.py:51
  8.7 0.1 collective-permute-start.2
  8.8 0.0 collective-permute-done.1
  8.8 0.8 %collective-permute-done = bf16[2,4,8192]{2,1,0:T(4,128)(2,1)S(1)} collective-permute-done((bf16[2,4,8192]{2,1,0:T(4,128)(2,1)S(1)}, bf16[2,4,8192]{2,1,0:T(4,128)(2,1)S(1)}, u32[]{:S(2)}, u32[]{:S(2)}) %collective-permute-start) | collective-permute-done | bytes 131104 | tf_op jit(solution)/shard_map/ppermute | solution.py:51
  9.6 0.4 collective-permute-start.4
  10.0 1.0 %or_select_fusion.1 = bf16[1,2,4,8192]{3,2,1,0:T(4,128)(2,1)S(1)} fusion(bf16[1,1,4,8192]{3,2,1,0:T(4,128)(2,1)} %bitcast.22, bf16[1,1,4,8192]{3,2,1,0:T(4,128)(2,1)} %bitcast.24, pred[4]{0:T(512)(128)(4,1)S(1)} %iota_compare_fusion, pred[2]{0:T(512)(128)(4,1)S(1)} %iota_compare_fusion.1), kind=kLoop, calls=%fused_computation.5 | loop fusion | flops 393216 | bytes 262150 | tf_op jit(solution)/shard_map/jit(_where)/select_n | solution.py:245
  11.0 4.9 %collective-permute-done.3 = bf16[2,4,8192]{2,1,0:T(4,128)(2,1)S(1)} collective-permute-done((bf16[2,4,8192]{2,1,0:T(4,128)(2,1)S(1)}, bf16[2,4,8192]{2,1,0:T(4,128)(2,1)S(1)}, u32[]{:S(2)}, u32[]{:S(2)}) %collective-permute-start.3) | collective-permute-done | bytes 131104 | tf_op jit(solution)/shard_map/ppermute | solution.py:51
  15.9 4.3 %collective-permute-done.2 = bf16[2,4,8192]{2,1,0:T(4,128)(2,1)S(1)} collective-permute-done((bf16[2,4,8192]{2,1,0:T(4,128)(2,1)S(1)}, bf16[2,4,8192]{2,1,0:T(4,128)(2,1)S(1)}, u32[]{:S(2)}, u32[]{:S(2)}) %collective-permute-start.2) | collective-permute-done | bytes 131104 | tf_op jit(solution)/shard_map/ppermute | solution.py:51
  20.2 0.0 collective-permute-done.4
  20.2 0.2 pad_maximum_fusion.2
  20.4 0.6 collective-permute-start.7
  21.0 0.5 pad_maximum_fusion.refs_0_
  21.5 0.1 collective-permute-start.5
  21.5 0.2 pad_maximum_fusion.1.refs_1_
  21.7 0.6 collective-permute-start.6
  22.3 5.4 %collective-permute-done.7.refs_4_ = bf16[2,2,4,8192]{3,2,1,0:T(4,128)(2,1)S(1)} collective-permute-done((bf16[2,2,4,8192]{3,2,1,0:T(4,128)(2,1)S(1)}, bf16[2,2,4,8192]{3,2,1,0:T(4,128)(2,1)S(1)}, u32[]{:S(2)}, u32[]{:S(2)}) %collective-permute-start.7) | collective-permute-done | bytes 262176 | tf_op jit(solution)/shard_map/ppermute | solution.py:51
  27.7 0.0 collective-permute-start.8
  27.7 0.0 collective-permute-done.6.refs_3_
  27.7 1.5 %collective-permute-done.8.refs_5_ = bf16[2,2,4,8192]{3,2,1,0:T(4,128)(2,1)S(1)} collective-permute-done((bf16[2,2,4,8192]{3,2,1,0:T(4,128)(2,1)S(1)}, bf16[2,2,4,8192]{3,2,1,0:T(4,128)(2,1)S(1)}, u32[]{:S(2)}, u32[]{:S(2)}) %collective-permute-start.8) | collective-permute-done | bytes 262176 | tf_op jit(solution)/shard_map/ppermute | solution.py:51
  29.2 0.0 collective-permute-done.5.refs_2_
  29.2 4.1 %shard_map.64 = bf16[64,512]{1,0:T(8,128)(2,1)S(1)} custom-call(s32[1]{0:T(128)} %bitcast.own_ref, bf16[4,2,4,8192]{3,2,1,0:T(4,128)(2,1)S(1)} %pad_maximum_fusion.refs_0_, bf16[2,2,4,8192]{3,2,1,0:T(4,128)(2,1)S(1)} %pad_maximum_fusion.1.refs_1_, bf16[4,2,4,8192]{3,2,1,0:T(4,128)(2,1)S(1)} %collective-permute-done.5.refs_2_, ...), custom_call_target="tpu_custom_call" | custom-call | flops 64 | bytes 64 | tf_op jit(solution)/shard_map/pallas_call | solution.py:116
  33.3 2.5 %collective-permute-start.11 = (bf16[64,512]{1,0:T(8,128)(2,1)S(1)}, bf16[64,512]{1,0:T(8,128)(2,1)S(1)}, u32[]{:S(2)}, u32[]{:S(2)}) collective-permute-start(bf16[64,512]{1,0:T(8,128)(2,1)S(1)} %shard_map.64), channel_id=1, source_target_pairs={{0,12},{1,13},{2,14},{3,15},{4,8},{5,9},{6,10},{7,11},{8,4},{9,5},... | collective-permute-start | bytes 196616 | tf_op jit(solution)/shard_map/ppermute | solution.py:51
  35.8 0.0 collective-permute-start.10
  35.8 2.0 %collective-permute-start.9 = (bf16[64,512]{1,0:T(8,128)(2,1)S(1)}, bf16[64,512]{1,0:T(8,128)(2,1)S(1)}, u32[]{:S(2)}, u32[]{:S(2)}) collective-permute-start(bf16[64,512]{1,0:T(8,128)(2,1)S(1)} %shard_map.64), channel_id=1, source_target_pairs={{0,4},{1,5},{2,6},{3,7},{4,0},{5,1},{6,2},{7,3},{8,12},{9,13},{10,... | collective-permute-start | bytes 196616 | tf_op jit(solution)/shard_map/ppermute | solution.py:51
  37.8 4.2 %shard_map.65.refs_1_.refs_3_ = bf16[4,512,64]{2,1,0:T(8,128)(2,1)S(1)} custom-call(s32[1]{0:T(128)} %bitcast.own_ref, bf16[4,2,4,8192]{3,2,1,0:T(4,128)(2,1)S(1)} %pad_maximum_fusion.refs_0_, bf16[2,2,4,8192]{3,2,1,0:T(4,128)(2,1)S(1)} %pad_maximum_fusion.1.refs_1_, bf16[4,2,4,8192]{3,2,1,0:T(4,128)(2,1)S(1)} %collective-permute-done.5.refs_2_, ...), custom_call_target="tpu_custom_call" | custom-call | flops 64 | bytes 64 | tf_op jit(solution)/shard_map/pallas_call | solution.py:116
  42.0 0.0 collective-permute-done.11
  42.1 0.1 collective-permute-done.10
  42.1 0.0 collective-permute-done.9
  42.2 0.6 collective-permute-start.13
  42.8 0.0 collective-permute-start.12
  42.8 5.4 %shard_map.66.refs_5_ = bf16[4,512,8192]{2,1,0:T(8,128)(2,1)} custom-call(s32[1]{0:T(128)} %bitcast.own_ref, bf16[4,64,512]{2,1,0:T(8,128)(2,1)S(1)} %pad_maximum_fusion.3.refs_0_, bf16[4,512,64]{2,1,0:T(8,128)(2,1)S(1)} %shard_map.65.refs_1_.refs_3_, bf16[512,8192]{1,0:T(8,128)(2,1)} %refs_4_.1), custom_call_target="tpu_custom_call" | custom-call | flops 134217728 | bytes 10485760 | tf_op jit(solution)/shard_map/pallas_call | solution.py:209
  48.1 2.3 %collective-permute-done.13.refs_1_ = bf16[4,64,512]{2,1,0:T(8,128)(2,1)S(1)} collective-permute-done((bf16[4,64,512]{2,1,0:T(8,128)(2,1)S(1)}, bf16[4,64,512]{2,1,0:T(8,128)(2,1)S(1)}, u32[]{:S(2)}, u32[]{:S(2)}) %collective-permute-start.13) | collective-permute-done | bytes 262176 | tf_op jit(solution)/shard_map/ppermute | solution.py:51
  50.5 0.0 collective-permute-start.14
  50.5 0.0 collective-permute-done.12.refs_0_
  50.5 1.5 %collective-permute-done.14.refs_2_ = bf16[4,64,512]{2,1,0:T(8,128)(2,1)S(1)} collective-permute-done((bf16[4,64,512]{2,1,0:T(8,128)(2,1)S(1)}, bf16[4,64,512]{2,1,0:T(8,128)(2,1)S(1)}, u32[]{:S(2)}, u32[]{:S(2)}) %collective-permute-start.14) | collective-permute-done | bytes 262176 | tf_op jit(solution)/shard_map/ppermute | solution.py:51
  52.0 11.4 %shard_map.67 = bf16[4,512,8192]{2,1,0:T(8,128)(2,1)} custom-call(s32[1]{0:T(128)} %bitcast.own_ref, bf16[4,64,512]{2,1,0:T(8,128)(2,1)S(1)} %collective-permute-done.12.refs_0_, bf16[4,64,512]{2,1,0:T(8,128)(2,1)S(1)} %collective-permute-done.13.refs_1_, bf16[4,64,512]{2,1,0:T(8,128)(2,1)S(1)} %collective-permute-done.14.refs_2_, ...), custom_call_target="tpu_custom_call", output_to_operand_aliasing={{}: (6, {})} | custom-call | flops 402653184 | bytes 31457280 | tf_op jit(solution)/shard_map/pallas_call | solution.py:209
  (3 shorter events, 0.0 us)
Async XLA Ops:
  1.7 7.2 %collective-permute-start.1 = (bf16[2,4,8192]{2,1,0:T(4,128)(2,1)S(1)}, bf16[2,4,8192]{2,1,0:T(4,128)(2,1)S(1)}, u32[]{:S(2)}, u32[]{:S(2)}) collective-permute-start(bf16[2,4,8192]{2,1,0:T(4,128)(2,1)S(1)} %or_select_fusion), channel_id=1, source_target_pairs={{0,2},{1,3},{2,0},{3,1},{4,6},{5,7},{6,4},{7,5},{8,10},{9,11},{10,... | collective-permute-start | bytes 393224 | tf_op jit(solution)/shard_map/ppermute | solution.py:51
  4.7 5.0 %collective-permute-start = (bf16[2,4,8192]{2,1,0:T(4,128)(2,1)S(1)}, bf16[2,4,8192]{2,1,0:T(4,128)(2,1)S(1)}, u32[]{:S(2)}, u32[]{:S(2)}) collective-permute-start(bf16[2,4,8192]{2,1,0:T(4,128)(2,1)S(1)} %or_select_fusion), channel_id=1, source_target_pairs={{0,4},{1,5},{2,6},{3,7},{4,0},{5,1},{6,2},{7,3},{8,12},{9,13},{10,... | collective-permute-start | bytes 393224 | tf_op jit(solution)/shard_map/ppermute | solution.py:51
  6.2 9.6 %collective-permute-start.3 = (bf16[2,4,8192]{2,1,0:T(4,128)(2,1)S(1)}, bf16[2,4,8192]{2,1,0:T(4,128)(2,1)S(1)}, u32[]{:S(2)}, u32[]{:S(2)}) collective-permute-start(bf16[2,4,8192]{2,1,0:T(4,128)(2,1)S(1)} %or_select_fusion), channel_id=1, source_target_pairs={{0,12},{1,13},{2,14},{3,15},{4,8},{5,9},{6,10},{7,11},{8,4},{9,5},... | collective-permute-start | bytes 393224 | tf_op jit(solution)/shard_map/ppermute | solution.py:51
  8.7 11.5 %collective-permute-start.2 = (bf16[2,4,8192]{2,1,0:T(4,128)(2,1)S(1)}, bf16[2,4,8192]{2,1,0:T(4,128)(2,1)S(1)}, u32[]{:S(2)}, u32[]{:S(2)}) collective-permute-start(bf16[2,4,8192]{2,1,0:T(4,128)(2,1)S(1)} %or_select_fusion), channel_id=1, source_target_pairs={{0,8},{1,9},{2,10},{3,11},{4,12},{5,13},{6,14},{7,15},{8,0},{9,1},... | collective-permute-start | bytes 393224 | tf_op jit(solution)/shard_map/ppermute | solution.py:51
  9.6 10.6 %collective-permute-start.4 = (bf16[2,4,8192]{2,1,0:T(4,128)(2,1)S(1)}, bf16[2,4,8192]{2,1,0:T(4,128)(2,1)S(1)}, u32[]{:S(2)}, u32[]{:S(2)}) collective-permute-start(bf16[2,4,8192]{2,1,0:T(4,128)(2,1)S(1)} %collective-permute-done), channel_id=1, source_target_pairs={{0,2},{1,3},{2,0},{3,1},{4,6},{5,7},{6,4},{7,5},{8,10},{9,11},{10,... | collective-permute-start | bytes 393224 | tf_op jit(solution)/shard_map/ppermute | solution.py:51
  20.4 7.3 %collective-permute-start.7 = (bf16[2,2,4,8192]{3,2,1,0:T(4,128)(2,1)S(1)}, bf16[2,2,4,8192]{3,2,1,0:T(4,128)(2,1)S(1)}, u32[]{:S(2)}, u32[]{:S(2)}) collective-permute-start(bf16[2,2,4,8192]{3,2,1,0:T(4,128)(2,1)S(1)} %pad_maximum_fusion.2), channel_id=1, source_target_pairs={{0,2},{1,3},{2,0},{3,1},{4,6},{5,7},{6,4},{7,5},{8,10},{9,11},{10,... | collective-permute-start | bytes 786440 | tf_op jit(solution)/shard_map/ppermute | solution.py:51
  21.5 7.8 %collective-permute-start.5 = (bf16[4,2,4,8192]{3,2,1,0:T(4,128)(2,1)S(1)}, bf16[4,2,4,8192]{3,2,1,0:T(4,128)(2,1)S(1)}, u32[]{:S(2)}, u32[]{:S(2)}) collective-permute-start(bf16[4,2,4,8192]{3,2,1,0:T(4,128)(2,1)S(1)} %pad_maximum_fusion.refs_0_), channel_id=1, source_target_pairs={{0,1},{1,0},{2,3},{3,2},{4,5},{5,4},{6,7},{7,6},{8,9},{9,8},{10,11... | collective-permute-start | bytes 1572872 | tf_op jit(solution)/shard_map/ppermute | solution.py:51
  21.7 6.0 %collective-permute-start.6 = (bf16[2,2,4,8192]{3,2,1,0:T(4,128)(2,1)S(1)}, bf16[2,2,4,8192]{3,2,1,0:T(4,128)(2,1)S(1)}, u32[]{:S(2)}, u32[]{:S(2)}) collective-permute-start(bf16[2,2,4,8192]{3,2,1,0:T(4,128)(2,1)S(1)} %pad_maximum_fusion.1.refs_1_), channel_id=1, source_target_pairs={{0,1},{1,0},{2,3},{3,2},{4,5},{5,4},{6,7},{7,6},{8,9},{9,8},{10,11... | collective-permute-start | bytes 786440 | tf_op jit(solution)/shard_map/ppermute | solution.py:51
  27.7 1.5 %collective-permute-start.8 = (bf16[2,2,4,8192]{3,2,1,0:T(4,128)(2,1)S(1)}, bf16[2,2,4,8192]{3,2,1,0:T(4,128)(2,1)S(1)}, u32[]{:S(2)}, u32[]{:S(2)}) collective-permute-start(bf16[2,2,4,8192]{3,2,1,0:T(4,128)(2,1)S(1)} %collective-permute-done.7.refs_4_), channel_id=1, source_target_pairs={{0,1},{1,0},{2,3},{3,2},{4,5},{5,4},{6,7},{7,6},{8,9},{9,8},{10,11... | collective-permute-start | bytes 786440 | tf_op jit(solution)/shard_map/ppermute | solution.py:51
  33.3 8.7 %collective-permute-start.11 = (bf16[64,512]{1,0:T(8,128)(2,1)S(1)}, bf16[64,512]{1,0:T(8,128)(2,1)S(1)}, u32[]{:S(2)}, u32[]{:S(2)}) collective-permute-start(bf16[64,512]{1,0:T(8,128)(2,1)S(1)} %shard_map.64), channel_id=1, source_target_pairs={{0,12},{1,13},{2,14},{3,15},{4,8},{5,9},{6,10},{7,11},{8,4},{9,5},... | collective-permute-start | bytes 196616 | tf_op jit(solution)/shard_map/ppermute | solution.py:51
  35.8 6.3 %collective-permute-start.10 = (bf16[64,512]{1,0:T(8,128)(2,1)S(1)}, bf16[64,512]{1,0:T(8,128)(2,1)S(1)}, u32[]{:S(2)}, u32[]{:S(2)}) collective-permute-start(bf16[64,512]{1,0:T(8,128)(2,1)S(1)} %shard_map.64), channel_id=1, source_target_pairs={{0,8},{1,9},{2,10},{3,11},{4,12},{5,13},{6,14},{7,15},{8,0},{9,1},... | collective-permute-start | bytes 196616 | tf_op jit(solution)/shard_map/ppermute | solution.py:51
  35.8 6.3 %collective-permute-start.9 = (bf16[64,512]{1,0:T(8,128)(2,1)S(1)}, bf16[64,512]{1,0:T(8,128)(2,1)S(1)}, u32[]{:S(2)}, u32[]{:S(2)}) collective-permute-start(bf16[64,512]{1,0:T(8,128)(2,1)S(1)} %shard_map.64), channel_id=1, source_target_pairs={{0,4},{1,5},{2,6},{3,7},{4,0},{5,1},{6,2},{7,3},{8,12},{9,13},{10,... | collective-permute-start | bytes 196616 | tf_op jit(solution)/shard_map/ppermute | solution.py:51
  42.2 8.3 %collective-permute-start.13 = (bf16[4,64,512]{2,1,0:T(8,128)(2,1)S(1)}, bf16[4,64,512]{2,1,0:T(8,128)(2,1)S(1)}, u32[]{:S(2)}, u32[]{:S(2)}) collective-permute-start(bf16[4,64,512]{2,1,0:T(8,128)(2,1)S(1)} %pad_maximum_fusion.3.refs_0_), channel_id=1, source_target_pairs={{0,2},{1,3},{2,0},{3,1},{4,6},{5,7},{6,4},{7,5},{8,10},{9,11},{10,... | collective-permute-start | bytes 786440 | tf_op jit(solution)/shard_map/ppermute | solution.py:51
  42.8 7.7 %collective-permute-start.12 = (bf16[4,64,512]{2,1,0:T(8,128)(2,1)S(1)}, bf16[4,64,512]{2,1,0:T(8,128)(2,1)S(1)}, u32[]{:S(2)}, u32[]{:S(2)}) collective-permute-start(bf16[4,64,512]{2,1,0:T(8,128)(2,1)S(1)} %pad_maximum_fusion.3.refs_0_), channel_id=1, source_target_pairs={{0,1},{1,0},{2,3},{3,2},{4,5},{5,4},{6,7},{7,6},{8,9},{9,8},{10,11... | collective-permute-start | bytes 786440 | tf_op jit(solution)/shard_map/ppermute | solution.py:51
  50.5 1.5 %collective-permute-start.14 = (bf16[4,64,512]{2,1,0:T(8,128)(2,1)S(1)}, bf16[4,64,512]{2,1,0:T(8,128)(2,1)S(1)}, u32[]{:S(2)}, u32[]{:S(2)}) collective-permute-start(bf16[4,64,512]{2,1,0:T(8,128)(2,1)S(1)} %collective-permute-done.13.refs_1_), channel_id=1, source_target_pairs={{0,1},{1,0},{2,3},{3,2},{4,5},{5,4},{6,7},{7,6},{8,9},{9,8},{10,11... | collective-permute-start | bytes 786440 | tf_op jit(solution)/shard_map/ppermute | solution.py:51

commit v10 on v9

--- a/solution.py
+++ b/solution.py
@@ -62,7 +62,9 @@
     chunks, width = held.shape[:2]
     slots = pieces[0].shape[-2]
     copies = [
-        pltpu.make_async_copy(source.at[:, which], piece, piece_sems.at[k])
+        pltpu.make_async_copy(
+            source if len(source.shape) == 3 else source.at[:, which], piece, piece_sems.at[k]
+        )
         for k, (source, piece) in enumerate(zip(sources, pieces))
     ]
     reads = [
@@ -239,26 +241,37 @@
     other = (3, 7, 11, 15)
     tie = lax.optimization_barrier
 
-    shape = (2,) + factors_in.shape
-    plane, slot = [lax.broadcasted_iota(jnp.int32, shape, k) for k in (0, 1)]
-    keep = (plane == 0) | (slot < live_counts[0])
-    f = jnp.where(keep, jnp.stack([factors_in, factors_out]), jnp.zeros((), factors_in.dtype))
-    f1, fp, f2, f3 = [swap(f, m) for m in (4, 2, 8, 12)]
-    f1, fp = tie((f1, fp))
+    a2, a3 = [swap(factors_in, m) for m in (8, 12)]
+    keep = (lax.iota(jnp.int32, factors_in.shape[0]) < live_counts[0])[:, None]
+    masked = tie(jnp.where(keep, factors_out, jnp.zeros_like(factors_out)))
+    b2, b3 = [swap(masked, m) for m in (8, 12)]
+    f = tie(jnp.stack([factors_in, masked]))
+    f1, fp = tie((swap(f, 4), swap(f, 2)))
     fp1 = swap(f1, 2)
-    f2, f3, near = tie((f2, f3, fp1))
-    near = jnp.stack([fp, near])
-    far = swap(jnp.stack([f2, f3]), 2)
-    f_column = jnp.stack([f, f1, f2, f3])
-    f_core = swap(f_column, 1)
+    a2, a3 = tie((a2, a3))[:2]
+    a_far = jnp.stack([a2, a3])
+    a_far_pair = swap(a_far, 2)
+    a_far_core = swap(a_far, 1)
+    near = jnp.stack([f, f1, fp, fp1])
     near_core = swap(near, 1)
-    far_core = swap(far, 1)
-    blocks = [
-        (f_column, column), (near, pair[:2]), (f_core, core), (near_core, other[:2]),
-        (far, pair[2:]), (far_core, other[2:]),
-    ]
-    pin = project(own, blocks, basis_in, 0, False)
-
+    a_far_other = swap(a_far_pair, 1)
+    a_far_other, b2, b3 = tie((a_far_other, b2, b3))
+    b_far = jnp.stack([b2, b3])
+    b_far_pair = swap(b_far, 2)
+    joined = [(near, (0, 4, 2, 6)), (near_core, (1, 5, 3, 7))]
+    pin = project(
+        own,
+        joined + [
+            (a_far, column[2:]), (a_far_pair, pair[2:]), (a_far_core, core[2:]),
+            (a_far_other, other[2:]),
+        ],
+        basis_in, 0, False,
+    )
+
+    b_far_pair = after(b_far_pair, pin)
+    b_far = jnp.concatenate([b_far, b_far_pair])
+    b_far_core = swap(b_far, 1)
+    blocks = joined + [(b_far, column[2:] + pair[2:]), (b_far_core, core[2:] + other[2:])]
     g1, g2, g3 = [swap(pin, m) for m in (4, 8, 12)]
     left = project(own, blocks, basis_out, 1, True)
     g1, g2, g3 = tie((g1, g2, g3, left))[:3]

time: 63.7 us -> 59.9 us (0.940)
  waiting for transfers between devices: 20.9 us -> 10.2 us
  starting transfers between devices: 13.8 us -> 20.7 us
    ppermute x15 -> x19, waiting for transfers between devices: 20.9 us -> 10.2 us  [swap(): return lax.ppermute(x, 'dp', [(d, d ^ m) for d in range(n)])]
    ppermute x15 -> x19, starting transfers between devices: 13.8 us -> 20.7 us  [swap(): return lax.ppermute(x, 'dp', [(d, d ^ m) for d in range(n)])]
    select_n x2 -> x1, other arithmetic: 1.97 us -> 0.94 us  [by_swaps(): masked = tie(jnp.where(keep, factors_out, jnp.zeros_like(factors_out)))]
    another operation x3 -> x4, other arithmetic: 0.84 us -> 1.59 us  [the longest x1 0.94 us: by_swaps(): f = tie(jnp.stack([factors_in, masked]))]
  transfers between devices with their start and end apart: 15 -> 19, of which waited for: 8 -> 8; matrix products, arithmetic and copies ran while one was open for 3% -> 4% of each run, Pallas kernels for 15% -> 23%
where the time goes in v10:
time: 59.9 us; the launch traced here: 59.7 us
  Pallas kernels  25.3 us (42%)
  starting transfers between devices  20.7 us (35%)
  waiting for transfers between devices  10.2 us (17%)
  other arithmetic  2.76 us (5%)
  between operations  0.76 us (1%)
    ppermute x19, starting transfers between devices, swap(): return lax.ppermute(x, 'dp', [(d, d ^ m) for d in range(n)])  20.7 us
    pallas_call x2, Pallas kernels, outer(): pl.pallas_call(functools.partial(outer_kernel, [entries for _, entries in...  16.8 us
    ppermute x19, waiting for transfers between devices, swap(): return lax.ppermute(x, 'dp', [(d, d ^ m) for d in range(n)])  10.2 us
    pallas_call x2, Pallas kernels, project(): pl.pallas_call(functools.partial(project_kernel, [entries for _, entries...  8.55 us
  transfers between devices with their start and end apart: 19, of which 8 were waited for; matrix products, arithmetic and copies ran while one was open for 4% of the time, Pallas kernels for 23%

profile of v10, /device:TPU:0, one launch (start us, length us, event | category | flops | bytes accessed | tf_op | source)
XLA Modules:
  0.0 59.7 jit_solution(1944175608350838027)
XLA Ops:
  0.0 5.0 %collective-permute-start.5 = (bf16[4,8192]{1,0:T(4,128)(2,1)}, bf16[4,8192]{1,0:T(4,128)(2,1)S(1)}, u32[]{:S(2)}, u32[]{:S(2)}) collective-permute-start(bf16[4,8192]{1,0:T(4,128)(2,1)} %param.6), channel_id=1, source_target_pairs={{0,12},{1,13},{2,14},{3,15},{4,8},{5,9},{6,10},{7,11},{8,4},{9,5},... | collective-permute-start | bytes 196616 | tf_op jit(solution)/shard_map/ppermute | solution.py:51
  5.0 0.0 collective-permute-start.4
  5.7 0.9 %broadcast_select_fusion = bf16[4,8192]{1,0:T(4,128)(2,1)S(1)} fusion(bf16[4,8192]{1,0:T(4,128)(2,1)} %param.7, pred[4]{0:T(512)(128)(4,1)S(1)} %iota_compare_fusion), kind=kLoop, calls=%fused_computation.6 | loop fusion | flops 32768 | bytes 131076 | tf_op jit(solution)/shard_map/jit(_where)/select_n | solution.py:246
  6.7 0.9 %pad_maximum_fusion.3 = bf16[2,4,8192]{2,1,0:T(4,128)(2,1)S(1)} fusion(bf16[1,4,8192]{2,1,0:T(4,128)(2,1)S(1)} %bitcast.19, bf16[1,4,8192]{2,1,0:T(4,128)(2,1)} %bitcast.27), kind=kLoop, calls=%fused_computation.3 | loop fusion | flops 65536 | bytes 262144 | tf_op jit(solution)/shard_map/stack | solution.py:248
  7.6 1.6 %collective-permute-start.1 = (bf16[2,4,8192]{2,1,0:T(4,128)(2,1)S(1)}, bf16[2,4,8192]{2,1,0:T(4,128)(2,1)S(1)}, u32[]{:S(2)}, u32[]{:S(2)}) collective-permute-start(bf16[2,4,8192]{2,1,0:T(4,128)(2,1)S(1)} %pad_maximum_fusion.3), channel_id=1, source_target_pairs={{0,2},{1,3},{2,0},{3,1},{4,6},{5,7},{6,4},{7,5},{8,10},{9,11},{10,... | collective-permute-start | bytes 393224 | tf_op jit(solution)/shard_map/ppermute | solution.py:51
  9.2 0.8 %collective-permute-start = (bf16[2,4,8192]{2,1,0:T(4,128)(2,1)S(1)}, bf16[2,4,8192]{2,1,0:T(4,128)(2,1)S(1)}, u32[]{:S(2)}, u32[]{:S(2)}) collective-permute-start(bf16[2,4,8192]{2,1,0:T(4,128)(2,1)S(1)} %pad_maximum_fusion.3), channel_id=1, source_target_pairs={{0,4},{1,5},{2,6},{3,7},{4,0},{5,1},{6,2},{7,3},{8,12},{9,13},{10,... | collective-permute-start | bytes 393224 | tf_op jit(solution)/shard_map/ppermute | solution.py:51
  9.9 0.0 collective-permute-done.5
  9.9 0.9 %collective-permute-done.4 = bf16[4,8192]{1,0:T(4,128)(2,1)S(1)} collective-permute-done((bf16[4,8192]{1,0:T(4,128)(2,1)}, bf16[4,8192]{1,0:T(4,128)(2,1)S(1)}, u32[]{:S(2)}, u32[]{:S(2)}) %collective-permute-start.4) | collective-permute-done | bytes 65568 | tf_op jit(solution)/shard_map/ppermute | solution.py:51
  10.9 0.1 pad_maximum_fusion.4.refs_2_
  11.0 1.6 %collective-permute-start.6 = (bf16[2,4,8192]{2,1,0:T(4,128)(2,1)S(1)}, bf16[2,4,8192]{2,1,0:T(4,128)(2,1)S(1)}, u32[]{:S(2)}, u32[]{:S(2)}) collective-permute-start(bf16[2,4,8192]{2,1,0:T(4,128)(2,1)S(1)} %pad_maximum_fusion.4.refs_2_), channel_id=1, source_target_pairs={{0,2},{1,3},{2,0},{3,1},{4,6},{5,7},{6,4},{7,5},{8,10},{9,11},{10,... | collective-permute-start | bytes 393224 | tf_op jit(solution)/shard_map/ppermute | solution.py:51
  12.6 0.0 collective-permute-done.1
  12.6 1.5 %collective-permute-done = bf16[2,4,8192]{2,1,0:T(4,128)(2,1)S(1)} collective-permute-done((bf16[2,4,8192]{2,1,0:T(4,128)(2,1)S(1)}, bf16[2,4,8192]{2,1,0:T(4,128)(2,1)S(1)}, u32[]{:S(2)}, u32[]{:S(2)}) %collective-permute-start) | collective-permute-done | bytes 131104 | tf_op jit(solution)/shard_map/ppermute | solution.py:51
  14.1 1.0 %collective-permute-start.2 = (bf16[2,4,8192]{2,1,0:T(4,128)(2,1)S(1)}, bf16[2,4,8192]{2,1,0:T(4,128)(2,1)S(1)}, u32[]{:S(2)}, u32[]{:S(2)}) collective-permute-start(bf16[2,4,8192]{2,1,0:T(4,128)(2,1)S(1)} %collective-permute-done), channel_id=1, source_target_pairs={{0,2},{1,3},{2,0},{3,1},{4,6},{5,7},{6,4},{7,5},{8,10},{9,11},{10,... | collective-permute-start | bytes 393224 | tf_op jit(solution)/shard_map/ppermute | solution.py:51
  15.2 2.4 %collective-permute-start.10 = (bf16[4,8192]{1,0:T(4,128)(2,1)S(1)}, bf16[4,8192]{1,0:T(4,128)(2,1)S(1)}, u32[]{:S(2)}, u32[]{:S(2)}) collective-permute-start(bf16[4,8192]{1,0:T(4,128)(2,1)S(1)} %broadcast_select_fusion), channel_id=1, source_target_pairs={{0,12},{1,13},{2,14},{3,15},{4,8},{5,9},{6,10},{7,11},{8,4},{9,5},... | collective-permute-start | bytes 196616 | tf_op jit(solution)/shard_map/ppermute | solution.py:51
  17.6 0.6 %collective-permute-start.9 = (bf16[4,8192]{1,0:T(4,128)(2,1)S(1)}, bf16[4,8192]{1,0:T(4,128)(2,1)S(1)}, u32[]{:S(2)}, u32[]{:S(2)}) collective-permute-start(bf16[4,8192]{1,0:T(4,128)(2,1)S(1)} %broadcast_select_fusion), channel_id=1, source_target_pairs={{0,8},{1,9},{2,10},{3,11},{4,12},{5,13},{6,14},{7,15},{8,0},{9,1},... | collective-permute-start | bytes 196616 | tf_op jit(solution)/shard_map/ppermute | solution.py:51
  18.2 0.0 collective-permute-start.7
  18.2 0.0 collective-permute-done.6.refs_3_
  18.2 0.5 collective-permute-start.8
  18.7 0.4 collective-permute-done.2
  19.1 0.5 pad_maximum_fusion.refs_0_
  19.6 0.1 collective-permute-start.3
  19.6 1.7 %collective-permute-done.10 = bf16[4,8192]{1,0:T(4,128)(2,1)S(1)} collective-permute-done((bf16[4,8192]{1,0:T(4,128)(2,1)S(1)}, bf16[4,8192]{1,0:T(4,128)(2,1)S(1)}, u32[]{:S(2)}, u32[]{:S(2)}) %collective-permute-start.10) | collective-permute-done | bytes 65568 | tf_op jit(solution)/shard_map/ppermute | solution.py:51
  21.3 1.4 %collective-permute-done.9 = bf16[4,8192]{1,0:T(4,128)(2,1)S(1)} collective-permute-done((bf16[4,8192]{1,0:T(4,128)(2,1)S(1)}, bf16[4,8192]{1,0:T(4,128)(2,1)S(1)}, u32[]{:S(2)}, u32[]{:S(2)}) %collective-permute-start.9) | collective-permute-done | bytes 65568 | tf_op jit(solution)/shard_map/ppermute | solution.py:51
  22.7 0.0 collective-permute-done.8.refs_5_
  22.7 0.1 pad_maximum_fusion.5
  22.8 1.7 %collective-permute-start.14 = (bf16[2,4,8192]{2,1,0:T(4,128)(2,1)S(1)}, bf16[2,4,8192]{2,1,0:T(4,128)(2,1)S(1)}, u32[]{:S(2)}, u32[]{:S(2)}) collective-permute-start(bf16[2,4,8192]{2,1,0:T(4,128)(2,1)S(1)} %pad_maximum_fusion.5), channel_id=1, source_target_pairs={{0,2},{1,3},{2,0},{3,1},{4,6},{5,7},{6,4},{7,5},{8,10},{9,11},{10,... | collective-permute-start | bytes 393224 | tf_op jit(solution)/shard_map/ppermute | solution.py:51
  24.5 0.0 collective-permute-done.7.refs_4_
  24.5 0.0 collective-permute-done.3.refs_1_
  24.5 4.4 %shard_map.64 = bf16[64,512]{1,0:T(8,128)(2,1)S(1)} custom-call(s32[1]{0:T(128)} %bitcast.own_ref, bf16[4,2,4,8192]{3,2,1,0:T(4,128)(2,1)S(1)} %pad_maximum_fusion.refs_0_, bf16[4,2,4,8192]{3,2,1,0:T(4,128)(2,1)S(1)} %collective-permute-done.3.refs_1_, bf16[2,4,8192]{2,1,0:T(4,128)(2,1)S(1)} %pad_maximum_fusion.4.refs_2_, ...), custom_call_target="tpu_custom_call" | custom-call | flops 64 | bytes 64 | tf_op jit(solution)/shard_map/pallas_call | solution.py:118
  29.0 0.0 collective-permute-done.14
  29.0 0.2 pad_maximum_fusion.1.refs_2_
  29.2 0.1 collective-permute-start.15
  29.3 2.0 %collective-permute-start.13 = (bf16[64,512]{1,0:T(8,128)(2,1)S(1)}, bf16[64,512]{1,0:T(8,128)(2,1)S(1)}, u32[]{:S(2)}, u32[]{:S(2)}) collective-permute-start(bf16[64,512]{1,0:T(8,128)(2,1)S(1)} %shard_map.64), channel_id=1, source_target_pairs={{0,12},{1,13},{2,14},{3,15},{4,8},{5,9},{6,10},{7,11},{8,4},{9,5},... | collective-permute-start | bytes 196616 | tf_op jit(solution)/shard_map/ppermute | solution.py:51
  31.3 0.0 collective-permute-start.12
  31.3 2.4 %collective-permute-start.11 = (bf16[64,512]{1,0:T(8,128)(2,1)S(1)}, bf16[64,512]{1,0:T(8,128)(2,1)S(1)}, u32[]{:S(2)}, u32[]{:S(2)}) collective-permute-start(bf16[64,512]{1,0:T(8,128)(2,1)S(1)} %shard_map.64), channel_id=1, source_target_pairs={{0,4},{1,5},{2,6},{3,7},{4,0},{5,1},{6,2},{7,3},{8,12},{9,13},{10,... | collective-permute-start | bytes 196616 | tf_op jit(solution)/shard_map/ppermute | solution.py:51
  33.7 0.0 collective-permute-done.15.refs_3_
  33.7 4.1 %shard_map.65.refs_1_.refs_3_ = bf16[4,512,64]{2,1,0:T(8,128)(2,1)S(1)} custom-call(s32[1]{0:T(128)} %bitcast.own_ref, bf16[4,2,4,8192]{3,2,1,0:T(4,128)(2,1)S(1)} %pad_maximum_fusion.refs_0_, bf16[4,2,4,8192]{3,2,1,0:T(4,128)(2,1)S(1)} %collective-permute-done.3.refs_1_, bf16[4,4,8192]{2,1,0:T(4,128)(2,1)S(1)} %pad_maximum_fusion.1.refs_2_, ...), custom_call_target="tpu_custom_call" | custom-call | flops 64 | bytes 64 | tf_op jit(solution)/shard_map/pallas_call | solution.py:118
  37.9 0.0 collective-permute-done.13
  37.9 0.5 collective-permute-done.12
  38.4 0.0 collective-permute-done.11
  38.4 0.7 %collective-permute-start.17 = (bf16[4,64,512]{2,1,0:T(8,128)(2,1)S(1)}, bf16[4,64,512]{2,1,0:T(8,128)(2,1)S(1)}, u32[]{:S(2)}, u32[]{:S(2)}) collective-permute-start(bf16[4,64,512]{2,1,0:T(8,128)(2,1)S(1)} %pad_maximum_fusion.2.refs_0_), channel_id=1, source_target_pairs={{0,2},{1,3},{2,0},{3,1},{4,6},{5,7},{6,4},{7,5},{8,10},{9,11},{10,... | collective-permute-start | bytes 786440 | tf_op jit(solution)/shard_map/ppermute | solution.py:51
  39.2 0.0 collective-permute-start.16
  39.2 5.4 %shard_map.66.refs_5_ = bf16[4,512,8192]{2,1,0:T(8,128)(2,1)} custom-call(s32[1]{0:T(128)} %bitcast.own_ref, bf16[4,64,512]{2,1,0:T(8,128)(2,1)S(1)} %pad_maximum_fusion.2.refs_0_, bf16[4,512,64]{2,1,0:T(8,128)(2,1)S(1)} %shard_map.65.refs_1_.refs_3_, bf16[512,8192]{1,0:T(8,128)(2,1)} %refs_4_.3), custom_call_target="tpu_custom_call" | custom-call | flops 134217728 | bytes 10485760 | tf_op jit(solution)/shard_map/pallas_call | solution.py:211
  44.5 2.2 %collective-permute-done.17.refs_1_ = bf16[4,64,512]{2,1,0:T(8,128)(2,1)S(1)} collective-permute-done((bf16[4,64,512]{2,1,0:T(8,128)(2,1)S(1)}, bf16[4,64,512]{2,1,0:T(8,128)(2,1)S(1)}, u32[]{:S(2)}, u32[]{:S(2)}) %collective-permute-start.17) | collective-permute-done | bytes 262176 | tf_op jit(solution)/shard_map/ppermute | solution.py:51
  46.7 0.0 collective-permute-start.18
  46.7 0.0 collective-permute-done.16.refs_0_
  46.7 1.5 %collective-permute-done.18.refs_2_ = bf16[4,64,512]{2,1,0:T(8,128)(2,1)S(1)} collective-permute-done((bf16[4,64,512]{2,1,0:T(8,128)(2,1)S(1)}, bf16[4,64,512]{2,1,0:T(8,128)(2,1)S(1)}, u32[]{:S(2)}, u32[]{:S(2)}) %collective-permute-start.18) | collective-permute-done | bytes 262176 | tf_op jit(solution)/shard_map/ppermute | solution.py:51
  48.3 11.4 %shard_map.67 = bf16[4,512,8192]{2,1,0:T(8,128)(2,1)} custom-call(s32[1]{0:T(128)} %bitcast.own_ref, bf16[4,64,512]{2,1,0:T(8,128)(2,1)S(1)} %collective-permute-done.16.refs_0_, bf16[4,64,512]{2,1,0:T(8,128)(2,1)S(1)} %collective-permute-done.17.refs_1_, bf16[4,64,512]{2,1,0:T(8,128)(2,1)S(1)} %collective-permute-done.18.refs_2_, ...), custom_call_target="tpu_custom_call", output_to_operand_aliasing={{}: (6, {})} | custom-call | flops 402653184 | bytes 31457280 | tf_op jit(solution)/shard_map/pallas_call | solution.py:211
  (2 shorter events, 0.0 us)
Async XLA Ops:
  0.0 9.9 %collective-permute-start.5 = (bf16[4,8192]{1,0:T(4,128)(2,1)}, bf16[4,8192]{1,0:T(4,128)(2,1)S(1)}, u32[]{:S(2)}, u32[]{:S(2)}) collective-permute-start(bf16[4,8192]{1,0:T(4,128)(2,1)} %param.6), channel_id=1, source_target_pairs={{0,12},{1,13},{2,14},{3,15},{4,8},{5,9},{6,10},{7,11},{8,4},{9,5},... | collective-permute-start | bytes 196616 | tf_op jit(solution)/shard_map/ppermute | solution.py:51
  5.0 5.8 %collective-permute-start.4 = (bf16[4,8192]{1,0:T(4,128)(2,1)}, bf16[4,8192]{1,0:T(4,128)(2,1)S(1)}, u32[]{:S(2)}, u32[]{:S(2)}) collective-permute-start(bf16[4,8192]{1,0:T(4,128)(2,1)} %param.6), channel_id=1, source_target_pairs={{0,8},{1,9},{2,10},{3,11},{4,12},{5,13},{6,14},{7,15},{8,0},{9,1},... | collective-permute-start | bytes 196616 | tf_op jit(solution)/shard_map/ppermute | solution.py:51
  7.6 5.0 %collective-permute-start.1 = (bf16[2,4,8192]{2,1,0:T(4,128)(2,1)S(1)}, bf16[2,4,8192]{2,1,0:T(4,128)(2,1)S(1)}, u32[]{:S(2)}, u32[]{:S(2)}) collective-permute-start(bf16[2,4,8192]{2,1,0:T(4,128)(2,1)S(1)} %pad_maximum_fusion.3), channel_id=1, source_target_pairs={{0,2},{1,3},{2,0},{3,1},{4,6},{5,7},{6,4},{7,5},{8,10},{9,11},{10,... | collective-permute-start | bytes 393224 | tf_op jit(solution)/shard_map/ppermute | solution.py:51
  9.2 5.0 %collective-permute-start = (bf16[2,4,8192]{2,1,0:T(4,128)(2,1)S(1)}, bf16[2,4,8192]{2,1,0:T(4,128)(2,1)S(1)}, u32[]{:S(2)}, u32[]{:S(2)}) collective-permute-start(bf16[2,4,8192]{2,1,0:T(4,128)(2,1)S(1)} %pad_maximum_fusion.3), channel_id=1, source_target_pairs={{0,4},{1,5},{2,6},{3,7},{4,0},{5,1},{6,2},{7,3},{8,12},{9,13},{10,... | collective-permute-start | bytes 393224 | tf_op jit(solution)/shard_map/ppermute | solution.py:51
  11.0 7.2 %collective-permute-start.6 = (bf16[2,4,8192]{2,1,0:T(4,128)(2,1)S(1)}, bf16[2,4,8192]{2,1,0:T(4,128)(2,1)S(1)}, u32[]{:S(2)}, u32[]{:S(2)}) collective-permute-start(bf16[2,4,8192]{2,1,0:T(4,128)(2,1)S(1)} %pad_maximum_fusion.4.refs_2_), channel_id=1, source_target_pairs={{0,2},{1,3},{2,0},{3,1},{4,6},{5,7},{6,4},{7,5},{8,10},{9,11},{10,... | collective-permute-start | bytes 393224 | tf_op jit(solution)/shard_map/ppermute | solution.py:51
  14.1 5.0 %collective-permute-start.2 = (bf16[2,4,8192]{2,1,0:T(4,128)(2,1)S(1)}, bf16[2,4,8192]{2,1,0:T(4,128)(2,1)S(1)}, u32[]{:S(2)}, u32[]{:S(2)}) collective-permute-start(bf16[2,4,8192]{2,1,0:T(4,128)(2,1)S(1)} %collective-permute-done), channel_id=1, source_target_pairs={{0,2},{1,3},{2,0},{3,1},{4,6},{5,7},{6,4},{7,5},{8,10},{9,11},{10,... | collective-permute-start | bytes 393224 | tf_op jit(solution)/shard_map/ppermute | solution.py:51
  15.2 6.2 %collective-permute-start.10 = (bf16[4,8192]{1,0:T(4,128)(2,1)S(1)}, bf16[4,8192]{1,0:T(4,128)(2,1)S(1)}, u32[]{:S(2)}, u32[]{:S(2)}) collective-permute-start(bf16[4,8192]{1,0:T(4,128)(2,1)S(1)} %broadcast_select_fusion), channel_id=1, source_target_pairs={{0,12},{1,13},{2,14},{3,15},{4,8},{5,9},{6,10},{7,11},{8,4},{9,5},... | collective-permute-start | bytes 196616 | tf_op jit(solution)/shard_map/ppermute | solution.py:51
  17.6 5.2 %collective-permute-start.9 = (bf16[4,8192]{1,0:T(4,128)(2,1)S(1)}, bf16[4,8192]{1,0:T(4,128)(2,1)S(1)}, u32[]{:S(2)}, u32[]{:S(2)}) collective-permute-start(bf16[4,8192]{1,0:T(4,128)(2,1)S(1)} %broadcast_select_fusion), channel_id=1, source_target_pairs={{0,8},{1,9},{2,10},{3,11},{4,12},{5,13},{6,14},{7,15},{8,0},{9,1},... | collective-permute-start | bytes 196616 | tf_op jit(solution)/shard_map/ppermute | solution.py:51
  18.2 6.4 %collective-permute-start.7 = (bf16[2,4,8192]{2,1,0:T(4,128)(2,1)S(1)}, bf16[2,4,8192]{2,1,0:T(4,128)(2,1)S(1)}, u32[]{:S(2)}, u32[]{:S(2)}) collective-permute-start(bf16[2,4,8192]{2,1,0:T(4,128)(2,1)S(1)} %pad_maximum_fusion.4.refs_2_), channel_id=1, source_target_pairs={{0,1},{1,0},{2,3},{3,2},{4,5},{5,4},{6,7},{7,6},{8,9},{9,8},{10,11... | collective-permute-start | bytes 393224 | tf_op jit(solution)/shard_map/ppermute | solution.py:51
  18.2 4.5 %collective-permute-start.8 = (bf16[2,4,8192]{2,1,0:T(4,128)(2,1)S(1)}, bf16[2,4,8192]{2,1,0:T(4,128)(2,1)S(1)}, u32[]{:S(2)}, u32[]{:S(2)}) collective-permute-start(bf16[2,4,8192]{2,1,0:T(4,128)(2,1)S(1)} %collective-permute-done.6.refs_3_), channel_id=1, source_target_pairs={{0,1},{1,0},{2,3},{3,2},{4,5},{5,4},{6,7},{7,6},{8,9},{9,8},{10,11... | collective-permute-start | bytes 393224 | tf_op jit(solution)/shard_map/ppermute | solution.py:51
  19.6 5.0 %collective-permute-start.3 = (bf16[4,2,4,8192]{3,2,1,0:T(4,128)(2,1)S(1)}, bf16[4,2,4,8192]{3,2,1,0:T(4,128)(2,1)S(1)}, u32[]{:S(2)}, u32[]{:S(2)}) collective-permute-start(bf16[4,2,4,8192]{3,2,1,0:T(4,128)(2,1)S(1)} %pad_maximum_fusion.refs_0_), channel_id=1, source_target_pairs={{0,1},{1,0},{2,3},{3,2},{4,5},{5,4},{6,7},{7,6},{8,9},{9,8},{10,11... | collective-permute-start | bytes 1572872 | tf_op jit(solution)/shard_map/ppermute | solution.py:51
  22.8 6.2 %collective-permute-start.14 = (bf16[2,4,8192]{2,1,0:T(4,128)(2,1)S(1)}, bf16[2,4,8192]{2,1,0:T(4,128)(2,1)S(1)}, u32[]{:S(2)}, u32[]{:S(2)}) collective-permute-start(bf16[2,4,8192]{2,1,0:T(4,128)(2,1)S(1)} %pad_maximum_fusion.5), channel_id=1, source_target_pairs={{0,2},{1,3},{2,0},{3,1},{4,6},{5,7},{6,4},{7,5},{8,10},{9,11},{10,... | collective-permute-start | bytes 393224 | tf_op jit(solution)/shard_map/ppermute | solution.py:51
  29.2 4.5 %collective-permute-start.15 = (bf16[4,4,8192]{2,1,0:T(4,128)(2,1)S(1)}, bf16[4,4,8192]{2,1,0:T(4,128)(2,1)S(1)}, u32[]{:S(2)}, u32[]{:S(2)}) collective-permute-start(bf16[4,4,8192]{2,1,0:T(4,128)(2,1)S(1)} %pad_maximum_fusion.1.refs_2_), channel_id=1, source_target_pairs={{0,1},{1,0},{2,3},{3,2},{4,5},{5,4},{6,7},{7,6},{8,9},{9,8},{10,11... | collective-permute-start | bytes 786440 | tf_op jit(solution)/shard_map/ppermute | solution.py:51
  29.3 8.6 %collective-permute-start.13 = (bf16[64,512]{1,0:T(8,128)(2,1)S(1)}, bf16[64,512]{1,0:T(8,128)(2,1)S(1)}, u32[]{:S(2)}, u32[]{:S(2)}) collective-permute-start(bf16[64,512]{1,0:T(8,128)(2,1)S(1)} %shard_map.64), channel_id=1, source_target_pairs={{0,12},{1,13},{2,14},{3,15},{4,8},{5,9},{6,10},{7,11},{8,4},{9,5},... | collective-permute-start | bytes 196616 | tf_op jit(solution)/shard_map/ppermute | solution.py:51
  31.3 7.1 %collective-permute-start.12 = (bf16[64,512]{1,0:T(8,128)(2,1)S(1)}, bf16[64,512]{1,0:T(8,128)(2,1)S(1)}, u32[]{:S(2)}, u32[]{:S(2)}) collective-permute-start(bf16[64,512]{1,0:T(8,128)(2,1)S(1)} %shard_map.64), channel_id=1, source_target_pairs={{0,8},{1,9},{2,10},{3,11},{4,12},{5,13},{6,14},{7,15},{8,0},{9,1},... | collective-permute-start | bytes 196616 | tf_op jit(solution)/shard_map/ppermute | solution.py:51
  31.3 7.1 %collective-permute-start.11 = (bf16[64,512]{1,0:T(8,128)(2,1)S(1)}, bf16[64,512]{1,0:T(8,128)(2,1)S(1)}, u32[]{:S(2)}, u32[]{:S(2)}) collective-permute-start(bf16[64,512]{1,0:T(8,128)(2,1)S(1)} %shard_map.64), channel_id=1, source_target_pairs={{0,4},{1,5},{2,6},{3,7},{4,0},{5,1},{6,2},{7,3},{8,12},{9,13},{10,... | collective-permute-start | bytes 196616 | tf_op jit(solution)/shard_map/ppermute | solution.py:51
  38.4 8.3 %collective-permute-start.17 = (bf16[4,64,512]{2,1,0:T(8,128)(2,1)S(1)}, bf16[4,64,512]{2,1,0:T(8,128)(2,1)S(1)}, u32[]{:S(2)}, u32[]{:S(2)}) collective-permute-start(bf16[4,64,512]{2,1,0:T(8,128)(2,1)S(1)} %pad_maximum_fusion.2.refs_0_), channel_id=1, source_target_pairs={{0,2},{1,3},{2,0},{3,1},{4,6},{5,7},{6,4},{7,5},{8,10},{9,11},{10,... | collective-permute-start | bytes 786440 | tf_op jit(solution)/shard_map/ppermute | solution.py:51
  39.2 7.6 %collective-permute-start.16 = (bf16[4,64,512]{2,1,0:T(8,128)(2,1)S(1)}, bf16[4,64,512]{2,1,0:T(8,128)(2,1)S(1)}, u32[]{:S(2)}, u32[]{:S(2)}) collective-permute-start(bf16[4,64,512]{2,1,0:T(8,128)(2,1)S(1)} %pad_maximum_fusion.2.refs_0_), channel_id=1, source_target_pairs={{0,1},{1,0},{2,3},{3,2},{4,5},{5,4},{6,7},{7,6},{8,9},{9,8},{10,11... | collective-permute-start | bytes 786440 | tf_op jit(solution)/shard_map/ppermute | solution.py:51
  46.7 1.5 %collective-permute-start.18 = (bf16[4,64,512]{2,1,0:T(8,128)(2,1)S(1)}, bf16[4,64,512]{2,1,0:T(8,128)(2,1)S(1)}, u32[]{:S(2)}, u32[]{:S(2)}) collective-permute-start(bf16[4,64,512]{2,1,0:T(8,128)(2,1)S(1)} %collective-permute-done.17.refs_1_), channel_id=1, source_target_pairs={{0,1},{1,0},{2,3},{3,2},{4,5},{5,4},{6,7},{7,6},{8,9},{9,8},{10,11... | collective-permute-start | bytes 786440 | tf_op jit(solution)/shard_map/ppermute | solution.py:51

commit v11 on v10

--- a/solution.py
+++ b/solution.py
@@ -10,7 +10,7 @@
 CAND = 4
 KBLK = 1024
 RBLK = 256
-FLIGHT = 3
+FLIGHT = 4
 VMEM = 50 << 20
 
 
@@ -242,10 +242,12 @@
     tie = lax.optimization_barrier
 
     a2, a3 = [swap(factors_in, m) for m in (8, 12)]
-    keep = (lax.iota(jnp.int32, factors_in.shape[0]) < live_counts[0])[:, None]
-    masked = tie(jnp.where(keep, factors_out, jnp.zeros_like(factors_out)))
-    b2, b3 = [swap(masked, m) for m in (8, 12)]
-    f = tie(jnp.stack([factors_in, masked]))
+    shape = (2,) + factors_in.shape
+    plane, slot = [lax.broadcasted_iota(jnp.int32, shape, k) for k in (0, 1)]
+    keep = (plane == 0) | (slot < live_counts[0])
+    zero = jnp.zeros((), factors_in.dtype)
+    f = tie(jnp.where(keep, jnp.stack([factors_in, factors_out]), zero))
+    b2, b3 = [swap(f[1], m) for m in (8, 12)]
     f1, fp = tie((swap(f, 4), swap(f, 2)))
     fp1 = swap(f1, 2)
     a2, a3 = tie((a2, a3))[:2]
@@ -277,8 +279,8 @@
     g1, g2, g3 = tie((g1, g2, g3, left))[:3]
     g_column = jnp.stack([pin, g1, g2, g3])
     g_pair = swap(g_column, 2)
-    g_core = swap(g_column, 1)
     out = outer(own, [(g_column, column)], left, eigvals, None)
+    g_core = swap(after(g_column, out), 1)
     g_other = swap(after(g_pair, out), 1)
     return outer(own, [(g_core, core), (g_pair, pair), (g_other, other)], left, eigvals, out)
 

time: 59.9 us -> 59.7 us (level)
  other arithmetic: 2.76 us -> 1.87 us
  waiting for transfers between devices: 10.2 us -> 11 us
    another operation x1 -> x0, other arithmetic: 0.94 us -> none  [by_swaps(): f = tie(jnp.stack([factors_in, masked]))]
    ppermute x19, waiting for transfers between devices: 10.2 us -> 11 us  [swap(): return lax.ppermute(x, 'dp', [(d, d ^ m) for d in range(n)])]
  transfers between devices with their start and end apart: 19 -> 19, of which waited for: 8 -> 9; matrix products, arithmetic and copies ran while one was open for 4% -> 3% of each run, Pallas kernels for 23% -> 23%
where the time goes in v11:
time: 59.7 us; the launch traced here: 59.5 us
  Pallas kernels  25.5 us (43%)
  starting transfers between devices  20.4 us (34%)
  waiting for transfers between devices  11 us (18%)
  other arithmetic  1.87 us (3%)
  between operations  0.77 us (1%)
    ppermute x19, starting transfers between devices, swap(): return lax.ppermute(x, 'dp', [(d, d ^ m) for d in range(n)])  20.4 us
    pallas_call x2, Pallas kernels, outer(): pl.pallas_call(functools.partial(outer_kernel, [entries for _, entries in...  16.9 us
    ppermute x19, waiting for transfers between devices, swap(): return lax.ppermute(x, 'dp', [(d, d ^ m) for d in range(n)])  11 us
    pallas_call x2, Pallas kernels, project(): pl.pallas_call(functools.partial(project_kernel, [entries for _, entries...  8.55 us
  transfers between devices with their start and end apart: 19, of which 9 were waited for; matrix products, arithmetic and copies ran while one was open for 3% of the time, Pallas kernels for 23%

profile of v11, /device:TPU:0, one launch (start us, length us, event | category | flops | bytes accessed | tf_op | source)
XLA Modules:
  0.0 59.5 jit_solution(15044804868718998626)
XLA Ops:
  0.0 5.0 %collective-permute-start.5 = (bf16[4,8192]{1,0:T(4,128)(2,1)}, bf16[4,8192]{1,0:T(4,128)(2,1)S(1)}, u32[]{:S(2)}, u32[]{:S(2)}) collective-permute-start(bf16[4,8192]{1,0:T(4,128)(2,1)} %param.6), channel_id=1, source_target_pairs={{0,12},{1,13},{2,14},{3,15},{4,8},{5,9},{6,10},{7,11},{8,4},{9,5},... | collective-permute-start | bytes 196616 | tf_op jit(solution)/shard_map/ppermute | solution.py:51
  5.0 0.0 collective-permute-start.4
  5.7 1.0 %or_select_fusion = bf16[2,4,8192]{2,1,0:T(4,128)(2,1)S(1)} fusion(bf16[1,4,8192]{2,1,0:T(4,128)(2,1)} %bitcast.28, bf16[1,4,8192]{2,1,0:T(4,128)(2,1)} %bitcast.29, pred[4]{0:T(512)(128)(4,1)S(1)} %iota_compare_fusion, pred[2]{0:T(512)(128)(4,1)S(1)} %iota_compare_fusion.1), kind=kLoop, calls=%fused_computation.3 | loop fusion | flops 393216 | bytes 262150 | tf_op jit(solution)/shard_map/jit(_where)/select_n | solution.py:249
  6.7 1.6 %collective-permute-start.1 = (bf16[2,4,8192]{2,1,0:T(4,128)(2,1)S(1)}, bf16[2,4,8192]{2,1,0:T(4,128)(2,1)S(1)}, u32[]{:S(2)}, u32[]{:S(2)}) collective-permute-start(bf16[2,4,8192]{2,1,0:T(4,128)(2,1)S(1)} %or_select_fusion), channel_id=1, source_target_pairs={{0,2},{1,3},{2,0},{3,1},{4,6},{5,7},{6,4},{7,5},{8,10},{9,11},{10,... | collective-permute-start | bytes 393224 | tf_op jit(solution)/shard_map/ppermute | solution.py:51
  8.3 0.8 %collective-permute-start = (bf16[2,4,8192]{2,1,0:T(4,128)(2,1)S(1)}, bf16[2,4,8192]{2,1,0:T(4,128)(2,1)S(1)}, u32[]{:S(2)}, u32[]{:S(2)}) collective-permute-start(bf16[2,4,8192]{2,1,0:T(4,128)(2,1)S(1)} %or_select_fusion), channel_id=1, source_target_pairs={{0,4},{1,5},{2,6},{3,7},{4,0},{5,1},{6,2},{7,3},{8,12},{9,13},{10,... | collective-permute-start | bytes 393224 | tf_op jit(solution)/shard_map/ppermute | solution.py:51
  9.1 0.0 collective-permute-done.5
  9.1 1.9 %collective-permute-done.4 = bf16[4,8192]{1,0:T(4,128)(2,1)S(1)} collective-permute-done((bf16[4,8192]{1,0:T(4,128)(2,1)}, bf16[4,8192]{1,0:T(4,128)(2,1)S(1)}, u32[]{:S(2)}, u32[]{:S(2)}) %collective-permute-start.4) | collective-permute-done | bytes 65568 | tf_op jit(solution)/shard_map/ppermute | solution.py:51
  10.9 0.1 pad_maximum_fusion.3.refs_2_
  11.0 1.6 %collective-permute-start.6 = (bf16[2,4,8192]{2,1,0:T(4,128)(2,1)S(1)}, bf16[2,4,8192]{2,1,0:T(4,128)(2,1)S(1)}, u32[]{:S(2)}, u32[]{:S(2)}) collective-permute-start(bf16[2,4,8192]{2,1,0:T(4,128)(2,1)S(1)} %pad_maximum_fusion.3.refs_2_), channel_id=1, source_target_pairs={{0,2},{1,3},{2,0},{3,1},{4,6},{5,7},{6,4},{7,5},{8,10},{9,11},{10,... | collective-permute-start | bytes 393224 | tf_op jit(solution)/shard_map/ppermute | solution.py:51
  12.6 0.0 collective-permute-done.1
  12.6 1.0 %collective-permute-done = bf16[2,4,8192]{2,1,0:T(4,128)(2,1)S(1)} collective-permute-done((bf16[2,4,8192]{2,1,0:T(4,128)(2,1)S(1)}, bf16[2,4,8192]{2,1,0:T(4,128)(2,1)S(1)}, u32[]{:S(2)}, u32[]{:S(2)}) %collective-permute-start) | collective-permute-done | bytes 131104 | tf_op jit(solution)/shard_map/ppermute | solution.py:51
  13.7 1.1 %collective-permute-start.2 = (bf16[2,4,8192]{2,1,0:T(4,128)(2,1)S(1)}, bf16[2,4,8192]{2,1,0:T(4,128)(2,1)S(1)}, u32[]{:S(2)}, u32[]{:S(2)}) collective-permute-start(bf16[2,4,8192]{2,1,0:T(4,128)(2,1)S(1)} %collective-permute-done), channel_id=1, source_target_pairs={{0,2},{1,3},{2,0},{3,1},{4,6},{5,7},{6,4},{7,5},{8,10},{9,11},{10,... | collective-permute-start | bytes 393224 | tf_op jit(solution)/shard_map/ppermute | solution.py:51
  14.8 2.1 %collective-permute-start.10 = (bf16[4,8192]{1,0:T(4,128)(2,1)S(1)}, bf16[4,8192]{1,0:T(4,128)(2,1)S(1)}, u32[]{:S(2)}, u32[]{:S(2)}) collective-permute-start(bf16[4,8192]{1,0:T(4,128)(2,1)S(1)} %slice_bitcast_fusion), channel_id=1, source_target_pairs={{0,12},{1,13},{2,14},{3,15},{4,8},{5,9},{6,10},{7,11},{8,4},{9,5},... | collective-permute-start | bytes 196616 | tf_op jit(solution)/shard_map/ppermute | solution.py:51
  16.9 0.8 %collective-permute-start.9 = (bf16[4,8192]{1,0:T(4,128)(2,1)S(1)}, bf16[4,8192]{1,0:T(4,128)(2,1)S(1)}, u32[]{:S(2)}, u32[]{:S(2)}) collective-permute-start(bf16[4,8192]{1,0:T(4,128)(2,1)S(1)} %slice_bitcast_fusion), channel_id=1, source_target_pairs={{0,8},{1,9},{2,10},{3,11},{4,12},{5,13},{6,14},{7,15},{8,0},{9,1},... | collective-permute-start | bytes 196616 | tf_op jit(solution)/shard_map/ppermute | solution.py:51
  17.7 0.0 collective-permute-start.7
  17.7 0.0 collective-permute-done.6.refs_3_
  17.7 0.5 collective-permute-start.8
  18.3 0.6 %collective-permute-done.2 = bf16[2,4,8192]{2,1,0:T(4,128)(2,1)S(1)} collective-permute-done((bf16[2,4,8192]{2,1,0:T(4,128)(2,1)S(1)}, bf16[2,4,8192]{2,1,0:T(4,128)(2,1)S(1)}, u32[]{:S(2)}, u32[]{:S(2)}) %collective-permute-start.2) | collective-permute-done | bytes 131104 | tf_op jit(solution)/shard_map/ppermute | solution.py:51
  18.9 0.5 pad_maximum_fusion.refs_0_
  19.4 0.1 collective-permute-start.3
  19.4 1.5 %collective-permute-done.10 = bf16[4,8192]{1,0:T(4,128)(2,1)S(1)} collective-permute-done((bf16[4,8192]{1,0:T(4,128)(2,1)S(1)}, bf16[4,8192]{1,0:T(4,128)(2,1)S(1)}, u32[]{:S(2)}, u32[]{:S(2)}) %collective-permute-start.10) | collective-permute-done | bytes 65568 | tf_op jit(solution)/shard_map/ppermute | solution.py:51
  21.0 2.6 %collective-permute-done.9 = bf16[4,8192]{1,0:T(4,128)(2,1)S(1)} collective-permute-done((bf16[4,8192]{1,0:T(4,128)(2,1)S(1)}, bf16[4,8192]{1,0:T(4,128)(2,1)S(1)}, u32[]{:S(2)}, u32[]{:S(2)}) %collective-permute-start.9) | collective-permute-done | bytes 65568 | tf_op jit(solution)/shard_map/ppermute | solution.py:51
  23.5 0.0 collective-permute-done.8.refs_5_
  23.5 0.1 pad_maximum_fusion.4
  23.6 0.6 %collective-permute-start.14 = (bf16[2,4,8192]{2,1,0:T(4,128)(2,1)S(1)}, bf16[2,4,8192]{2,1,0:T(4,128)(2,1)S(1)}, u32[]{:S(2)}, u32[]{:S(2)}) collective-permute-start(bf16[2,4,8192]{2,1,0:T(4,128)(2,1)S(1)} %pad_maximum_fusion.4), channel_id=1, source_target_pairs={{0,2},{1,3},{2,0},{3,1},{4,6},{5,7},{6,4},{7,5},{8,10},{9,11},{10,... | collective-permute-start | bytes 393224 | tf_op jit(solution)/shard_map/ppermute | solution.py:51
  24.3 0.0 collective-permute-done.7.refs_4_
  24.3 0.0 collective-permute-done.3.refs_1_
  24.3 4.4 %shard_map.64 = bf16[64,512]{1,0:T(8,128)(2,1)S(1)} custom-call(s32[1]{0:T(128)} %bitcast.own_ref, bf16[4,2,4,8192]{3,2,1,0:T(4,128)(2,1)S(1)} %pad_maximum_fusion.refs_0_, bf16[4,2,4,8192]{3,2,1,0:T(4,128)(2,1)S(1)} %collective-permute-done.3.refs_1_, bf16[2,4,8192]{2,1,0:T(4,128)(2,1)S(1)} %pad_maximum_fusion.3.refs_2_, ...), custom_call_target="tpu_custom_call" | custom-call | flops 64 | bytes 64 | tf_op jit(solution)/shard_map/pallas_call | solution.py:118
  28.7 0.0 collective-permute-done.14
  28.7 0.2 pad_maximum_fusion.1.refs_2_
  28.9 0.1 collective-permute-start.15
  29.0 2.4 %collective-permute-start.13 = (bf16[64,512]{1,0:T(8,128)(2,1)S(1)}, bf16[64,512]{1,0:T(8,128)(2,1)S(1)}, u32[]{:S(2)}, u32[]{:S(2)}) collective-permute-start(bf16[64,512]{1,0:T(8,128)(2,1)S(1)} %shard_map.64), channel_id=1, source_target_pairs={{0,12},{1,13},{2,14},{3,15},{4,8},{5,9},{6,10},{7,11},{8,4},{9,5},... | collective-permute-start | bytes 196616 | tf_op jit(solution)/shard_map/ppermute | solution.py:51
  31.3 0.0 collective-permute-start.12
  31.4 2.1 %collective-permute-start.11 = (bf16[64,512]{1,0:T(8,128)(2,1)S(1)}, bf16[64,512]{1,0:T(8,128)(2,1)S(1)}, u32[]{:S(2)}, u32[]{:S(2)}) collective-permute-start(bf16[64,512]{1,0:T(8,128)(2,1)S(1)} %shard_map.64), channel_id=1, source_target_pairs={{0,4},{1,5},{2,6},{3,7},{4,0},{5,1},{6,2},{7,3},{8,12},{9,13},{10,... | collective-permute-start | bytes 196616 | tf_op jit(solution)/shard_map/ppermute | solution.py:51
  33.4 0.0 collective-permute-done.15.refs_3_
  33.4 4.1 %shard_map.65.refs_1_.refs_3_ = bf16[4,512,64]{2,1,0:T(8,128)(2,1)S(1)} custom-call(s32[1]{0:T(128)} %bitcast.own_ref, bf16[4,2,4,8192]{3,2,1,0:T(4,128)(2,1)S(1)} %pad_maximum_fusion.refs_0_, bf16[4,2,4,8192]{3,2,1,0:T(4,128)(2,1)S(1)} %collective-permute-done.3.refs_1_, bf16[4,4,8192]{2,1,0:T(4,128)(2,1)S(1)} %pad_maximum_fusion.1.refs_2_, ...), custom_call_target="tpu_custom_call" | custom-call | flops 64 | bytes 64 | tf_op jit(solution)/shard_map/pallas_call | solution.py:118
  37.6 0.0 collective-permute-done.13
  37.6 0.5 collective-permute-done.12
  38.1 0.0 collective-permute-done.11
  38.1 1.5 %collective-permute-start.17 = (bf16[4,64,512]{2,1,0:T(8,128)(2,1)S(1)}, bf16[4,64,512]{2,1,0:T(8,128)(2,1)S(1)}, u32[]{:S(2)}, u32[]{:S(2)}) collective-permute-start(bf16[4,64,512]{2,1,0:T(8,128)(2,1)S(1)} %pad_maximum_fusion.2.refs_0_), channel_id=1, source_target_pairs={{0,2},{1,3},{2,0},{3,1},{4,6},{5,7},{6,4},{7,5},{8,10},{9,11},{10,... | collective-permute-start | bytes 786440 | tf_op jit(solution)/shard_map/ppermute | solution.py:51
  39.6 5.4 %shard_map.66.refs_5_ = bf16[4,512,8192]{2,1,0:T(8,128)(2,1)} custom-call(s32[1]{0:T(128)} %bitcast.own_ref, bf16[4,64,512]{2,1,0:T(8,128)(2,1)S(1)} %pad_maximum_fusion.2.refs_0_, bf16[4,512,64]{2,1,0:T(8,128)(2,1)S(1)} %shard_map.65.refs_1_.refs_3_, bf16[512,8192]{1,0:T(8,128)(2,1)} %refs_4_.3), custom_call_target="tpu_custom_call" | custom-call | flops 134217728 | bytes 10485760 | tf_op jit(solution)/shard_map/pallas_call | solution.py:211
  45.0 0.1 collective-permute-start.16
  45.1 1.3 %collective-permute-done.17.refs_1_ = bf16[4,64,512]{2,1,0:T(8,128)(2,1)S(1)} collective-permute-done((bf16[4,64,512]{2,1,0:T(8,128)(2,1)S(1)}, bf16[4,64,512]{2,1,0:T(8,128)(2,1)S(1)}, u32[]{:S(2)}, u32[]{:S(2)}) %collective-permute-start.17) | collective-permute-done | bytes 262176 | tf_op jit(solution)/shard_map/ppermute | solution.py:51
  46.5 0.0 collective-permute-start.18
  46.5 0.2 collective-permute-done.16.refs_0_
  46.6 1.3 %collective-permute-done.18.refs_2_ = bf16[4,64,512]{2,1,0:T(8,128)(2,1)S(1)} collective-permute-done((bf16[4,64,512]{2,1,0:T(8,128)(2,1)S(1)}, bf16[4,64,512]{2,1,0:T(8,128)(2,1)S(1)}, u32[]{:S(2)}, u32[]{:S(2)}) %collective-permute-start.18) | collective-permute-done | bytes 262176 | tf_op jit(solution)/shard_map/ppermute | solution.py:51
  48.0 11.5 %shard_map.67 = bf16[4,512,8192]{2,1,0:T(8,128)(2,1)} custom-call(s32[1]{0:T(128)} %bitcast.own_ref, bf16[4,64,512]{2,1,0:T(8,128)(2,1)S(1)} %collective-permute-done.16.refs_0_, bf16[4,64,512]{2,1,0:T(8,128)(2,1)S(1)} %collective-permute-done.17.refs_1_, bf16[4,64,512]{2,1,0:T(8,128)(2,1)S(1)} %collective-permute-done.18.refs_2_, ...), custom_call_target="tpu_custom_call", output_to_operand_aliasing={{}: (6, {})} | custom-call | flops 402653184 | bytes 31457280 | tf_op jit(solution)/shard_map/pallas_call | solution.py:211
  (4 shorter events, 0.1 us)
Async XLA Ops:
  0.0 9.1 %collective-permute-start.5 = (bf16[4,8192]{1,0:T(4,128)(2,1)}, bf16[4,8192]{1,0:T(4,128)(2,1)S(1)}, u32[]{:S(2)}, u32[]{:S(2)}) collective-permute-start(bf16[4,8192]{1,0:T(4,128)(2,1)} %param.6), channel_id=1, source_target_pairs={{0,12},{1,13},{2,14},{3,15},{4,8},{5,9},{6,10},{7,11},{8,4},{9,5},... | collective-permute-start | bytes 196616 | tf_op jit(solution)/shard_map/ppermute | solution.py:51
  5.0 5.9 %collective-permute-start.4 = (bf16[4,8192]{1,0:T(4,128)(2,1)}, bf16[4,8192]{1,0:T(4,128)(2,1)S(1)}, u32[]{:S(2)}, u32[]{:S(2)}) collective-permute-start(bf16[4,8192]{1,0:T(4,128)(2,1)} %param.6), channel_id=1, source_target_pairs={{0,8},{1,9},{2,10},{3,11},{4,12},{5,13},{6,14},{7,15},{8,0},{9,1},... | collective-permute-start | bytes 196616 | tf_op jit(solution)/shard_map/ppermute | solution.py:51
  6.7 5.9 %collective-permute-start.1 = (bf16[2,4,8192]{2,1,0:T(4,128)(2,1)S(1)}, bf16[2,4,8192]{2,1,0:T(4,128)(2,1)S(1)}, u32[]{:S(2)}, u32[]{:S(2)}) collective-permute-start(bf16[2,4,8192]{2,1,0:T(4,128)(2,1)S(1)} %or_select_fusion), channel_id=1, source_target_pairs={{0,2},{1,3},{2,0},{3,1},{4,6},{5,7},{6,4},{7,5},{8,10},{9,11},{10,... | collective-permute-start | bytes 393224 | tf_op jit(solution)/shard_map/ppermute | solution.py:51
  8.3 5.4 %collective-permute-start = (bf16[2,4,8192]{2,1,0:T(4,128)(2,1)S(1)}, bf16[2,4,8192]{2,1,0:T(4,128)(2,1)S(1)}, u32[]{:S(2)}, u32[]{:S(2)}) collective-permute-start(bf16[2,4,8192]{2,1,0:T(4,128)(2,1)S(1)} %or_select_fusion), channel_id=1, source_target_pairs={{0,4},{1,5},{2,6},{3,7},{4,0},{5,1},{6,2},{7,3},{8,12},{9,13},{10,... | collective-permute-start | bytes 393224 | tf_op jit(solution)/shard_map/ppermute | solution.py:51
  11.0 6.7 %collective-permute-start.6 = (bf16[2,4,8192]{2,1,0:T(4,128)(2,1)S(1)}, bf16[2,4,8192]{2,1,0:T(4,128)(2,1)S(1)}, u32[]{:S(2)}, u32[]{:S(2)}) collective-permute-start(bf16[2,4,8192]{2,1,0:T(4,128)(2,1)S(1)} %pad_maximum_fusion.3.refs_2_), channel_id=1, source_target_pairs={{0,2},{1,3},{2,0},{3,1},{4,6},{5,7},{6,4},{7,5},{8,10},{9,11},{10,... | collective-permute-start | bytes 393224 | tf_op jit(solution)/shard_map/ppermute | solution.py:51
  13.7 5.2 %collective-permute-start.2 = (bf16[2,4,8192]{2,1,0:T(4,128)(2,1)S(1)}, bf16[2,4,8192]{2,1,0:T(4,128)(2,1)S(1)}, u32[]{:S(2)}, u32[]{:S(2)}) collective-permute-start(bf16[2,4,8192]{2,1,0:T(4,128)(2,1)S(1)} %collective-permute-done), channel_id=1, source_target_pairs={{0,2},{1,3},{2,0},{3,1},{4,6},{5,7},{6,4},{7,5},{8,10},{9,11},{10,... | collective-permute-start | bytes 393224 | tf_op jit(solution)/shard_map/ppermute | solution.py:51
  14.8 6.1 %collective-permute-start.10 = (bf16[4,8192]{1,0:T(4,128)(2,1)S(1)}, bf16[4,8192]{1,0:T(4,128)(2,1)S(1)}, u32[]{:S(2)}, u32[]{:S(2)}) collective-permute-start(bf16[4,8192]{1,0:T(4,128)(2,1)S(1)} %slice_bitcast_fusion), channel_id=1, source_target_pairs={{0,12},{1,13},{2,14},{3,15},{4,8},{5,9},{6,10},{7,11},{8,4},{9,5},... | collective-permute-start | bytes 196616 | tf_op jit(solution)/shard_map/ppermute | solution.py:51
  16.9 6.6 %collective-permute-start.9 = (bf16[4,8192]{1,0:T(4,128)(2,1)S(1)}, bf16[4,8192]{1,0:T(4,128)(2,1)S(1)}, u32[]{:S(2)}, u32[]{:S(2)}) collective-permute-start(bf16[4,8192]{1,0:T(4,128)(2,1)S(1)} %slice_bitcast_fusion), channel_id=1, source_target_pairs={{0,8},{1,9},{2,10},{3,11},{4,12},{5,13},{6,14},{7,15},{8,0},{9,1},... | collective-permute-start | bytes 196616 | tf_op jit(solution)/shard_map/ppermute | solution.py:51
  17.7 6.5 %collective-permute-start.7 = (bf16[2,4,8192]{2,1,0:T(4,128)(2,1)S(1)}, bf16[2,4,8192]{2,1,0:T(4,128)(2,1)S(1)}, u32[]{:S(2)}, u32[]{:S(2)}) collective-permute-start(bf16[2,4,8192]{2,1,0:T(4,128)(2,1)S(1)} %pad_maximum_fusion.3.refs_2_), channel_id=1, source_target_pairs={{0,1},{1,0},{2,3},{3,2},{4,5},{5,4},{6,7},{7,6},{8,9},{9,8},{10,11... | collective-permute-start | bytes 393224 | tf_op jit(solution)/shard_map/ppermute | solution.py:51
  17.7 5.8 %collective-permute-start.8 = (bf16[2,4,8192]{2,1,0:T(4,128)(2,1)S(1)}, bf16[2,4,8192]{2,1,0:T(4,128)(2,1)S(1)}, u32[]{:S(2)}, u32[]{:S(2)}) collective-permute-start(bf16[2,4,8192]{2,1,0:T(4,128)(2,1)S(1)} %collective-permute-done.6.refs_3_), channel_id=1, source_target_pairs={{0,1},{1,0},{2,3},{3,2},{4,5},{5,4},{6,7},{7,6},{8,9},{9,8},{10,11... | collective-permute-start | bytes 393224 | tf_op jit(solution)/shard_map/ppermute | solution.py:51
  19.4 4.9 %collective-permute-start.3 = (bf16[4,2,4,8192]{3,2,1,0:T(4,128)(2,1)S(1)}, bf16[4,2,4,8192]{3,2,1,0:T(4,128)(2,1)S(1)}, u32[]{:S(2)}, u32[]{:S(2)}) collective-permute-start(bf16[4,2,4,8192]{3,2,1,0:T(4,128)(2,1)S(1)} %pad_maximum_fusion.refs_0_), channel_id=1, source_target_pairs={{0,1},{1,0},{2,3},{3,2},{4,5},{5,4},{6,7},{7,6},{8,9},{9,8},{10,11... | collective-permute-start | bytes 1572872 | tf_op jit(solution)/shard_map/ppermute | solution.py:51
  23.6 5.1 %collective-permute-start.14 = (bf16[2,4,8192]{2,1,0:T(4,128)(2,1)S(1)}, bf16[2,4,8192]{2,1,0:T(4,128)(2,1)S(1)}, u32[]{:S(2)}, u32[]{:S(2)}) collective-permute-start(bf16[2,4,8192]{2,1,0:T(4,128)(2,1)S(1)} %pad_maximum_fusion.4), channel_id=1, source_target_pairs={{0,2},{1,3},{2,0},{3,1},{4,6},{5,7},{6,4},{7,5},{8,10},{9,11},{10,... | collective-permute-start | bytes 393224 | tf_op jit(solution)/shard_map/ppermute | solution.py:51
  28.9 4.5 %collective-permute-start.15 = (bf16[4,4,8192]{2,1,0:T(4,128)(2,1)S(1)}, bf16[4,4,8192]{2,1,0:T(4,128)(2,1)S(1)}, u32[]{:S(2)}, u32[]{:S(2)}) collective-permute-start(bf16[4,4,8192]{2,1,0:T(4,128)(2,1)S(1)} %pad_maximum_fusion.1.refs_2_), channel_id=1, source_target_pairs={{0,1},{1,0},{2,3},{3,2},{4,5},{5,4},{6,7},{7,6},{8,9},{9,8},{10,11... | collective-permute-start | bytes 786440 | tf_op jit(solution)/shard_map/ppermute | solution.py:51
  29.0 8.6 %collective-permute-start.13 = (bf16[64,512]{1,0:T(8,128)(2,1)S(1)}, bf16[64,512]{1,0:T(8,128)(2,1)S(1)}, u32[]{:S(2)}, u32[]{:S(2)}) collective-permute-start(bf16[64,512]{1,0:T(8,128)(2,1)S(1)} %shard_map.64), channel_id=1, source_target_pairs={{0,12},{1,13},{2,14},{3,15},{4,8},{5,9},{6,10},{7,11},{8,4},{9,5},... | collective-permute-start | bytes 196616 | tf_op jit(solution)/shard_map/ppermute | solution.py:51
  31.3 6.8 %collective-permute-start.12 = (bf16[64,512]{1,0:T(8,128)(2,1)S(1)}, bf16[64,512]{1,0:T(8,128)(2,1)S(1)}, u32[]{:S(2)}, u32[]{:S(2)}) collective-permute-start(bf16[64,512]{1,0:T(8,128)(2,1)S(1)} %shard_map.64), channel_id=1, source_target_pairs={{0,8},{1,9},{2,10},{3,11},{4,12},{5,13},{6,14},{7,15},{8,0},{9,1},... | collective-permute-start | bytes 196616 | tf_op jit(solution)/shard_map/ppermute | solution.py:51
  31.4 6.8 %collective-permute-start.11 = (bf16[64,512]{1,0:T(8,128)(2,1)S(1)}, bf16[64,512]{1,0:T(8,128)(2,1)S(1)}, u32[]{:S(2)}, u32[]{:S(2)}) collective-permute-start(bf16[64,512]{1,0:T(8,128)(2,1)S(1)} %shard_map.64), channel_id=1, source_target_pairs={{0,4},{1,5},{2,6},{3,7},{4,0},{5,1},{6,2},{7,3},{8,12},{9,13},{10,... | collective-permute-start | bytes 196616 | tf_op jit(solution)/shard_map/ppermute | solution.py:51
  38.1 8.3 %collective-permute-start.17 = (bf16[4,64,512]{2,1,0:T(8,128)(2,1)S(1)}, bf16[4,64,512]{2,1,0:T(8,128)(2,1)S(1)}, u32[]{:S(2)}, u32[]{:S(2)}) collective-permute-start(bf16[4,64,512]{2,1,0:T(8,128)(2,1)S(1)} %pad_maximum_fusion.2.refs_0_), channel_id=1, source_target_pairs={{0,2},{1,3},{2,0},{3,1},{4,6},{5,7},{6,4},{7,5},{8,10},{9,11},{10,... | collective-permute-start | bytes 786440 | tf_op jit(solution)/shard_map/ppermute | solution.py:51
  45.0 1.6 %collective-permute-start.16 = (bf16[4,64,512]{2,1,0:T(8,128)(2,1)S(1)}, bf16[4,64,512]{2,1,0:T(8,128)(2,1)S(1)}, u32[]{:S(2)}, u32[]{:S(2)}) collective-permute-start(bf16[4,64,512]{2,1,0:T(8,128)(2,1)S(1)} %pad_maximum_fusion.2.refs_0_), channel_id=1, source_target_pairs={{0,1},{1,0},{2,3},{3,2},{4,5},{5,4},{6,7},{7,6},{8,9},{9,8},{10,11... | collective-permute-start | bytes 786440 | tf_op jit(solution)/shard_map/ppermute | solution.py:51
  46.5 1.5 %collective-permute-start.18 = (bf16[4,64,512]{2,1,0:T(8,128)(2,1)S(1)}, bf16[4,64,512]{2,1,0:T(8,128)(2,1)S(1)}, u32[]{:S(2)}, u32[]{:S(2)}) collective-permute-start(bf16[4,64,512]{2,1,0:T(8,128)(2,1)S(1)} %collective-permute-done.17.refs_1_), channel_id=1, source_target_pairs={{0,1},{1,0},{2,3},{3,2},{4,5},{5,4},{6,7},{7,6},{8,9},{9,8},{10,11... | collective-permute-start | bytes 786440 | tf_op jit(solution)/shard_map/ppermute | solution.py:51

commit v12 on v11

--- a/solution.py
+++ b/solution.py
@@ -151,11 +151,15 @@
     def read(s):
         return pltpu.make_async_copy(eig_ref.at[:, columns(s)], eig.at[s], eig_sems.at[s])
 
-    def write(s, c):
-        slot = lax.rem(s, depth)
+    def write(s, r, c):
+        slot, part = lax.rem(s, depth), pl.ds(r, RBLK)
         return pltpu.make_async_copy(
-            out.at[slot, c], out_ref.at[c, :, columns(s)], out_sems.at[slot, c]
+            out.at[slot, c, part],
+            out_ref.at[c, part, columns(s)],
+            out_sems.at[slot, r // RBLK, c],
         )
+
+    parts = [(r, c) for r in range(0, rows, RBLK) for c in range(CAND)]
 
     copies, at = [pltpu.make_async_copy(left_any, left, left_sem)], 0
     for k, (source, entries) in enumerate(zip(sources, blocks)):
@@ -181,21 +185,21 @@
                     left[c, r:r + RBLK, :], right[s], preferred_element_type=jnp.float32
                 )
                 out[slot, c, r:r + RBLK, :] = (summed * scale).astype(jnp.bfloat16)
-        for c in range(CAND):
-            write(s, c).start()
+            for c in range(CAND):
+                write(s, r, c).start()
 
     for s in range(depth):
         work(s, s)
 
     @pl.loop(depth, count)
     def _(s):
-        for c in range(CAND):
-            write(s - depth, c).wait()
+        for r, c in parts:
+            write(s - depth, r, c).wait()
         work(s, lax.rem(s, depth))
 
     for s in range(max(0, count - depth), count):
-        for c in range(CAND):
-            write(s, c).wait()
+        for r, c in parts:
+            write(s, r, c).wait()
 
 
 def outer(own, blocks, left, eigvals, before):
@@ -219,7 +223,7 @@
             pltpu.VMEM((count, rows, cols), jnp.bfloat16),
             pltpu.VMEM((FLIGHT, CAND, rows, cols), jnp.bfloat16),
             pltpu.SemaphoreType.DMA((count,)),
-            pltpu.SemaphoreType.DMA((FLIGHT, CAND)),
+            pltpu.SemaphoreType.DMA((FLIGHT, rows // RBLK, CAND)),
             pltpu.SemaphoreType.DMA((len(blocks),)),
             pltpu.SemaphoreType.DMA(()),
         ],

time: 59.7 us -> 59.5 us (level)
  transfers between devices with their start and end apart: 19 -> 19, of which waited for: 9 -> 8; matrix products, arithmetic and copies ran while one was open for 3% -> 3% of each run, Pallas kernels for 23% -> 23%
where the time goes in v12:
time: 59.5 us; the launch traced here: 59.3 us
  Pallas kernels  25.1 us (42%)
  starting transfers between devices  20.4 us (34%)
  waiting for transfers between devices  11.2 us (19%)
  other arithmetic  1.87 us (3%)
  between operations  0.77 us (1%)
    ppermute x19, starting transfers between devices, swap(): return lax.ppermute(x, 'dp', [(d, d ^ m) for d in range(n)])  20.4 us
    pallas_call x2, Pallas kernels, outer(): pl.pallas_call(functools.partial(outer_kernel, [entries for _, entries in...  16.6 us
    ppermute x19, waiting for transfers between devices, swap(): return lax.ppermute(x, 'dp', [(d, d ^ m) for d in range(n)])  11.2 us
    pallas_call x2, Pallas kernels, project(): pl.pallas_call(functools.partial(project_kernel, [entries for _, entries...  8.55 us
  transfers between devices with their start and end apart: 19, of which 8 were waited for; matrix products, arithmetic and copies ran while one was open for 3% of the time, Pallas kernels for 23%

profile of v12, /device:TPU:0, one launch (start us, length us, event | category | flops | bytes accessed | tf_op | source)
XLA Modules:
  0.0 59.3 jit_solution(7767367904960955523)
XLA Ops:
  0.0 5.0 %collective-permute-start.5 = (bf16[4,8192]{1,0:T(4,128)(2,1)}, bf16[4,8192]{1,0:T(4,128)(2,1)S(1)}, u32[]{:S(2)}, u32[]{:S(2)}) collective-permute-start(bf16[4,8192]{1,0:T(4,128)(2,1)} %param.6), channel_id=1, source_target_pairs={{0,12},{1,13},{2,14},{3,15},{4,8},{5,9},{6,10},{7,11},{8,4},{9,5},... | collective-permute-start | bytes 196616 | tf_op jit(solution)/shard_map/ppermute | solution.py:51
  5.0 0.0 collective-permute-start.4
  5.7 1.0 %or_select_fusion = bf16[2,4,8192]{2,1,0:T(4,128)(2,1)S(1)} fusion(bf16[1,4,8192]{2,1,0:T(4,128)(2,1)} %bitcast.28, bf16[1,4,8192]{2,1,0:T(4,128)(2,1)} %bitcast.29, pred[4]{0:T(512)(128)(4,1)S(1)} %iota_compare_fusion, pred[2]{0:T(512)(128)(4,1)S(1)} %iota_compare_fusion.1), kind=kLoop, calls=%fused_computation.3 | loop fusion | flops 393216 | bytes 262150 | tf_op jit(solution)/shard_map/jit(_where)/select_n | solution.py:253
  6.7 1.6 %collective-permute-start.1 = (bf16[2,4,8192]{2,1,0:T(4,128)(2,1)S(1)}, bf16[2,4,8192]{2,1,0:T(4,128)(2,1)S(1)}, u32[]{:S(2)}, u32[]{:S(2)}) collective-permute-start(bf16[2,4,8192]{2,1,0:T(4,128)(2,1)S(1)} %or_select_fusion), channel_id=1, source_target_pairs={{0,2},{1,3},{2,0},{3,1},{4,6},{5,7},{6,4},{7,5},{8,10},{9,11},{10,... | collective-permute-start | bytes 393224 | tf_op jit(solution)/shard_map/ppermute | solution.py:51
  8.3 0.8 %collective-permute-start = (bf16[2,4,8192]{2,1,0:T(4,128)(2,1)S(1)}, bf16[2,4,8192]{2,1,0:T(4,128)(2,1)S(1)}, u32[]{:S(2)}, u32[]{:S(2)}) collective-permute-start(bf16[2,4,8192]{2,1,0:T(4,128)(2,1)S(1)} %or_select_fusion), channel_id=1, source_target_pairs={{0,4},{1,5},{2,6},{3,7},{4,0},{5,1},{6,2},{7,3},{8,12},{9,13},{10,... | collective-permute-start | bytes 393224 | tf_op jit(solution)/shard_map/ppermute | solution.py:51
  9.1 0.0 collective-permute-done.5
  9.1 1.9 %collective-permute-done.4 = bf16[4,8192]{1,0:T(4,128)(2,1)S(1)} collective-permute-done((bf16[4,8192]{1,0:T(4,128)(2,1)}, bf16[4,8192]{1,0:T(4,128)(2,1)S(1)}, u32[]{:S(2)}, u32[]{:S(2)}) %collective-permute-start.4) | collective-permute-done | bytes 65568 | tf_op jit(solution)/shard_map/ppermute | solution.py:51
  10.9 0.1 pad_maximum_fusion.3.refs_2_
  11.0 1.6 %collective-permute-start.6 = (bf16[2,4,8192]{2,1,0:T(4,128)(2,1)S(1)}, bf16[2,4,8192]{2,1,0:T(4,128)(2,1)S(1)}, u32[]{:S(2)}, u32[]{:S(2)}) collective-permute-start(bf16[2,4,8192]{2,1,0:T(4,128)(2,1)S(1)} %pad_maximum_fusion.3.refs_2_), channel_id=1, source_target_pairs={{0,2},{1,3},{2,0},{3,1},{4,6},{5,7},{6,4},{7,5},{8,10},{9,11},{10,... | collective-permute-start | bytes 393224 | tf_op jit(solution)/shard_map/ppermute | solution.py:51
  12.6 0.0 collective-permute-done.1
  12.6 1.0 %collective-permute-done = bf16[2,4,8192]{2,1,0:T(4,128)(2,1)S(1)} collective-permute-done((bf16[2,4,8192]{2,1,0:T(4,128)(2,1)S(1)}, bf16[2,4,8192]{2,1,0:T(4,128)(2,1)S(1)}, u32[]{:S(2)}, u32[]{:S(2)}) %collective-permute-start) | collective-permute-done | bytes 131104 | tf_op jit(solution)/shard_map/ppermute | solution.py:51
  13.7 1.1 %collective-permute-start.2 = (bf16[2,4,8192]{2,1,0:T(4,128)(2,1)S(1)}, bf16[2,4,8192]{2,1,0:T(4,128)(2,1)S(1)}, u32[]{:S(2)}, u32[]{:S(2)}) collective-permute-start(bf16[2,4,8192]{2,1,0:T(4,128)(2,1)S(1)} %collective-permute-done), channel_id=1, source_target_pairs={{0,2},{1,3},{2,0},{3,1},{4,6},{5,7},{6,4},{7,5},{8,10},{9,11},{10,... | collective-permute-start | bytes 393224 | tf_op jit(solution)/shard_map/ppermute | solution.py:51
  14.8 2.1 %collective-permute-start.10 = (bf16[4,8192]{1,0:T(4,128)(2,1)S(1)}, bf16[4,8192]{1,0:T(4,128)(2,1)S(1)}, u32[]{:S(2)}, u32[]{:S(2)}) collective-permute-start(bf16[4,8192]{1,0:T(4,128)(2,1)S(1)} %slice_bitcast_fusion), channel_id=1, source_target_pairs={{0,12},{1,13},{2,14},{3,15},{4,8},{5,9},{6,10},{7,11},{8,4},{9,5},... | collective-permute-start | bytes 196616 | tf_op jit(solution)/shard_map/ppermute | solution.py:51
  16.9 0.8 %collective-permute-start.9 = (bf16[4,8192]{1,0:T(4,128)(2,1)S(1)}, bf16[4,8192]{1,0:T(4,128)(2,1)S(1)}, u32[]{:S(2)}, u32[]{:S(2)}) collective-permute-start(bf16[4,8192]{1,0:T(4,128)(2,1)S(1)} %slice_bitcast_fusion), channel_id=1, source_target_pairs={{0,8},{1,9},{2,10},{3,11},{4,12},{5,13},{6,14},{7,15},{8,0},{9,1},... | collective-permute-start | bytes 196616 | tf_op jit(solution)/shard_map/ppermute | solution.py:51
  17.7 0.0 collective-permute-start.7
  17.7 0.0 collective-permute-done.6.refs_3_
  17.7 0.5 collective-permute-start.8
  18.3 0.6 %collective-permute-done.2 = bf16[2,4,8192]{2,1,0:T(4,128)(2,1)S(1)} collective-permute-done((bf16[2,4,8192]{2,1,0:T(4,128)(2,1)S(1)}, bf16[2,4,8192]{2,1,0:T(4,128)(2,1)S(1)}, u32[]{:S(2)}, u32[]{:S(2)}) %collective-permute-start.2) | collective-permute-done | bytes 131104 | tf_op jit(solution)/shard_map/ppermute | solution.py:51
  18.9 0.5 pad_maximum_fusion.refs_0_
  19.4 0.1 collective-permute-start.3
  19.4 1.5 %collective-permute-done.10 = bf16[4,8192]{1,0:T(4,128)(2,1)S(1)} collective-permute-done((bf16[4,8192]{1,0:T(4,128)(2,1)S(1)}, bf16[4,8192]{1,0:T(4,128)(2,1)S(1)}, u32[]{:S(2)}, u32[]{:S(2)}) %collective-permute-start.10) | collective-permute-done | bytes 65568 | tf_op jit(solution)/shard_map/ppermute | solution.py:51
  21.0 2.6 %collective-permute-done.9 = bf16[4,8192]{1,0:T(4,128)(2,1)S(1)} collective-permute-done((bf16[4,8192]{1,0:T(4,128)(2,1)S(1)}, bf16[4,8192]{1,0:T(4,128)(2,1)S(1)}, u32[]{:S(2)}, u32[]{:S(2)}) %collective-permute-start.9) | collective-permute-done | bytes 65568 | tf_op jit(solution)/shard_map/ppermute | solution.py:51
  23.5 0.0 collective-permute-done.8.refs_5_
  23.5 0.1 pad_maximum_fusion.4
  23.6 0.6 %collective-permute-start.14 = (bf16[2,4,8192]{2,1,0:T(4,128)(2,1)S(1)}, bf16[2,4,8192]{2,1,0:T(4,128)(2,1)S(1)}, u32[]{:S(2)}, u32[]{:S(2)}) collective-permute-start(bf16[2,4,8192]{2,1,0:T(4,128)(2,1)S(1)} %pad_maximum_fusion.4), channel_id=1, source_target_pairs={{0,2},{1,3},{2,0},{3,1},{4,6},{5,7},{6,4},{7,5},{8,10},{9,11},{10,... | collective-permute-start | bytes 393224 | tf_op jit(solution)/shard_map/ppermute | solution.py:51
  24.3 0.0 collective-permute-done.7.refs_4_
  24.3 0.0 collective-permute-done.3.refs_1_
  24.3 4.4 %shard_map.64 = bf16[64,512]{1,0:T(8,128)(2,1)S(1)} custom-call(s32[1]{0:T(128)} %bitcast.own_ref, bf16[4,2,4,8192]{3,2,1,0:T(4,128)(2,1)S(1)} %pad_maximum_fusion.refs_0_, bf16[4,2,4,8192]{3,2,1,0:T(4,128)(2,1)S(1)} %collective-permute-done.3.refs_1_, bf16[2,4,8192]{2,1,0:T(4,128)(2,1)S(1)} %pad_maximum_fusion.3.refs_2_, ...), custom_call_target="tpu_custom_call" | custom-call | flops 64 | bytes 64 | tf_op jit(solution)/shard_map/pallas_call | solution.py:118
  28.7 0.0 collective-permute-done.14
  28.7 0.2 pad_maximum_fusion.1.refs_2_
  28.9 0.1 collective-permute-start.15
  29.0 2.4 %collective-permute-start.13 = (bf16[64,512]{1,0:T(8,128)(2,1)S(1)}, bf16[64,512]{1,0:T(8,128)(2,1)S(1)}, u32[]{:S(2)}, u32[]{:S(2)}) collective-permute-start(bf16[64,512]{1,0:T(8,128)(2,1)S(1)} %shard_map.64), channel_id=1, source_target_pairs={{0,12},{1,13},{2,14},{3,15},{4,8},{5,9},{6,10},{7,11},{8,4},{9,5},... | collective-permute-start | bytes 196616 | tf_op jit(solution)/shard_map/ppermute | solution.py:51
  31.3 0.0 collective-permute-start.12
  31.4 2.1 %collective-permute-start.11 = (bf16[64,512]{1,0:T(8,128)(2,1)S(1)}, bf16[64,512]{1,0:T(8,128)(2,1)S(1)}, u32[]{:S(2)}, u32[]{:S(2)}) collective-permute-start(bf16[64,512]{1,0:T(8,128)(2,1)S(1)} %shard_map.64), channel_id=1, source_target_pairs={{0,4},{1,5},{2,6},{3,7},{4,0},{5,1},{6,2},{7,3},{8,12},{9,13},{10,... | collective-permute-start | bytes 196616 | tf_op jit(solution)/shard_map/ppermute | solution.py:51
  33.4 0.0 collective-permute-done.15.refs_3_
  33.4 4.1 %shard_map.65.refs_1_.refs_3_ = bf16[4,512,64]{2,1,0:T(8,128)(2,1)S(1)} custom-call(s32[1]{0:T(128)} %bitcast.own_ref, bf16[4,2,4,8192]{3,2,1,0:T(4,128)(2,1)S(1)} %pad_maximum_fusion.refs_0_, bf16[4,2,4,8192]{3,2,1,0:T(4,128)(2,1)S(1)} %collective-permute-done.3.refs_1_, bf16[4,4,8192]{2,1,0:T(4,128)(2,1)S(1)} %pad_maximum_fusion.1.refs_2_, ...), custom_call_target="tpu_custom_call" | custom-call | flops 64 | bytes 64 | tf_op jit(solution)/shard_map/pallas_call | solution.py:118
  37.6 0.0 collective-permute-done.13
  37.6 0.5 collective-permute-done.12
  38.1 0.0 collective-permute-done.11
  38.1 1.5 %collective-permute-start.17 = (bf16[4,64,512]{2,1,0:T(8,128)(2,1)S(1)}, bf16[4,64,512]{2,1,0:T(8,128)(2,1)S(1)}, u32[]{:S(2)}, u32[]{:S(2)}) collective-permute-start(bf16[4,64,512]{2,1,0:T(8,128)(2,1)S(1)} %pad_maximum_fusion.2.refs_0_), channel_id=1, source_target_pairs={{0,2},{1,3},{2,0},{3,1},{4,6},{5,7},{6,4},{7,5},{8,10},{9,11},{10,... | collective-permute-start | bytes 786440 | tf_op jit(solution)/shard_map/ppermute | solution.py:51
  39.6 5.2 %shard_map.66.refs_5_ = bf16[4,512,8192]{2,1,0:T(8,128)(2,1)} custom-call(s32[1]{0:T(128)} %bitcast.own_ref, bf16[4,64,512]{2,1,0:T(8,128)(2,1)S(1)} %pad_maximum_fusion.2.refs_0_, bf16[4,512,64]{2,1,0:T(8,128)(2,1)S(1)} %shard_map.65.refs_1_.refs_3_, bf16[512,8192]{1,0:T(8,128)(2,1)} %refs_4_.3), custom_call_target="tpu_custom_call" | custom-call | flops 134217728 | bytes 10485760 | tf_op jit(solution)/shard_map/pallas_call | solution.py:215
  44.9 0.1 collective-permute-start.16
  45.0 1.5 %collective-permute-done.17.refs_1_ = bf16[4,64,512]{2,1,0:T(8,128)(2,1)S(1)} collective-permute-done((bf16[4,64,512]{2,1,0:T(8,128)(2,1)S(1)}, bf16[4,64,512]{2,1,0:T(8,128)(2,1)S(1)}, u32[]{:S(2)}, u32[]{:S(2)}) %collective-permute-start.17) | collective-permute-done | bytes 262176 | tf_op jit(solution)/shard_map/ppermute | solution.py:51
  46.5 0.0 collective-permute-start.18
  46.5 0.0 collective-permute-done.16.refs_0_
  46.5 1.5 %collective-permute-done.18.refs_2_ = bf16[4,64,512]{2,1,0:T(8,128)(2,1)S(1)} collective-permute-done((bf16[4,64,512]{2,1,0:T(8,128)(2,1)S(1)}, bf16[4,64,512]{2,1,0:T(8,128)(2,1)S(1)}, u32[]{:S(2)}, u32[]{:S(2)}) %collective-permute-start.18) | collective-permute-done | bytes 262176 | tf_op jit(solution)/shard_map/ppermute | solution.py:51
  48.0 11.3 %shard_map.67 = bf16[4,512,8192]{2,1,0:T(8,128)(2,1)} custom-call(s32[1]{0:T(128)} %bitcast.own_ref, bf16[4,64,512]{2,1,0:T(8,128)(2,1)S(1)} %collective-permute-done.16.refs_0_, bf16[4,64,512]{2,1,0:T(8,128)(2,1)S(1)} %collective-permute-done.17.refs_1_, bf16[4,64,512]{2,1,0:T(8,128)(2,1)S(1)} %collective-permute-done.18.refs_2_, ...), custom_call_target="tpu_custom_call", output_to_operand_aliasing={{}: (6, {})} | custom-call | flops 402653184 | bytes 31457280 | tf_op jit(solution)/shard_map/pallas_call | solution.py:215
  (4 shorter events, 0.1 us)
Async XLA Ops:
  0.0 9.1 %collective-permute-start.5 = (bf16[4,8192]{1,0:T(4,128)(2,1)}, bf16[4,8192]{1,0:T(4,128)(2,1)S(1)}, u32[]{:S(2)}, u32[]{:S(2)}) collective-permute-start(bf16[4,8192]{1,0:T(4,128)(2,1)} %param.6), channel_id=1, source_target_pairs={{0,12},{1,13},{2,14},{3,15},{4,8},{5,9},{6,10},{7,11},{8,4},{9,5},... | collective-permute-start | bytes 196616 | tf_op jit(solution)/shard_map/ppermute | solution.py:51
  5.0 5.9 %collective-permute-start.4 = (bf16[4,8192]{1,0:T(4,128)(2,1)}, bf16[4,8192]{1,0:T(4,128)(2,1)S(1)}, u32[]{:S(2)}, u32[]{:S(2)}) collective-permute-start(bf16[4,8192]{1,0:T(4,128)(2,1)} %param.6), channel_id=1, source_target_pairs={{0,8},{1,9},{2,10},{3,11},{4,12},{5,13},{6,14},{7,15},{8,0},{9,1},... | collective-permute-start | bytes 196616 | tf_op jit(solution)/shard_map/ppermute | solution.py:51
  6.7 5.9 %collective-permute-start.1 = (bf16[2,4,8192]{2,1,0:T(4,128)(2,1)S(1)}, bf16[2,4,8192]{2,1,0:T(4,128)(2,1)S(1)}, u32[]{:S(2)}, u32[]{:S(2)}) collective-permute-start(bf16[2,4,8192]{2,1,0:T(4,128)(2,1)S(1)} %or_select_fusion), channel_id=1, source_target_pairs={{0,2},{1,3},{2,0},{3,1},{4,6},{5,7},{6,4},{7,5},{8,10},{9,11},{10,... | collective-permute-start | bytes 393224 | tf_op jit(solution)/shard_map/ppermute | solution.py:51
  8.3 5.4 %collective-permute-start = (bf16[2,4,8192]{2,1,0:T(4,128)(2,1)S(1)}, bf16[2,4,8192]{2,1,0:T(4,128)(2,1)S(1)}, u32[]{:S(2)}, u32[]{:S(2)}) collective-permute-start(bf16[2,4,8192]{2,1,0:T(4,128)(2,1)S(1)} %or_select_fusion), channel_id=1, source_target_pairs={{0,4},{1,5},{2,6},{3,7},{4,0},{5,1},{6,2},{7,3},{8,12},{9,13},{10,... | collective-permute-start | bytes 393224 | tf_op jit(solution)/shard_map/ppermute | solution.py:51
  11.0 6.7 %collective-permute-start.6 = (bf16[2,4,8192]{2,1,0:T(4,128)(2,1)S(1)}, bf16[2,4,8192]{2,1,0:T(4,128)(2,1)S(1)}, u32[]{:S(2)}, u32[]{:S(2)}) collective-permute-start(bf16[2,4,8192]{2,1,0:T(4,128)(2,1)S(1)} %pad_maximum_fusion.3.refs_2_), channel_id=1, source_target_pairs={{0,2},{1,3},{2,0},{3,1},{4,6},{5,7},{6,4},{7,5},{8,10},{9,11},{10,... | collective-permute-start | bytes 393224 | tf_op jit(solution)/shard_map/ppermute | solution.py:51
  13.7 5.2 %collective-permute-start.2 = (bf16[2,4,8192]{2,1,0:T(4,128)(2,1)S(1)}, bf16[2,4,8192]{2,1,0:T(4,128)(2,1)S(1)}, u32[]{:S(2)}, u32[]{:S(2)}) collective-permute-start(bf16[2,4,8192]{2,1,0:T(4,128)(2,1)S(1)} %collective-permute-done), channel_id=1, source_target_pairs={{0,2},{1,3},{2,0},{3,1},{4,6},{5,7},{6,4},{7,5},{8,10},{9,11},{10,... | collective-permute-start | bytes 393224 | tf_op jit(solution)/shard_map/ppermute | solution.py:51
  14.8 6.1 %collective-permute-start.10 = (bf16[4,8192]{1,0:T(4,128)(2,1)S(1)}, bf16[4,8192]{1,0:T(4,128)(2,1)S(1)}, u32[]{:S(2)}, u32[]{:S(2)}) collective-permute-start(bf16[4,8192]{1,0:T(4,128)(2,1)S(1)} %slice_bitcast_fusion), channel_id=1, source_target_pairs={{0,12},{1,13},{2,14},{3,15},{4,8},{5,9},{6,10},{7,11},{8,4},{9,5},... | collective-permute-start | bytes 196616 | tf_op jit(solution)/shard_map/ppermute | solution.py:51
  16.9 6.6 %collective-permute-start.9 = (bf16[4,8192]{1,0:T(4,128)(2,1)S(1)}, bf16[4,8192]{1,0:T(4,128)(2,1)S(1)}, u32[]{:S(2)}, u32[]{:S(2)}) collective-permute-start(bf16[4,8192]{1,0:T(4,128)(2,1)S(1)} %slice_bitcast_fusion), channel_id=1, source_target_pairs={{0,8},{1,9},{2,10},{3,11},{4,12},{5,13},{6,14},{7,15},{8,0},{9,1},... | collective-permute-start | bytes 196616 | tf_op jit(solution)/shard_map/ppermute | solution.py:51
  17.7 6.5 %collective-permute-start.7 = (bf16[2,4,8192]{2,1,0:T(4,128)(2,1)S(1)}, bf16[2,4,8192]{2,1,0:T(4,128)(2,1)S(1)}, u32[]{:S(2)}, u32[]{:S(2)}) collective-permute-start(bf16[2,4,8192]{2,1,0:T(4,128)(2,1)S(1)} %pad_maximum_fusion.3.refs_2_), channel_id=1, source_target_pairs={{0,1},{1,0},{2,3},{3,2},{4,5},{5,4},{6,7},{7,6},{8,9},{9,8},{10,11... | collective-permute-start | bytes 393224 | tf_op jit(solution)/shard_map/ppermute | solution.py:51
  17.7 5.8 %collective-permute-start.8 = (bf16[2,4,8192]{2,1,0:T(4,128)(2,1)S(1)}, bf16[2,4,8192]{2,1,0:T(4,128)(2,1)S(1)}, u32[]{:S(2)}, u32[]{:S(2)}) collective-permute-start(bf16[2,4,8192]{2,1,0:T(4,128)(2,1)S(1)} %collective-permute-done.6.refs_3_), channel_id=1, source_target_pairs={{0,1},{1,0},{2,3},{3,2},{4,5},{5,4},{6,7},{7,6},{8,9},{9,8},{10,11... | collective-permute-start | bytes 393224 | tf_op jit(solution)/shard_map/ppermute | solution.py:51
  19.4 4.9 %collective-permute-start.3 = (bf16[4,2,4,8192]{3,2,1,0:T(4,128)(2,1)S(1)}, bf16[4,2,4,8192]{3,2,1,0:T(4,128)(2,1)S(1)}, u32[]{:S(2)}, u32[]{:S(2)}) collective-permute-start(bf16[4,2,4,8192]{3,2,1,0:T(4,128)(2,1)S(1)} %pad_maximum_fusion.refs_0_), channel_id=1, source_target_pairs={{0,1},{1,0},{2,3},{3,2},{4,5},{5,4},{6,7},{7,6},{8,9},{9,8},{10,11... | collective-permute-start | bytes 1572872 | tf_op jit(solution)/shard_map/ppermute | solution.py:51
  23.6 5.1 %collective-permute-start.14 = (bf16[2,4,8192]{2,1,0:T(4,128)(2,1)S(1)}, bf16[2,4,8192]{2,1,0:T(4,128)(2,1)S(1)}, u32[]{:S(2)}, u32[]{:S(2)}) collective-permute-start(bf16[2,4,8192]{2,1,0:T(4,128)(2,1)S(1)} %pad_maximum_fusion.4), channel_id=1, source_target_pairs={{0,2},{1,3},{2,0},{3,1},{4,6},{5,7},{6,4},{7,5},{8,10},{9,11},{10,... | collective-permute-start | bytes 393224 | tf_op jit(solution)/shard_map/ppermute | solution.py:51
  28.9 4.5 %collective-permute-start.15 = (bf16[4,4,8192]{2,1,0:T(4,128)(2,1)S(1)}, bf16[4,4,8192]{2,1,0:T(4,128)(2,1)S(1)}, u32[]{:S(2)}, u32[]{:S(2)}) collective-permute-start(bf16[4,4,8192]{2,1,0:T(4,128)(2,1)S(1)} %pad_maximum_fusion.1.refs_2_), channel_id=1, source_target_pairs={{0,1},{1,0},{2,3},{3,2},{4,5},{5,4},{6,7},{7,6},{8,9},{9,8},{10,11... | collective-permute-start | bytes 786440 | tf_op jit(solution)/shard_map/ppermute | solution.py:51
  29.0 8.6 %collective-permute-start.13 = (bf16[64,512]{1,0:T(8,128)(2,1)S(1)}, bf16[64,512]{1,0:T(8,128)(2,1)S(1)}, u32[]{:S(2)}, u32[]{:S(2)}) collective-permute-start(bf16[64,512]{1,0:T(8,128)(2,1)S(1)} %shard_map.64), channel_id=1, source_target_pairs={{0,12},{1,13},{2,14},{3,15},{4,8},{5,9},{6,10},{7,11},{8,4},{9,5},... | collective-permute-start | bytes 196616 | tf_op jit(solution)/shard_map/ppermute | solution.py:51
  31.3 6.8 %collective-permute-start.12 = (bf16[64,512]{1,0:T(8,128)(2,1)S(1)}, bf16[64,512]{1,0:T(8,128)(2,1)S(1)}, u32[]{:S(2)}, u32[]{:S(2)}) collective-permute-start(bf16[64,512]{1,0:T(8,128)(2,1)S(1)} %shard_map.64), channel_id=1, source_target_pairs={{0,8},{1,9},{2,10},{3,11},{4,12},{5,13},{6,14},{7,15},{8,0},{9,1},... | collective-permute-start | bytes 196616 | tf_op jit(solution)/shard_map/ppermute | solution.py:51
  31.4 6.8 %collective-permute-start.11 = (bf16[64,512]{1,0:T(8,128)(2,1)S(1)}, bf16[64,512]{1,0:T(8,128)(2,1)S(1)}, u32[]{:S(2)}, u32[]{:S(2)}) collective-permute-start(bf16[64,512]{1,0:T(8,128)(2,1)S(1)} %shard_map.64), channel_id=1, source_target_pairs={{0,4},{1,5},{2,6},{3,7},{4,0},{5,1},{6,2},{7,3},{8,12},{9,13},{10,... | collective-permute-start | bytes 196616 | tf_op jit(solution)/shard_map/ppermute | solution.py:51
  38.1 8.3 %collective-permute-start.17 = (bf16[4,64,512]{2,1,0:T(8,128)(2,1)S(1)}, bf16[4,64,512]{2,1,0:T(8,128)(2,1)S(1)}, u32[]{:S(2)}, u32[]{:S(2)}) collective-permute-start(bf16[4,64,512]{2,1,0:T(8,128)(2,1)S(1)} %pad_maximum_fusion.2.refs_0_), channel_id=1, source_target_pairs={{0,2},{1,3},{2,0},{3,1},{4,6},{5,7},{6,4},{7,5},{8,10},{9,11},{10,... | collective-permute-start | bytes 786440 | tf_op jit(solution)/shard_map/ppermute | solution.py:51
  44.9 1.6 %collective-permute-start.16 = (bf16[4,64,512]{2,1,0:T(8,128)(2,1)S(1)}, bf16[4,64,512]{2,1,0:T(8,128)(2,1)S(1)}, u32[]{:S(2)}, u32[]{:S(2)}) collective-permute-start(bf16[4,64,512]{2,1,0:T(8,128)(2,1)S(1)} %pad_maximum_fusion.2.refs_0_), channel_id=1, source_target_pairs={{0,1},{1,0},{2,3},{3,2},{4,5},{5,4},{6,7},{7,6},{8,9},{9,8},{10,11... | collective-permute-start | bytes 786440 | tf_op jit(solution)/shard_map/ppermute | solution.py:51
  46.5 1.5 %collective-permute-start.18 = (bf16[4,64,512]{2,1,0:T(8,128)(2,1)S(1)}, bf16[4,64,512]{2,1,0:T(8,128)(2,1)S(1)}, u32[]{:S(2)}, u32[]{:S(2)}) collective-permute-start(bf16[4,64,512]{2,1,0:T(8,128)(2,1)S(1)} %collective-permute-done.17.refs_1_), channel_id=1, source_target_pairs={{0,1},{1,0},{2,3},{3,2},{4,5},{5,4},{6,7},{7,6},{8,9},{9,8},{10,11... | collective-permute-start | bytes 786440 | tf_op jit(solution)/shard_map/ppermute | solution.py:51

commit v13 on v12

--- a/solution.py
+++ b/solution.py
@@ -76,15 +76,17 @@
         copy.start()
     for read in reads[1:]:
         read.start()
-    for copy, piece, entries in zip(copies, pieces, blocks):
+    for copy in copies:
         copy.wait()
-        for e, m in enumerate(entries):
-            rows[m * slots:(m + 1) * slots, :] = piece[e].astype(jnp.float32)
     acc = None
     for k in range(chunks):
+        part = slice(k * width, (k + 1) * width)
+        for piece, entries in zip(pieces, blocks):
+            for e, m in enumerate(entries):
+                rows[m * slots:(m + 1) * slots, part] = piece[e, :, part].astype(jnp.float32)
         reads[k].wait()
         part = jnp.dot(
-            rows[:, k * width:(k + 1) * width].astype(jnp.bfloat16),
+            rows[:, part].astype(jnp.bfloat16),
             held[k],
             preferred_element_type=jnp.float32,
         )

time: 59.5 us -> 59.5 us (level)
  no operation moved by 1% of the time
where the time goes in v13:
time: 59.5 us; the launch traced here: 59.3 us
  Pallas kernels  25.1 us (42%)
  starting transfers between devices  20.4 us (34%)
  waiting for transfers between devices  11.2 us (19%)
  other arithmetic  1.87 us (3%)
  between operations  0.77 us (1%)
    ppermute x19, starting transfers between devices, swap(): return lax.ppermute(x, 'dp', [(d, d ^ m) for d in range(n)])  20.4 us
    pallas_call x2, Pallas kernels, outer(): pl.pallas_call(functools.partial(outer_kernel, [entries for _, entries in...  16.6 us
    ppermute x19, waiting for transfers between devices, swap(): return lax.ppermute(x, 'dp', [(d, d ^ m) for d in range(n)])  11.2 us
    pallas_call x2, Pallas kernels, project(): pl.pallas_call(functools.partial(project_kernel, [entries for _, entries...  8.55 us
  transfers between devices with their start and end apart: 19, of which 8 were waited for; matrix products, arithmetic and copies ran while one was open for 3% of the time, Pallas kernels for 23%

profile of v13, /device:TPU:0, one launch (start us, length us, event | category | flops | bytes accessed | tf_op | source)
XLA Modules:
  0.0 59.3 jit_solution(10718775283767506318)
XLA Ops:
  0.0 5.0 %collective-permute-start.5 = (bf16[4,8192]{1,0:T(4,128)(2,1)}, bf16[4,8192]{1,0:T(4,128)(2,1)S(1)}, u32[]{:S(2)}, u32[]{:S(2)}) collective-permute-start(bf16[4,8192]{1,0:T(4,128)(2,1)} %param.6), channel_id=1, source_target_pairs={{0,12},{1,13},{2,14},{3,15},{4,8},{5,9},{6,10},{7,11},{8,4},{9,5},... | collective-permute-start | bytes 196616 | tf_op jit(solution)/shard_map/ppermute | solution.py:51
  5.0 0.0 collective-permute-start.4
  5.7 1.0 %or_select_fusion = bf16[2,4,8192]{2,1,0:T(4,128)(2,1)S(1)} fusion(bf16[1,4,8192]{2,1,0:T(4,128)(2,1)} %bitcast.28, bf16[1,4,8192]{2,1,0:T(4,128)(2,1)} %bitcast.29, pred[4]{0:T(512)(128)(4,1)S(1)} %iota_compare_fusion, pred[2]{0:T(512)(128)(4,1)S(1)} %iota_compare_fusion.1), kind=kLoop, calls=%fused_computation.3 | loop fusion | flops 393216 | bytes 262150 | tf_op jit(solution)/shard_map/jit(_where)/select_n | solution.py:255
  6.7 1.6 %collective-permute-start.1 = (bf16[2,4,8192]{2,1,0:T(4,128)(2,1)S(1)}, bf16[2,4,8192]{2,1,0:T(4,128)(2,1)S(1)}, u32[]{:S(2)}, u32[]{:S(2)}) collective-permute-start(bf16[2,4,8192]{2,1,0:T(4,128)(2,1)S(1)} %or_select_fusion), channel_id=1, source_target_pairs={{0,2},{1,3},{2,0},{3,1},{4,6},{5,7},{6,4},{7,5},{8,10},{9,11},{10,... | collective-permute-start | bytes 393224 | tf_op jit(solution)/shard_map/ppermute | solution.py:51
  8.3 0.8 %collective-permute-start = (bf16[2,4,8192]{2,1,0:T(4,128)(2,1)S(1)}, bf16[2,4,8192]{2,1,0:T(4,128)(2,1)S(1)}, u32[]{:S(2)}, u32[]{:S(2)}) collective-permute-start(bf16[2,4,8192]{2,1,0:T(4,128)(2,1)S(1)} %or_select_fusion), channel_id=1, source_target_pairs={{0,4},{1,5},{2,6},{3,7},{4,0},{5,1},{6,2},{7,3},{8,12},{9,13},{10,... | collective-permute-start | bytes 393224 | tf_op jit(solution)/shard_map/ppermute | solution.py:51
  9.1 0.0 collective-permute-done.5
  9.1 1.9 %collective-permute-done.4 = bf16[4,8192]{1,0:T(4,128)(2,1)S(1)} collective-permute-done((bf16[4,8192]{1,0:T(4,128)(2,1)}, bf16[4,8192]{1,0:T(4,128)(2,1)S(1)}, u32[]{:S(2)}, u32[]{:S(2)}) %collective-permute-start.4) | collective-permute-done | bytes 65568 | tf_op jit(solution)/shard_map/ppermute | solution.py:51
  10.9 0.1 pad_maximum_fusion.3.refs_2_
  11.0 1.6 %collective-permute-start.6 = (bf16[2,4,8192]{2,1,0:T(4,128)(2,1)S(1)}, bf16[2,4,8192]{2,1,0:T(4,128)(2,1)S(1)}, u32[]{:S(2)}, u32[]{:S(2)}) collective-permute-start(bf16[2,4,8192]{2,1,0:T(4,128)(2,1)S(1)} %pad_maximum_fusion.3.refs_2_), channel_id=1, source_target_pairs={{0,2},{1,3},{2,0},{3,1},{4,6},{5,7},{6,4},{7,5},{8,10},{9,11},{10,... | collective-permute-start | bytes 393224 | tf_op jit(solution)/shard_map/ppermute | solution.py:51
  12.6 0.0 collective-permute-done.1
  12.6 1.0 %collective-permute-done = bf16[2,4,8192]{2,1,0:T(4,128)(2,1)S(1)} collective-permute-done((bf16[2,4,8192]{2,1,0:T(4,128)(2,1)S(1)}, bf16[2,4,8192]{2,1,0:T(4,128)(2,1)S(1)}, u32[]{:S(2)}, u32[]{:S(2)}) %collective-permute-start) | collective-permute-done | bytes 131104 | tf_op jit(solution)/shard_map/ppermute | solution.py:51
  13.7 1.1 %collective-permute-start.2 = (bf16[2,4,8192]{2,1,0:T(4,128)(2,1)S(1)}, bf16[2,4,8192]{2,1,0:T(4,128)(2,1)S(1)}, u32[]{:S(2)}, u32[]{:S(2)}) collective-permute-start(bf16[2,4,8192]{2,1,0:T(4,128)(2,1)S(1)} %collective-permute-done), channel_id=1, source_target_pairs={{0,2},{1,3},{2,0},{3,1},{4,6},{5,7},{6,4},{7,5},{8,10},{9,11},{10,... | collective-permute-start | bytes 393224 | tf_op jit(solution)/shard_map/ppermute | solution.py:51
  14.8 2.1 %collective-permute-start.10 = (bf16[4,8192]{1,0:T(4,128)(2,1)S(1)}, bf16[4,8192]{1,0:T(4,128)(2,1)S(1)}, u32[]{:S(2)}, u32[]{:S(2)}) collective-permute-start(bf16[4,8192]{1,0:T(4,128)(2,1)S(1)} %slice_bitcast_fusion), channel_id=1, source_target_pairs={{0,12},{1,13},{2,14},{3,15},{4,8},{5,9},{6,10},{7,11},{8,4},{9,5},... | collective-permute-start | bytes 196616 | tf_op jit(solution)/shard_map/ppermute | solution.py:51
  16.9 0.8 %collective-permute-start.9 = (bf16[4,8192]{1,0:T(4,128)(2,1)S(1)}, bf16[4,8192]{1,0:T(4,128)(2,1)S(1)}, u32[]{:S(2)}, u32[]{:S(2)}) collective-permute-start(bf16[4,8192]{1,0:T(4,128)(2,1)S(1)} %slice_bitcast_fusion), channel_id=1, source_target_pairs={{0,8},{1,9},{2,10},{3,11},{4,12},{5,13},{6,14},{7,15},{8,0},{9,1},... | collective-permute-start | bytes 196616 | tf_op jit(solution)/shard_map/ppermute | solution.py:51
  17.7 0.0 collective-permute-start.7
  17.7 0.0 collective-permute-done.6.refs_3_
  17.7 0.5 collective-permute-start.8
  18.3 0.6 %collective-permute-done.2 = bf16[2,4,8192]{2,1,0:T(4,128)(2,1)S(1)} collective-permute-done((bf16[2,4,8192]{2,1,0:T(4,128)(2,1)S(1)}, bf16[2,4,8192]{2,1,0:T(4,128)(2,1)S(1)}, u32[]{:S(2)}, u32[]{:S(2)}) %collective-permute-start.2) | collective-permute-done | bytes 131104 | tf_op jit(solution)/shard_map/ppermute | solution.py:51
  18.9 0.5 pad_maximum_fusion.refs_0_
  19.4 0.1 collective-permute-start.3
  19.4 1.5 %collective-permute-done.10 = bf16[4,8192]{1,0:T(4,128)(2,1)S(1)} collective-permute-done((bf16[4,8192]{1,0:T(4,128)(2,1)S(1)}, bf16[4,8192]{1,0:T(4,128)(2,1)S(1)}, u32[]{:S(2)}, u32[]{:S(2)}) %collective-permute-start.10) | collective-permute-done | bytes 65568 | tf_op jit(solution)/shard_map/ppermute | solution.py:51
  21.0 2.6 %collective-permute-done.9 = bf16[4,8192]{1,0:T(4,128)(2,1)S(1)} collective-permute-done((bf16[4,8192]{1,0:T(4,128)(2,1)S(1)}, bf16[4,8192]{1,0:T(4,128)(2,1)S(1)}, u32[]{:S(2)}, u32[]{:S(2)}) %collective-permute-start.9) | collective-permute-done | bytes 65568 | tf_op jit(solution)/shard_map/ppermute | solution.py:51
  23.5 0.0 collective-permute-done.8.refs_5_
  23.5 0.1 pad_maximum_fusion.4
  23.6 0.6 %collective-permute-start.14 = (bf16[2,4,8192]{2,1,0:T(4,128)(2,1)S(1)}, bf16[2,4,8192]{2,1,0:T(4,128)(2,1)S(1)}, u32[]{:S(2)}, u32[]{:S(2)}) collective-permute-start(bf16[2,4,8192]{2,1,0:T(4,128)(2,1)S(1)} %pad_maximum_fusion.4), channel_id=1, source_target_pairs={{0,2},{1,3},{2,0},{3,1},{4,6},{5,7},{6,4},{7,5},{8,10},{9,11},{10,... | collective-permute-start | bytes 393224 | tf_op jit(solution)/shard_map/ppermute | solution.py:51
  24.3 0.0 collective-permute-done.7.refs_4_
  24.3 0.0 collective-permute-done.3.refs_1_
  24.3 4.4 %shard_map.64 = bf16[64,512]{1,0:T(8,128)(2,1)S(1)} custom-call(s32[1]{0:T(128)} %bitcast.own_ref, bf16[4,2,4,8192]{3,2,1,0:T(4,128)(2,1)S(1)} %pad_maximum_fusion.refs_0_, bf16[4,2,4,8192]{3,2,1,0:T(4,128)(2,1)S(1)} %collective-permute-done.3.refs_1_, bf16[2,4,8192]{2,1,0:T(4,128)(2,1)S(1)} %pad_maximum_fusion.3.refs_2_, ...), custom_call_target="tpu_custom_call" | custom-call | flops 64 | bytes 64 | tf_op jit(solution)/shard_map/pallas_call | solution.py:120
  28.7 0.0 collective-permute-done.14
  28.7 0.2 pad_maximum_fusion.1.refs_2_
  28.9 0.1 collective-permute-start.15
  29.0 2.4 %collective-permute-start.13 = (bf16[64,512]{1,0:T(8,128)(2,1)S(1)}, bf16[64,512]{1,0:T(8,128)(2,1)S(1)}, u32[]{:S(2)}, u32[]{:S(2)}) collective-permute-start(bf16[64,512]{1,0:T(8,128)(2,1)S(1)} %shard_map.64), channel_id=1, source_target_pairs={{0,12},{1,13},{2,14},{3,15},{4,8},{5,9},{6,10},{7,11},{8,4},{9,5},... | collective-permute-start | bytes 196616 | tf_op jit(solution)/shard_map/ppermute | solution.py:51
  31.3 0.0 collective-permute-start.12
  31.4 2.1 %collective-permute-start.11 = (bf16[64,512]{1,0:T(8,128)(2,1)S(1)}, bf16[64,512]{1,0:T(8,128)(2,1)S(1)}, u32[]{:S(2)}, u32[]{:S(2)}) collective-permute-start(bf16[64,512]{1,0:T(8,128)(2,1)S(1)} %shard_map.64), channel_id=1, source_target_pairs={{0,4},{1,5},{2,6},{3,7},{4,0},{5,1},{6,2},{7,3},{8,12},{9,13},{10,... | collective-permute-start | bytes 196616 | tf_op jit(solution)/shard_map/ppermute | solution.py:51
  33.4 0.0 collective-permute-done.15.refs_3_
  33.4 4.1 %shard_map.65.refs_1_.refs_3_ = bf16[4,512,64]{2,1,0:T(8,128)(2,1)S(1)} custom-call(s32[1]{0:T(128)} %bitcast.own_ref, bf16[4,2,4,8192]{3,2,1,0:T(4,128)(2,1)S(1)} %pad_maximum_fusion.refs_0_, bf16[4,2,4,8192]{3,2,1,0:T(4,128)(2,1)S(1)} %collective-permute-done.3.refs_1_, bf16[4,4,8192]{2,1,0:T(4,128)(2,1)S(1)} %pad_maximum_fusion.1.refs_2_, ...), custom_call_target="tpu_custom_call" | custom-call | flops 64 | bytes 64 | tf_op jit(solution)/shard_map/pallas_call | solution.py:120
  37.6 0.0 collective-permute-done.13
  37.6 0.5 collective-permute-done.12
  38.1 0.0 collective-permute-done.11
  38.1 1.5 %collective-permute-start.17 = (bf16[4,64,512]{2,1,0:T(8,128)(2,1)S(1)}, bf16[4,64,512]{2,1,0:T(8,128)(2,1)S(1)}, u32[]{:S(2)}, u32[]{:S(2)}) collective-permute-start(bf16[4,64,512]{2,1,0:T(8,128)(2,1)S(1)} %pad_maximum_fusion.2.refs_0_), channel_id=1, source_target_pairs={{0,2},{1,3},{2,0},{3,1},{4,6},{5,7},{6,4},{7,5},{8,10},{9,11},{10,... | collective-permute-start | bytes 786440 | tf_op jit(solution)/shard_map/ppermute | solution.py:51
  39.6 5.2 %shard_map.66.refs_5_ = bf16[4,512,8192]{2,1,0:T(8,128)(2,1)} custom-call(s32[1]{0:T(128)} %bitcast.own_ref, bf16[4,64,512]{2,1,0:T(8,128)(2,1)S(1)} %pad_maximum_fusion.2.refs_0_, bf16[4,512,64]{2,1,0:T(8,128)(2,1)S(1)} %shard_map.65.refs_1_.refs_3_, bf16[512,8192]{1,0:T(8,128)(2,1)} %refs_4_.3), custom_call_target="tpu_custom_call" | custom-call | flops 134217728 | bytes 10485760 | tf_op jit(solution)/shard_map/pallas_call | solution.py:217
  44.9 0.1 collective-permute-start.16
  45.0 1.5 %collective-permute-done.17.refs_1_ = bf16[4,64,512]{2,1,0:T(8,128)(2,1)S(1)} collective-permute-done((bf16[4,64,512]{2,1,0:T(8,128)(2,1)S(1)}, bf16[4,64,512]{2,1,0:T(8,128)(2,1)S(1)}, u32[]{:S(2)}, u32[]{:S(2)}) %collective-permute-start.17) | collective-permute-done | bytes 262176 | tf_op jit(solution)/shard_map/ppermute | solution.py:51
  46.5 0.0 collective-permute-start.18
  46.5 0.0 collective-permute-done.16.refs_0_
  46.5 1.5 %collective-permute-done.18.refs_2_ = bf16[4,64,512]{2,1,0:T(8,128)(2,1)S(1)} collective-permute-done((bf16[4,64,512]{2,1,0:T(8,128)(2,1)S(1)}, bf16[4,64,512]{2,1,0:T(8,128)(2,1)S(1)}, u32[]{:S(2)}, u32[]{:S(2)}) %collective-permute-start.18) | collective-permute-done | bytes 262176 | tf_op jit(solution)/shard_map/ppermute | solution.py:51
  48.0 11.3 %shard_map.67 = bf16[4,512,8192]{2,1,0:T(8,128)(2,1)} custom-call(s32[1]{0:T(128)} %bitcast.own_ref, bf16[4,64,512]{2,1,0:T(8,128)(2,1)S(1)} %collective-permute-done.16.refs_0_, bf16[4,64,512]{2,1,0:T(8,128)(2,1)S(1)} %collective-permute-done.17.refs_1_, bf16[4,64,512]{2,1,0:T(8,128)(2,1)S(1)} %collective-permute-done.18.refs_2_, ...), custom_call_target="tpu_custom_call", output_to_operand_aliasing={{}: (6, {})} | custom-call | flops 402653184 | bytes 31457280 | tf_op jit(solution)/shard_map/pallas_call | solution.py:217
  (4 shorter events, 0.1 us)
Async XLA Ops:
  0.0 9.1 %collective-permute-start.5 = (bf16[4,8192]{1,0:T(4,128)(2,1)}, bf16[4,8192]{1,0:T(4,128)(2,1)S(1)}, u32[]{:S(2)}, u32[]{:S(2)}) collective-permute-start(bf16[4,8192]{1,0:T(4,128)(2,1)} %param.6), channel_id=1, source_target_pairs={{0,12},{1,13},{2,14},{3,15},{4,8},{5,9},{6,10},{7,11},{8,4},{9,5},... | collective-permute-start | bytes 196616 | tf_op jit(solution)/shard_map/ppermute | solution.py:51
  5.0 5.9 %collective-permute-start.4 = (bf16[4,8192]{1,0:T(4,128)(2,1)}, bf16[4,8192]{1,0:T(4,128)(2,1)S(1)}, u32[]{:S(2)}, u32[]{:S(2)}) collective-permute-start(bf16[4,8192]{1,0:T(4,128)(2,1)} %param.6), channel_id=1, source_target_pairs={{0,8},{1,9},{2,10},{3,11},{4,12},{5,13},{6,14},{7,15},{8,0},{9,1},... | collective-permute-start | bytes 196616 | tf_op jit(solution)/shard_map/ppermute | solution.py:51
  6.7 5.9 %collective-permute-start.1 = (bf16[2,4,8192]{2,1,0:T(4,128)(2,1)S(1)}, bf16[2,4,8192]{2,1,0:T(4,128)(2,1)S(1)}, u32[]{:S(2)}, u32[]{:S(2)}) collective-permute-start(bf16[2,4,8192]{2,1,0:T(4,128)(2,1)S(1)} %or_select_fusion), channel_id=1, source_target_pairs={{0,2},{1,3},{2,0},{3,1},{4,6},{5,7},{6,4},{7,5},{8,10},{9,11},{10,... | collective-permute-start | bytes 393224 | tf_op jit(solution)/shard_map/ppermute | solution.py:51
  8.3 5.4 %collective-permute-start = (bf16[2,4,8192]{2,1,0:T(4,128)(2,1)S(1)}, bf16[2,4,8192]{2,1,0:T(4,128)(2,1)S(1)}, u32[]{:S(2)}, u32[]{:S(2)}) collective-permute-start(bf16[2,4,8192]{2,1,0:T(4,128)(2,1)S(1)} %or_select_fusion), channel_id=1, source_target_pairs={{0,4},{1,5},{2,6},{3,7},{4,0},{5,1},{6,2},{7,3},{8,12},{9,13},{10,... | collective-permute-start | bytes 393224 | tf_op jit(solution)/shard_map/ppermute | solution.py:51
  11.0 6.7 %collective-permute-start.6 = (bf16[2,4,8192]{2,1,0:T(4,128)(2,1)S(1)}, bf16[2,4,8192]{2,1,0:T(4,128)(2,1)S(1)}, u32[]{:S(2)}, u32[]{:S(2)}) collective-permute-start(bf16[2,4,8192]{2,1,0:T(4,128)(2,1)S(1)} %pad_maximum_fusion.3.refs_2_), channel_id=1, source_target_pairs={{0,2},{1,3},{2,0},{3,1},{4,6},{5,7},{6,4},{7,5},{8,10},{9,11},{10,... | collective-permute-start | bytes 393224 | tf_op jit(solution)/shard_map/ppermute | solution.py:51
  13.7 5.2 %collective-permute-start.2 = (bf16[2,4,8192]{2,1,0:T(4,128)(2,1)S(1)}, bf16[2,4,8192]{2,1,0:T(4,128)(2,1)S(1)}, u32[]{:S(2)}, u32[]{:S(2)}) collective-permute-start(bf16[2,4,8192]{2,1,0:T(4,128)(2,1)S(1)} %collective-permute-done), channel_id=1, source_target_pairs={{0,2},{1,3},{2,0},{3,1},{4,6},{5,7},{6,4},{7,5},{8,10},{9,11},{10,... | collective-permute-start | bytes 393224 | tf_op jit(solution)/shard_map/ppermute | solution.py:51
  14.8 6.1 %collective-permute-start.10 = (bf16[4,8192]{1,0:T(4,128)(2,1)S(1)}, bf16[4,8192]{1,0:T(4,128)(2,1)S(1)}, u32[]{:S(2)}, u32[]{:S(2)}) collective-permute-start(bf16[4,8192]{1,0:T(4,128)(2,1)S(1)} %slice_bitcast_fusion), channel_id=1, source_target_pairs={{0,12},{1,13},{2,14},{3,15},{4,8},{5,9},{6,10},{7,11},{8,4},{9,5},... | collective-permute-start | bytes 196616 | tf_op jit(solution)/shard_map/ppermute | solution.py:51
  16.9 6.6 %collective-permute-start.9 = (bf16[4,8192]{1,0:T(4,128)(2,1)S(1)}, bf16[4,8192]{1,0:T(4,128)(2,1)S(1)}, u32[]{:S(2)}, u32[]{:S(2)}) collective-permute-start(bf16[4,8192]{1,0:T(4,128)(2,1)S(1)} %slice_bitcast_fusion), channel_id=1, source_target_pairs={{0,8},{1,9},{2,10},{3,11},{4,12},{5,13},{6,14},{7,15},{8,0},{9,1},... | collective-permute-start | bytes 196616 | tf_op jit(solution)/shard_map/ppermute | solution.py:51
  17.7 6.5 %collective-permute-start.7 = (bf16[2,4,8192]{2,1,0:T(4,128)(2,1)S(1)}, bf16[2,4,8192]{2,1,0:T(4,128)(2,1)S(1)}, u32[]{:S(2)}, u32[]{:S(2)}) collective-permute-start(bf16[2,4,8192]{2,1,0:T(4,128)(2,1)S(1)} %pad_maximum_fusion.3.refs_2_), channel_id=1, source_target_pairs={{0,1},{1,0},{2,3},{3,2},{4,5},{5,4},{6,7},{7,6},{8,9},{9,8},{10,11... | collective-permute-start | bytes 393224 | tf_op jit(solution)/shard_map/ppermute | solution.py:51
  17.7 5.8 %collective-permute-start.8 = (bf16[2,4,8192]{2,1,0:T(4,128)(2,1)S(1)}, bf16[2,4,8192]{2,1,0:T(4,128)(2,1)S(1)}, u32[]{:S(2)}, u32[]{:S(2)}) collective-permute-start(bf16[2,4,8192]{2,1,0:T(4,128)(2,1)S(1)} %collective-permute-done.6.refs_3_), channel_id=1, source_target_pairs={{0,1},{1,0},{2,3},{3,2},{4,5},{5,4},{6,7},{7,6},{8,9},{9,8},{10,11... | collective-permute-start | bytes 393224 | tf_op jit(solution)/shard_map/ppermute | solution.py:51
  19.4 4.9 %collective-permute-start.3 = (bf16[4,2,4,8192]{3,2,1,0:T(4,128)(2,1)S(1)}, bf16[4,2,4,8192]{3,2,1,0:T(4,128)(2,1)S(1)}, u32[]{:S(2)}, u32[]{:S(2)}) collective-permute-start(bf16[4,2,4,8192]{3,2,1,0:T(4,128)(2,1)S(1)} %pad_maximum_fusion.refs_0_), channel_id=1, source_target_pairs={{0,1},{1,0},{2,3},{3,2},{4,5},{5,4},{6,7},{7,6},{8,9},{9,8},{10,11... | collective-permute-start | bytes 1572872 | tf_op jit(solution)/shard_map/ppermute | solution.py:51
  23.6 5.1 %collective-permute-start.14 = (bf16[2,4,8192]{2,1,0:T(4,128)(2,1)S(1)}, bf16[2,4,8192]{2,1,0:T(4,128)(2,1)S(1)}, u32[]{:S(2)}, u32[]{:S(2)}) collective-permute-start(bf16[2,4,8192]{2,1,0:T(4,128)(2,1)S(1)} %pad_maximum_fusion.4), channel_id=1, source_target_pairs={{0,2},{1,3},{2,0},{3,1},{4,6},{5,7},{6,4},{7,5},{8,10},{9,11},{10,... | collective-permute-start | bytes 393224 | tf_op jit(solution)/shard_map/ppermute | solution.py:51
  28.9 4.5 %collective-permute-start.15 = (bf16[4,4,8192]{2,1,0:T(4,128)(2,1)S(1)}, bf16[4,4,8192]{2,1,0:T(4,128)(2,1)S(1)}, u32[]{:S(2)}, u32[]{:S(2)}) collective-permute-start(bf16[4,4,8192]{2,1,0:T(4,128)(2,1)S(1)} %pad_maximum_fusion.1.refs_2_), channel_id=1, source_target_pairs={{0,1},{1,0},{2,3},{3,2},{4,5},{5,4},{6,7},{7,6},{8,9},{9,8},{10,11... | collective-permute-start | bytes 786440 | tf_op jit(solution)/shard_map/ppermute | solution.py:51
  29.0 8.6 %collective-permute-start.13 = (bf16[64,512]{1,0:T(8,128)(2,1)S(1)}, bf16[64,512]{1,0:T(8,128)(2,1)S(1)}, u32[]{:S(2)}, u32[]{:S(2)}) collective-permute-start(bf16[64,512]{1,0:T(8,128)(2,1)S(1)} %shard_map.64), channel_id=1, source_target_pairs={{0,12},{1,13},{2,14},{3,15},{4,8},{5,9},{6,10},{7,11},{8,4},{9,5},... | collective-permute-start | bytes 196616 | tf_op jit(solution)/shard_map/ppermute | solution.py:51
  31.3 6.8 %collective-permute-start.12 = (bf16[64,512]{1,0:T(8,128)(2,1)S(1)}, bf16[64,512]{1,0:T(8,128)(2,1)S(1)}, u32[]{:S(2)}, u32[]{:S(2)}) collective-permute-start(bf16[64,512]{1,0:T(8,128)(2,1)S(1)} %shard_map.64), channel_id=1, source_target_pairs={{0,8},{1,9},{2,10},{3,11},{4,12},{5,13},{6,14},{7,15},{8,0},{9,1},... | collective-permute-start | bytes 196616 | tf_op jit(solution)/shard_map/ppermute | solution.py:51
  31.4 6.8 %collective-permute-start.11 = (bf16[64,512]{1,0:T(8,128)(2,1)S(1)}, bf16[64,512]{1,0:T(8,128)(2,1)S(1)}, u32[]{:S(2)}, u32[]{:S(2)}) collective-permute-start(bf16[64,512]{1,0:T(8,128)(2,1)S(1)} %shard_map.64), channel_id=1, source_target_pairs={{0,4},{1,5},{2,6},{3,7},{4,0},{5,1},{6,2},{7,3},{8,12},{9,13},{10,... | collective-permute-start | bytes 196616 | tf_op jit(solution)/shard_map/ppermute | solution.py:51
  38.1 8.3 %collective-permute-start.17 = (bf16[4,64,512]{2,1,0:T(8,128)(2,1)S(1)}, bf16[4,64,512]{2,1,0:T(8,128)(2,1)S(1)}, u32[]{:S(2)}, u32[]{:S(2)}) collective-permute-start(bf16[4,64,512]{2,1,0:T(8,128)(2,1)S(1)} %pad_maximum_fusion.2.refs_0_), channel_id=1, source_target_pairs={{0,2},{1,3},{2,0},{3,1},{4,6},{5,7},{6,4},{7,5},{8,10},{9,11},{10,... | collective-permute-start | bytes 786440 | tf_op jit(solution)/shard_map/ppermute | solution.py:51
  44.9 1.6 %collective-permute-start.16 = (bf16[4,64,512]{2,1,0:T(8,128)(2,1)S(1)}, bf16[4,64,512]{2,1,0:T(8,128)(2,1)S(1)}, u32[]{:S(2)}, u32[]{:S(2)}) collective-permute-start(bf16[4,64,512]{2,1,0:T(8,128)(2,1)S(1)} %pad_maximum_fusion.2.refs_0_), channel_id=1, source_target_pairs={{0,1},{1,0},{2,3},{3,2},{4,5},{5,4},{6,7},{7,6},{8,9},{9,8},{10,11... | collective-permute-start | bytes 786440 | tf_op jit(solution)/shard_map/ppermute | solution.py:51
  46.5 1.5 %collective-permute-start.18 = (bf16[4,64,512]{2,1,0:T(8,128)(2,1)S(1)}, bf16[4,64,512]{2,1,0:T(8,128)(2,1)S(1)}, u32[]{:S(2)}, u32[]{:S(2)}) collective-permute-start(bf16[4,64,512]{2,1,0:T(8,128)(2,1)S(1)} %collective-permute-done.17.refs_1_), channel_id=1, source_target_pairs={{0,1},{1,0},{2,3},{3,2},{4,5},{5,4},{6,7},{7,6},{8,9},{9,8},{10,11... | collective-permute-start | bytes 786440 | tf_op jit(solution)/shard_map/ppermute | solution.py:51
